TPU v7x, 32 devices: a whole 2x2x4 slice. The times are simulated.
32 devices in a mesh: date: 16 (over z, x, core), row: 2 (over y).
Axes of the slice: x: 2, y: 2, z: 4, core: 2. Of those that a mesh axis runs over, the one named last changes fastest.
Arguments:
- tokens: bfloat16 [32, 32, 16, 384], P('date', 'row'), may hold values from -6 to 6
- clear_flags: int32 [32, 32, 16], P('date', 'row'), may hold values 0 or 1
- date_numbers: int32 [32], P('date'), may hold values from 0 to 255, as said below
- decay_slopes: float32 [12], replicated, may hold values from 0.001953125 to 0.03
- time_project: bfloat16 [384, 1152], replicated, may hold values from -0.35 to 0.35
- time_output: bfloat16 [384, 384], replicated, may hold values from -0.3125 to 0.3125
- column_project: bfloat16 [384, 1152], replicated, may hold values from -0.35 to 0.35
- column_output: bfloat16 [384, 384], replicated, may hold values from -0.3125 to 0.3125
- cotangent: bfloat16 [32, 32, 16, 384], P('date', 'row'), may hold values from -6 to 6
Outputs:
- mixed_tokens: bfloat16 [32, 32, 16, 384], P('date', 'row')
- column_project_grad: float32 [384, 1152], P('row', 'date')
- column_output_grad: float32 [384, 384], P('row', 'date')
Inputs may be any that keep to these rules, and one draw needn't show every extreme that they name: `date_numbers`: strictly increasing; consecutive dates lie 1 to 15 days apart.
All inputs are finite; a program needn't handle non-finite values. No bound on the sum of `clear_flags` on one device may be relied on, other than what follows from the above.
Results may differ from a plain program's by a relative error of at most 0.018.
The roundings to bfloat16 on the way count: a program that leaves them out, or rounds other values in their place, can miss the bound.
Values may be sent and summed in bfloat16 or wider, within the bound.
No kernel may reach another device: no remote copies, remote signals or barrier semaphores. Data moves between devices by JAX's collectives and lax.ppermute only.
A program may use at most 64 MiB of HBM per device.

v0:
```python
import math

import jax
import jax.numpy as jnp
from jax import lax
from jax.sharding import PartitionSpec as P

epsilon = 1e-06
masked_score = -1e30


def rms_norm(values):
    widened = values.astype(jnp.float32)
    factor = lax.rsqrt(jnp.mean(widened * widened, axis=-1, keepdims=True) + epsilon)
    return (widened * factor).astype(jnp.bfloat16)


def softmax_rows(scores):
    top_score = jnp.max(scores, axis=-1, keepdims=True)
    raised = jnp.exp(scores - top_score)
    return raised / jnp.sum(raised, axis=-1, keepdims=True)


def matmul(left, right):
    return jnp.dot(left, right, preferred_element_type=jnp.float32)


def contract_rows(left, right):
    return lax.dot_general(
        left, right, (((0,), (0,)), ((), ())), preferred_element_type=jnp.float32
    )


def contract_last(left, right):
    return lax.dot_general(
        left, right, (((1,), (1,)), ((), ())), preferred_element_type=jnp.float32
    )


def body(
    tokens,
    clear_flags,
    date_numbers,
    decay_slopes,
    time_project,
    time_output,
    column_project,
    column_output,
    cotangent,
):
    date_local, row_local, column_count, model_width = tokens.shape
    head_count = decay_slopes.shape[0]
    head_size = model_width // head_count
    inverse_root = 1.0 / math.sqrt(head_size)
    patch_count = row_local * column_count
    flat_tokens = tokens.reshape(date_local, patch_count, model_width)
    flags_low = clear_flags.reshape(date_local, patch_count).astype(jnp.bfloat16)
    normed = rms_norm(flat_tokens)
    normed_moved, flags_moved = (
        lax.all_to_all(normed, "date", split_axis=1, concat_axis=0, tiled=True),
        lax.all_to_all(flags_low, "date", split_axis=1, concat_axis=0, tiled=True),
    )
    moved = matmul(normed_moved.reshape(-1, model_width), time_project).astype(jnp.bfloat16)
    moved = moved.reshape(normed_moved.shape[0], normed_moved.shape[1], 3 * model_width)
    numbers_all = lax.all_gather(date_numbers, "date", axis=0, tiled=True)
    date_count = moved.shape[0]
    local_patches = moved.shape[1]
    split_heads = moved.reshape(date_count, local_patches, 3, head_count, head_size)
    gap_days = jnp.abs(numbers_all[:, None] - numbers_all[None, :]).astype(jnp.float32)
    time_bias = -decay_slopes[:, None, None] * gap_days[None, :, :]
    positions = jnp.arange(date_count)
    same_date = positions[:, None] == positions[None, :]

    def time_patch(patch_index, buffer):
        series = lax.dynamic_index_in_dim(split_heads, patch_index, 1, keepdims=False)
        day_flags = lax.dynamic_index_in_dim(flags_moved, patch_index, 1, keepdims=False)
        scores = jnp.einsum(
            "qhe,khe->hqk", series[:, 0], series[:, 1], preferred_element_type=jnp.float32
        )
        scores = scores * inverse_root + time_bias
        allowed = (day_flags[None, :] > 0) | same_date
        scores = jnp.where(allowed[None], scores, masked_score)
        weights_low = softmax_rows(scores).astype(jnp.bfloat16)
        patch_heads = jnp.einsum(
            "hqk,khe->qhe", weights_low, series[:, 2], preferred_element_type=jnp.float32
        )
        patch_heads = patch_heads.astype(jnp.bfloat16).reshape(date_count, model_width)
        return lax.dynamic_update_index_in_dim(buffer, patch_heads, patch_index, 1)

    empty_heads = jnp.zeros((date_count, local_patches, model_width), jnp.bfloat16)
    time_heads = lax.fori_loop(0, local_patches, time_patch, empty_heads)
    returned = lax.all_to_all(time_heads, "date", split_axis=0, concat_axis=1, tiled=True)
    update = matmul(returned.reshape(-1, model_width), time_output)
    hidden = (flat_tokens.reshape(-1, model_width).astype(jnp.float32) + update).astype(
        jnp.bfloat16
    )
    hidden = hidden.reshape(date_local, row_local, column_count, model_width)
    plane, plane_grad = (
        lax.all_to_all(hidden, "row", split_axis=2, concat_axis=1, tiled=True),
        lax.all_to_all(cotangent, "row", split_axis=2, concat_axis=1, tiled=True),
    )
    row_count = plane.shape[1]
    local_columns = plane.shape[2]

    def column_date(totals, inputs):
        plane_one, grad_one = inputs
        column_normed = rms_norm(plane_one).reshape(-1, model_width)
        column_qkv = matmul(column_normed, column_project).astype(jnp.bfloat16)
        column_qkv = column_qkv.reshape(row_count, local_columns, 3, head_count, head_size)
        queries = column_qkv[:, :, 0]
        key_block = column_qkv[:, :, 1]
        value_block = column_qkv[:, :, 2]
        column_scores = (
            jnp.einsum("ache,bche->chab", queries, key_block, preferred_element_type=jnp.float32)
            * inverse_root
        )
        weights = softmax_rows(column_scores)
        column_low = weights.astype(jnp.bfloat16)
        column_heads = jnp.einsum(
            "chab,bche->ache", column_low, value_block, preferred_element_type=jnp.float32
        )
        column_heads = column_heads.astype(jnp.bfloat16).reshape(-1, model_width)
        result = plane_one.reshape(-1, model_width).astype(jnp.float32) + matmul(
            column_heads, column_output
        )
        result = result.astype(jnp.bfloat16).reshape(row_count, local_columns, model_width)
        grad_flat = grad_one.reshape(-1, model_width)
        output_term = contract_rows(column_heads, grad_flat)
        heads_grad = contract_last(grad_flat, column_output).astype(jnp.bfloat16)
        heads_grad = heads_grad.reshape(row_count, local_columns, head_count, head_size)
        product_grad = jnp.einsum(
            "ache,bche->chab", heads_grad, value_block, preferred_element_type=jnp.float32
        )
        score_grad = weights * (
            product_grad - jnp.sum(weights * product_grad, axis=-1, keepdims=True)
        )
        score_low = score_grad.astype(jnp.bfloat16)
        query_grad = jnp.einsum(
            "chab,bche->ache", score_low, key_block, preferred_element_type=jnp.float32
        )
        query_grad = (query_grad * inverse_root).astype(jnp.bfloat16)
        key_grad = jnp.einsum(
            "chab,ache->bche", score_low, queries, preferred_element_type=jnp.float32
        )
        key_grad = (key_grad * inverse_root).astype(jnp.bfloat16)
        value_grad = jnp.einsum(
            "chab,ache->bche", column_low, heads_grad, preferred_element_type=jnp.float32
        )
        value_grad = value_grad.astype(jnp.bfloat16)
        qkv_grad = jnp.stack([query_grad, key_grad, value_grad], axis=2).reshape(
            -1, 3 * model_width
        )
        project_term = contract_rows(column_normed, qkv_grad)
        return ((totals[0] + project_term, totals[1] + output_term), result)

    start = (
        jnp.zeros((model_width, 3 * model_width), jnp.float32),
        jnp.zeros((model_width, model_width), jnp.float32),
    )
    totals, result_planes = lax.scan(column_date, start, (plane, plane_grad))
    project_grad, output_grad = totals
    mixed_tokens = lax.all_to_all(result_planes, "row", split_axis=1, concat_axis=2, tiled=True)
    partial_project, partial_output = (
        lax.psum_scatter(
            project_grad.astype(jnp.bfloat16), "row", scatter_dimension=0, tiled=True
        ).astype(jnp.float32),
        lax.psum_scatter(
            output_grad.astype(jnp.bfloat16), "row", scatter_dimension=0, tiled=True
        ).astype(jnp.float32),
    )
    owned_project, owned_output = (
        lax.psum_scatter(partial_project, "date", scatter_dimension=1, tiled=True),
        lax.psum_scatter(partial_output, "date", scatter_dimension=1, tiled=True),
    )
    return (mixed_tokens, owned_project, owned_output)


def solution(mesh):
    return jax.shard_map(
        body,
        mesh=mesh,
        in_specs=(
            P("date", "row", None, None),
            P("date", "row", None),
            P("date"),
            P(),
            P(),
            P(),
            P(),
            P(),
            P("date", "row", None, None),
        ),
        out_specs=(P("date", "row", None, None), P("row", "date"), P("row", "date")),
        check_vma=False,
    )
```

profile of v0, /device:TPU:0, one launch (start us, length us, event | category | flops | bytes accessed | tf_op | source)
XLA Modules:
  0.0 403.9 jit_solution(16900925978195966536)
XLA Ops:
  7.2 1.4 copy_convert_fusion
  8.6 7.4 %all-to-all-start.1 = ((bf16[2,16,16]{2,0,1:T(2,128)(2,1)}), bf16[2,16,16]{2,0,1:T(2,128)(2,1)S(1)}, u32[]{:S(2)}, u32[]{:S(2)}) async-start(bf16[2,16,16]{2,0,1:T(2,128)(2,1)} %copy_convert_fusion), calls=%async_computation.1 | async-start | bytes 16384 | tf_op jit(solution)/shard_map/all_to_all | solution.py:61
  15.9 1.4 copy.149
  19.9 2.3 all-to-all-done.1
  22.3 3.7 all-to-all-start
  27.5 12.5 %all-reduce = s32[32]{0:T(128)S(1)} all-reduce(s32[32]{0:T(128)S(1)} %dynamic-update-slice), channel_id=1, replica_groups=mesh['date'=16,'row'=2] {'date'}, use_global_device_ids=true, to_apply=%add | all-reduce | flops 32 | bytes 256
  41.1 5.9 %reshape_reshape.4 = bf16[32,16,3,12,32]{4,3,2,1,0:T(8,128)(2,1)} reshape(bf16[512,1152]{1,0:T(8,128)(2,1)S(1)} %convolution_convert_fusion.5) | data formatting | bytes 2359296 | tf_op jit(solution)/shard_map/reshape;reshape | solution.py:68
  47.0 10.5 %copy.154 = bf16[32,16,3,12,32]{4,0,3,2,1:T(8,128)(2,1)} copy(bf16[32,16,3,12,32]{4,3,2,1,0:T(8,128)(2,1)} %reshape_reshape.4) | data formatting | bytes 2359296
  57.5 61.1 %while.29 = (s32[]{:T(128)}, bf16[32,16,384]{2,1,0:T(8,128)(2,1)}, bf16[32,16,3,12,32]{4,0,3,2,1:T(8,128)(2,1)}, bf16[32,16]{0,1:T(8,128)(2,1)S(1)}, f32[32,32]{...) while((s32[]{:T(128)}, bf16[32,16,384]{2,1,0:T(8,128)(2,1)}, ...), condition=%wide.region_4.5_spmd.clone, body=%wide.region_1.4_spmd.clone.sunk | while | flops 1698336 | bytes 713441 | solution.py:91
  59.2 2.1 dynamic_update_slice.17
  63.0 2.1 dynamic_update_slice.17
  66.8 2.1 dynamic_update_slice.17
  70.7 2.1 dynamic_update_slice.17
  74.5 2.1 dynamic_update_slice.17
  78.3 2.1 dynamic_update_slice.17
  82.1 2.1 dynamic_update_slice.17
  85.9 2.1 dynamic_update_slice.17
  89.7 2.1 dynamic_update_slice.17
  93.5 2.1 dynamic_update_slice.17
  97.4 2.1 dynamic_update_slice.17
  101.2 2.1 dynamic_update_slice.17
  105.0 2.1 dynamic_update_slice.17
  108.8 2.1 dynamic_update_slice.17
  112.6 2.1 dynamic_update_slice.17
  116.4 2.1 dynamic_update_slice.17
  118.5 3.7 all-to-all-start.2
  123.1 11.2 %all-to-all-done.2 = bf16[32,16,384]{2,1,0:T(8,128)(2,1)S(1)} async-done(((bf16[32,16,384]{2,1,0:T(8,128)(2,1)}), bf16[32,16,384]{2,1,0:T(8,128)(2,1)S(1)}, u32[]{:S(2)}, u32[]{:S(2)}) %all-to-all-start.2) | async-done | bytes 393248 | tf_op jit(solution)/shard_map/all_to_all | solution.py:92
  134.4 3.5 all-to-all-start.4
  139.2 5.8 %all-to-all-done.4 = bf16[2,16,16,384]{3,1,0,2:T(8,128)(2,1)S(1)} async-done(((bf16[2,16,16,384]{3,1,0,2:T(8,128)(2,1)}), bf16[2,16,16,384]{3,1,0,2:T(8,128)(2,1)S(1)}, u32[]{:S(2)}, u32[]{:S(2)}) %all-to-all-start.4) | async-done | bytes 393248 | tf_op jit(solution)/shard_map/all_to_all | solution.py:100
  145.0 3.5 all-to-all-start.3
  149.4 5.3 %all-to-all-done.3 = bf16[2,16,16,384]{3,1,0,2:T(8,128)(2,1)S(1)} async-done(((bf16[2,16,16,384]{3,1,0,2:T(8,128)(2,1)}), bf16[2,16,16,384]{3,1,0,2:T(8,128)(2,1)S(1)}, u32[]{:S(2)}, u32[]{:S(2)}) %all-to-all-start.3) | async-done | bytes 393248 | tf_op jit(solution)/shard_map/all_to_all | solution.py:99
  155.6 86.8 %while.30 = (s32[]{:T(128)}, f32[384,1152]{1,0:T(8,128)}, f32[384,384]{1,0:T(8,128)}, bf16[2,32,8,384]{3,2,0,1:T(8,128)(2,1)}, bf16[2,32,8,384]{3,2,1,0:T(8,128)...) while((s32[]{:T(128)}, f32[384,1152]{1,0:T(8,128)}, ...), condition=%wide.region_10.11_spmd.clone, body=%wide.region_5.10_spmd.clone.sunk | while | flops 722531584 | bytes 45413236 | solution.py:160
  156.8 1.8 convolution_convert_fusion.11
  158.6 3.5 reshape.192
  162.1 3.7 fusion.118
  165.8 2.6 fusion.119
  168.3 3.3 fusion.123
  171.6 2.7 copy.235
  175.1 2.1 convolution_add_fusion.7
  180.2 1.7 copy.233
  181.9 2.9 multiply_reduce_fusion.3
  189.1 2.7 copy.234
  191.8 4.1 %reshape.193 = bf16[256,1152]{1,0:T(8,128)(2,1)S(1)} reshape(bf16[32,8,3,12,32]{4,3,2,1,0:T(8,128)(2,1)} %copy.234) | data formatting | bytes 1179648 | tf_op jit(solution)/shard_map/while/body/eval_jaxpr/reshape | solution.py:150
  195.9 1.8 convolution_add_fusion.6
  200.1 1.8 convolution_convert_fusion.11
  201.9 3.5 reshape.192
  205.4 3.7 fusion.118
  209.1 2.6 fusion.119
  211.6 3.3 fusion.123
  214.9 2.7 copy.235
  218.4 2.3 convolution_add_fusion.7
  223.8 1.7 copy.233
  225.5 2.9 multiply_reduce_fusion.3
  232.6 2.7 copy.234
  235.3 4.1 %reshape.193 = bf16[256,1152]{1,0:T(8,128)(2,1)S(1)} reshape(bf16[32,8,3,12,32]{4,3,2,1,0:T(8,128)(2,1)} %copy.234) | data formatting | bytes 1179648 | tf_op jit(solution)/shard_map/while/body/eval_jaxpr/reshape | solution.py:150
  239.4 1.8 convolution_add_fusion.6
  242.5 1.4 copy.165
  245.8 1.6 copy.179
  247.4 7.8 %reduce-scatter.15.cloned.1.call-done = bf16[192,384]{1,0:T(8,128)(2,1)} async-done(((bf16[384,384]{1,0:T(8,128)(2,1)}), bf16[192,384]{1,0:T(8,128)(2,1)}) %reduce-scatter.15.cloned.1.call-update) | async-done | bytes 147472
  257.1 18.9 %reduce-scatter.13.cloned.1.call-done = bf16[192,1152]{1,0:T(8,128)(2,1)} async-done(((bf16[384,1152]{1,0:T(8,128)(2,1)}), bf16[192,1152]{1,0:T(8,128)(2,1)}) %reduce-scatter.13.cloned.1.call-update) | async-done | bytes 442384
  276.0 1.2 copy.180
  278.4 9.2 %all_to_all.100 = bf16[2,32,8,384]{3,2,0,1:T(8,128)(2,1)S(1)} all-to-all(bf16[2,32,8,384]{3,2,0,1:T(8,128)(2,1)S(1)} %copy-done.14), channel_id=1, replica_groups=mesh['date'=16,'row'=2] {'row'}, dimensions={1} | all-to-all | bytes 786432 | tf_op jit(solution)/shard_map/all_to_all | solution.py:162
  288.5 47.2 %reduce-scatter.11.cloned.1.call-done = f32[192,24]{0,1:T(8,128)} async-done(((f32[192,384]{0,1:T(8,128)}), f32[192,24]{0,1:T(8,128)}) %reduce-scatter.11.cloned.1.call-update) | async-done | bytes 18448 | tf_op jit(solution)/shard_map/reduce_scatter | solution.py:173
  335.7 61.7 %reduce-scatter.9.cloned.1.call-done = f32[192,72]{0,1:T(8,128)} async-done(((f32[192,1152]{0,1:T(8,128)}), f32[192,72]{0,1:T(8,128)}) %reduce-scatter.9.cloned.1.call-update) | async-done | bytes 55312 | tf_op jit(solution)/shard_map/reduce_scatter | solution.py:172
  (231 shorter events, 61.5 us)
Async XLA Ops:
  7.2 33.1 %copy-start = (bf16[384,1152]{1,0:T(8,128)(2,1)S(1)}, bf16[384,1152]{1,0:T(8,128)(2,1)}, u32[]{:S(2)}) copy-start(bf16[384,1152]{1,0:T(8,128)(2,1)} %param.17) | copy-start | bytes 2654212
  8.6 13.7 %all-to-all-start.1 = ((bf16[2,16,16]{2,0,1:T(2,128)(2,1)}), bf16[2,16,16]{2,0,1:T(2,128)(2,1)S(1)}, u32[]{:S(2)}, u32[]{:S(2)}) async-start(bf16[2,16,16]{2,0,1:T(2,128)(2,1)} %copy_convert_fusion), calls=%async_computation.1 | async-start | bytes 16384 | tf_op jit(solution)/shard_map/all_to_all | solution.py:61
  17.4 8.6 %copy-start.16 = (f32[12]{0:T(128)S(1)}, f32[12]{0:T(128)}, u32[]{:S(2)}) copy-start(f32[12]{0:T(128)} %param.16) | copy-start | bytes 148
  17.4 8.6 %copy-start.18 = (u32[32]{0:T(128)S(1)}, u32[32]{0:T(128)}, u32[]{:S(2)}) copy-start(u32[32]{0:T(128)} %constant.104) | copy-start | bytes 388
  17.4 9.9 %copy-start.17 = (s32[2]{0:T(128)S(1)}, s32[2]{0:T(128)}, u32[]{:S(2)}) copy-start(s32[2]{0:T(128)} %param.15) | copy-start | bytes 28
  22.3 17.9 %all-to-all-start = ((bf16[2,256,384]{2,0,1:T(2,128)(2,1)}), bf16[2,256,384]{2,0,1:T(2,128)(2,1)S(1)}, u32[]{:S(2)}, u32[]{:S(2)}) async-start(bf16[2,256,384]{2,0,1:T(2,128)(2,1)} %fusion.47), calls=%async_computation | async-start | bytes 786432 | tf_op jit(solution)/shard_map/all_to_all | solution.py:60
  57.5 64.8 %copy-start.10 = (bf16[2,16,16,384]{3,2,1,0:T(8,128)(2,1)S(1)}, bf16[2,16,16,384]{3,2,1,0:T(8,128)(2,1)}, u32[]{:S(2)}) copy-start(bf16[2,16,16,384]{3,2,1,0:T(8,128)(2,1)} %param.13) | copy-start | bytes 1179652
  118.5 3.8 copy-start.11
  118.5 15.8 %all-to-all-start.2 = ((bf16[32,16,384]{2,1,0:T(8,128)(2,1)}), bf16[32,16,384]{2,1,0:T(8,128)(2,1)S(1)}, u32[]{:S(2)}, u32[]{:S(2)}) async-start(bf16[32,16,384]{2,1,0:T(8,128)(2,1)} %get-tuple-element.156), calls=%async_computation.2 | async-start | bytes 786432 | tf_op jit(solution)/shard_map/all_to_all | solution.py:92
  122.2 15.7 %copy-start.15 = (bf16[384,384]{1,0:T(8,128)(2,1)S(1)}, bf16[384,384]{1,0:T(8,128)(2,1)}, u32[]{:S(2)}) copy-start(bf16[384,384]{1,0:T(8,128)(2,1)} %param.18) | copy-start | bytes 884740
  134.4 10.6 %all-to-all-start.4 = ((bf16[2,16,16,384]{3,1,0,2:T(8,128)(2,1)}), bf16[2,16,16,384]{3,1,0,2:T(8,128)(2,1)S(1)}, u32[]{:S(2)}, u32[]{:S(2)}) async-start(bf16[2,16,16,384]{3,1,0,2:T(8,128)(2,1)} %copy.160), calls=%async_computation.4 | async-start | bytes 786432 | tf_op jit(solution)/shard_map/all_to_all | solution.py:100
  138.3 17.3 %copy-start.7 = (bf16[384,384]{1,0:T(8,128)(2,1)S(1)}, bf16[384,384]{1,0:T(8,128)(2,1)}, u32[]{:S(2)}) copy-start(bf16[384,384]{1,0:T(8,128)(2,1)} %param.20) | copy-start | bytes 884740
  145.0 9.8 %all-to-all-start.3 = ((bf16[2,16,16,384]{3,1,0,2:T(8,128)(2,1)}), bf16[2,16,16,384]{3,1,0,2:T(8,128)(2,1)S(1)}, u32[]{:S(2)}, u32[]{:S(2)}) async-start(bf16[2,16,16,384]{3,1,0,2:T(8,128)(2,1)} %copy.158), calls=%async_computation.3 | async-start | bytes 786432 | tf_op jit(solution)/shard_map/all_to_all | solution.py:99
  148.4 106.8 %reduce-scatter.15.cloned.1.call-start = ((), (), s32[]{:S(2)}) async-start(), calls=%async_computation.13 | async-start | bytes 442368
  165.8 2.6 copy-start.1
  175.0 2.1 copy-start.12
  175.1 4.1 %copy-start.9 = (bf16[2,32,8,384]{3,2,1,0:T(8,128)(2,1)S(1)}, bf16[2,32,8,384]{3,2,1,0:T(8,128)(2,1)}, u32[]{:S(2)}) copy-start(bf16[2,32,8,384]{3,2,1,0:T(8,128)(2,1)} %get-tuple-element.419) | copy-start | bytes 1179652 | tf_op jit(solution)/shard_map/while
  178.4 0.7 copy-start.13
  181.9 2.9 copy-start.6
  184.9 1.2 copy-start.2
  186.8 1.1 copy-start.8
  191.8 4.1 %copy-start.3 = (f32[384,1152]{1,0:T(8,128)S(1)}, f32[384,1152]{1,0:T(8,128)}, u32[]{:S(2)}) copy-start(f32[384,1152]{1,0:T(8,128)} %get-tuple-element.404) | copy-start | bytes 5308420 | tf_op jit(solution)/shard_map/while
  197.7 1.2 copy-start.4
  209.1 2.6 copy-start.1
  218.3 2.4 copy-start.12
  218.4 4.3 %copy-start.9 = (bf16[2,32,8,384]{3,2,1,0:T(8,128)(2,1)S(1)}, bf16[2,32,8,384]{3,2,1,0:T(8,128)(2,1)}, u32[]{:S(2)}) copy-start(bf16[2,32,8,384]{3,2,1,0:T(8,128)(2,1)} %get-tuple-element.419) | copy-start | bytes 1179652 | tf_op jit(solution)/shard_map/while
  221.9 0.7 copy-start.13
  225.5 2.9 copy-start.6
  228.4 1.2 copy-start.2
  230.3 1.1 copy-start.8
  235.3 4.1 %copy-start.3 = (f32[384,1152]{1,0:T(8,128)S(1)}, f32[384,1152]{1,0:T(8,128)}, u32[]{:S(2)}) copy-start(f32[384,1152]{1,0:T(8,128)} %get-tuple-element.404) | copy-start | bytes 5308420 | tf_op jit(solution)/shard_map/while
  241.2 1.2 copy-start.4
  242.5 2.4 copy-start.5
  244.8 31.3 %reduce-scatter.13.cloned.1.call-start = ((), (), s32[]{:S(2)}) async-start(), calls=%async_computation.12 | async-start | bytes 1327104
  247.4 88.3 %reduce-scatter.11.cloned.1.call-start = ((), (), s32[]{:S(2)}) async-start(), calls=%async_computation.11 | async-start | bytes 417792 | tf_op jit(solution)/shard_map/reduce_scatter | solution.py:173
  257.1 140.3 %reduce-scatter.9.cloned.1.call-start = ((), (), s32[]{:S(2)}) async-start(), calls=%async_computation.10 | async-start | bytes 1253376 | tf_op jit(solution)/shard_map/reduce_scatter | solution.py:172
  277.3 1.1 copy-start.14
Sparse Core Ops, SparseCore 0:
  244.9 10.2 reduce-scatter.14
  257.5 18.5 reduce-scatter.12
  280.1 55.5 reduce-scatter.10
  340.2 57.1 reduce-scatter.8
where the time goes:
time: 406 us; the launch traced here: 404 us
  waiting for transfers between devices  160 us (39%)
  local copies, waits for them, and re-layouts  128 us (32%)
  matrix products  43.4 us (11%)
  starting transfers between devices  21.8 us (5%)
  blocking collectives  21.7 us (5%)
  between operations  14.7 us (4%)
  other arithmetic  12.7 us (3%)
    reduce_scatter x1, waiting for transfers between devices, body(): lax.psum_scatter(partial_project, 'date', scatter_dimension=1, tiled=True)  61.7 us
    reduce_scatter x1, waiting for transfers between devices, body(): lax.psum_scatter(partial_output, 'date', scatter_dimension=1, tiled=True)  47.2 us
    dynamic_update_slice x32, local copies, waits for them, and re-layouts, time_patch(): return lax.dynamic_update_index_in_dim(buffer, patch_heads, patch_index, 1)  36.1 us
    unnamed x6, waiting for transfers between devices  26.8 us
    unnamed x30, local copies, waits for them, and re-layouts  17 us
    squeeze x16, local copies, waits for them, and re-layouts, time_patch(): lax.dynamic_index_in_dim(split_heads, patch_index, 1, keepdims=False)  15.7 us
    unnamed x1, blocking collectives  12.5 us
    all_to_all x1, waiting for transfers between devices, body(): lax.all_to_all(time_heads, 'date', split_axis=0, concat_axis=1, tiled=True)  11.2 us
  transfers between devices with their start and end apart: 9, of which 8 were waited for; matrix products, arithmetic and copies ran while one was open for 4% of the time, Pallas kernels for 0%

commit v1 on v0

v1 whole, which is shorter than its diff:
```python
import functools
import math

import jax
import jax.numpy as jnp
from jax import lax
from jax.experimental import pallas as pl
from jax.experimental.pallas import tpu as pltpu
from jax.sharding import PartitionSpec as P

epsilon = 1e-06
masked_score = -1e30
vmem_limit = 48 * 1024 * 1024
low = jnp.bfloat16
wide = jnp.float32


def rms_norm(values):
    factor = lax.rsqrt(jnp.mean(values * values, axis=-1, keepdims=True) + epsilon)
    return (values * factor).astype(low)


def matmul(left, right):
    return jnp.dot(left, right, preferred_element_type=wide)


def contract_rows(left, right):
    return lax.dot_general(left, right, (((0,), (0,)), ((), ())), preferred_element_type=wide)


def contract_last(left, right):
    return lax.dot_general(left, right, (((1,), (1,)), ((), ())), preferred_element_type=wide)


def block_mask(length, packed, head_size):
    shape = (packed * length, packed * head_size)
    rows = lax.broadcasted_iota(jnp.int32, shape, 0) // length
    lanes = lax.broadcasted_iota(jnp.int32, shape, 1) // head_size
    return rows == lanes


def spread(values, mask, packed):
    tiled = jnp.concatenate([values] * packed, axis=0)
    return jnp.where(mask, tiled, jnp.zeros_like(tiled))


def own_blocks(full, length, packed, head_size):
    lanes = lax.broadcasted_iota(jnp.int32, (length, packed * head_size), 1) // head_size
    out = full[:length]
    for head in range(1, packed):
        out = jnp.where(lanes == head, full[head * length : (head + 1) * length], out)
    return out


def softmax_first(scores):
    raised = jnp.exp(scores - jnp.max(scores, axis=0, keepdims=True))
    return raised * (1.0 / jnp.sum(raised, axis=0, keepdims=True))


def put_tiles(scratch, rows, values):
    tiles, _, lanes = scratch.shape
    for tile in range(tiles):
        scratch[tile, rows, :] = values[:, tile * lanes : (tile + 1) * lanes]


def get_tiles(scratch, rows):
    return jnp.concatenate([scratch[tile, rows, :] for tile in range(scratch.shape[0])], axis=-1)


def time_kernel(
    sizes, slopes_ref, block_ref, project_ref, output_ref, out_ref, seq_scr, token_scr, qkv_scr, heads_scr
):
    sources, dates_each, groups, head_count, packed, columns_each = sizes
    width = block_ref.shape[2]
    head_size = width // head_count
    lanes = packed * head_size
    length = sources * dates_each
    token_rows = dates_each * groups
    inverse_root = 1.0 / math.sqrt(head_size)
    info = []
    for source in range(sources):
        plane = block_ref[source].astype(wide)
        put_tiles(
            seq_scr, slice(source * token_rows, (source + 1) * token_rows), plane[:token_rows]
        )
        info.append(plane[token_rows : token_rows + dates_each])
    info = jnp.concatenate(info, axis=0)
    for group in range(groups):
        token_scr[group * length : (group + 1) * length, :] = get_tiles(
            seq_scr, pl.ds(group, length, stride=groups)
        )
    tokens = token_scr[...]
    qkv_scr[...] = matmul(rms_norm(tokens), project_ref[...]).astype(low)
    numbers = info[:, groups : groups + 1] * 32.0 + info[:, groups + 1 : groups + 2]
    key_at = lax.broadcasted_iota(jnp.int32, (length, packed * length), 0)
    column_at = lax.broadcasted_iota(jnp.int32, (length, packed * length), 1)
    same_date = key_at == column_at % length
    query_numbers = jnp.sum(jnp.where(same_date, numbers, 0.0), axis=0, keepdims=True)
    gap_days = jnp.abs(numbers - query_numbers)
    head_at = column_at // length
    mask = block_mask(length, packed, head_size)
    biases = []
    for first in range(0, head_count, packed):
        slope = jnp.full((length, packed * length), slopes_ref[first], wide)
        for head in range(1, packed):
            slope = jnp.where(head_at == head, slopes_ref[first + head], slope)
        biases.append(-slope * gap_days)
    for group in range(groups):
        rows = slice(group * length, (group + 1) * length)
        allowed = (info[:, group : group + 1] > 0) | same_date
        for part in range(head_count // packed):
            start = part * lanes
            query = qkv_scr[rows, start : start + lanes]
            key = qkv_scr[rows, width + start : width + start + lanes]
            value = qkv_scr[rows, 2 * width + start : 2 * width + start + lanes]
            scores = contract_last(key, spread(query, mask, packed)) * inverse_root + biases[part]
            weights = softmax_first(jnp.where(allowed, scores, masked_score)).astype(low)
            full = contract_rows(weights, value)
            heads_scr[rows, start : start + lanes] = own_blocks(
                full, length, packed, head_size
            ).astype(low)
    hidden = token_scr[...] + matmul(heads_scr[...], output_ref[...])
    for group in range(groups):
        first = (group // columns_each) * (length * columns_each) + group % columns_each
        put_tiles(
            seq_scr,
            pl.ds(first, length, stride=columns_each),
            hidden[group * length : (group + 1) * length],
        )
    out_ref[...] = get_tiles(seq_scr, slice(None)).astype(low)


def column_kernel(
    sizes,
    hidden_ref,
    cotangent_ref,
    project_ref,
    output_ref,
    mixed_ref,
    project_grad_ref,
    output_grad_ref,
    seq_scr,
    grad_scr,
    plane_scr,
    normed_scr,
    qkv_scr,
    grad_low_scr,
    heads_grad_scr,
    heads_scr,
    qkv_grad_scr,
):
    dates_each, row_parts, rows_each, columns_each, head_count, packed, row_major = sizes
    width = hidden_ref.shape[1]
    head_size = width // head_count
    lanes = packed * head_size
    length = row_parts * rows_each
    groups = dates_each * columns_each
    inverse_root = 1.0 / math.sqrt(head_size)
    put_tiles(seq_scr, slice(None), hidden_ref[...].astype(wide))
    put_tiles(grad_scr, slice(None), cotangent_ref[...].astype(wide))
    for group in range(groups):
        rows = slice(group * length, (group + 1) * length)
        first = (group // columns_each) * (length * columns_each) + group % columns_each
        if row_major:
            plane_scr[rows, :] = get_tiles(seq_scr, pl.ds(group, length, stride=groups))
        else:
            plane_scr[rows, :] = get_tiles(seq_scr, pl.ds(first, length, stride=columns_each))
        grad_low_scr[rows, :] = get_tiles(
            grad_scr, pl.ds(first, length, stride=columns_each)
        ).astype(low)
    normed_scr[...] = rms_norm(plane_scr[...])
    qkv_scr[...] = matmul(normed_scr[...], project_ref[...]).astype(low)
    heads_grad_scr[...] = contract_last(grad_low_scr[...], output_ref[...]).astype(low)
    mask = block_mask(length, packed, head_size)
    for group in range(groups):
        rows = slice(group * length, (group + 1) * length)
        for part in range(head_count // packed):
            start = part * lanes
            at_query = slice(start, start + lanes)
            at_key = slice(width + start, width + start + lanes)
            at_value = slice(2 * width + start, 2 * width + start + lanes)
            query = spread(qkv_scr[rows, at_query], mask, packed)
            key = qkv_scr[rows, at_key]
            value = qkv_scr[rows, at_value]
            heads_grad = spread(heads_grad_scr[rows, at_query], mask, packed)
            weights = softmax_first(contract_last(key, query) * inverse_root)
            weights_low = weights.astype(low)
            heads_scr[rows, at_query] = own_blocks(
                contract_rows(weights_low, value), length, packed, head_size
            ).astype(low)
            product_grad = contract_last(value, heads_grad)
            score_grad = weights * (
                product_grad - jnp.sum(weights * product_grad, axis=0, keepdims=True)
            )
            score_low = score_grad.astype(low)
            query_grad = own_blocks(contract_rows(score_low, key), length, packed, head_size)
            qkv_grad_scr[rows, at_query] = (query_grad * inverse_root).astype(low)
            qkv_grad_scr[rows, at_key] = (matmul(score_low, query) * inverse_root).astype(low)
            qkv_grad_scr[rows, at_value] = matmul(weights_low, heads_grad).astype(low)
    mixed = plane_scr[...] + matmul(heads_scr[...], output_ref[...])
    part_rows = dates_each * rows_each * columns_each
    for group in range(groups):
        inner = (group // columns_each) * (rows_each * columns_each) + group % columns_each
        for part in range(row_parts):
            begin = group * length + part * rows_each
            put_tiles(
                seq_scr,
                pl.ds(part * part_rows + inner, rows_each, stride=columns_each),
                mixed[begin : begin + rows_each],
            )
    mixed_ref[...] = get_tiles(seq_scr, slice(None)).astype(low)
    project_grad_ref[...] = contract_rows(qkv_grad_scr[...], normed_scr[...])
    output_grad_ref[...] = contract_rows(grad_low_scr[...], heads_scr[...])


def body(
    row_size,
    date_size,
    tokens,
    clear_flags,
    date_numbers,
    decay_slopes,
    time_project,
    time_output,
    column_project,
    column_output,
    cotangent,
):
    date_local, row_local, column_count, width = tokens.shape
    head_count = decay_slopes.shape[0]
    head_size = width // head_count
    packed = max(1, 128 // head_size)
    local_patches = row_local * column_count
    patches_each = local_patches // date_size
    columns_each = column_count // row_size
    row_count = row_local * row_size
    date_count = date_local * date_size
    direct = patches_each == column_count

    cotangent_planes = lax.all_to_all(cotangent, "row", split_axis=2, concat_axis=1, tiled=True)
    token_rows = date_local * patches_each
    block_rows = -(-(token_rows + date_local) // 8) * 8
    flags = jnp.transpose(
        clear_flags.reshape(date_local, date_size, patches_each), (1, 0, 2)
    ).astype(low)
    numbers = jnp.stack([date_numbers // 32, date_numbers % 32], axis=-1).astype(low)
    numbers = jnp.broadcast_to(numbers[None], (date_size, date_local, 2))
    info = jnp.concatenate([flags, numbers], axis=-1)
    info = jnp.pad(
        info, ((0, 0), (0, block_rows - token_rows - date_local), (0, width - patches_each - 2))
    )
    outgoing = jnp.transpose(
        tokens.reshape(date_local, date_size, patches_each, width), (1, 0, 2, 3)
    ).reshape(date_size, token_rows, width)
    outgoing = jnp.concatenate([outgoing, info], axis=1)
    incoming = lax.all_to_all(outgoing, "date", split_axis=0, concat_axis=0, tiled=True)

    time_tokens = date_count * patches_each
    hidden = pl.pallas_call(
        functools.partial(
            time_kernel,
            (
                date_size,
                date_local,
                patches_each,
                head_count,
                packed,
                columns_each if direct else patches_each,
            ),
        ),
        out_shape=jax.ShapeDtypeStruct((time_tokens, width), low),
        in_specs=[pl.BlockSpec(memory_space=pltpu.SMEM)]
        + [pl.BlockSpec(memory_space=pltpu.VMEM)] * 3,
        out_specs=pl.BlockSpec(memory_space=pltpu.VMEM),
        scratch_shapes=[
            pltpu.VMEM((width // 128, time_tokens, 128), wide),
            pltpu.VMEM((time_tokens, width), wide),
            pltpu.VMEM((time_tokens, 3 * width), low),
            pltpu.VMEM((time_tokens, width), low),
        ],
        compiler_params=pltpu.CompilerParams(vmem_limit_bytes=vmem_limit),
        name="time_attention",
    )(decay_slopes, incoming, time_project, time_output)

    column_tokens = date_local * row_count * columns_each
    if direct:
        parts = hidden.reshape(row_size * date_size, date_local * columns_each, width)
        plane = lax.all_to_all(parts, ("row", "date"), split_axis=0, concat_axis=0, tiled=True)
    else:
        parts = hidden.reshape(date_size, date_local, patches_each, width)
        back = lax.all_to_all(parts, "date", split_axis=0, concat_axis=0, tiled=True)
        back = jnp.transpose(back, (1, 0, 2, 3)).reshape(
            date_local, row_local, column_count, width
        )
        plane = lax.all_to_all(back, "row", split_axis=2, concat_axis=1, tiled=True)
    plane = plane.reshape(column_tokens, width)
    mixed, project_grad, output_grad = pl.pallas_call(
        functools.partial(
            column_kernel,
            (date_local, row_size, row_local, columns_each, head_count, packed, direct),
        ),
        out_shape=(
            jax.ShapeDtypeStruct((column_tokens, width), low),
            jax.ShapeDtypeStruct((3 * width, width), wide),
            jax.ShapeDtypeStruct((width, width), wide),
        ),
        scratch_shapes=[
            pltpu.VMEM((width // 128, column_tokens, 128), wide),
            pltpu.VMEM((width // 128, column_tokens, 128), wide),
            pltpu.VMEM((column_tokens, width), wide),
            pltpu.VMEM((column_tokens, width), low),
            pltpu.VMEM((column_tokens, 3 * width), low),
            pltpu.VMEM((column_tokens, width), low),
            pltpu.VMEM((column_tokens, width), low),
            pltpu.VMEM((column_tokens, width), low),
            pltpu.VMEM((column_tokens, 3 * width), low),
        ],
        compiler_params=pltpu.CompilerParams(vmem_limit_bytes=vmem_limit),
        name="column_attention",
    )(plane, cotangent_planes.reshape(column_tokens, width), column_project, column_output)

    project_each = 3 * width // date_size
    output_each = width // date_size
    lane_each = width // row_size
    grads = jnp.concatenate(
        [
            project_grad.reshape(date_size, project_each, row_size, lane_each),
            output_grad.reshape(date_size, output_each, row_size, lane_each),
        ],
        axis=1,
    ).astype(low)
    grads = jnp.transpose(grads, (2, 0, 1, 3)).reshape(
        row_size * date_size, project_each + output_each, lane_each
    )
    terms = lax.all_to_all(grads, ("row", "date"), split_axis=0, concat_axis=0, tiled=True)
    owned = jnp.sum(terms.astype(wide), axis=0)

    mixed = mixed.reshape(row_size, date_local, row_local, columns_each, width)
    mixed = lax.all_to_all(mixed, "row", split_axis=0, concat_axis=0, tiled=True)
    mixed = jnp.transpose(mixed, (1, 2, 0, 3, 4)).reshape(
        date_local, row_local, column_count, width
    )
    owned_project = jnp.transpose(owned[:project_each])
    owned_output = jnp.transpose(owned[project_each:])
    return (mixed, owned_project, owned_output)


def solution(mesh):
    return jax.shard_map(
        functools.partial(body, mesh.shape["row"], mesh.shape["date"]),
        mesh=mesh,
        in_specs=(
            P("date", "row", None, None),
            P("date", "row", None),
            P("date"),
            P(),
            P(),
            P(),
            P(),
            P(),
            P("date", "row", None, None),
        ),
        out_specs=(P("date", "row", None, None), P("row", "date"), P("row", "date")),
        check_vma=False,
    )
```

time: 406 us -> 142 us (0.35)
  local copies, waits for them, and re-layouts: 128 us -> 8.73 us
  waiting for transfers between devices: 160 us -> 65.3 us
  matrix products: 43.4 us -> 0 us
  Pallas kernels: 0 us -> 39.7 us
  blocking collectives: 21.7 us -> 0 us
  between operations: 14.7 us -> 0.84 us
  other arithmetic: 12.7 us -> 5.32 us
    reduce_scatter x2 -> x0, waiting for transfers between devices: 109 us -> none  [the longest x1 61.7 us: body(): lax.psum_scatter(partial_project, 'date', scatter_dimension=1, tiled=True)]
    all_to_all x4, waiting for transfers between devices: 18.9 us -> 65.3 us  [the longest x1 37.6 us: body(): lax.all_to_all(grads, ('row', 'date'), split_axis=0, concat_axis=0, tiled...]
    pallas_call x0 -> x2, Pallas kernels: none -> 39.7 us  [the longest x1 25.5 us: body(): pl.pallas_call(functools.partial(column_kernel, (date_local, row_size, ro...]
    dot_general x54 -> x0, matrix products: 38.3 us -> none  [the longest x4 8.05 us: contract_rows(): lax.dot_general(left, right, (((0,), (0,)), ((), ())), preferred_element_...]
    dynamic_update_slice x32 -> x0, local copies, waits for them, and re-layouts: 36.1 us -> none  [time_patch(): return lax.dynamic_update_index_in_dim(buffer, patch_heads, patch_index, 1)]
    unnamed x6 -> x0, waiting for transfers between devices: 26.8 us -> none
    reshape x11 -> x5, local copies, waits for them, and re-layouts: 22.4 us -> 1.81 us  [the longest x1 0.79 us: body(): jnp.transpose(mixed, (1, 2, 0, 3, 4))]
    squeeze x16 -> x0, local copies, waits for them, and re-layouts: 15.7 us -> none  [time_patch(): lax.dynamic_index_in_dim(split_heads, patch_index, 1, keepdims=False)]
  transfers between devices with their start and end apart: 9 -> 5, of which waited for: 8 -> 4; matrix products, arithmetic and copies ran while one was open for 4% -> 5% of each run, Pallas kernels for 0% -> 10%
where the time goes in v1:
time: 142 us; the launch traced here: 141 us
  waiting for transfers between devices  65.3 us (46%)
  Pallas kernels  39.7 us (28%)
  starting transfers between devices  21.6 us (15%)
  local copies, waits for them, and re-layouts  8.73 us (6%)
  other arithmetic  5.32 us (4%)
    all_to_all x1, waiting for transfers between devices, body(): lax.all_to_all(grads, ('row', 'date'), split_axis=0, concat_axis=0, tiled...  37.6 us
    pallas_call x1, Pallas kernels, body(): pl.pallas_call(functools.partial(column_kernel, (date_local, row_size, ro...  25.5 us
    pallas_call x1, Pallas kernels, body(): pl.pallas_call(functools.partial(time_kernel, (date_size, date_local, pat...  14.2 us
    all_to_all x1, waiting for transfers between devices, body(): lax.all_to_all(outgoing, 'date', split_axis=0, concat_axis=0, tiled=True)  12.9 us
    all_to_all x1, waiting for transfers between devices, body(): lax.all_to_all(parts, ('row', 'date'), split_axis=0, concat_axis=0, tiled...  11.8 us
    all_to_all x1, starting transfers between devices, body(): lax.all_to_all(outgoing, 'date', split_axis=0, concat_axis=0, tiled=True)  7.36 us
    all_to_all x1, starting transfers between devices, body(): lax.all_to_all(parts, ('row', 'date'), split_axis=0, concat_axis=0, tiled...  4.67 us
    all_to_all x1, starting transfers between devices, body(): lax.all_to_all(mixed, 'row', split_axis=0, concat_axis=0, tiled=True)  3.47 us
  transfers between devices with their start and end apart: 5, of which 4 were waited for; matrix products, arithmetic and copies ran while one was open for 5% of the time, Pallas kernels for 10%

profile of v1, /device:TPU:0, one launch (start us, length us, event | category | flops | bytes accessed | tf_op | source)
XLA Modules:
  0.0 141.5 jit_solution(15921618100778221909)
XLA Ops:
  0.6 0.0 copy-start.8
  0.6 0.7 convert_bitcast_fusion
  1.4 0.1 copy.26
  1.5 0.7 convert_element_type.20
  2.2 1.0 copy.24
  3.3 0.1 fusion.5
  3.4 0.0 copy-start
  3.4 0.0 copy-start.4
  3.4 0.0 copy-start.6
  3.4 0.8 pad_maximum_fusion.1
  4.2 7.4 %all-to-all-start = ((bf16[16,40,384]{2,1,0:T(8,128)(2,1)}), bf16[16,40,384]{2,1,0:T(8,128)(2,1)S(1)}, u32[]{:S(2)}, u32[]{:S(2)}) async-start(bf16[16,40,384]{2,1,0:T(8,128)(2,1)} %pad_maximum_fusion.1), calls=%async_computation | async-start | bytes 983040 | tf_op jit(solution)/shard_map/all_to_all | solution.py:256
  11.6 0.0 copy-done.8
  11.6 0.8 copy.27
  12.4 12.9 %all-to-all-done.block_ref = bf16[16,40,384]{2,1,0:T(8,128)(2,1)S(1)} async-done(((bf16[16,40,384]{2,1,0:T(8,128)(2,1)}), bf16[16,40,384]{2,1,0:T(8,128)(2,1)S(1)}, u32[]{:S(2)}, u32[]{:S(2)}) %all-to-all-start) | async-done | bytes 491552 | tf_op jit(solution)/shard_map/all_to_all | solution.py:256
  25.4 3.5 %all-to-all-start.2 = ((bf16[2,16,16,384]{3,1,0,2:T(8,128)(2,1)}), bf16[2,16,16,384]{3,1,0,2:T(8,128)(2,1)S(1)}, u32[]{:S(2)}, u32[]{:S(2)}) async-start(bf16[2,16,16,384]{3,1,0,2:T(8,128)(2,1)} %copy.27), calls=%async_computation.2 | async-start | bytes 786432 | tf_op jit(solution)/shard_map/all_to_all | solution.py:240
  28.9 0.0 copy-done
  28.9 0.0 copy-done.4
  28.9 0.0 copy-done.6
  28.9 0.0 copy-start.1
  28.9 14.2 %time_attention.1 = bf16[512,384]{1,0:T(8,128)(2,1)} custom-call(f32[12]{0:T(128)S(1)} %copy-done.6, bf16[16,40,384]{2,1,0:T(8,128)(2,1)S(1)} %all-to-all-done.block_ref, bf16[384,1152]{1,0:T(8,128)(2,1)S(1)} %copy-done, bf16[384,384]{1,0:T(8,128)(2,1)S(1)} %copy-done.4), custom_call_target="tpu_custom_call" | custom-call | tf_op jit(solution)/shard_map/time_attention/pallas_call | solution.py:259
  43.1 0.0 all-to-all-done.2
  43.1 0.0 copy-start.7
  43.1 4.7 %all-to-all-start.1 = ((bf16[32,16,384]{2,1,0:T(8,128)(2,1)}), bf16[32,16,384]{2,1,0:T(8,128)(2,1)S(1)}, u32[]{:S(2)}, u32[]{:S(2)}) async-start(bf16[32,16,384]{2,1,0:T(8,128)(2,1)} %bitcast.5), calls=%async_computation.1 | async-start | bytes 786432 | tf_op jit(solution)/shard_map/all_to_all | solution.py:288
  47.8 0.0 copy-done.7
  47.8 1.1 copy.28
  48.9 11.8 %all-to-all-done.1 = bf16[32,16,384]{2,1,0:T(8,128)(2,1)S(1)} async-done(((bf16[32,16,384]{2,1,0:T(8,128)(2,1)}), bf16[32,16,384]{2,1,0:T(8,128)(2,1)S(1)}, u32[]{:S(2)}, u32[]{:S(2)}) %all-to-all-start.1) | async-done | bytes 393248 | tf_op jit(solution)/shard_map/all_to_all | solution.py:288
  60.7 0.0 copy-done.1
  60.7 0.0 copy-start.5
  60.7 1.0 copy-done.5
  61.7 25.5 %column_attention.1 = (bf16[512,384]{1,0:T(8,128)(2,1)S(1)}, f32[1152,384]{1,0:T(8,128)S(1)}, f32[384,384]{1,0:T(8,128)S(1)}) custom-call(bf16[512,384]{1,0:T(8,128)(2,1)S(1)} %bitcast.28, bf16[512,384]{1,0:T(8,128)(2,1)S(1)} %bitcast.29, bf16[384,1152]{1,0:T(8,128)(2,1)S(1)} %copy-done.1, bf16[384,384]{1,0:T(8,128)(2,1)S(1)} %copy-done.5), custom_call_target="tpu_custom_call" | custom-call | tf_op jit(solution)/shard_map/column_attention/pallas_call | solution.py:297
  87.2 0.0 copy-start.2
  87.2 0.8 copy-done.2
  88.0 0.0 copy-start.3
  88.0 0.7 copy-done.3
  88.7 3.5 %all-to-all-start.3 = ((bf16[2,2,16,8,384]{4,3,2,1,0:T(8,128)(2,1)}), bf16[2,2,16,8,384]{4,3,2,1,0:T(8,128)(2,1)S(1)}, u32[]{:S(2)}, u32[]{:S(2)}) async-start(bf16[2,2,16,8,384]{4,3,2,1,0:T(8,128)(2,1)} %bitcast.30), calls=%async_computation.3 | async-start | bytes 786432 | tf_op jit(solution)/shard_map/all_to_all | solution.py:339
  92.2 1.1 convert.19
  93.3 0.2 reshape.62
  93.6 0.1 convert.18
  93.7 0.6 reshape.61
  94.3 0.2 copy.30
  94.5 1.5 %pad_maximum_fusion = bf16[16,96,2,192]{3,1,0,2:T(8,128)(2,1)} fusion(bf16[16,24,2,192]{3,1,0,2:T(8,128)(2,1)S(1)} %copy.31, bf16[16,72,2,192]{3,1,0,2:T(8,128)(2,1)S(1)} %copy.30), kind=kLoop, calls=%fused_computation.1 | loop fusion | flops 2359296 | bytes 2359296 | tf_op jit(solution)/shard_map/concatenate | solution.py:325
  95.9 2.9 %all-to-all-done.3 = bf16[2,2,16,8,384]{4,3,2,1,0:T(8,128)(2,1)S(1)} async-done(((bf16[2,2,16,8,384]{4,3,2,1,0:T(8,128)(2,1)}), bf16[2,2,16,8,384]{4,3,2,1,0:T(8,128)(2,1)S(1)}, u32[]{:S(2)}, u32[]{:S(2)}) %all-to-all-start.3) | async-done | bytes 393248 | tf_op jit(solution)/shard_map/all_to_all | solution.py:339
  98.8 2.7 %all-to-all-start.4 = ((bf16[32,96,192]{2,1,0:T(8,128)(2,1)}), bf16[32,96,192]{2,1,0:T(8,128)(2,1)S(1)}, u32[]{:S(2)}, u32[]{:S(2)}) async-start(bf16[32,96,192]{2,1,0:T(8,128)(2,1)} %bitcast.14), calls=%async_computation.4 | async-start | bytes 3145728 | tf_op jit(solution)/shard_map/all_to_all | solution.py:335
  101.5 0.8 copy_bitcast_fusion
  102.3 37.6 %all-to-all-done.4 = bf16[32,96,192]{2,1,0:T(8,128)(2,1)S(1)} async-done(((bf16[32,96,192]{2,1,0:T(8,128)(2,1)}), bf16[32,96,192]{2,1,0:T(8,128)(2,1)S(1)}, u32[]{:S(2)}, u32[]{:S(2)}) %all-to-all-start.4) | async-done | bytes 1179680 | tf_op jit(solution)/shard_map/all_to_all | solution.py:335
  139.9 0.3 convert_reduce_fusion
  140.2 0.6 slice_bitcast_fusion.1
  140.8 0.6 slice_bitcast_fusion
  (4 shorter events, 0.1 us)
Async XLA Ops:
  0.6 11.0 %copy-start.8 = (bf16[2,16,16,384]{3,2,1,0:T(8,128)(2,1)S(1)}, bf16[2,16,16,384]{3,2,1,0:T(8,128)(2,1)}, u32[]{:S(2)}) copy-start(bf16[2,16,16,384]{3,2,1,0:T(8,128)(2,1)} %param.17) | copy-start | bytes 1179652
  3.4 25.5 %copy-start = (bf16[384,1152]{1,0:T(8,128)(2,1)S(1)}, bf16[384,1152]{1,0:T(8,128)(2,1)}, u32[]{:S(2)}) copy-start(bf16[384,1152]{1,0:T(8,128)(2,1)} %project_ref.2) | copy-start | bytes 2654212
  3.4 25.5 %copy-start.4 = (bf16[384,384]{1,0:T(8,128)(2,1)S(1)}, bf16[384,384]{1,0:T(8,128)(2,1)}, u32[]{:S(2)}) copy-start(bf16[384,384]{1,0:T(8,128)(2,1)} %output_ref.2) | copy-start | bytes 884740
  3.4 25.5 %copy-start.6 = (f32[12]{0:T(128)S(1)}, f32[12]{0:T(128)}, u32[]{:S(2)}) copy-start(f32[12]{0:T(128)} %slopes_ref.1) | copy-start | bytes 148
  4.2 21.1 %all-to-all-start = ((bf16[16,40,384]{2,1,0:T(8,128)(2,1)}), bf16[16,40,384]{2,1,0:T(8,128)(2,1)S(1)}, u32[]{:S(2)}, u32[]{:S(2)}) async-start(bf16[16,40,384]{2,1,0:T(8,128)(2,1)} %pad_maximum_fusion.1), calls=%async_computation | async-start | bytes 983040 | tf_op jit(solution)/shard_map/all_to_all | solution.py:256
  25.4 17.7 %all-to-all-start.2 = ((bf16[2,16,16,384]{3,1,0,2:T(8,128)(2,1)}), bf16[2,16,16,384]{3,1,0,2:T(8,128)(2,1)S(1)}, u32[]{:S(2)}, u32[]{:S(2)}) async-start(bf16[2,16,16,384]{3,1,0,2:T(8,128)(2,1)} %copy.27), calls=%async_computation.2 | async-start | bytes 786432 | tf_op jit(solution)/shard_map/all_to_all | solution.py:240
  28.9 31.8 %copy-start.1 = (bf16[384,1152]{1,0:T(8,128)(2,1)S(1)}, bf16[384,1152]{1,0:T(8,128)(2,1)}, u32[]{:S(2)}) copy-start(bf16[384,1152]{1,0:T(8,128)(2,1)} %project_ref.3) | copy-start | bytes 2654212
  43.1 4.7 %copy-start.7 = (bf16[2,16,16,384]{3,1,0,2:T(8,128)(2,1)}, bf16[2,16,16,384]{3,1,0,2:T(8,128)(2,1)S(1)}, u32[]{:S(2)}) copy-start(bf16[2,16,16,384]{3,1,0,2:T(8,128)(2,1)S(1)} %all-to-all-done.2) | copy-start | bytes 1179652
  43.1 17.6 %all-to-all-start.1 = ((bf16[32,16,384]{2,1,0:T(8,128)(2,1)}), bf16[32,16,384]{2,1,0:T(8,128)(2,1)S(1)}, u32[]{:S(2)}, u32[]{:S(2)}) async-start(bf16[32,16,384]{2,1,0:T(8,128)(2,1)} %bitcast.5), calls=%async_computation.1 | async-start | bytes 786432 | tf_op jit(solution)/shard_map/all_to_all | solution.py:288
  60.7 1.0 copy-start.5
  87.2 0.8 copy-start.2
  88.0 0.7 copy-start.3
  88.7 10.1 %all-to-all-start.3 = ((bf16[2,2,16,8,384]{4,3,2,1,0:T(8,128)(2,1)}), bf16[2,2,16,8,384]{4,3,2,1,0:T(8,128)(2,1)S(1)}, u32[]{:S(2)}, u32[]{:S(2)}) async-start(bf16[2,2,16,8,384]{4,3,2,1,0:T(8,128)(2,1)} %bitcast.30), calls=%async_computation.3 | async-start | bytes 786432 | tf_op jit(solution)/shard_map/all_to_all | solution.py:339
  98.8 41.1 %all-to-all-start.4 = ((bf16[32,96,192]{2,1,0:T(8,128)(2,1)}), bf16[32,96,192]{2,1,0:T(8,128)(2,1)S(1)}, u32[]{:S(2)}, u32[]{:S(2)}) async-start(bf16[32,96,192]{2,1,0:T(8,128)(2,1)} %bitcast.14), calls=%async_computation.4 | async-start | bytes 3145728 | tf_op jit(solution)/shard_map/all_to_all | solution.py:335

commit v2 on v1

--- a/solution.py
+++ b/solution.py
@@ -10,6 +10,8 @@
 
 epsilon = 1e-06
 masked_score = -1e30
+units_each = 6
+dates = ("outer", "pair")
 vmem_limit = 48 * 1024 * 1024
 low = jnp.bfloat16
 wide = jnp.float32
@@ -36,12 +38,16 @@
     shape = (packed * length, packed * head_size)
     rows = lax.broadcasted_iota(jnp.int32, shape, 0) // length
     lanes = lax.broadcasted_iota(jnp.int32, shape, 1) // head_size
-    return rows == lanes
+    return jnp.where(rows == lanes, 1.0, 0.0).astype(low)
 
 
 def spread(values, mask, packed):
-    tiled = jnp.concatenate([values] * packed, axis=0)
-    return jnp.where(mask, tiled, jnp.zeros_like(tiled))
+    return jnp.concatenate([values] * packed, axis=0) * mask
+
+
+def batches(groups, parts, each):
+    units = [(group, part) for group in range(groups) for part in range(parts)]
+    return [units[first : first + each] for first in range(0, len(units), each)]
 
 
 def own_blocks(full, length, packed, head_size):
@@ -105,18 +111,27 @@
         for head in range(1, packed):
             slope = jnp.where(head_at == head, slopes_ref[first + head], slope)
         biases.append(-slope * gap_days)
-    for group in range(groups):
-        rows = slice(group * length, (group + 1) * length)
-        allowed = (info[:, group : group + 1] > 0) | same_date
-        for part in range(head_count // packed):
+    for units in batches(groups, head_count // packed, units_each):
+        all_scores = []
+        for group, part in units:
+            rows = slice(group * length, (group + 1) * length)
             start = part * lanes
             query = qkv_scr[rows, start : start + lanes]
             key = qkv_scr[rows, width + start : width + start + lanes]
-            value = qkv_scr[rows, 2 * width + start : 2 * width + start + lanes]
-            scores = contract_last(key, spread(query, mask, packed)) * inverse_root + biases[part]
-            weights = softmax_first(jnp.where(allowed, scores, masked_score)).astype(low)
-            full = contract_rows(weights, value)
-            heads_scr[rows, start : start + lanes] = own_blocks(
+            all_scores.append(contract_last(key, spread(query, mask, packed)))
+        all_weights = []
+        for (group, part), scores in zip(units, all_scores):
+            allowed = (info[:, group : group + 1] > 0) | same_date
+            scores = jnp.where(allowed, scores * inverse_root + biases[part], masked_score)
+            all_weights.append(softmax_first(scores).astype(low))
+        all_heads = []
+        for (group, part), weights in zip(units, all_weights):
+            rows = slice(group * length, (group + 1) * length)
+            start = 2 * width + part * lanes
+            all_heads.append(contract_rows(weights, qkv_scr[rows, start : start + lanes]))
+        for (group, part), full in zip(units, all_heads):
+            rows = slice(group * length, (group + 1) * length)
+            heads_scr[rows, part * lanes : (part + 1) * lanes] = own_blocks(
                 full, length, packed, head_size
             ).astype(low)
     hidden = token_scr[...] + matmul(heads_scr[...], output_ref[...])
@@ -132,13 +147,14 @@
 
 def column_kernel(
     sizes,
+    pair_ref,
     hidden_ref,
     cotangent_ref,
     project_ref,
     output_ref,
     mixed_ref,
-    project_grad_ref,
-    output_grad_ref,
+    first_grad_ref,
+    second_grad_ref,
     seq_scr,
     grad_scr,
     plane_scr,
@@ -149,7 +165,7 @@
     heads_scr,
     qkv_grad_scr,
 ):
-    dates_each, row_parts, rows_each, columns_each, head_count, packed, row_major = sizes
+    dates_each, row_parts, rows_each, columns_each, head_count, packed, row_major, date_size = sizes
     width = hidden_ref.shape[1]
     head_size = width // head_count
     lanes = packed * head_size
@@ -172,31 +188,53 @@
     qkv_scr[...] = matmul(normed_scr[...], project_ref[...]).astype(low)
     heads_grad_scr[...] = contract_last(grad_low_scr[...], output_ref[...]).astype(low)
     mask = block_mask(length, packed, head_size)
-    for group in range(groups):
-        rows = slice(group * length, (group + 1) * length)
-        for part in range(head_count // packed):
+    for units in batches(groups, head_count // packed, units_each):
+        places = []
+        for group, part in units:
             start = part * lanes
-            at_query = slice(start, start + lanes)
-            at_key = slice(width + start, width + start + lanes)
-            at_value = slice(2 * width + start, 2 * width + start + lanes)
+            places.append(
+                (
+                    slice(group * length, (group + 1) * length),
+                    slice(start, start + lanes),
+                    slice(width + start, width + start + lanes),
+                    slice(2 * width + start, 2 * width + start + lanes),
+                )
+            )
+        all_scores = []
+        for rows, at_query, at_key, at_value in places:
             query = spread(qkv_scr[rows, at_query], mask, packed)
-            key = qkv_scr[rows, at_key]
-            value = qkv_scr[rows, at_value]
             heads_grad = spread(heads_grad_scr[rows, at_query], mask, packed)
-            weights = softmax_first(contract_last(key, query) * inverse_root)
-            weights_low = weights.astype(low)
-            heads_scr[rows, at_query] = own_blocks(
-                contract_rows(weights_low, value), length, packed, head_size
-            ).astype(low)
-            product_grad = contract_last(value, heads_grad)
+            all_scores.append(
+                (
+                    contract_last(qkv_scr[rows, at_key], query),
+                    contract_last(qkv_scr[rows, at_value], heads_grad),
+                )
+            )
+        all_weights = []
+        for scores, product_grad in all_scores:
+            weights = softmax_first(scores * inverse_root)
             score_grad = weights * (
                 product_grad - jnp.sum(weights * product_grad, axis=0, keepdims=True)
             )
-            score_low = score_grad.astype(low)
-            query_grad = own_blocks(contract_rows(score_low, key), length, packed, head_size)
-            qkv_grad_scr[rows, at_query] = (query_grad * inverse_root).astype(low)
-            qkv_grad_scr[rows, at_key] = (matmul(score_low, query) * inverse_root).astype(low)
-            qkv_grad_scr[rows, at_value] = matmul(weights_low, heads_grad).astype(low)
+            all_weights.append((weights.astype(low), score_grad.astype(low)))
+        all_full = []
+        for (rows, at_query, at_key, at_value), (weights, score_low) in zip(places, all_weights):
+            all_full.append(
+                (
+                    contract_rows(weights, qkv_scr[rows, at_value]),
+                    contract_rows(score_low, qkv_scr[rows, at_key]),
+                )
+            )
+            query = spread(qkv_scr[rows, at_query], mask, packed)
+            heads_grad = spread(heads_grad_scr[rows, at_query], mask, packed)
+            key_grad = matmul(score_low, query) * inverse_root
+            qkv_grad_scr[rows, at_key] = key_grad.astype(low)
+            qkv_grad_scr[rows, at_value] = matmul(weights, heads_grad).astype(low)
+        for (rows, at_query, _, _), (heads_full, query_full) in zip(places, all_full):
+            heads = own_blocks(heads_full, length, packed, head_size)
+            heads_scr[rows, at_query] = heads.astype(low)
+            query_grad = own_blocks(query_full, length, packed, head_size) * inverse_root
+            qkv_grad_scr[rows, at_query] = query_grad.astype(low)
     mixed = plane_scr[...] + matmul(heads_scr[...], output_ref[...])
     part_rows = dates_each * rows_each * columns_each
     for group in range(groups):
@@ -209,13 +247,62 @@
                 mixed[begin : begin + rows_each],
             )
     mixed_ref[...] = get_tiles(seq_scr, slice(None)).astype(low)
-    project_grad_ref[...] = contract_rows(qkv_grad_scr[...], normed_scr[...])
-    output_grad_ref[...] = contract_rows(grad_low_scr[...], heads_scr[...])
+    project_grad = contract_rows(qkv_grad_scr[...], normed_scr[...])
+    output_grad = contract_rows(grad_low_scr[...], heads_scr[...])
+    if date_size is None:
+        first_grad_ref[...] = project_grad
+        second_grad_ref[...] = output_grad
+        return
+    keep_ref, send_ref = first_grad_ref, second_grad_ref
+    even = pair_ref[0] == 0
+    project_each = project_grad.shape[0] // date_size
+    output_each = output_grad.shape[0] // date_size
+    half = (project_each + output_each) // 2
+    lower = lax.broadcasted_iota(jnp.int32, (half, 128), 1) < 64
+    for outer in range(date_size // 2):
+        pair = []
+        for part in (2 * outer, 2 * outer + 1):
+            block = jnp.concatenate(
+                [
+                    project_grad[part * project_each : (part + 1) * project_each],
+                    output_grad[part * output_each : (part + 1) * output_each],
+                ],
+                axis=0,
+            )
+            top, bottom = block[:half, 128:256], block[half:, 128:256]
+            pair.append(
+                (
+                    (block[:, :128], jnp.where(lower, top, pltpu.roll(bottom, 64, 1))),
+                    (block[:, 256:], jnp.where(lower, pltpu.roll(top, 64, 1), bottom)),
+                )
+            )
+        for row_part in range(2):
+            for first, one, two in zip((0, 2 * half), pair[0][row_part], pair[1][row_part]):
+                at = slice(first, first + one.shape[0])
+                keep_ref[row_part, outer, at, :] = jnp.where(even, one, two).astype(low)
+                send_ref[row_part, outer, at, :] = jnp.where(even, two, one).astype(low)
+
+
+def finish_kernel(project_each, row_ref, terms_ref, project_ref, output_ref):
+    total = terms_ref[0].astype(wide)
+    for source in range(1, terms_ref.shape[0]):
+        total = total + terms_ref[source].astype(wide)
+    whole = 2 * total.shape[0] // 3
+    main = jnp.transpose(total[:whole])
+    tail = jnp.transpose(total[whole:])
+    tail = jnp.concatenate([tail[:64], tail[64:]], axis=1)
+    first = row_ref[0] == 0
+    front = jnp.concatenate([main, tail], axis=0)
+    back = jnp.concatenate([tail, main], axis=0)
+    owned = jnp.where(first, front, back)
+    project_ref[...] = owned[:, :project_each]
+    output_ref[...] = owned[:, project_each:]
 
 
 def body(
     row_size,
     date_size,
+    pair_size,
     tokens,
     clear_flags,
     date_numbers,
@@ -253,7 +340,7 @@
         tokens.reshape(date_local, date_size, patches_each, width), (1, 0, 2, 3)
     ).reshape(date_size, token_rows, width)
     outgoing = jnp.concatenate([outgoing, info], axis=1)
-    incoming = lax.all_to_all(outgoing, "date", split_axis=0, concat_axis=0, tiled=True)
+    incoming = lax.all_to_all(outgoing, dates, split_axis=0, concat_axis=0, tiled=True)
 
     time_tokens = date_count * patches_each
     hidden = pl.pallas_call(
@@ -285,25 +372,54 @@
     column_tokens = date_local * row_count * columns_each
     if direct:
         parts = hidden.reshape(row_size * date_size, date_local * columns_each, width)
-        plane = lax.all_to_all(parts, ("row", "date"), split_axis=0, concat_axis=0, tiled=True)
+        plane = lax.all_to_all(parts, ("row", *dates), split_axis=0, concat_axis=0, tiled=True)
     else:
         parts = hidden.reshape(date_size, date_local, patches_each, width)
-        back = lax.all_to_all(parts, "date", split_axis=0, concat_axis=0, tiled=True)
+        back = lax.all_to_all(parts, dates, split_axis=0, concat_axis=0, tiled=True)
         back = jnp.transpose(back, (1, 0, 2, 3)).reshape(
             date_local, row_local, column_count, width
         )
         plane = lax.all_to_all(back, "row", split_axis=2, concat_axis=1, tiled=True)
     plane = plane.reshape(column_tokens, width)
-    mixed, project_grad, output_grad = pl.pallas_call(
+    project_each = 3 * width // date_size
+    output_each = width // date_size
+    lane_each = width // row_size
+    paired = (
+        pair_size == 2
+        and row_size == 2
+        and lane_each == 192
+        and project_each % 8 == 0
+        and output_each % 8 == 0
+        and (project_each + output_each) % 32 == 0
+    )
+    pair_at = lax.axis_index("pair")
+    if paired:
+        packed_rows = (project_each + output_each) * 3 // 2
+        grad_shapes = (
+            jax.ShapeDtypeStruct((row_size, date_size // 2, packed_rows, 128), low),
+        ) * 2
+    else:
+        grad_shapes = (
+            jax.ShapeDtypeStruct((3 * width, width), wide),
+            jax.ShapeDtypeStruct((width, width), wide),
+        )
+    mixed, first_grad, second_grad = pl.pallas_call(
         functools.partial(
             column_kernel,
-            (date_local, row_size, row_local, columns_each, head_count, packed, direct),
+            (
+                date_local,
+                row_size,
+                row_local,
+                columns_each,
+                head_count,
+                packed,
+                direct,
+                date_size if paired else None,
+            ),
         ),
-        out_shape=(
-            jax.ShapeDtypeStruct((column_tokens, width), low),
-            jax.ShapeDtypeStruct((3 * width, width), wide),
-            jax.ShapeDtypeStruct((width, width), wide),
-        ),
+        out_shape=(jax.ShapeDtypeStruct((column_tokens, width), low), *grad_shapes),
+        in_specs=[pl.BlockSpec(memory_space=pltpu.SMEM)]
+        + [pl.BlockSpec(memory_space=pltpu.VMEM)] * 4,
         scratch_shapes=[
             pltpu.VMEM((width // 128, column_tokens, 128), wide),
             pltpu.VMEM((width // 128, column_tokens, 128), wide),
@@ -317,49 +433,77 @@
         ],
         compiler_params=pltpu.CompilerParams(vmem_limit_bytes=vmem_limit),
         name="column_attention",
-    )(plane, cotangent_planes.reshape(column_tokens, width), column_project, column_output)
-
-    project_each = 3 * width // date_size
-    output_each = width // date_size
-    lane_each = width // row_size
-    grads = jnp.concatenate(
-        [
-            project_grad.reshape(date_size, project_each, row_size, lane_each),
-            output_grad.reshape(date_size, output_each, row_size, lane_each),
-        ],
-        axis=1,
-    ).astype(low)
-    grads = jnp.transpose(grads, (2, 0, 1, 3)).reshape(
-        row_size * date_size, project_each + output_each, lane_each
+    )(
+        pair_at.reshape(1),
+        plane,
+        cotangent_planes.reshape(column_tokens, width),
+        column_project,
+        column_output,
     )
-    terms = lax.all_to_all(grads, ("row", "date"), split_axis=0, concat_axis=0, tiled=True)
-    owned = jnp.sum(terms.astype(wide), axis=0)
+
+
+    if paired:
+        arrived = lax.ppermute(second_grad, "pair", [(0, 1), (1, 0)])
+        halves = (first_grad.astype(wide) + arrived.astype(wide)).astype(low)
+        halves = halves.reshape(row_size * date_size // 2, packed_rows, 128)
+        terms = lax.all_to_all(halves, ("row", "outer"), split_axis=0, concat_axis=0, tiled=True)
+        owned_project, owned_output = pl.pallas_call(
+            functools.partial(finish_kernel, project_each),
+            out_shape=(
+                jax.ShapeDtypeStruct((lane_each, project_each), wide),
+                jax.ShapeDtypeStruct((lane_each, output_each), wide),
+            ),
+            in_specs=[
+                pl.BlockSpec(memory_space=pltpu.SMEM),
+                pl.BlockSpec(memory_space=pltpu.VMEM),
+            ],
+            name="gradient_sum",
+        )(lax.axis_index("row").reshape(1), terms)
+    else:
+        grads = jnp.concatenate(
+            [
+                first_grad.reshape(date_size, project_each, row_size, lane_each),
+                second_grad.reshape(date_size, output_each, row_size, lane_each),
+            ],
+            axis=1,
+        ).astype(low)
+        grads = jnp.transpose(grads, (2, 0, 1, 3)).reshape(
+            row_size * date_size, project_each + output_each, lane_each
+        )
+        terms = lax.all_to_all(grads, ("row", *dates), split_axis=0, concat_axis=0, tiled=True)
+        owned = jnp.sum(terms.astype(wide), axis=0)
+        owned_project = jnp.transpose(owned[:project_each])
+        owned_output = jnp.transpose(owned[project_each:])
 
     mixed = mixed.reshape(row_size, date_local, row_local, columns_each, width)
     mixed = lax.all_to_all(mixed, "row", split_axis=0, concat_axis=0, tiled=True)
     mixed = jnp.transpose(mixed, (1, 2, 0, 3, 4)).reshape(
         date_local, row_local, column_count, width
     )
-    owned_project = jnp.transpose(owned[:project_each])
-    owned_output = jnp.transpose(owned[project_each:])
     return (mixed, owned_project, owned_output)
 
 
 def solution(mesh):
+    date_size, row_size = mesh.shape["date"], mesh.shape["row"]
+    pair_size = 2 if date_size % 2 == 0 else 1
+    split = jax.sharding.Mesh(
+        mesh.devices.reshape(date_size // pair_size, pair_size, row_size),
+        ("outer", "pair", "row"),
+    )
     return jax.shard_map(
-        functools.partial(body, mesh.shape["row"], mesh.shape["date"]),
-        mesh=mesh,
+        functools.partial(body, row_size, date_size, pair_size),
+        mesh=split,
         in_specs=(
-            P("date", "row", None, None),
-            P("date", "row", None),
-            P("date"),
+            P(dates, "row", None, None),
+            P(dates, "row", None),
+            P(dates),
             P(),
             P(),
             P(),
             P(),
             P(),
-            P("date", "row", None, None),
+            P(dates, "row", None, None),
         ),
-        out_specs=(P("date", "row", None, None), P("row", "date"), P("row", "date")),
+        out_specs=(P(dates, "row", None, None), P("row", dates), P("row", dates)),
         check_vma=False,
     )

time: 142 us -> 96.9 us (0.68)
  Pallas kernels: 39.7 us -> 14.4 us
  waiting for transfers between devices: 65.3 us -> 49.6 us
  other arithmetic: 5.32 us -> 3.31 us
  local copies, waits for them, and re-layouts: 8.73 us -> 6.94 us
    all_to_all x3, waiting for transfers between devices: 62.4 us -> 41.5 us  [the longest x1 15.6 us: body(): lax.all_to_all(halves, ('row', 'outer'), split_axis=0, concat_axis=0, til...]
    pallas_call x1, Pallas kernels: 25.5 us -> 6.99 us  [body(): pl.pallas_call(functools.partial(column_kernel, (date_local, row_size, ro...]
    pallas_call x1, Pallas kernels: 14.2 us -> 5.47 us  [body(): pl.pallas_call(functools.partial(time_kernel, (date_size, date_local, pat...]
    all_to_all x1, waiting for transfers between devices: 2.88 us -> 6.51 us  [body(): lax.all_to_all(mixed, 'row', split_axis=0, concat_axis=0, tiled=True)]
    pallas_call x0 -> x1, Pallas kernels: none -> 1.97 us  [body(): pl.pallas_call(functools.partial(finish_kernel, project_each), out_shape=...]
    all_to_all x1, waiting for transfers between devices: 0.01 us -> 1.61 us  [body(): lax.all_to_all(cotangent, 'row', split_axis=2, concat_axis=1, tiled=True)]
    concatenate x1 -> x0, other arithmetic: 1.48 us -> none  [body(): jnp.concatenate([project_grad.reshape(date_size, project_each, row_size,...]
    unnamed x20 -> x18, local copies, waits for them, and re-layouts: 3.39 us -> 4.86 us
  transfers between devices with their start and end apart: 5 -> 6, of which waited for: 4 -> 5; matrix products, arithmetic and copies ran while one was open for 5% -> 3% of each run, Pallas kernels for 10% -> 6%
where the time goes in v2:
time: 96.9 us; the launch traced here: 96.2 us
  waiting for transfers between devices  49.6 us (51%)
  starting transfers between devices  21.1 us (22%)
  Pallas kernels  14.4 us (15%)
  local copies, waits for them, and re-layouts  6.94 us (7%)
  other arithmetic  3.31 us (3%)
    all_to_all x1, waiting for transfers between devices, body(): lax.all_to_all(halves, ('row', 'outer'), split_axis=0, concat_axis=0, til...  15.6 us
    all_to_all x1, waiting for transfers between devices, body(): lax.all_to_all(parts, ('row', *dates), split_axis=0, concat_axis=0, tiled...  13 us
    all_to_all x1, waiting for transfers between devices, body(): lax.all_to_all(outgoing, dates, split_axis=0, concat_axis=0, tiled=True)  12.9 us
    all_to_all x1, starting transfers between devices, body(): lax.all_to_all(outgoing, dates, split_axis=0, concat_axis=0, tiled=True)  7.36 us
    pallas_call x1, Pallas kernels, body(): pl.pallas_call(functools.partial(column_kernel, (date_local, row_size, ro...  6.99 us
    all_to_all x1, waiting for transfers between devices, body(): lax.all_to_all(mixed, 'row', split_axis=0, concat_axis=0, tiled=True)  6.51 us
    pallas_call x1, Pallas kernels, body(): pl.pallas_call(functools.partial(time_kernel, (date_size, date_local, pat...  5.47 us
    unnamed x18, local copies, waits for them, and re-layouts  4.86 us
  transfers between devices with their start and end apart: 6, of which 5 were waited for; matrix products, arithmetic and copies ran while one was open for 3% of the time, Pallas kernels for 6%

profile of v2, /device:TPU:0, one launch (start us, length us, event | category | flops | bytes accessed | tf_op | source)
XLA Modules:
  0.0 96.2 jit_solution(8648575649522715675)
XLA Ops:
  0.6 0.7 convert_bitcast_fusion
  1.3 0.1 copy.21
  1.4 0.7 convert_element_type.27
  2.2 1.0 %copy.19 = bf16[16,2,16,384]{3,2,1,0:T(8,128)(2,1)S(1)} copy(bf16[16,2,16,384]{3,2,0,1:T(8,128)(2,1)} %bitcast.28) | data formatting | bytes 786432 | tf_op jit(solution)/shard_map/transpose | solution.py:339
  3.2 0.1 fusion.5
  3.3 0.0 copy-start.6
  3.3 0.8 pad_maximum_fusion
  4.2 7.4 %all-to-all-start = ((bf16[16,40,384]{2,1,0:T(8,128)(2,1)}), bf16[16,40,384]{2,1,0:T(8,128)(2,1)S(1)}, u32[]{:S(2)}, u32[]{:S(2)}) async-start(bf16[16,40,384]{2,1,0:T(8,128)(2,1)} %pad_maximum_fusion), calls=%async_computation | async-start | bytes 983040 | tf_op jit(solution)/shard_map/all_to_all | solution.py:343
  11.5 0.0 copy-done.6
  11.5 0.0 copy-start
  11.5 0.0 copy-start.2
  11.6 0.0 copy-start.4
  11.6 0.8 copy.22
  12.4 12.9 %all-to-all-done.block_ref = bf16[16,40,384]{2,1,0:T(8,128)(2,1)S(1)} async-done(((bf16[16,40,384]{2,1,0:T(8,128)(2,1)}), bf16[16,40,384]{2,1,0:T(8,128)(2,1)S(1)}, u32[]{:S(2)}, u32[]{:S(2)}) %all-to-all-start) | async-done | bytes 491552 | tf_op jit(solution)/shard_map/all_to_all | solution.py:343
  25.3 3.5 %all-to-all-start.2 = ((bf16[2,16,16,384]{3,1,0,2:T(8,128)(2,1)}), bf16[2,16,16,384]{3,1,0,2:T(8,128)(2,1)S(1)}, u32[]{:S(2)}, u32[]{:S(2)}) async-start(bf16[2,16,16,384]{3,1,0,2:T(8,128)(2,1)} %copy.22), calls=%async_computation.2 | async-start | bytes 786432 | tf_op jit(solution)/shard_map/all_to_all | solution.py:327
  28.8 0.0 copy-done
  28.8 0.0 copy-done.2
  28.8 0.0 copy-done.4
  28.8 5.5 %time_attention.1 = bf16[512,384]{1,0:T(8,128)(2,1)} custom-call(f32[12]{0:T(128)S(1)} %copy-done.4, bf16[16,40,384]{2,1,0:T(8,128)(2,1)S(1)} %all-to-all-done.block_ref, bf16[384,1152]{1,0:T(8,128)(2,1)S(1)} %copy-done, bf16[384,384]{1,0:T(8,128)(2,1)S(1)} %copy-done.2), custom_call_target="tpu_custom_call" | custom-call | tf_op jit(solution)/shard_map/time_attention/pallas_call | solution.py:346
  34.3 0.0 copy-start.1
  34.3 0.0 copy-start.3
  34.3 1.6 %all-to-all-done.2 = bf16[2,16,16,384]{3,1,0,2:T(8,128)(2,1)S(1)} async-done(((bf16[2,16,16,384]{3,1,0,2:T(8,128)(2,1)}), bf16[2,16,16,384]{3,1,0,2:T(8,128)(2,1)S(1)}, u32[]{:S(2)}, u32[]{:S(2)}) %all-to-all-start.2) | async-done | bytes 393248 | tf_op jit(solution)/shard_map/all_to_all | solution.py:327
  35.9 3.3 %all-to-all-start.1 = ((bf16[32,16,384]{2,1,0:T(8,128)(2,1)}), bf16[32,16,384]{2,1,0:T(8,128)(2,1)S(1)}, u32[]{:S(2)}, u32[]{:S(2)}) async-start(bf16[32,16,384]{2,1,0:T(8,128)(2,1)} %bitcast.6), calls=%async_computation.1 | async-start | bytes 786432 | tf_op jit(solution)/shard_map/all_to_all | solution.py:375
  39.1 0.1 copy.23
  39.3 13.0 %all-to-all-done.1 = bf16[32,16,384]{2,1,0:T(8,128)(2,1)S(1)} async-done(((bf16[32,16,384]{2,1,0:T(8,128)(2,1)}), bf16[32,16,384]{2,1,0:T(8,128)(2,1)S(1)}, u32[]{:S(2)}, u32[]{:S(2)}) %all-to-all-start.1) | async-done | bytes 393248 | tf_op jit(solution)/shard_map/all_to_all | solution.py:375
  52.2 0.0 copy-done.1
  52.2 0.0 copy-done.3
  52.3 7.0 %column_attention.1 = (bf16[512,384]{1,0:T(8,128)(2,1)}, bf16[2,8,144,128]{3,2,1,0:T(8,128)(2,1)S(1)}, bf16[2,8,144,128]{3,2,1,0:T(8,128)(2,1)S(1)}) custom-call(s32[1]{0:T(128)} %bitcast.pair_ref, bf16[512,384]{1,0:T(8,128)(2,1)S(1)} %bitcast.24, bf16[512,384]{1,0:T(8,128)(2,1)S(1)} %bitcast.25, bf16[384,1152]{1,0:T(8,128)(2,1)S(1)} %copy-done.1, ...), custom_call_target="tpu_custom_call" | custom-call | tf_op jit(solution)/shard_map/column_attention/pallas_call | solution.py:406
  59.2 0.0 collective-permute-start
  59.2 3.5 %all-to-all-start.3 = ((bf16[2,2,16,8,384]{4,3,2,1,0:T(8,128)(2,1)}), bf16[2,2,16,8,384]{4,3,2,1,0:T(8,128)(2,1)S(1)}, u32[]{:S(2)}, u32[]{:S(2)}) async-start(bf16[2,2,16,8,384]{4,3,2,1,0:T(8,128)(2,1)} %bitcast.11), calls=%async_computation.3 | async-start | bytes 786432 | tf_op jit(solution)/shard_map/all_to_all | solution.py:479
  62.7 0.0 collective-permute-done
  62.7 1.0 %add_convert_fusion = bf16[2,8,144,128]{3,2,1,0:T(8,128)(2,1)} fusion(bf16[2,8,144,128]{3,2,1,0:T(8,128)(2,1)S(1)} %collective-permute-done, bf16[2,8,144,128]{3,2,1,0:T(8,128)(2,1)S(1)} %get-tuple-element.9), kind=kLoop, calls=%fused_computation | loop fusion | flops 1179648 | bytes 1769472 | tf_op jit(solution)/shard_map/convert_element_type | solution.py:447
  63.7 6.5 %all-to-all-done.3 = bf16[2,2,16,8,384]{4,3,2,1,0:T(8,128)(2,1)S(1)} async-done(((bf16[2,2,16,8,384]{4,3,2,1,0:T(8,128)(2,1)}), bf16[2,2,16,8,384]{4,3,2,1,0:T(8,128)(2,1)S(1)}, u32[]{:S(2)}, u32[]{:S(2)}) %all-to-all-start.3) | async-done | bytes 393248 | tf_op jit(solution)/shard_map/all_to_all | solution.py:479
  70.2 3.6 %all-to-all-start.4 = ((bf16[16,144,128]{2,1,0:T(8,128)(2,1)}), bf16[16,144,128]{2,1,0:T(8,128)(2,1)S(1)}, u32[]{:S(2)}, u32[]{:S(2)}) async-start(bf16[16,144,128]{2,1,0:T(8,128)(2,1)} %bitcast.15), calls=%async_computation.4 | async-start | bytes 1179648 | tf_op jit(solution)/shard_map/all_to_all | solution.py:449
  73.8 0.8 copy_bitcast_fusion
  74.6 15.6 %all-to-all-done.4.terms_ref = bf16[16,144,128]{2,1,0:T(8,128)(2,1)S(1)} async-done(((bf16[16,144,128]{2,1,0:T(8,128)(2,1)}), bf16[16,144,128]{2,1,0:T(8,128)(2,1)S(1)}, u32[]{:S(2)}, u32[]{:S(2)}) %all-to-all-start.4) | async-done | bytes 589856 | tf_op jit(solution)/shard_map/all_to_all | solution.py:449
  90.2 0.0 copy-start.5
  90.2 0.8 copy-done.5
  91.0 2.0 %gradient_sum.1 = (f32[192,72]{1,0:T(8,128)}, f32[192,24]{1,0:T(8,128)}) custom-call(s32[1]{0:T(128)} %bitcast.14.row_ref, bf16[16,144,128]{2,1,0:T(8,128)(2,1)} %copy-done.5), custom_call_target="tpu_custom_call" | custom-call | tf_op jit(solution)/shard_map/gradient_sum/pallas_call | solution.py:450
  93.0 1.6 %copy.25 = f32[192,72]{0,1:T(8,128)} copy(f32[192,72]{1,0:T(8,128)} %get-tuple-element.17) | data formatting | bytes 110592
  94.6 1.6 %copy.26 = f32[192,24]{0,1:T(8,128)} copy(f32[192,24]{1,0:T(8,128)} %get-tuple-element.18) | data formatting | bytes 36864
  (3 shorter events, 0.0 us)
Async XLA Ops:
  3.3 8.2 %copy-start.6 = (bf16[2,16,16,384]{3,2,1,0:T(8,128)(2,1)S(1)}, bf16[2,16,16,384]{3,2,1,0:T(8,128)(2,1)}, u32[]{:S(2)}) copy-start(bf16[2,16,16,384]{3,2,1,0:T(8,128)(2,1)} %param.17) | copy-start | bytes 1179652
  4.2 21.1 %all-to-all-start = ((bf16[16,40,384]{2,1,0:T(8,128)(2,1)}), bf16[16,40,384]{2,1,0:T(8,128)(2,1)S(1)}, u32[]{:S(2)}, u32[]{:S(2)}) async-start(bf16[16,40,384]{2,1,0:T(8,128)(2,1)} %pad_maximum_fusion), calls=%async_computation | async-start | bytes 983040 | tf_op jit(solution)/shard_map/all_to_all | solution.py:343
  11.5 17.2 %copy-start = (bf16[384,1152]{1,0:T(8,128)(2,1)S(1)}, bf16[384,1152]{1,0:T(8,128)(2,1)}, u32[]{:S(2)}) copy-start(bf16[384,1152]{1,0:T(8,128)(2,1)} %project_ref.2) | copy-start | bytes 2654212
  11.5 17.2 %copy-start.2 = (bf16[384,384]{1,0:T(8,128)(2,1)S(1)}, bf16[384,384]{1,0:T(8,128)(2,1)}, u32[]{:S(2)}) copy-start(bf16[384,384]{1,0:T(8,128)(2,1)} %output_ref.2) | copy-start | bytes 884740
  11.6 17.2 %copy-start.4 = (f32[12]{0:T(128)S(1)}, f32[12]{0:T(128)}, u32[]{:S(2)}) copy-start(f32[12]{0:T(128)} %slopes_ref.1) | copy-start | bytes 148
  25.3 10.6 %all-to-all-start.2 = ((bf16[2,16,16,384]{3,1,0,2:T(8,128)(2,1)}), bf16[2,16,16,384]{3,1,0,2:T(8,128)(2,1)S(1)}, u32[]{:S(2)}, u32[]{:S(2)}) async-start(bf16[2,16,16,384]{3,1,0,2:T(8,128)(2,1)} %copy.22), calls=%async_computation.2 | async-start | bytes 786432 | tf_op jit(solution)/shard_map/all_to_all | solution.py:327
  34.3 18.0 %copy-start.1 = (bf16[384,1152]{1,0:T(8,128)(2,1)S(1)}, bf16[384,1152]{1,0:T(8,128)(2,1)}, u32[]{:S(2)}) copy-start(bf16[384,1152]{1,0:T(8,128)(2,1)} %project_ref.3) | copy-start | bytes 2654212
  34.3 18.0 %copy-start.3 = (bf16[384,384]{1,0:T(8,128)(2,1)S(1)}, bf16[384,384]{1,0:T(8,128)(2,1)}, u32[]{:S(2)}) copy-start(bf16[384,384]{1,0:T(8,128)(2,1)} %output_ref.3) | copy-start | bytes 884740
  35.9 16.4 %all-to-all-start.1 = ((bf16[32,16,384]{2,1,0:T(8,128)(2,1)}), bf16[32,16,384]{2,1,0:T(8,128)(2,1)S(1)}, u32[]{:S(2)}, u32[]{:S(2)}) async-start(bf16[32,16,384]{2,1,0:T(8,128)(2,1)} %bitcast.6), calls=%async_computation.1 | async-start | bytes 786432 | tf_op jit(solution)/shard_map/all_to_all | solution.py:375
  59.2 3.5 %collective-permute-start = (bf16[2,8,144,128]{3,2,1,0:T(8,128)(2,1)S(1)}, bf16[2,8,144,128]{3,2,1,0:T(8,128)(2,1)S(1)}, u32[]{:S(2)}, u32[]{:S(2)}) collective-permute-start(bf16[2,8,144,128]{3,2,1,0:T(8,128)(2,1)S(1)} %get-tuple-element.10), channel_id=1, source_target_pairs={{0,2},{2,0},{1,3},{3,1},{4,6},{6,4},{5,7},{7,5},{8,10},{10,8},{9,1... | collective-permute-start | bytes 1769480 | tf_op jit(solution)/shard_map/ppermute | solution.py:446
  59.2 11.0 %all-to-all-start.3 = ((bf16[2,2,16,8,384]{4,3,2,1,0:T(8,128)(2,1)}), bf16[2,2,16,8,384]{4,3,2,1,0:T(8,128)(2,1)S(1)}, u32[]{:S(2)}, u32[]{:S(2)}) async-start(bf16[2,2,16,8,384]{4,3,2,1,0:T(8,128)(2,1)} %bitcast.11), calls=%async_computation.3 | async-start | bytes 786432 | tf_op jit(solution)/shard_map/all_to_all | solution.py:479
  70.2 20.0 %all-to-all-start.4 = ((bf16[16,144,128]{2,1,0:T(8,128)(2,1)}), bf16[16,144,128]{2,1,0:T(8,128)(2,1)S(1)}, u32[]{:S(2)}, u32[]{:S(2)}) async-start(bf16[16,144,128]{2,1,0:T(8,128)(2,1)} %bitcast.15), calls=%async_computation.4 | async-start | bytes 1179648 | tf_op jit(solution)/shard_map/all_to_all | solution.py:449
  90.2 0.8 copy-start.5

commit v3 on v2

--- a/solution.py
+++ b/solution.py
@@ -71,6 +71,30 @@
 
 def get_tiles(scratch, rows):
     return jnp.concatenate([scratch[tile, rows, :] for tile in range(scratch.shape[0])], axis=-1)
+
+
+def pack_kernel(numbers_ref, tokens_ref, flags_ref, out_ref):
+    dates_each, parts, patches, width = tokens_ref.shape
+    spare = out_ref.shape[1] - dates_each * patches
+    place = lax.broadcasted_iota(jnp.int32, (patches, width), 0)
+    lane = lax.broadcasted_iota(jnp.int32, (patches, width), 1)
+    place = jnp.where(place == lane, 1.0, 0.0).astype(low)
+    lane = lax.broadcasted_iota(jnp.int32, (parts, width), 1)
+    infos = []
+    for date in range(dates_each):
+        number = numbers_ref[date]
+        upper = (number // 32).astype(wide)
+        under = (number % 32).astype(wide)
+        info = matmul(flags_ref[date].astype(wide).astype(low), place)
+        info = jnp.where(lane == patches, upper, info)
+        infos.append(jnp.where(lane == patches + 1, under, info))
+    row = lax.broadcasted_iota(jnp.int32, (spare, width), 0)
+    for part in range(parts):
+        pieces = [tokens_ref[date, part].astype(wide) for date in range(dates_each)]
+        extra = jnp.zeros((spare, width), wide)
+        for date in range(dates_each):
+            extra = jnp.where(row == date, infos[date][part : part + 1], extra)
+        out_ref[part] = jnp.concatenate(pieces + [extra], axis=0).astype(low)
 
 
 def time_kernel(
@@ -145,45 +169,67 @@
     out_ref[...] = get_tiles(seq_scr, slice(None)).astype(low)
 
 
-def column_kernel(
-    sizes,
-    pair_ref,
-    hidden_ref,
-    cotangent_ref,
-    project_ref,
-    output_ref,
-    mixed_ref,
-    first_grad_ref,
-    second_grad_ref,
-    seq_scr,
-    grad_scr,
-    plane_scr,
-    normed_scr,
-    qkv_scr,
-    grad_low_scr,
-    heads_grad_scr,
-    heads_scr,
-    qkv_grad_scr,
-):
-    dates_each, row_parts, rows_each, columns_each, head_count, packed, row_major, date_size = sizes
+def column_kernel(sizes, *refs):
+    dates_each, row_parts, rows_each, columns_each, head_count, packed, date_size, direct = sizes
+    if direct:
+        row_ref, pair_ref, hidden_ref, own_ref, other_ref, project_ref, output_ref = refs[:7]
+        kept_ref, sent_ref, first_grad_ref, second_grad_ref = refs[7:11]
+    else:
+        hidden_ref, cotangent_ref, project_ref, output_ref = refs[:4]
+        mixed_ref, first_grad_ref, second_grad_ref = refs[4:7]
+    (
+        seq_scr,
+        grad_scr,
+        plane_scr,
+        normed_scr,
+        qkv_scr,
+        grad_low_scr,
+        heads_grad_scr,
+        heads_scr,
+        qkv_grad_scr,
+    ) = refs[-9:]
     width = hidden_ref.shape[1]
     head_size = width // head_count
     lanes = packed * head_size
     length = row_parts * rows_each
     groups = dates_each * columns_each
+    part_rows = rows_each * groups
     inverse_root = 1.0 / math.sqrt(head_size)
-    put_tiles(seq_scr, slice(None), hidden_ref[...].astype(wide))
-    put_tiles(grad_scr, slice(None), cotangent_ref[...].astype(wide))
+    if direct:
+        row_at = row_ref[0]
+        for part in range(row_parts):
+            source = pl.multiple_of(((row_at + part) % row_parts) * part_rows, part_rows)
+            put_tiles(
+                seq_scr,
+                slice(part * part_rows, (part + 1) * part_rows),
+                hidden_ref[pl.ds(source, part_rows), :].astype(wide),
+            )
+        own_rows = dates_each * rows_each
+        own = own_ref[...].astype(wide)
+        own = own.reshape(own_rows, row_parts, columns_each, width)
+        own = jnp.where(row_at == 0, own[:, 0], own[:, 1]).reshape(part_rows, width)
+        put_tiles(grad_scr, slice(0, part_rows), own)
+        put_tiles(grad_scr, slice(part_rows, 2 * part_rows), other_ref[...].astype(wide))
+    else:
+        put_tiles(seq_scr, slice(None), hidden_ref[...].astype(wide))
+        put_tiles(grad_scr, slice(None), cotangent_ref[...].astype(wide))
     for group in range(groups):
         rows = slice(group * length, (group + 1) * length)
-        first = (group // columns_each) * (length * columns_each) + group % columns_each
-        if row_major:
+        if direct:
+            inner = (group // columns_each) * (rows_each * columns_each) + group % columns_each
             plane_scr[rows, :] = get_tiles(seq_scr, pl.ds(group, length, stride=groups))
+            pieces = [
+                get_tiles(
+                    grad_scr, pl.ds(part * part_rows + inner, rows_each, stride=columns_each)
+                )
+                for part in range(row_parts)
+            ]
+            grad_low_scr[rows, :] = jnp.concatenate(pieces, axis=0).astype(low)
         else:
-            plane_scr[rows, :] = get_tiles(seq_scr, pl.ds(first, length, stride=columns_each))
-        grad_low_scr[rows, :] = get_tiles(
-            grad_scr, pl.ds(first, length, stride=columns_each)
-        ).astype(low)
+            first = (group // columns_each) * (length * columns_each) + group % columns_each
+            at = pl.ds(first, length, stride=columns_each)
+            plane_scr[rows, :] = get_tiles(seq_scr, at)
+            grad_low_scr[rows, :] = get_tiles(grad_scr, at).astype(low)
     normed_scr[...] = rms_norm(plane_scr[...])
     qkv_scr[...] = matmul(normed_scr[...], project_ref[...]).astype(low)
     heads_grad_scr[...] = contract_last(grad_low_scr[...], output_ref[...]).astype(low)
@@ -236,7 +282,6 @@
             query_grad = own_blocks(query_full, length, packed, head_size) * inverse_root
             qkv_grad_scr[rows, at_query] = query_grad.astype(low)
     mixed = plane_scr[...] + matmul(heads_scr[...], output_ref[...])
-    part_rows = dates_each * rows_each * columns_each
     for group in range(groups):
         inner = (group // columns_each) * (rows_each * columns_each) + group % columns_each
         for part in range(row_parts):
@@ -246,10 +291,14 @@
                 pl.ds(part * part_rows + inner, rows_each, stride=columns_each),
                 mixed[begin : begin + rows_each],
             )
-    mixed_ref[...] = get_tiles(seq_scr, slice(None)).astype(low)
+    if direct:
+        kept_ref[...] = get_tiles(seq_scr, slice(0, part_rows)).astype(low)
+        sent_ref[...] = get_tiles(seq_scr, slice(part_rows, 2 * part_rows)).astype(low)
+    else:
+        mixed_ref[...] = get_tiles(seq_scr, slice(None)).astype(low)
     project_grad = contract_rows(qkv_grad_scr[...], normed_scr[...])
     output_grad = contract_rows(grad_low_scr[...], heads_scr[...])
-    if date_size is None:
+    if not direct:
         first_grad_ref[...] = project_grad
         second_grad_ref[...] = output_grad
         return
@@ -288,15 +337,17 @@
     for source in range(1, terms_ref.shape[0]):
         total = total + terms_ref[source].astype(wide)
     whole = 2 * total.shape[0] // 3
-    main = jnp.transpose(total[:whole])
-    tail = jnp.transpose(total[whole:])
-    tail = jnp.concatenate([tail[:64], tail[64:]], axis=1)
-    first = row_ref[0] == 0
-    front = jnp.concatenate([main, tail], axis=0)
-    back = jnp.concatenate([tail, main], axis=0)
-    owned = jnp.where(first, front, back)
-    project_ref[...] = owned[:, :project_each]
-    output_ref[...] = owned[:, project_each:]
+    main = total[:whole]
+    tail = total[whole:]
+    swapped = pltpu.roll(tail, 64, 1)
+    lower = lax.broadcasted_iota(jnp.int32, (whole, 128), 1) < 64
+    tail_first = jnp.concatenate([tail, swapped], axis=0)
+    turned = pltpu.roll(main, 64, 1)
+    front = jnp.concatenate([main, tail_first[:, :64]], axis=1)
+    back = jnp.concatenate([jnp.where(lower, tail_first, turned), turned[:, :64]], axis=1)
+    owned = jnp.where(row_ref[0] == 0, front, back)
+    project_ref[...] = owned[:project_each]
+    output_ref[...] = owned[project_each:]
 
 
 def body(
@@ -322,24 +373,50 @@
     columns_each = column_count // row_size
     row_count = row_local * row_size
     date_count = date_local * date_size
-    direct = patches_each == column_count
-
-    cotangent_planes = lax.all_to_all(cotangent, "row", split_axis=2, concat_axis=1, tiled=True)
+    project_each = 3 * width // date_size
+    output_each = width // date_size
+    lane_each = width // row_size
+    direct = (
+        patches_each == column_count
+        and column_count % 16 == 0
+        and pair_size == 2
+        and row_size == 2
+        and lane_each == 192
+        and project_each % 8 == 0
+        and output_each % 8 == 0
+        and (project_each + output_each) % 32 == 0
+    )
     token_rows = date_local * patches_each
     block_rows = -(-(token_rows + date_local) // 8) * 8
-    flags = jnp.transpose(
-        clear_flags.reshape(date_local, date_size, patches_each), (1, 0, 2)
-    ).astype(low)
-    numbers = jnp.stack([date_numbers // 32, date_numbers % 32], axis=-1).astype(low)
-    numbers = jnp.broadcast_to(numbers[None], (date_size, date_local, 2))
-    info = jnp.concatenate([flags, numbers], axis=-1)
-    info = jnp.pad(
-        info, ((0, 0), (0, block_rows - token_rows - date_local), (0, width - patches_each - 2))
-    )
-    outgoing = jnp.transpose(
-        tokens.reshape(date_local, date_size, patches_each, width), (1, 0, 2, 3)
-    ).reshape(date_size, token_rows, width)
-    outgoing = jnp.concatenate([outgoing, info], axis=1)
+    params = pltpu.CompilerParams(vmem_limit_bytes=vmem_limit)
+    in_vmem = pl.BlockSpec(memory_space=pltpu.VMEM)
+    in_smem = pl.BlockSpec(memory_space=pltpu.SMEM)
+    if direct:
+        outgoing = pl.pallas_call(
+            pack_kernel,
+            out_shape=jax.ShapeDtypeStruct((date_size, block_rows, width), low),
+            in_specs=[in_smem, in_vmem, in_vmem],
+            compiler_params=params,
+            name="pack_tokens",
+        )(date_numbers, tokens, clear_flags)
+        row_at = lax.axis_index("row")
+        halves = cotangent.reshape(date_local, row_local, row_size, columns_each, width)
+        leaving = lax.dynamic_index_in_dim(halves, 1 - row_at, 2, keepdims=False)
+        other_grad = lax.ppermute(leaving, "row", [(0, 1), (1, 0)])
+    else:
+        flags = jnp.transpose(
+            clear_flags.reshape(date_local, date_size, patches_each), (1, 0, 2)
+        ).astype(low)
+        numbers = jnp.stack([date_numbers // 32, date_numbers % 32], axis=-1).astype(low)
+        numbers = jnp.broadcast_to(numbers[None], (date_size, date_local, 2))
+        info = jnp.concatenate([flags, numbers], axis=-1)
+        info = jnp.pad(
+            info, ((0, 0), (0, block_rows - token_rows - date_local), (0, width - patches_each - 2))
+        )
+        outgoing = jnp.transpose(
+            tokens.reshape(date_local, date_size, patches_each, width), (1, 0, 2, 3)
+        ).reshape(date_size, token_rows, width)
+        outgoing = jnp.concatenate([outgoing, info], axis=1)
     incoming = lax.all_to_all(outgoing, dates, split_axis=0, concat_axis=0, tiled=True)
 
     time_tokens = date_count * patches_each
@@ -356,16 +433,14 @@
             ),
         ),
         out_shape=jax.ShapeDtypeStruct((time_tokens, width), low),
-        in_specs=[pl.BlockSpec(memory_space=pltpu.SMEM)]
-        + [pl.BlockSpec(memory_space=pltpu.VMEM)] * 3,
-        out_specs=pl.BlockSpec(memory_space=pltpu.VMEM),
+        in_specs=[in_smem, in_vmem, in_vmem, in_vmem],
         scratch_shapes=[
             pltpu.VMEM((width // 128, time_tokens, 128), wide),
             pltpu.VMEM((time_tokens, width), wide),
             pltpu.VMEM((time_tokens, 3 * width), low),
             pltpu.VMEM((time_tokens, width), low),
         ],
-        compiler_params=pltpu.CompilerParams(vmem_limit_bytes=vmem_limit),
+        compiler_params=params,
         name="time_attention",
     )(decay_slopes, incoming, time_project, time_output)
 
@@ -381,29 +456,34 @@
         )
         plane = lax.all_to_all(back, "row", split_axis=2, concat_axis=1, tiled=True)
     plane = plane.reshape(column_tokens, width)
-    project_each = 3 * width // date_size
-    output_each = width // date_size
-    lane_each = width // row_size
-    paired = (
-        pair_size == 2
-        and row_size == 2
-        and lane_each == 192
-        and project_each % 8 == 0
-        and output_each % 8 == 0
-        and (project_each + output_each) % 32 == 0
-    )
-    pair_at = lax.axis_index("pair")
-    if paired:
-        packed_rows = (project_each + output_each) * 3 // 2
-        grad_shapes = (
-            jax.ShapeDtypeStruct((row_size, date_size // 2, packed_rows, 128), low),
-        ) * 2
-    else:
-        grad_shapes = (
+    half_tokens = column_tokens // row_size
+    half_shape = jax.ShapeDtypeStruct((half_tokens, width), low)
+    packed_rows = (project_each + output_each) * 3 // 2
+    if direct:
+        operands = (
+            row_at.reshape(1),
+            lax.axis_index("pair").reshape(1),
+            plane,
+            cotangent.reshape(local_patches * date_local, width),
+            other_grad.reshape(half_tokens, width),
+        )
+        half_grads = jax.ShapeDtypeStruct((row_size, date_size // 2, packed_rows, 128), low)
+        out_shape = (half_shape, half_shape, half_grads, half_grads)
+        in_specs = [in_smem] * 2 + [in_vmem] * 5
+    else:
+        operands = (
+            plane,
+            lax.all_to_all(cotangent, "row", split_axis=2, concat_axis=1, tiled=True).reshape(
+                column_tokens, width
+            ),
+        )
+        out_shape = (
+            jax.ShapeDtypeStruct((column_tokens, width), low),
             jax.ShapeDtypeStruct((3 * width, width), wide),
             jax.ShapeDtypeStruct((width, width), wide),
         )
-    mixed, first_grad, second_grad = pl.pallas_call(
+        in_specs = [in_vmem] * 4
+    results = pl.pallas_call(
         functools.partial(
             column_kernel,
             (
@@ -413,13 +493,12 @@
                 columns_each,
                 head_count,
                 packed,
+                date_size,
                 direct,
-                date_size if paired else None,
             ),
         ),
-        out_shape=(jax.ShapeDtypeStruct((column_tokens, width), low), *grad_shapes),
-        in_specs=[pl.BlockSpec(memory_space=pltpu.SMEM)]
-        + [pl.BlockSpec(memory_space=pltpu.VMEM)] * 4,
+        out_shape=out_shape,
+        in_specs=in_specs,
         scratch_shapes=[
             pltpu.VMEM((width // 128, column_tokens, 128), wide),
             pltpu.VMEM((width // 128, column_tokens, 128), wide),
@@ -431,39 +510,38 @@
             pltpu.VMEM((column_tokens, width), low),
             pltpu.VMEM((column_tokens, 3 * width), low),
         ],
-        compiler_params=pltpu.CompilerParams(vmem_limit_bytes=vmem_limit),
+        compiler_params=params,
         name="column_attention",
-    )(
-        pair_at.reshape(1),
-        plane,
-        cotangent_planes.reshape(column_tokens, width),
-        column_project,
-        column_output,
-    )
-
-
-    if paired:
-        arrived = lax.ppermute(second_grad, "pair", [(0, 1), (1, 0)])
-        halves = (first_grad.astype(wide) + arrived.astype(wide)).astype(low)
-        halves = halves.reshape(row_size * date_size // 2, packed_rows, 128)
-        terms = lax.all_to_all(halves, ("row", "outer"), split_axis=0, concat_axis=0, tiled=True)
+    )(*operands, column_project, column_output)
+
+    if direct:
+        kept, sent, kept_grad, sent_grad = results
+        arrived_grad = lax.ppermute(sent_grad, "pair", [(0, 1), (1, 0)])
+        arrived = lax.ppermute(sent, "row", [(0, 1), (1, 0)])
+        pair_sum = (kept_grad.astype(wide) + arrived_grad.astype(wide)).astype(low)
+        pair_sum = pair_sum.reshape(row_size * date_size // 2, packed_rows, 128)
+        terms = lax.all_to_all(pair_sum, ("row", "outer"), split_axis=0, concat_axis=0, tiled=True)
         owned_project, owned_output = pl.pallas_call(
             functools.partial(finish_kernel, project_each),
             out_shape=(
-                jax.ShapeDtypeStruct((lane_each, project_each), wide),
-                jax.ShapeDtypeStruct((lane_each, output_each), wide),
+                jax.ShapeDtypeStruct((project_each, lane_each), wide),
+                jax.ShapeDtypeStruct((output_each, lane_each), wide),
             ),
-            in_specs=[
-                pl.BlockSpec(memory_space=pltpu.SMEM),
-                pl.BlockSpec(memory_space=pltpu.VMEM),
-            ],
+            in_specs=[in_smem, in_vmem],
+            compiler_params=params,
             name="gradient_sum",
-        )(lax.axis_index("row").reshape(1), terms)
-    else:
+        )(row_at.reshape(1), terms)
+        quarter = (date_local, row_local, 1, columns_each, width)
+        kept, arrived = kept.reshape(quarter), arrived.reshape(quarter)
+        mixed = jnp.concatenate(
+            [jnp.where(row_at == 0, kept, arrived), jnp.where(row_at == 0, arrived, kept)], axis=2
+        )
+    else:
+        mixed, project_grad, output_grad = results
         grads = jnp.concatenate(
             [
-                first_grad.reshape(date_size, project_each, row_size, lane_each),
-                second_grad.reshape(date_size, output_each, row_size, lane_each),
+                project_grad.reshape(date_size, project_each, row_size, lane_each),
+                output_grad.reshape(date_size, output_each, row_size, lane_each),
             ],
             axis=1,
         ).astype(low)
@@ -472,15 +550,12 @@
         )
         terms = lax.all_to_all(grads, ("row", *dates), split_axis=0, concat_axis=0, tiled=True)
         owned = jnp.sum(terms.astype(wide), axis=0)
-        owned_project = jnp.transpose(owned[:project_each])
-        owned_output = jnp.transpose(owned[project_each:])
-
-    mixed = mixed.reshape(row_size, date_local, row_local, columns_each, width)
-    mixed = lax.all_to_all(mixed, "row", split_axis=0, concat_axis=0, tiled=True)
-    mixed = jnp.transpose(mixed, (1, 2, 0, 3, 4)).reshape(
-        date_local, row_local, column_count, width
-    )
-    return (mixed, owned_project, owned_output)
+        owned_project, owned_output = owned[:project_each], owned[project_each:]
+        mixed = mixed.reshape(row_size, date_local, row_local, columns_each, width)
+        mixed = lax.all_to_all(mixed, "row", split_axis=0, concat_axis=0, tiled=True)
+        mixed = jnp.transpose(mixed, (1, 2, 0, 3, 4))
+    mixed = mixed.reshape(date_local, row_local, column_count, width)
+    return (mixed, jnp.transpose(owned_project), jnp.transpose(owned_output))
 
 
 def solution(mesh):

time: 96.9 us -> 78.4 us (0.81)
  waiting for transfers between devices: 49.6 us -> 27.1 us
  blocking collectives: 0 us -> 20.9 us
  starting transfers between devices: 21.1 us -> 11.6 us
  local copies, waits for them, and re-layouts: 6.94 us -> 2.49 us
  other arithmetic: 3.31 us -> 1.81 us
  Pallas kernels: 14.4 us -> 13.3 us
    all_to_all x4 -> x1, waiting for transfers between devices: 36.6 us -> 4.06 us  [body(): lax.all_to_all(pair_sum, ('row', 'outer'), split_axis=0, concat_axis=0, t...]
    all_to_all x0 -> x1, blocking collectives: none -> 20.9 us  [body(): lax.all_to_all(outgoing, dates, split_axis=0, concat_axis=0, tiled=True)]
    ppermute x1 -> x3, waiting for transfers between devices: 0.01 us -> 20.1 us  [the longest x1 9.79 us: body(): arrived = lax.ppermute(sent, 'row', [(0, 1), (1, 0)])]
    all_to_all x4 -> x1, starting transfers between devices: 17.9 us -> 3.75 us  [body(): lax.all_to_all(pair_sum, ('row', 'outer'), split_axis=0, concat_axis=0, t...]
    all_to_all x1, waiting for transfers between devices: 13 us -> 2.86 us  [body(): lax.all_to_all(parts, ('row', *dates), split_axis=0, concat_axis=0, tiled...]
    ppermute x1 -> x3, starting transfers between devices: 0.01 us -> 3.83 us  [the longest x1 1.93 us: body(): arrived = lax.ppermute(sent, 'row', [(0, 1), (1, 0)])]
    unnamed x18, local copies, waits for them, and re-layouts: 4.86 us -> 2.46 us
    pallas_call x1, Pallas kernels: 1.97 us -> 0.78 us  [body(): pl.pallas_call(functools.partial(finish_kernel, project_each), out_shape=...]
  transfers between devices with their start and end apart: 6 -> 5, of which waited for: 5 -> 5; matrix products, arithmetic and copies ran while one was open for 3% -> 1% of each run, Pallas kernels for 6% -> 0%
where the time goes in v3:
time: 78.4 us; the launch traced here: 77.9 us
  waiting for transfers between devices  27.1 us (35%)
  blocking collectives  20.9 us (27%)
  Pallas kernels  13.3 us (17%)
  starting transfers between devices  11.6 us (15%)
  local copies, waits for them, and re-layouts  2.49 us (3%)
  other arithmetic  1.81 us (2%)
    all_to_all x1, blocking collectives, body(): lax.all_to_all(outgoing, dates, split_axis=0, concat_axis=0, tiled=True)  20.9 us
    ppermute x1, waiting for transfers between devices, body(): arrived = lax.ppermute(sent, 'row', [(0, 1), (1, 0)])  9.79 us
    ppermute x1, waiting for transfers between devices, body(): other_grad = lax.ppermute(leaving, 'row', [(0, 1), (1, 0)])  8.36 us
    pallas_call x1, Pallas kernels, body(): pl.pallas_call(functools.partial(column_kernel, (date_local, row_size, ro...  6.33 us
    pallas_call x1, Pallas kernels, body(): pl.pallas_call(functools.partial(time_kernel, (date_size, date_local, pat...  5.51 us
    all_to_all x1, waiting for transfers between devices, body(): lax.all_to_all(pair_sum, ('row', 'outer'), split_axis=0, concat_axis=0, t...  4.06 us
    all_to_all x1, starting transfers between devices, body(): lax.all_to_all(parts, ('row', *dates), split_axis=0, concat_axis=0, tiled...  4.02 us
    all_to_all x1, starting transfers between devices, body(): lax.all_to_all(pair_sum, ('row', 'outer'), split_axis=0, concat_axis=0, t...  3.75 us
  transfers between devices with their start and end apart: 5, of which 5 were waited for; matrix products, arithmetic and copies ran while one was open for 1% of the time, Pallas kernels for 0%

profile of v3, /device:TPU:0, one launch (start us, length us, event | category | flops | bytes accessed | tf_op | source)
XLA Modules:
  0.0 77.9 jit_solution(18391098950475402848)
XLA Ops:
  0.6 0.0 copy-start
  0.6 0.0 copy-start.3
  0.7 1.1 %copy-done.3 = bf16[2,16,16,384]{3,2,1,0:T(8,128)(2,1)S(1)} copy-done((bf16[2,16,16,384]{3,2,1,0:T(8,128)(2,1)S(1)}, bf16[2,16,16,384]{3,2,1,0:T(8,128)(2,1)}, u32[]{:S(2)}) %copy-start.3) | copy-done | bytes 393240
  1.7 0.0 copy-start.6
  1.7 0.7 copy-done.6
  2.4 0.0 copy-start.7
  2.4 0.7 copy-done.7
  3.1 0.0 copy-start.4
  3.1 0.0 copy-start.8
  3.1 0.7 pack_tokens.1
  3.8 20.9 %all_to_all.15.block_ref = bf16[16,40,384]{2,1,0:T(8,128)(2,1)S(1)} all-to-all(bf16[16,40,384]{2,1,0:T(8,128)(2,1)S(1)} %pack_tokens.1), channel_id=1, replica_groups=mesh['outer'=8,'pair'=2,'row'=2] {'outer','pair'}, dimensions={0} | all-to-all | bytes 983040 | tf_op jit(solution)/shard_map/all_to_all | solution.py:420
  24.7 0.0 copy-done
  24.7 0.0 copy-done.4
  24.7 0.0 copy-done.8
  24.7 0.0 copy-start.2
  24.7 5.5 %time_attention.1 = bf16[512,384]{1,0:T(8,128)(2,1)} custom-call(f32[12]{0:T(128)S(1)} %copy-done.8, bf16[16,40,384]{2,1,0:T(8,128)(2,1)S(1)} %all_to_all.15.block_ref, bf16[384,1152]{1,0:T(8,128)(2,1)S(1)} %copy-done, bf16[384,384]{1,0:T(8,128)(2,1)S(1)} %copy-done.4), custom_call_target="tpu_custom_call" | custom-call | tf_op jit(solution)/shard_map/time_attention/pallas_call | solution.py:423
  30.2 0.0 copy-start.1
  30.2 0.0 copy-start.5
  30.2 4.0 %all-to-all-start.1 = ((bf16[32,16,384]{2,1,0:T(8,128)(2,1)}), bf16[32,16,384]{2,1,0:T(8,128)(2,1)S(1)}, u32[]{:S(2)}, u32[]{:S(2)}) async-start(bf16[32,16,384]{2,1,0:T(8,128)(2,1)} %bitcast.2), calls=%async_computation.1 | async-start | bytes 786432 | tf_op jit(solution)/shard_map/all_to_all | solution.py:450
  34.3 0.0 copy-done.2
  34.3 1.8 %collective-permute-start = (bf16[2,16,8,384]{3,2,1,0:T(8,128)(2,1)S(1)}, bf16[2,16,8,384]{3,2,1,0:T(8,128)(2,1)S(1)}, u32[]{:S(2)}, u32[]{:S(2)}) collective-permute-start(bf16[2,16,8,384]{3,2,1,0:T(8,128)(2,1)S(1)} %dynamic-slice_bitcast_fusion), channel_id=1, source_target_pairs={{0,1},{1,0},{2,3},{3,2},{4,5},{5,4},{6,7},{7,6},{8,9},{9,8},{10,11... | collective-permute-start | bytes 589832 | tf_op jit(solution)/shard_map/ppermute | solution.py:405
  36.2 8.4 %collective-permute-done = bf16[2,16,8,384]{3,2,1,0:T(8,128)(2,1)S(1)} collective-permute-done((bf16[2,16,8,384]{3,2,1,0:T(8,128)(2,1)S(1)}, bf16[2,16,8,384]{3,2,1,0:T(8,128)(2,1)S(1)}, u32[]{:S(2)}, u32[]{:S(2)}) %collective-permute-start) | collective-permute-done | bytes 196640 | tf_op jit(solution)/shard_map/ppermute | solution.py:405
  44.5 2.9 %all-to-all-done.1 = bf16[32,16,384]{2,1,0:T(8,128)(2,1)S(1)} async-done(((bf16[32,16,384]{2,1,0:T(8,128)(2,1)}), bf16[32,16,384]{2,1,0:T(8,128)(2,1)S(1)}, u32[]{:S(2)}, u32[]{:S(2)}) %all-to-all-start.1) | async-done | bytes 393248 | tf_op jit(solution)/shard_map/all_to_all | solution.py:450
  47.4 0.0 copy-done.1
  47.4 0.0 copy-done.5
  47.4 6.3 %column_attention.1 = (bf16[256,384]{1,0:T(8,128)(2,1)S(1)}, bf16[256,384]{1,0:T(8,128)(2,1)S(1)}, bf16[2,8,144,128]{3,2,1,0:T(8,128)(2,1)S(1)}, bf16[2,8,144,128]{3,2,1,0:T(8,128)(2,1)S(1)}) custom-call(s32[1]{0:T(128)} %bitcast.refs_0_.row_ref, s32[1]{0:T(128)} %bitcast.1.refs_1_, bf16[512,384]{1,0:T(8,128)(2,1)S(1)} %bitcast.16, ...), custom_call_target="tpu_custom_call" | custom-call | tf_op jit(solution)/shard_map/column_attention/pallas_call | solution.py:486
  53.7 0.1 collective-permute-start.2
  53.8 2.0 %collective-permute-done.2 = bf16[2,8,144,128]{3,2,1,0:T(8,128)(2,1)S(1)} collective-permute-done((bf16[2,8,144,128]{3,2,1,0:T(8,128)(2,1)S(1)}, bf16[2,8,144,128]{3,2,1,0:T(8,128)(2,1)S(1)}, u32[]{:S(2)}, u32[]{:S(2)}) %collective-permute-start.2) | collective-permute-done | bytes 589856 | tf_op jit(solution)/shard_map/ppermute | solution.py:519
  55.8 1.0 %add_convert_fusion = bf16[2,8,144,128]{3,2,1,0:T(8,128)(2,1)} fusion(bf16[2,8,144,128]{3,2,1,0:T(8,128)(2,1)S(1)} %collective-permute-done.2, bf16[2,8,144,128]{3,2,1,0:T(8,128)(2,1)S(1)} %get-tuple-element.11), kind=kLoop, calls=%fused_computation | loop fusion | flops 1179648 | bytes 1769472 | tf_op jit(solution)/shard_map/convert_element_type | solution.py:521
  56.8 3.8 %all-to-all-start.2 = ((bf16[16,144,128]{2,1,0:T(8,128)(2,1)}), bf16[16,144,128]{2,1,0:T(8,128)(2,1)S(1)}, u32[]{:S(2)}, u32[]{:S(2)}) async-start(bf16[16,144,128]{2,1,0:T(8,128)(2,1)} %bitcast.11), calls=%async_computation.2 | async-start | bytes 1179648 | tf_op jit(solution)/shard_map/all_to_all | solution.py:523
  60.5 1.9 %collective-permute-start.1 = (bf16[256,384]{1,0:T(8,128)(2,1)S(1)}, bf16[256,384]{1,0:T(8,128)(2,1)S(1)}, u32[]{:S(2)}, u32[]{:S(2)}) collective-permute-start(bf16[256,384]{1,0:T(8,128)(2,1)S(1)} %get-tuple-element.10), channel_id=1, source_target_pairs={{0,1},{1,0},{2,3},{3,2},{4,5},{5,4},{6,7},{7,6},{8,9},{9,8},{10,11... | collective-permute-start | bytes 589832 | tf_op jit(solution)/shard_map/ppermute | solution.py:520
  62.5 9.8 %collective-permute-done.1 = bf16[256,384]{1,0:T(8,128)(2,1)S(1)} collective-permute-done((bf16[256,384]{1,0:T(8,128)(2,1)S(1)}, bf16[256,384]{1,0:T(8,128)(2,1)S(1)}, u32[]{:S(2)}, u32[]{:S(2)}) %collective-permute-start.1) | collective-permute-done | bytes 196640 | tf_op jit(solution)/shard_map/ppermute | solution.py:520
  72.3 0.8 %copy_bitcast_fusion = bf16[2,16,16,384]{3,2,1,0:T(8,128)(2,1)} fusion(bf16[2,16,1,8,384]{4,3,1,0,2:T(8,128)(2,1)S(1)} %bitcast.21, bf16[2,16,1,8,384]{4,3,1,0,2:T(8,128)(2,1)S(1)} %bitcast.20), kind=kLoop, calls=%fused_computation.2 | loop fusion | flops 196608 | bytes 786432 | tf_op jit(solution)/shard_map/reshape | solution.py:557
  73.1 4.1 %all-to-all-done.2.terms_ref = bf16[16,144,128]{2,1,0:T(8,128)(2,1)S(1)} async-done(((bf16[16,144,128]{2,1,0:T(8,128)(2,1)}), bf16[16,144,128]{2,1,0:T(8,128)(2,1)S(1)}, u32[]{:S(2)}, u32[]{:S(2)}) %all-to-all-start.2) | async-done | bytes 589856 | tf_op jit(solution)/shard_map/all_to_all | solution.py:523
  77.2 0.8 gradient_sum.1
  (2 shorter events, 0.1 us)
Async XLA Ops:
  0.6 24.1 %copy-start = (bf16[384,1152]{1,0:T(8,128)(2,1)S(1)}, bf16[384,1152]{1,0:T(8,128)(2,1)}, u32[]{:S(2)}) copy-start(bf16[384,1152]{1,0:T(8,128)(2,1)} %project_ref.1) | copy-start | bytes 2654212
  0.6 1.1 %copy-start.3 = (bf16[2,16,16,384]{3,2,1,0:T(8,128)(2,1)S(1)}, bf16[2,16,16,384]{3,2,1,0:T(8,128)(2,1)}, u32[]{:S(2)}) copy-start(bf16[2,16,16,384]{3,2,1,0:T(8,128)(2,1)} %tokens_ref.1) | copy-start | bytes 1179652
  1.7 0.7 copy-start.6
  2.4 0.7 copy-start.7
  3.1 21.6 %copy-start.4 = (bf16[384,384]{1,0:T(8,128)(2,1)S(1)}, bf16[384,384]{1,0:T(8,128)(2,1)}, u32[]{:S(2)}) copy-start(bf16[384,384]{1,0:T(8,128)(2,1)} %output_ref.1) | copy-start | bytes 884740
  3.1 21.6 %copy-start.8 = (f32[12]{0:T(128)S(1)}, f32[12]{0:T(128)}, u32[]{:S(2)}) copy-start(f32[12]{0:T(128)} %slopes_ref.1) | copy-start | bytes 148
  24.7 9.6 %copy-start.2 = (bf16[2,16,16,384]{3,2,1,0:T(8,128)(2,1)S(1)}, bf16[2,16,16,384]{3,2,1,0:T(8,128)(2,1)}, u32[]{:S(2)}) copy-start(bf16[2,16,16,384]{3,2,1,0:T(8,128)(2,1)} %param.17) | copy-start | bytes 1179652
  30.2 17.1 %copy-start.1 = (bf16[384,1152]{1,0:T(8,128)(2,1)S(1)}, bf16[384,1152]{1,0:T(8,128)(2,1)}, u32[]{:S(2)}) copy-start(bf16[384,1152]{1,0:T(8,128)(2,1)} %refs_5_.1) | copy-start | bytes 2654212
  30.2 17.1 %copy-start.5 = (bf16[384,384]{1,0:T(8,128)(2,1)S(1)}, bf16[384,384]{1,0:T(8,128)(2,1)}, u32[]{:S(2)}) copy-start(bf16[384,384]{1,0:T(8,128)(2,1)} %refs_6_.1) | copy-start | bytes 884740
  30.2 17.1 %all-to-all-start.1 = ((bf16[32,16,384]{2,1,0:T(8,128)(2,1)}), bf16[32,16,384]{2,1,0:T(8,128)(2,1)S(1)}, u32[]{:S(2)}, u32[]{:S(2)}) async-start(bf16[32,16,384]{2,1,0:T(8,128)(2,1)} %bitcast.2), calls=%async_computation.1 | async-start | bytes 786432 | tf_op jit(solution)/shard_map/all_to_all | solution.py:450
  34.3 10.2 %collective-permute-start = (bf16[2,16,8,384]{3,2,1,0:T(8,128)(2,1)S(1)}, bf16[2,16,8,384]{3,2,1,0:T(8,128)(2,1)S(1)}, u32[]{:S(2)}, u32[]{:S(2)}) collective-permute-start(bf16[2,16,8,384]{3,2,1,0:T(8,128)(2,1)S(1)} %dynamic-slice_bitcast_fusion), channel_id=1, source_target_pairs={{0,1},{1,0},{2,3},{3,2},{4,5},{5,4},{6,7},{7,6},{8,9},{9,8},{10,11... | collective-permute-start | bytes 589832 | tf_op jit(solution)/shard_map/ppermute | solution.py:405
  53.7 2.1 %collective-permute-start.2 = (bf16[2,8,144,128]{3,2,1,0:T(8,128)(2,1)S(1)}, bf16[2,8,144,128]{3,2,1,0:T(8,128)(2,1)S(1)}, u32[]{:S(2)}, u32[]{:S(2)}) collective-permute-start(bf16[2,8,144,128]{3,2,1,0:T(8,128)(2,1)S(1)} %get-tuple-element.12), channel_id=1, source_target_pairs={{0,2},{2,0},{1,3},{3,1},{4,6},{6,4},{5,7},{7,5},{8,10},{10,8},{9,1... | collective-permute-start | bytes 1769480 | tf_op jit(solution)/shard_map/ppermute | solution.py:519
  56.8 20.4 %all-to-all-start.2 = ((bf16[16,144,128]{2,1,0:T(8,128)(2,1)}), bf16[16,144,128]{2,1,0:T(8,128)(2,1)S(1)}, u32[]{:S(2)}, u32[]{:S(2)}) async-start(bf16[16,144,128]{2,1,0:T(8,128)(2,1)} %bitcast.11), calls=%async_computation.2 | async-start | bytes 1179648 | tf_op jit(solution)/shard_map/all_to_all | solution.py:523
  60.5 11.7 %collective-permute-start.1 = (bf16[256,384]{1,0:T(8,128)(2,1)S(1)}, bf16[256,384]{1,0:T(8,128)(2,1)S(1)}, u32[]{:S(2)}, u32[]{:S(2)}) collective-permute-start(bf16[256,384]{1,0:T(8,128)(2,1)S(1)} %get-tuple-element.10), channel_id=1, source_target_pairs={{0,1},{1,0},{2,3},{3,2},{4,5},{5,4},{6,7},{7,6},{8,9},{9,8},{10,11... | collective-permute-start | bytes 589832 | tf_op jit(solution)/shard_map/ppermute | solution.py:520

commit v4 on v3

--- a/solution.py
+++ b/solution.py
@@ -11,7 +11,7 @@
 epsilon = 1e-06
 masked_score = -1e30
 units_each = 6
-dates = ("outer", "pair")
+dates = ("outer", "mid", "pair")
 vmem_limit = 48 * 1024 * 1024
 low = jnp.bfloat16
 wide = jnp.float32
@@ -73,35 +73,64 @@
     return jnp.concatenate([scratch[tile, rows, :] for tile in range(scratch.shape[0])], axis=-1)
 
 
-def pack_kernel(numbers_ref, tokens_ref, flags_ref, out_ref):
+def pack_kernel(
+    numbers_ref, tokens_ref, flags_ref, out_ref, numbers_scr, tokens_scr, flags_scr, copied
+):
+    copies = [
+        pltpu.make_async_copy(tokens_ref, tokens_scr, copied.at[0]),
+        pltpu.make_async_copy(flags_ref, flags_scr, copied.at[1]),
+        pltpu.make_async_copy(numbers_ref, numbers_scr, copied.at[2]),
+    ]
+    for copy in copies:
+        copy.start()
     dates_each, parts, patches, width = tokens_ref.shape
-    spare = out_ref.shape[1] - dates_each * patches
-    place = lax.broadcasted_iota(jnp.int32, (patches, width), 0)
-    lane = lax.broadcasted_iota(jnp.int32, (patches, width), 1)
+    lanes = out_ref.shape[2]
+    tiles = width // lanes
+    spare = out_ref.shape[1] - tiles * dates_each * patches
+    place = lax.broadcasted_iota(jnp.int32, (patches, lanes), 0)
+    lane = lax.broadcasted_iota(jnp.int32, (patches, lanes), 1)
     place = jnp.where(place == lane, 1.0, 0.0).astype(low)
-    lane = lax.broadcasted_iota(jnp.int32, (parts, width), 1)
+    lane = lax.broadcasted_iota(jnp.int32, (parts, lanes), 1)
+    row = lax.broadcasted_iota(jnp.int32, (spare, lanes), 0)
+    copies[1].wait()
+    copies[2].wait()
     infos = []
     for date in range(dates_each):
-        number = numbers_ref[date]
+        number = numbers_scr[date]
         upper = (number // 32).astype(wide)
         under = (number % 32).astype(wide)
-        info = matmul(flags_ref[date].astype(wide).astype(low), place)
+        info = matmul(flags_scr[date].astype(wide).astype(low), place)
         info = jnp.where(lane == patches, upper, info)
         infos.append(jnp.where(lane == patches + 1, under, info))
-    row = lax.broadcasted_iota(jnp.int32, (spare, width), 0)
+    copies[0].wait()
     for part in range(parts):
-        pieces = [tokens_ref[date, part].astype(wide) for date in range(dates_each)]
-        extra = jnp.zeros((spare, width), wide)
+        tokens = jnp.concatenate(
+            [tokens_scr[date, part].astype(wide) for date in range(dates_each)], axis=0
+        )
+        extra = jnp.zeros((spare, lanes), wide)
         for date in range(dates_each):
             extra = jnp.where(row == date, infos[date][part : part + 1], extra)
+        pieces = [tokens[:, tile * lanes : (tile + 1) * lanes] for tile in range(tiles)]
         out_ref[part] = jnp.concatenate(pieces + [extra], axis=0).astype(low)
 
 
 def time_kernel(
-    sizes, slopes_ref, block_ref, project_ref, output_ref, out_ref, seq_scr, token_scr, qkv_scr, heads_scr
+    sizes,
+    slopes_ref,
+    block_ref,
+    project_ref,
+    output_ref,
+    earlier_ref,
+    out_ref,
+    seq_scr,
+    token_scr,
+    qkv_scr,
+    heads_scr,
 ):
     sources, dates_each, groups, head_count, packed, columns_each = sizes
-    width = block_ref.shape[2]
+    width = project_ref.shape[0]
+    tile_lanes = block_ref.shape[2]
+    tiles = width // tile_lanes
     head_size = width // head_count
     lanes = packed * head_size
     length = sources * dates_each
@@ -110,10 +139,14 @@
     info = []
     for source in range(sources):
         plane = block_ref[source].astype(wide)
-        put_tiles(
-            seq_scr, slice(source * token_rows, (source + 1) * token_rows), plane[:token_rows]
-        )
-        info.append(plane[token_rows : token_rows + dates_each])
+        rows = slice(source * token_rows, (source + 1) * token_rows)
+        for tile in range(tiles):
+            at = slice(tile * token_rows, (tile + 1) * token_rows)
+            if tiles == 1:
+                put_tiles(seq_scr, rows, plane[at])
+            else:
+                seq_scr[tile, rows, :] = plane[at]
+        info.append(plane[tiles * token_rows : tiles * token_rows + dates_each])
     info = jnp.concatenate(info, axis=0)
     for group in range(groups):
         token_scr[group * length : (group + 1) * length, :] = get_tiles(
@@ -169,25 +202,48 @@
     out_ref[...] = get_tiles(seq_scr, slice(None)).astype(low)
 
 
+def cotangent_kernel(sizes, *refs):
+    dates_each, row_parts, rows_each, columns_each, direct = sizes
+    output_ref, grad_low_ref, heads_grad_ref, grad_scr = refs[-4:]
+    width = output_ref.shape[0]
+    length = row_parts * rows_each
+    groups = dates_each * columns_each
+    part_rows = rows_each * groups
+    if direct:
+        row_ref, own_ref, other_ref = refs[:3]
+        own = own_ref[...].astype(wide)
+        own = own.reshape(dates_each * rows_each, row_parts, columns_each, width)
+        own = jnp.where(row_ref[0] == 0, own[:, 0], own[:, 1]).reshape(part_rows, width)
+        put_tiles(grad_scr, slice(0, part_rows), own)
+        put_tiles(grad_scr, slice(part_rows, 2 * part_rows), other_ref[...].astype(wide))
+    else:
+        put_tiles(grad_scr, slice(None), refs[0][...].astype(wide))
+    for group in range(groups):
+        if direct:
+            inner = (group // columns_each) * (rows_each * columns_each) + group % columns_each
+            pieces = [
+                get_tiles(
+                    grad_scr, pl.ds(part * part_rows + inner, rows_each, stride=columns_each)
+                )
+                for part in range(row_parts)
+            ]
+            values = jnp.concatenate(pieces, axis=0)
+        else:
+            first = (group // columns_each) * (length * columns_each) + group % columns_each
+            values = get_tiles(grad_scr, pl.ds(first, length, stride=columns_each))
+        grad_low_ref[group * length : (group + 1) * length, :] = values.astype(low)
+    heads_grad_ref[...] = contract_last(grad_low_ref[...], output_ref[...]).astype(low)
+
+
 def column_kernel(sizes, *refs):
     dates_each, row_parts, rows_each, columns_each, head_count, packed, date_size, direct = sizes
     if direct:
-        row_ref, pair_ref, hidden_ref, own_ref, other_ref, project_ref, output_ref = refs[:7]
-        kept_ref, sent_ref, first_grad_ref, second_grad_ref = refs[7:11]
-    else:
-        hidden_ref, cotangent_ref, project_ref, output_ref = refs[:4]
-        mixed_ref, first_grad_ref, second_grad_ref = refs[4:7]
-    (
-        seq_scr,
-        grad_scr,
-        plane_scr,
-        normed_scr,
-        qkv_scr,
-        grad_low_scr,
-        heads_grad_scr,
-        heads_scr,
-        qkv_grad_scr,
-    ) = refs[-9:]
+        row_ref, pair_ref, *refs = refs
+        kept_ref, sent_ref, first_grad_ref, second_grad_ref = refs[5:9]
+    else:
+        mixed_ref, first_grad_ref, second_grad_ref = refs[5:8]
+    hidden_ref, grad_low_scr, heads_grad_scr, project_ref, output_ref = refs[:5]
+    seq_scr, plane_scr, normed_scr, qkv_scr, heads_scr, qkv_grad_scr = refs[-6:]
     width = hidden_ref.shape[1]
     head_size = width // head_count
     lanes = packed * head_size
@@ -196,43 +252,25 @@
     part_rows = rows_each * groups
     inverse_root = 1.0 / math.sqrt(head_size)
     if direct:
-        row_at = row_ref[0]
         for part in range(row_parts):
-            source = pl.multiple_of(((row_at + part) % row_parts) * part_rows, part_rows)
+            source = pl.multiple_of(((row_ref[0] + part) % row_parts) * part_rows, part_rows)
             put_tiles(
                 seq_scr,
                 slice(part * part_rows, (part + 1) * part_rows),
                 hidden_ref[pl.ds(source, part_rows), :].astype(wide),
             )
-        own_rows = dates_each * rows_each
-        own = own_ref[...].astype(wide)
-        own = own.reshape(own_rows, row_parts, columns_each, width)
-        own = jnp.where(row_at == 0, own[:, 0], own[:, 1]).reshape(part_rows, width)
-        put_tiles(grad_scr, slice(0, part_rows), own)
-        put_tiles(grad_scr, slice(part_rows, 2 * part_rows), other_ref[...].astype(wide))
     else:
         put_tiles(seq_scr, slice(None), hidden_ref[...].astype(wide))
-        put_tiles(grad_scr, slice(None), cotangent_ref[...].astype(wide))
     for group in range(groups):
         rows = slice(group * length, (group + 1) * length)
         if direct:
-            inner = (group // columns_each) * (rows_each * columns_each) + group % columns_each
-            plane_scr[rows, :] = get_tiles(seq_scr, pl.ds(group, length, stride=groups))
-            pieces = [
-                get_tiles(
-                    grad_scr, pl.ds(part * part_rows + inner, rows_each, stride=columns_each)
-                )
-                for part in range(row_parts)
-            ]
-            grad_low_scr[rows, :] = jnp.concatenate(pieces, axis=0).astype(low)
+            at = pl.ds(group, length, stride=groups)
         else:
             first = (group // columns_each) * (length * columns_each) + group % columns_each
             at = pl.ds(first, length, stride=columns_each)
-            plane_scr[rows, :] = get_tiles(seq_scr, at)
-            grad_low_scr[rows, :] = get_tiles(grad_scr, at).astype(low)
+        plane_scr[rows, :] = get_tiles(seq_scr, at)
     normed_scr[...] = rms_norm(plane_scr[...])
     qkv_scr[...] = matmul(normed_scr[...], project_ref[...]).astype(low)
-    heads_grad_scr[...] = contract_last(grad_low_scr[...], output_ref[...]).astype(low)
     mask = block_mask(length, packed, head_size)
     for units in batches(groups, head_count // packed, units_each):
         places = []
@@ -327,15 +365,54 @@
             )
         for row_part in range(2):
             for first, one, two in zip((0, 2 * half), pair[0][row_part], pair[1][row_part]):
-                at = slice(first, first + one.shape[0])
-                keep_ref[row_part, outer, at, :] = jnp.where(even, one, two).astype(low)
-                send_ref[row_part, outer, at, :] = jnp.where(even, two, one).astype(low)
-
-
-def finish_kernel(project_each, row_ref, terms_ref, project_ref, output_ref):
-    total = terms_ref[0].astype(wide)
-    for source in range(1, terms_ref.shape[0]):
-        total = total + terms_ref[source].astype(wide)
+                place = (row_part, outer // 2, outer % 2, slice(first, first + one.shape[0]))
+                keep_ref[place] = jnp.where(even, one, two).astype(low)
+                send_ref[place] = jnp.where(even, two, one).astype(low)
+
+
+def added(left, right):
+    return (left.astype(wide) + right.astype(wide)).astype(low)
+
+
+def halve_kernel(mid_ref, row_ref, kept_ref, came_ref, a_keep, a_send, b_keep, b_send):
+    rows, outers, mids = kept_ref.shape[:3]
+    mid, row = mid_ref[0], row_ref[0]
+    for outer in range(outers // 2):
+        for at in range(rows):
+            a_keep[at, outer] = added(kept_ref[at, outer, mid], came_ref[at, outer, mid])
+            a_send[at, outer] = added(kept_ref[at, outer, 1 - mid], came_ref[at, outer, 1 - mid])
+        later = outer + outers // 2
+        for at in range(mids):
+            b_keep[outer, at] = added(kept_ref[row, later, at], came_ref[row, later, at])
+            b_send[outer, at] = added(kept_ref[1 - row, later, at], came_ref[1 - row, later, at])
+
+
+def halve_again_kernel(
+    mid_ref, row_ref, a_kept, a_came, b_kept, b_came, a_keep, a_send, b_keep, b_send
+):
+    mid, row = mid_ref[0], row_ref[0]
+    for outer in range(a_kept.shape[1]):
+        a_keep[outer] = added(a_kept[row, outer], a_came[row, outer])
+        a_send[outer] = added(a_kept[1 - row, outer], a_came[1 - row, outer])
+        b_keep[outer] = added(b_kept[outer, mid], b_came[outer, mid])
+        b_send[outer] = added(b_kept[outer, 1 - mid], b_came[outer, 1 - mid])
+
+
+def spread_kernel(outer_ref, a_kept, a_came, b_kept, b_came, *refs):
+    total = refs[-1]
+    half = a_kept.shape[0]
+    for outer in range(half):
+        total[outer] = added(a_kept[outer], a_came[outer])
+        total[half + outer] = added(b_kept[outer], b_came[outer])
+    for step in range(2 * half):
+        refs[step][...] = total[(outer_ref[0] + step) % (2 * half)]
+
+
+def finish_kernel(project_each, row_ref, *refs):
+    *terms, project_ref, output_ref = refs
+    total = terms[0][...].astype(wide)
+    for term in terms[1:]:
+        total = total + term[...].astype(wide)
     whole = 2 * total.shape[0] // 3
     main = total[:whole]
     tail = total[whole:]
@@ -353,7 +430,6 @@
 def body(
     row_size,
     date_size,
-    pair_size,
     tokens,
     clear_flags,
     date_numbers,
@@ -379,7 +455,7 @@
     direct = (
         patches_each == column_count
         and column_count % 16 == 0
-        and pair_size == 2
+        and date_size % 8 == 0
         and row_size == 2
         and lane_each == 192
         and project_each % 8 == 0
@@ -388,21 +464,31 @@
     )
     token_rows = date_local * patches_each
     block_rows = -(-(token_rows + date_local) // 8) * 8
+    tile_rows = (width // 128) * token_rows + -(-date_local // 8) * 8
     params = pltpu.CompilerParams(vmem_limit_bytes=vmem_limit)
     in_vmem = pl.BlockSpec(memory_space=pltpu.VMEM)
     in_smem = pl.BlockSpec(memory_space=pltpu.SMEM)
+    swap = [(0, 1), (1, 0)]
+    column_tokens = date_local * row_count * columns_each
+    half_tokens = column_tokens // row_size
     if direct:
         outgoing = pl.pallas_call(
             pack_kernel,
-            out_shape=jax.ShapeDtypeStruct((date_size, block_rows, width), low),
-            in_specs=[in_smem, in_vmem, in_vmem],
+            out_shape=jax.ShapeDtypeStruct((date_size, tile_rows, 128), low),
+            in_specs=[pl.BlockSpec(memory_space=pl.ANY)] * 3,
+            scratch_shapes=[
+                pltpu.SMEM(date_numbers.shape, jnp.int32),
+                pltpu.VMEM(tokens.shape, low),
+                pltpu.VMEM(clear_flags.shape, jnp.int32),
+                pltpu.SemaphoreType.DMA((3,)),
+            ],
             compiler_params=params,
             name="pack_tokens",
         )(date_numbers, tokens, clear_flags)
         row_at = lax.axis_index("row")
         halves = cotangent.reshape(date_local, row_local, row_size, columns_each, width)
         leaving = lax.dynamic_index_in_dim(halves, 1 - row_at, 2, keepdims=False)
-        other_grad = lax.ppermute(leaving, "row", [(0, 1), (1, 0)])
+        other_grad = lax.ppermute(leaving, "row", swap)
     else:
         flags = jnp.transpose(
             clear_flags.reshape(date_local, date_size, patches_each), (1, 0, 2)
@@ -418,6 +504,31 @@
         ).reshape(date_size, token_rows, width)
         outgoing = jnp.concatenate([outgoing, info], axis=1)
     incoming = lax.all_to_all(outgoing, dates, split_axis=0, concat_axis=0, tiled=True)
+
+    if direct:
+        grads_in = (
+            row_at.reshape(1),
+            cotangent.reshape(local_patches * date_local, width),
+            other_grad.reshape(half_tokens, width),
+        )
+        in_specs = [in_smem] + [in_vmem] * 3
+    else:
+        grads_in = (
+            lax.all_to_all(cotangent, "row", split_axis=2, concat_axis=1, tiled=True).reshape(
+                column_tokens, width
+            ),
+        )
+        in_specs = [in_vmem] * 2
+    grad_low, heads_grad = pl.pallas_call(
+        functools.partial(
+            cotangent_kernel, (date_local, row_size, row_local, columns_each, direct)
+        ),
+        out_shape=(jax.ShapeDtypeStruct((column_tokens, width), low),) * 2,
+        in_specs=in_specs,
+        scratch_shapes=[pltpu.VMEM((width // 128, column_tokens, 128), wide)],
+        compiler_params=params,
+        name="cotangent_heads",
+    )(*grads_in, column_output)
 
     time_tokens = date_count * patches_each
     hidden = pl.pallas_call(
@@ -433,7 +544,7 @@
             ),
         ),
         out_shape=jax.ShapeDtypeStruct((time_tokens, width), low),
-        in_specs=[in_smem, in_vmem, in_vmem, in_vmem],
+        in_specs=[in_smem, in_vmem, in_vmem, in_vmem, pl.BlockSpec(memory_space=pl.ANY)],
         scratch_shapes=[
             pltpu.VMEM((width // 128, time_tokens, 128), wide),
             pltpu.VMEM((time_tokens, width), wide),
@@ -442,9 +553,8 @@
         ],
         compiler_params=params,
         name="time_attention",
-    )(decay_slopes, incoming, time_project, time_output)
-
-    column_tokens = date_local * row_count * columns_each
+    )(decay_slopes, incoming, time_project, time_output, heads_grad)
+
     if direct:
         parts = hidden.reshape(row_size * date_size, date_local * columns_each, width)
         plane = lax.all_to_all(parts, ("row", *dates), split_axis=0, concat_axis=0, tiled=True)
@@ -456,33 +566,23 @@
         )
         plane = lax.all_to_all(back, "row", split_axis=2, concat_axis=1, tiled=True)
     plane = plane.reshape(column_tokens, width)
-    half_tokens = column_tokens // row_size
     half_shape = jax.ShapeDtypeStruct((half_tokens, width), low)
     packed_rows = (project_each + output_each) * 3 // 2
-    if direct:
-        operands = (
-            row_at.reshape(1),
-            lax.axis_index("pair").reshape(1),
-            plane,
-            cotangent.reshape(local_patches * date_local, width),
-            other_grad.reshape(half_tokens, width),
-        )
-        half_grads = jax.ShapeDtypeStruct((row_size, date_size // 2, packed_rows, 128), low)
+    block = (packed_rows, 128)
+    outers = date_size // 4
+    if direct:
+        half_grads = jax.ShapeDtypeStruct((row_size, outers, 2, *block), low)
+        places = (row_at.reshape(1), lax.axis_index("pair").reshape(1))
         out_shape = (half_shape, half_shape, half_grads, half_grads)
         in_specs = [in_smem] * 2 + [in_vmem] * 5
     else:
-        operands = (
-            plane,
-            lax.all_to_all(cotangent, "row", split_axis=2, concat_axis=1, tiled=True).reshape(
-                column_tokens, width
-            ),
-        )
+        places = ()
         out_shape = (
             jax.ShapeDtypeStruct((column_tokens, width), low),
             jax.ShapeDtypeStruct((3 * width, width), wide),
             jax.ShapeDtypeStruct((width, width), wide),
         )
-        in_specs = [in_vmem] * 4
+        in_specs = [in_vmem] * 5
     results = pl.pallas_call(
         functools.partial(
             column_kernel,
@@ -501,36 +601,67 @@
         in_specs=in_specs,
         scratch_shapes=[
             pltpu.VMEM((width // 128, column_tokens, 128), wide),
-            pltpu.VMEM((width // 128, column_tokens, 128), wide),
             pltpu.VMEM((column_tokens, width), wide),
             pltpu.VMEM((column_tokens, width), low),
             pltpu.VMEM((column_tokens, 3 * width), low),
-            pltpu.VMEM((column_tokens, width), low),
-            pltpu.VMEM((column_tokens, width), low),
             pltpu.VMEM((column_tokens, width), low),
             pltpu.VMEM((column_tokens, 3 * width), low),
         ],
         compiler_params=params,
         name="column_attention",
-    )(*operands, column_project, column_output)
+    )(*places, plane, grad_low, heads_grad, column_project, column_output)
 
     if direct:
         kept, sent, kept_grad, sent_grad = results
-        arrived_grad = lax.ppermute(sent_grad, "pair", [(0, 1), (1, 0)])
-        arrived = lax.ppermute(sent, "row", [(0, 1), (1, 0)])
-        pair_sum = (kept_grad.astype(wide) + arrived_grad.astype(wide)).astype(low)
-        pair_sum = pair_sum.reshape(row_size * date_size // 2, packed_rows, 128)
-        terms = lax.all_to_all(pair_sum, ("row", "outer"), split_axis=0, concat_axis=0, tiled=True)
+        arrived_grad = lax.ppermute(sent_grad, "pair", swap)
+        arrived = lax.ppermute(sent, "row", swap)
+        mid_one, row_one = lax.axis_index("mid").reshape(1), row_at.reshape(1)
+        outer_one = lax.axis_index("outer").reshape(1)
+
+        def shaped(*lead):
+            return jax.ShapeDtypeStruct((*lead, *block), low)
+
+        half = outers // 2
+        a_kept, a_sent, b_kept, b_sent = pl.pallas_call(
+            halve_kernel,
+            out_shape=(shaped(2, half), shaped(2, half), shaped(half, 2), shaped(half, 2)),
+            in_specs=[in_smem] * 2 + [in_vmem] * 2,
+            compiler_params=params,
+            name="halve_gradients",
+        )(mid_one, row_one, kept_grad, arrived_grad)
+        a_came = lax.ppermute(a_sent, "mid", swap)
+        b_came = lax.ppermute(b_sent, "row", swap)
+        a_kept, a_sent, b_kept, b_sent = pl.pallas_call(
+            halve_again_kernel,
+            out_shape=(shaped(half),) * 4,
+            in_specs=[in_smem] * 2 + [in_vmem] * 4,
+            compiler_params=params,
+            name="halve_gradients_again",
+        )(mid_one, row_one, a_kept, a_came, b_kept, b_came)
+        a_came = lax.ppermute(a_sent, "row", swap)
+        b_came = lax.ppermute(b_sent, "mid", swap)
+        blocks = pl.pallas_call(
+            spread_kernel,
+            out_shape=(shaped(),) * outers,
+            in_specs=[in_smem] + [in_vmem] * 4,
+            scratch_shapes=[pltpu.VMEM((outers, *block), low)],
+            compiler_params=params,
+            name="spread_gradients",
+        )(outer_one, a_kept, a_came, b_kept, b_came)
+        terms = [blocks[0]]
+        for step in range(1, outers):
+            route = [(at, (at + step) % outers) for at in range(outers)]
+            terms.append(lax.ppermute(blocks[step], "outer", route))
         owned_project, owned_output = pl.pallas_call(
             functools.partial(finish_kernel, project_each),
             out_shape=(
                 jax.ShapeDtypeStruct((project_each, lane_each), wide),
                 jax.ShapeDtypeStruct((output_each, lane_each), wide),
             ),
-            in_specs=[in_smem, in_vmem],
+            in_specs=[in_smem] + [in_vmem] * outers,
             compiler_params=params,
             name="gradient_sum",
-        )(row_at.reshape(1), terms)
+        )(row_one, *terms)
         quarter = (date_local, row_local, 1, columns_each, width)
         kept, arrived = kept.reshape(quarter), arrived.reshape(quarter)
         mixed = jnp.concatenate(
@@ -561,12 +692,12 @@
 def solution(mesh):
     date_size, row_size = mesh.shape["date"], mesh.shape["row"]
     pair_size = 2 if date_size % 2 == 0 else 1
+    mid_size = 2 if date_size % 4 == 0 else 1
     split = jax.sharding.Mesh(
-        mesh.devices.reshape(date_size // pair_size, pair_size, row_size),
-        ("outer", "pair", "row"),
+        mesh.devices.reshape(-1, mid_size, pair_size, row_size), ("outer", "mid", "pair", "row")
     )
     return jax.shard_map(
-        functools.partial(body, row_size, date_size, pair_size),
+        functools.partial(body, row_size, date_size),
         mesh=split,
         in_specs=(
             P(dates, "row", None, None),

time: 78.4 us -> 78.9 us (level)
  blocking collectives: 20.9 us -> 0 us
  starting transfers between devices: 11.6 us -> 21.9 us
  waiting for transfers between devices: 27.1 us -> 36.1 us
  Pallas kernels: 13.3 us -> 15.5 us
  other arithmetic: 1.81 us -> 0.83 us
  local copies, waits for them, and re-layouts: 2.49 us -> 3.38 us
    all_to_all x1 -> x0, blocking collectives: 20.9 us -> none  [body(): lax.all_to_all(outgoing, dates, split_axis=0, concat_axis=0, tiled=True)]
    all_to_all x1, waiting for transfers between devices: 2.86 us -> 13.1 us  [body(): lax.all_to_all(parts, ('row', *dates), split_axis=0, concat_axis=0, tiled...]
    ppermute x3 -> x10, starting transfers between devices: 3.83 us -> 10.8 us  [the longest x3 3.88 us: body(): terms.append(lax.ppermute(blocks[step], 'outer', route))]
    all_to_all x1, starting transfers between devices: 3.75 us -> 7.5 us  [body(): lax.all_to_all(outgoing, dates, split_axis=0, concat_axis=0, tiled=True)]
    ppermute x3 -> x10, waiting for transfers between devices: 20.1 us -> 18.2 us  [the longest x1 5.72 us: body(): other_grad = lax.ppermute(leaving, 'row', swap)]
    pallas_call x1 -> x5, Pallas kernels: 0.68 us -> 2.45 us  [the longest x1 1.72 us: body(): pl.pallas_call(pack_kernel, out_shape=jax.ShapeDtypeStruct((date_size, ti...]
    convert_element_type x1 -> x0, other arithmetic: 0.98 us -> none  [body(): pair_sum = (kept_grad.astype(wide) + arrived_grad.astype(wide)).astype(low)]
    unnamed x18, local copies, waits for them, and re-layouts: 2.46 us -> 3.35 us
  transfers between devices with their start and end apart: 5 -> 12, of which waited for: 5 -> 10; matrix products, arithmetic and copies ran while one was open for 1% -> 1% of each run, Pallas kernels for 0% -> 1%
where the time goes in v4:
time: 78.9 us; the launch traced here: 78.5 us
  waiting for transfers between devices  36.1 us (46%)
  starting transfers between devices  21.9 us (28%)
  Pallas kernels  15.5 us (20%)
  local copies, waits for them, and re-layouts  3.38 us (4%)
  other arithmetic  0.83 us (1%)
    all_to_all x1, waiting for transfers between devices, body(): lax.all_to_all(parts, ('row', *dates), split_axis=0, concat_axis=0, tiled...  13.1 us
    all_to_all x1, starting transfers between devices, body(): lax.all_to_all(outgoing, dates, split_axis=0, concat_axis=0, tiled=True)  7.5 us
    pallas_call x1, Pallas kernels, body(): pl.pallas_call(functools.partial(column_kernel, (date_local, row_size, ro...  6.83 us
    ppermute x1, waiting for transfers between devices, body(): other_grad = lax.ppermute(leaving, 'row', swap)  5.72 us
    pallas_call x1, Pallas kernels, body(): pl.pallas_call(functools.partial(time_kernel, (date_size, date_local, pat...  5.48 us
    all_to_all x1, waiting for transfers between devices, body(): lax.all_to_all(outgoing, dates, split_axis=0, concat_axis=0, tiled=True)  4.85 us
    ppermute x3, starting transfers between devices, body(): terms.append(lax.ppermute(blocks[step], 'outer', route))  3.88 us
    ppermute x1, waiting for transfers between devices, body(): a_came = lax.ppermute(a_sent, 'mid', swap)  3.87 us
  transfers between devices with their start and end apart: 12, of which 10 were waited for; matrix products, arithmetic and copies ran while one was open for 1% of the time, Pallas kernels for 1%

profile of v4, /device:TPU:0, one launch (start us, length us, event | category | flops | bytes accessed | tf_op | source)
XLA Modules:
  0.0 78.5 jit_solution(17566811717403541673)
XLA Ops:
  0.6 0.0 copy-start.4
  0.6 1.0 %copy-done.4 = bf16[2,16,16,384]{3,2,1,0:T(8,128)(2,1)S(1)} copy-done((bf16[2,16,16,384]{3,2,1,0:T(8,128)(2,1)S(1)}, bf16[2,16,16,384]{3,2,1,0:T(8,128)(2,1)}, u32[]{:S(2)}) %copy-start.4) | copy-done | bytes 393240
  1.6 0.0 copy-start.6
  1.6 0.7 copy-done.6
  2.3 0.0 copy-start.7
  2.3 0.7 copy-done.7
  3.0 1.7 %pack_tokens.1 = bf16[16,104,128]{2,1,0:T(8,128)(2,1)} custom-call(s32[2]{0:T(128)S(1)} %copy-done.7, bf16[2,16,16,384]{3,2,1,0:T(8,128)(2,1)S(1)} %copy-done.4, s32[2,16,16]{2,1,0:T(8,128)S(1)} %copy-done.6), custom_call_target="tpu_custom_call" | custom-call | tf_op jit(solution)/shard_map/pack_tokens/pallas_call | solution.py:475
  4.7 0.0 copy-start.1
  4.7 7.5 %all-to-all-start = ((bf16[16,104,128]{2,1,0:T(8,128)(2,1)}), bf16[16,104,128]{2,1,0:T(8,128)(2,1)S(1)}, u32[]{:S(2)}, u32[]{:S(2)}) async-start(bf16[16,104,128]{2,1,0:T(8,128)(2,1)} %pack_tokens.1), calls=%async_computation | async-start | bytes 851968 | tf_op jit(solution)/shard_map/all_to_all | solution.py:506
  12.3 0.0 copy-start
  12.3 0.0 copy-start.3
  12.3 0.0 copy-done.1
  12.3 1.6 %collective-permute-start = (bf16[2,16,8,384]{3,2,1,0:T(8,128)(2,1)S(1)}, bf16[2,16,8,384]{3,2,1,0:T(8,128)(2,1)S(1)}, u32[]{:S(2)}, u32[]{:S(2)}) collective-permute-start(bf16[2,16,8,384]{3,2,1,0:T(8,128)(2,1)S(1)} %dynamic-slice_bitcast_fusion), channel_id=1, source_target_pairs={{0,1},{1,0},{2,3},{3,2},{4,5},{5,4},{6,7},{7,6},{8,9},{9,8},{10,11... | collective-permute-start | bytes 589832 | tf_op jit(solution)/shard_map/ppermute | solution.py:491
  13.9 5.7 %collective-permute-done = bf16[2,16,8,384]{3,2,1,0:T(8,128)(2,1)S(1)} collective-permute-done((bf16[2,16,8,384]{3,2,1,0:T(8,128)(2,1)S(1)}, bf16[2,16,8,384]{3,2,1,0:T(8,128)(2,1)S(1)}, u32[]{:S(2)}, u32[]{:S(2)}) %collective-permute-start) | collective-permute-done | bytes 196640 | tf_op jit(solution)/shard_map/ppermute | solution.py:491
  19.6 0.0 copy-done
  19.6 0.5 cotangent_heads.1
  20.1 0.0 copy-start.8
  20.1 4.9 %all-to-all-done.block_ref = bf16[16,104,128]{2,1,0:T(8,128)(2,1)S(1)} async-done(((bf16[16,104,128]{2,1,0:T(8,128)(2,1)}), bf16[16,104,128]{2,1,0:T(8,128)(2,1)S(1)}, u32[]{:S(2)}, u32[]{:S(2)}) %all-to-all-start) | async-done | bytes 426016 | tf_op jit(solution)/shard_map/all_to_all | solution.py:506
  25.0 0.0 copy-done.3
  25.0 0.0 copy-done.8
  25.0 0.0 copy-start.5
  25.0 1.0 %copy-done.5 = bf16[384,384]{1,0:T(8,128)(2,1)S(1)} copy-done((bf16[384,384]{1,0:T(8,128)(2,1)S(1)}, bf16[384,384]{1,0:T(8,128)(2,1)}, u32[]{:S(2)}) %copy-start.5) | copy-done | bytes 294936
  25.9 0.0 copy-start.2
  25.9 5.5 %time_attention.1 = bf16[512,384]{1,0:T(8,128)(2,1)} custom-call(f32[12]{0:T(128)S(1)} %copy-done.8, bf16[16,104,128]{2,1,0:T(8,128)(2,1)S(1)} %all-to-all-done.block_ref, bf16[384,1152]{1,0:T(8,128)(2,1)S(1)} %copy-done.3, bf16[384,384]{1,0:T(8,128)(2,1)S(1)} %copy-done.5, bf16[512,384]{1,0:T(8,128)(2,1)S(1)} %get-tuple-element.23.earlier_ref.refs_4_), custom_call_target="tpu_custom_call" | custom-call | tf_op jit(solution)/shard_map/time_attention/pallas_call | solution.py:534
  31.4 3.6 %all-to-all-start.1 = ((bf16[32,16,384]{2,1,0:T(8,128)(2,1)}), bf16[32,16,384]{2,1,0:T(8,128)(2,1)S(1)}, u32[]{:S(2)}, u32[]{:S(2)}) async-start(bf16[32,16,384]{2,1,0:T(8,128)(2,1)} %bitcast.6), calls=%async_computation.1 | async-start | bytes 786432 | tf_op jit(solution)/shard_map/all_to_all | solution.py:560
  35.1 13.1 %all-to-all-done.1 = bf16[32,16,384]{2,1,0:T(8,128)(2,1)S(1)} async-done(((bf16[32,16,384]{2,1,0:T(8,128)(2,1)}), bf16[32,16,384]{2,1,0:T(8,128)(2,1)S(1)}, u32[]{:S(2)}, u32[]{:S(2)}) %all-to-all-start.1) | async-done | bytes 393248 | tf_op jit(solution)/shard_map/all_to_all | solution.py:560
  48.2 0.0 copy-done.2
  48.2 6.8 %column_attention.1 = (bf16[256,384]{1,0:T(8,128)(2,1)S(1)}, bf16[256,384]{1,0:T(8,128)(2,1)S(1)}, bf16[2,4,2,144,128]{4,3,2,1,0:T(8,128)(2,1)S(1)}, bf16[2,4,2,144,128]{4,3,2,1,0:T(8,128)(2,1)}) custom-call(s32[1]{0:T(128)} %bitcast.refs_0_.row_ref, s32[1]{0:T(128)} %bitcast.1.refs_1_, bf16[512,384]{1,0:T(8,128)(2,1)S(1)} %bitcast.17, ...), custom_call_target="tpu_custom_call" | custom-call | tf_op jit(solution)/shard_map/column_attention/pallas_call | solution.py:586
  55.0 0.0 collective-permute-start.2
  55.0 1.1 %collective-permute-start.1 = (bf16[256,384]{1,0:T(8,128)(2,1)S(1)}, bf16[256,384]{1,0:T(8,128)(2,1)S(1)}, u32[]{:S(2)}, u32[]{:S(2)}) collective-permute-start(bf16[256,384]{1,0:T(8,128)(2,1)S(1)} %get-tuple-element.26), channel_id=1, source_target_pairs={{0,1},{1,0},{2,3},{3,2},{4,5},{5,4},{6,7},{7,6},{8,9},{9,8},{10,11... | collective-permute-start | bytes 589832 | tf_op jit(solution)/shard_map/ppermute | solution.py:617
  56.1 1.1 %collective-permute-done.2.came_ref = bf16[2,4,2,144,128]{4,3,2,1,0:T(8,128)(2,1)S(1)} collective-permute-done((bf16[2,4,2,144,128]{4,3,2,1,0:T(8,128)(2,1)}, bf16[2,4,2,144,128]{4,3,2,1,0:T(8,128)(2,1)S(1)}, u32[]{:S(2)}, u32[]{:S(2)}) %collective-permute-start.2) | collective-permute-done | bytes 589856 | tf_op jit(solution)/shard_map/ppermute | solution.py:616
  57.2 0.1 halve_gradients.1
  57.4 1.5 %collective-permute-start.3 = (bf16[2,2,144,128]{3,2,1,0:T(8,128)(2,1)S(1)}, bf16[2,2,144,128]{3,2,1,0:T(8,128)(2,1)S(1)}, u32[]{:S(2)}, u32[]{:S(2)}) collective-permute-start(bf16[2,2,144,128]{3,2,1,0:T(8,128)(2,1)S(1)} %get-tuple-element.30), channel_id=1, source_target_pairs={{0,4},{4,0},{1,5},{5,1},{2,6},{6,2},{3,7},{7,3},{8,12},{12,8},{9,1... | collective-permute-start | bytes 442376 | tf_op jit(solution)/shard_map/ppermute | solution.py:632
  58.9 0.5 collective-permute-start.4
  59.4 3.9 %collective-permute-done.3.a_came = bf16[2,2,144,128]{3,2,1,0:T(8,128)(2,1)S(1)} collective-permute-done((bf16[2,2,144,128]{3,2,1,0:T(8,128)(2,1)S(1)}, bf16[2,2,144,128]{3,2,1,0:T(8,128)(2,1)S(1)}, u32[]{:S(2)}, u32[]{:S(2)}) %collective-permute-start.3) | collective-permute-done | bytes 147488 | tf_op jit(solution)/shard_map/ppermute | solution.py:632
  63.3 2.2 %collective-permute-done.4.b_came = bf16[2,2,144,128]{3,2,1,0:T(8,128)(2,1)S(1)} collective-permute-done((bf16[2,2,144,128]{3,2,1,0:T(8,128)(2,1)S(1)}, bf16[2,2,144,128]{3,2,1,0:T(8,128)(2,1)S(1)}, u32[]{:S(2)}, u32[]{:S(2)}) %collective-permute-start.4) | collective-permute-done | bytes 147488 | tf_op jit(solution)/shard_map/ppermute | solution.py:633
  65.5 0.1 halve_gradients_again.1
  65.5 1.1 %collective-permute-start.5 = (bf16[2,144,128]{2,1,0:T(8,128)(2,1)S(1)}, bf16[2,144,128]{2,1,0:T(8,128)(2,1)S(1)}, u32[]{:S(2)}, u32[]{:S(2)}) collective-permute-start(bf16[2,144,128]{2,1,0:T(8,128)(2,1)S(1)} %get-tuple-element.34), channel_id=1, source_target_pairs={{0,1},{1,0},{2,3},{3,2},{4,5},{5,4},{6,7},{7,6},{8,9},{9,8},{10,11... | collective-permute-start | bytes 221192 | tf_op jit(solution)/shard_map/ppermute | solution.py:641
  66.6 1.0 %collective-permute-start.6 = (bf16[2,144,128]{2,1,0:T(8,128)(2,1)S(1)}, bf16[2,144,128]{2,1,0:T(8,128)(2,1)S(1)}, u32[]{:S(2)}, u32[]{:S(2)}) collective-permute-start(bf16[2,144,128]{2,1,0:T(8,128)(2,1)S(1)} %get-tuple-element.36), channel_id=1, source_target_pairs={{0,4},{4,0},{1,5},{5,1},{2,6},{6,2},{3,7},{7,3},{8,12},{12,8},{9,1... | collective-permute-start | bytes 221192 | tf_op jit(solution)/shard_map/ppermute | solution.py:642
  67.6 0.0 collective-permute-done.1
  67.7 2.3 %collective-permute-done.5.a_came = bf16[2,144,128]{2,1,0:T(8,128)(2,1)S(1)} collective-permute-done((bf16[2,144,128]{2,1,0:T(8,128)(2,1)S(1)}, bf16[2,144,128]{2,1,0:T(8,128)(2,1)S(1)}, u32[]{:S(2)}, u32[]{:S(2)}) %collective-permute-start.5) | collective-permute-done | bytes 73760 | tf_op jit(solution)/shard_map/ppermute | solution.py:641
  70.0 1.0 %collective-permute-done.6.b_came = bf16[2,144,128]{2,1,0:T(8,128)(2,1)S(1)} collective-permute-done((bf16[2,144,128]{2,1,0:T(8,128)(2,1)S(1)}, bf16[2,144,128]{2,1,0:T(8,128)(2,1)S(1)}, u32[]{:S(2)}, u32[]{:S(2)}) %collective-permute-start.6) | collective-permute-done | bytes 73760 | tf_op jit(solution)/shard_map/ppermute | solution.py:642
  71.0 1.0 %collective-permute-start.7 = (bf16[144,128]{1,0:T(8,128)(2,1)S(1)}, bf16[144,128]{1,0:T(8,128)(2,1)S(1)}, u32[]{:S(2)}, u32[]{:S(2)}) collective-permute-start(bf16[144,128]{1,0:T(8,128)(2,1)S(1)} %get-tuple-element.38), channel_id=1, source_target_pairs={{0,8},{8,16},{16,24},{24,0},{1,9},{9,17},{17,25},{25,1},{2,10},{10... | collective-permute-start | bytes 110600 | tf_op jit(solution)/shard_map/ppermute | solution.py:654
  72.0 1.2 %collective-permute-start.8 = (bf16[144,128]{1,0:T(8,128)(2,1)S(1)}, bf16[144,128]{1,0:T(8,128)(2,1)S(1)}, u32[]{:S(2)}, u32[]{:S(2)}) collective-permute-start(bf16[144,128]{1,0:T(8,128)(2,1)S(1)} %get-tuple-element.39), channel_id=1, source_target_pairs={{0,16},{8,24},{16,0},{24,8},{1,17},{9,25},{17,1},{25,9},{2,18},{10... | collective-permute-start | bytes 110600 | tf_op jit(solution)/shard_map/ppermute | solution.py:654
  73.1 1.8 %collective-permute-start.9 = (bf16[144,128]{1,0:T(8,128)(2,1)S(1)}, bf16[144,128]{1,0:T(8,128)(2,1)S(1)}, u32[]{:S(2)}, u32[]{:S(2)}) collective-permute-start(bf16[144,128]{1,0:T(8,128)(2,1)S(1)} %get-tuple-element.40), channel_id=1, source_target_pairs={{0,24},{8,0},{16,8},{24,16},{1,25},{9,1},{17,9},{25,17},{2,26},{10... | collective-permute-start | bytes 110600 | tf_op jit(solution)/shard_map/ppermute | solution.py:654
  74.9 0.8 %copy_bitcast_fusion = bf16[2,16,16,384]{3,2,1,0:T(8,128)(2,1)} fusion(bf16[2,16,1,8,384]{4,3,1,0,2:T(8,128)(2,1)S(1)} %bitcast.22, bf16[2,16,1,8,384]{4,3,1,0,2:T(8,128)(2,1)S(1)} %bitcast.21), kind=kLoop, calls=%fused_computation.1 | loop fusion | flops 196608 | bytes 786432 | tf_op jit(solution)/shard_map/reshape | solution.py:688
  75.7 1.2 %collective-permute-done.7.refs_1_ = bf16[144,128]{1,0:T(8,128)(2,1)S(1)} collective-permute-done((bf16[144,128]{1,0:T(8,128)(2,1)S(1)}, bf16[144,128]{1,0:T(8,128)(2,1)S(1)}, u32[]{:S(2)}, u32[]{:S(2)}) %collective-permute-start.7) | collective-permute-done | bytes 36896 | tf_op jit(solution)/shard_map/ppermute | solution.py:654
  76.9 0.9 %collective-permute-done.8.refs_2_ = bf16[144,128]{1,0:T(8,128)(2,1)S(1)} collective-permute-done((bf16[144,128]{1,0:T(8,128)(2,1)S(1)}, bf16[144,128]{1,0:T(8,128)(2,1)S(1)}, u32[]{:S(2)}, u32[]{:S(2)}) %collective-permute-start.8) | collective-permute-done | bytes 36896 | tf_op jit(solution)/shard_map/ppermute | solution.py:654
  77.7 0.0 collective-permute-done.9.refs_3_
  77.7 0.7 gradient_sum.1
  (3 shorter events, 0.1 us)
Async XLA Ops:
  0.6 1.0 %copy-start.4 = (bf16[2,16,16,384]{3,2,1,0:T(8,128)(2,1)S(1)}, bf16[2,16,16,384]{3,2,1,0:T(8,128)(2,1)}, u32[]{:S(2)}) copy-start(bf16[2,16,16,384]{3,2,1,0:T(8,128)(2,1)} %tokens_ref.1) | copy-start | bytes 1179652
  1.6 0.7 copy-start.6
  2.3 0.7 copy-start.7
  4.7 7.6 %copy-start.1 = (bf16[2,16,16,384]{3,2,1,0:T(8,128)(2,1)S(1)}, bf16[2,16,16,384]{3,2,1,0:T(8,128)(2,1)}, u32[]{:S(2)}) copy-start(bf16[2,16,16,384]{3,2,1,0:T(8,128)(2,1)} %param.17) | copy-start | bytes 1179652
  4.7 20.2 %all-to-all-start = ((bf16[16,104,128]{2,1,0:T(8,128)(2,1)}), bf16[16,104,128]{2,1,0:T(8,128)(2,1)S(1)}, u32[]{:S(2)}, u32[]{:S(2)}) async-start(bf16[16,104,128]{2,1,0:T(8,128)(2,1)} %pack_tokens.1), calls=%async_computation | async-start | bytes 851968 | tf_op jit(solution)/shard_map/all_to_all | solution.py:506
  12.3 7.4 %copy-start = (bf16[384,384]{1,0:T(8,128)(2,1)S(1)}, bf16[384,384]{1,0:T(8,128)(2,1)}, u32[]{:S(2)}) copy-start(bf16[384,384]{1,0:T(8,128)(2,1)} %refs_6_.1) | copy-start | bytes 884740
  12.3 12.7 %copy-start.3 = (bf16[384,1152]{1,0:T(8,128)(2,1)S(1)}, bf16[384,1152]{1,0:T(8,128)(2,1)}, u32[]{:S(2)}) copy-start(bf16[384,1152]{1,0:T(8,128)(2,1)} %project_ref.1) | copy-start | bytes 2654212
  12.3 7.3 %collective-permute-start = (bf16[2,16,8,384]{3,2,1,0:T(8,128)(2,1)S(1)}, bf16[2,16,8,384]{3,2,1,0:T(8,128)(2,1)S(1)}, u32[]{:S(2)}, u32[]{:S(2)}) collective-permute-start(bf16[2,16,8,384]{3,2,1,0:T(8,128)(2,1)S(1)} %dynamic-slice_bitcast_fusion), channel_id=1, source_target_pairs={{0,1},{1,0},{2,3},{3,2},{4,5},{5,4},{6,7},{7,6},{8,9},{9,8},{10,11... | collective-permute-start | bytes 589832 | tf_op jit(solution)/shard_map/ppermute | solution.py:491
  20.1 4.9 %copy-start.8 = (f32[12]{0:T(128)S(1)}, f32[12]{0:T(128)}, u32[]{:S(2)}) copy-start(f32[12]{0:T(128)} %slopes_ref.1) | copy-start | bytes 148
  25.0 1.0 %copy-start.5 = (bf16[384,384]{1,0:T(8,128)(2,1)S(1)}, bf16[384,384]{1,0:T(8,128)(2,1)}, u32[]{:S(2)}) copy-start(bf16[384,384]{1,0:T(8,128)(2,1)} %output_ref.1) | copy-start | bytes 884740
  25.9 22.2 %copy-start.2 = (bf16[384,1152]{1,0:T(8,128)(2,1)S(1)}, bf16[384,1152]{1,0:T(8,128)(2,1)}, u32[]{:S(2)}) copy-start(bf16[384,1152]{1,0:T(8,128)(2,1)} %refs_5_.1) | copy-start | bytes 2654212
  31.4 16.7 %all-to-all-start.1 = ((bf16[32,16,384]{2,1,0:T(8,128)(2,1)}), bf16[32,16,384]{2,1,0:T(8,128)(2,1)S(1)}, u32[]{:S(2)}, u32[]{:S(2)}) async-start(bf16[32,16,384]{2,1,0:T(8,128)(2,1)} %bitcast.6), calls=%async_computation.1 | async-start | bytes 786432 | tf_op jit(solution)/shard_map/all_to_all | solution.py:560
  55.0 2.2 %collective-permute-start.2 = (bf16[2,4,2,144,128]{4,3,2,1,0:T(8,128)(2,1)}, bf16[2,4,2,144,128]{4,3,2,1,0:T(8,128)(2,1)S(1)}, u32[]{:S(2)}, u32[]{:S(2)}) collective-permute-start(bf16[2,4,2,144,128]{4,3,2,1,0:T(8,128)(2,1)} %get-tuple-element.28), channel_id=1, source_target_pairs={{0,2},{2,0},{1,3},{3,1},{4,6},{6,4},{5,7},{7,5},{8,10},{10,8},{9,1... | collective-permute-start | bytes 1769480 | tf_op jit(solution)/shard_map/ppermute | solution.py:616
  55.0 12.6 %collective-permute-start.1 = (bf16[256,384]{1,0:T(8,128)(2,1)S(1)}, bf16[256,384]{1,0:T(8,128)(2,1)S(1)}, u32[]{:S(2)}, u32[]{:S(2)}) collective-permute-start(bf16[256,384]{1,0:T(8,128)(2,1)S(1)} %get-tuple-element.26), channel_id=1, source_target_pairs={{0,1},{1,0},{2,3},{3,2},{4,5},{5,4},{6,7},{7,6},{8,9},{9,8},{10,11... | collective-permute-start | bytes 589832 | tf_op jit(solution)/shard_map/ppermute | solution.py:617
  57.4 6.0 %collective-permute-start.3 = (bf16[2,2,144,128]{3,2,1,0:T(8,128)(2,1)S(1)}, bf16[2,2,144,128]{3,2,1,0:T(8,128)(2,1)S(1)}, u32[]{:S(2)}, u32[]{:S(2)}) collective-permute-start(bf16[2,2,144,128]{3,2,1,0:T(8,128)(2,1)S(1)} %get-tuple-element.30), channel_id=1, source_target_pairs={{0,4},{4,0},{1,5},{5,1},{2,6},{6,2},{3,7},{7,3},{8,12},{12,8},{9,1... | collective-permute-start | bytes 442376 | tf_op jit(solution)/shard_map/ppermute | solution.py:632
  58.9 6.6 %collective-permute-start.4 = (bf16[2,2,144,128]{3,2,1,0:T(8,128)(2,1)S(1)}, bf16[2,2,144,128]{3,2,1,0:T(8,128)(2,1)S(1)}, u32[]{:S(2)}, u32[]{:S(2)}) collective-permute-start(bf16[2,2,144,128]{3,2,1,0:T(8,128)(2,1)S(1)} %get-tuple-element.32), channel_id=1, source_target_pairs={{0,1},{1,0},{2,3},{3,2},{4,5},{5,4},{6,7},{7,6},{8,9},{9,8},{10,11... | collective-permute-start | bytes 442376 | tf_op jit(solution)/shard_map/ppermute | solution.py:633
  65.5 4.4 %collective-permute-start.5 = (bf16[2,144,128]{2,1,0:T(8,128)(2,1)S(1)}, bf16[2,144,128]{2,1,0:T(8,128)(2,1)S(1)}, u32[]{:S(2)}, u32[]{:S(2)}) collective-permute-start(bf16[2,144,128]{2,1,0:T(8,128)(2,1)S(1)} %get-tuple-element.34), channel_id=1, source_target_pairs={{0,1},{1,0},{2,3},{3,2},{4,5},{5,4},{6,7},{7,6},{8,9},{9,8},{10,11... | collective-permute-start | bytes 221192 | tf_op jit(solution)/shard_map/ppermute | solution.py:641
  66.6 4.4 %collective-permute-start.6 = (bf16[2,144,128]{2,1,0:T(8,128)(2,1)S(1)}, bf16[2,144,128]{2,1,0:T(8,128)(2,1)S(1)}, u32[]{:S(2)}, u32[]{:S(2)}) collective-permute-start(bf16[2,144,128]{2,1,0:T(8,128)(2,1)S(1)} %get-tuple-element.36), channel_id=1, source_target_pairs={{0,4},{4,0},{1,5},{5,1},{2,6},{6,2},{3,7},{7,3},{8,12},{12,8},{9,1... | collective-permute-start | bytes 221192 | tf_op jit(solution)/shard_map/ppermute | solution.py:642
  71.0 5.8 %collective-permute-start.7 = (bf16[144,128]{1,0:T(8,128)(2,1)S(1)}, bf16[144,128]{1,0:T(8,128)(2,1)S(1)}, u32[]{:S(2)}, u32[]{:S(2)}) collective-permute-start(bf16[144,128]{1,0:T(8,128)(2,1)S(1)} %get-tuple-element.38), channel_id=1, source_target_pairs={{0,8},{8,16},{16,24},{24,0},{1,9},{9,17},{17,25},{25,1},{2,10},{10... | collective-permute-start | bytes 110600 | tf_op jit(solution)/shard_map/ppermute | solution.py:654
  72.0 5.7 %collective-permute-start.8 = (bf16[144,128]{1,0:T(8,128)(2,1)S(1)}, bf16[144,128]{1,0:T(8,128)(2,1)S(1)}, u32[]{:S(2)}, u32[]{:S(2)}) collective-permute-start(bf16[144,128]{1,0:T(8,128)(2,1)S(1)} %get-tuple-element.39), channel_id=1, source_target_pairs={{0,16},{8,24},{16,0},{24,8},{1,17},{9,25},{17,1},{25,9},{2,18},{10... | collective-permute-start | bytes 110600 | tf_op jit(solution)/shard_map/ppermute | solution.py:654
  73.1 4.6 %collective-permute-start.9 = (bf16[144,128]{1,0:T(8,128)(2,1)S(1)}, bf16[144,128]{1,0:T(8,128)(2,1)S(1)}, u32[]{:S(2)}, u32[]{:S(2)}) collective-permute-start(bf16[144,128]{1,0:T(8,128)(2,1)S(1)} %get-tuple-element.40), channel_id=1, source_target_pairs={{0,24},{8,0},{16,8},{24,16},{1,25},{9,1},{17,9},{25,17},{2,26},{10... | collective-permute-start | bytes 110600 | tf_op jit(solution)/shard_map/ppermute | solution.py:654

commit v5 on v4

--- a/solution.py
+++ b/solution.py
@@ -10,9 +10,9 @@
 
 epsilon = 1e-06
 masked_score = -1e30
-units_each = 6
+units_each = 12
 dates = ("outer", "mid", "pair")
-vmem_limit = 48 * 1024 * 1024
+vmem_limit = 24 * 1024 * 1024
 low = jnp.bfloat16
 wide = jnp.float32
 
@@ -126,7 +126,11 @@
     token_scr,
     qkv_scr,
     heads_scr,
+    output_scr,
+    copied,
 ):
+    output_copy = pltpu.make_async_copy(output_ref, output_scr, copied)
+    output_copy.start()
     sources, dates_each, groups, head_count, packed, columns_each = sizes
     width = project_ref.shape[0]
     tile_lanes = block_ref.shape[2]
@@ -191,7 +195,8 @@
             heads_scr[rows, part * lanes : (part + 1) * lanes] = own_blocks(
                 full, length, packed, head_size
             ).astype(low)
-    hidden = token_scr[...] + matmul(heads_scr[...], output_ref[...])
+    output_copy.wait()
+    hidden = token_scr[...] + matmul(heads_scr[...], output_scr[...])
     for group in range(groups):
         first = (group // columns_each) * (length * columns_each) + group % columns_each
         put_tiles(
@@ -468,6 +473,7 @@
     params = pltpu.CompilerParams(vmem_limit_bytes=vmem_limit)
     in_vmem = pl.BlockSpec(memory_space=pltpu.VMEM)
     in_smem = pl.BlockSpec(memory_space=pltpu.SMEM)
+    in_hbm = pl.BlockSpec(memory_space=pltpu.HBM)
     swap = [(0, 1), (1, 0)]
     column_tokens = date_local * row_count * columns_each
     half_tokens = column_tokens // row_size
@@ -475,7 +481,7 @@
         outgoing = pl.pallas_call(
             pack_kernel,
             out_shape=jax.ShapeDtypeStruct((date_size, tile_rows, 128), low),
-            in_specs=[pl.BlockSpec(memory_space=pl.ANY)] * 3,
+            in_specs=[in_hbm] * 3,
             scratch_shapes=[
                 pltpu.SMEM(date_numbers.shape, jnp.int32),
                 pltpu.VMEM(tokens.shape, low),
@@ -544,12 +550,14 @@
             ),
         ),
         out_shape=jax.ShapeDtypeStruct((time_tokens, width), low),
-        in_specs=[in_smem, in_vmem, in_vmem, in_vmem, pl.BlockSpec(memory_space=pl.ANY)],
+        in_specs=[in_smem, in_vmem, in_vmem, in_hbm, pl.BlockSpec(memory_space=pl.ANY)],
         scratch_shapes=[
             pltpu.VMEM((width // 128, time_tokens, 128), wide),
             pltpu.VMEM((time_tokens, width), wide),
             pltpu.VMEM((time_tokens, 3 * width), low),
             pltpu.VMEM((time_tokens, width), low),
+            pltpu.VMEM(time_output.shape, low),
+            pltpu.SemaphoreType.DMA,
         ],
         compiler_params=params,
         name="time_attention",

time: 78.9 us -> 77.3 us (0.980)
  Pallas kernels: 15.5 us -> 13.9 us
    pallas_call x1, Pallas kernels: 6.83 us -> 5.93 us  [body(): pl.pallas_call(functools.partial(column_kernel, (date_local, row_size, ro...]
where the time goes in v5:
time: 77.3 us; the launch traced here: 76.9 us
  waiting for transfers between devices  36.1 us (47%)
  starting transfers between devices  21.9 us (28%)
  Pallas kernels  13.9 us (18%)
  local copies, waits for them, and re-layouts  3.38 us (4%)
  other arithmetic  0.83 us (1%)
    all_to_all x1, waiting for transfers between devices, body(): lax.all_to_all(parts, ('row', *dates), split_axis=0, concat_axis=0, tiled...  13.1 us
    all_to_all x1, starting transfers between devices, body(): lax.all_to_all(outgoing, dates, split_axis=0, concat_axis=0, tiled=True)  7.5 us
    pallas_call x1, Pallas kernels, body(): pl.pallas_call(functools.partial(column_kernel, (date_local, row_size, ro...  5.93 us
    ppermute x1, waiting for transfers between devices, body(): other_grad = lax.ppermute(leaving, 'row', swap)  5.72 us
    all_to_all x1, waiting for transfers between devices, body(): lax.all_to_all(outgoing, dates, split_axis=0, concat_axis=0, tiled=True)  4.85 us
    pallas_call x1, Pallas kernels, body(): pl.pallas_call(functools.partial(time_kernel, (date_size, date_local, pat...  4.77 us
    ppermute x3, starting transfers between devices, body(): terms.append(lax.ppermute(blocks[step], 'outer', route))  3.88 us
    ppermute x1, waiting for transfers between devices, body(): a_came = lax.ppermute(a_sent, 'mid', swap)  3.87 us
  transfers between devices with their start and end apart: 12, of which 10 were waited for; matrix products, arithmetic and copies ran while one was open for 1% of the time, Pallas kernels for 1%

profile of v5, /device:TPU:0, one launch (start us, length us, event | category | flops | bytes accessed | tf_op | source)
XLA Modules:
  0.0 76.9 jit_solution(76278957266321182)
XLA Ops:
  0.6 0.0 copy-start.4
  0.6 1.0 %copy-done.4 = bf16[2,16,16,384]{3,2,1,0:T(8,128)(2,1)S(1)} copy-done((bf16[2,16,16,384]{3,2,1,0:T(8,128)(2,1)S(1)}, bf16[2,16,16,384]{3,2,1,0:T(8,128)(2,1)}, u32[]{:S(2)}) %copy-start.4) | copy-done | bytes 393240
  1.6 0.0 copy-start.6
  1.6 0.7 copy-done.6
  2.3 0.0 copy-start.7
  2.3 0.7 copy-done.7
  3.0 1.7 %pack_tokens.1 = bf16[16,104,128]{2,1,0:T(8,128)(2,1)} custom-call(s32[2]{0:T(128)S(1)} %copy-done.7, bf16[2,16,16,384]{3,2,1,0:T(8,128)(2,1)S(1)} %copy-done.4, s32[2,16,16]{2,1,0:T(8,128)S(1)} %copy-done.6), custom_call_target="tpu_custom_call" | custom-call | tf_op jit(solution)/shard_map/pack_tokens/pallas_call | solution.py:481
  4.7 0.0 copy-start.1
  4.7 7.5 %all-to-all-start = ((bf16[16,104,128]{2,1,0:T(8,128)(2,1)}), bf16[16,104,128]{2,1,0:T(8,128)(2,1)S(1)}, u32[]{:S(2)}, u32[]{:S(2)}) async-start(bf16[16,104,128]{2,1,0:T(8,128)(2,1)} %pack_tokens.1), calls=%async_computation | async-start | bytes 851968 | tf_op jit(solution)/shard_map/all_to_all | solution.py:512
  12.3 0.0 copy-start
  12.3 0.0 copy-start.3
  12.3 0.0 copy-done.1
  12.3 1.6 %collective-permute-start = (bf16[2,16,8,384]{3,2,1,0:T(8,128)(2,1)S(1)}, bf16[2,16,8,384]{3,2,1,0:T(8,128)(2,1)S(1)}, u32[]{:S(2)}, u32[]{:S(2)}) collective-permute-start(bf16[2,16,8,384]{3,2,1,0:T(8,128)(2,1)S(1)} %dynamic-slice_bitcast_fusion), channel_id=1, source_target_pairs={{0,1},{1,0},{2,3},{3,2},{4,5},{5,4},{6,7},{7,6},{8,9},{9,8},{10,11... | collective-permute-start | bytes 589832 | tf_op jit(solution)/shard_map/ppermute | solution.py:497
  13.9 5.7 %collective-permute-done = bf16[2,16,8,384]{3,2,1,0:T(8,128)(2,1)S(1)} collective-permute-done((bf16[2,16,8,384]{3,2,1,0:T(8,128)(2,1)S(1)}, bf16[2,16,8,384]{3,2,1,0:T(8,128)(2,1)S(1)}, u32[]{:S(2)}, u32[]{:S(2)}) %collective-permute-start) | collective-permute-done | bytes 196640 | tf_op jit(solution)/shard_map/ppermute | solution.py:497
  19.6 0.0 copy-done
  19.6 0.5 cotangent_heads.1
  20.1 0.0 copy-start.8
  20.1 4.9 %all-to-all-done.block_ref = bf16[16,104,128]{2,1,0:T(8,128)(2,1)S(1)} async-done(((bf16[16,104,128]{2,1,0:T(8,128)(2,1)}), bf16[16,104,128]{2,1,0:T(8,128)(2,1)S(1)}, u32[]{:S(2)}, u32[]{:S(2)}) %all-to-all-start) | async-done | bytes 426016 | tf_op jit(solution)/shard_map/all_to_all | solution.py:512
  25.0 0.0 copy-done.3
  25.0 0.0 copy-done.8
  25.0 0.0 copy-start.5
  25.0 1.0 %copy-done.5 = bf16[384,384]{1,0:T(8,128)(2,1)S(1)} copy-done((bf16[384,384]{1,0:T(8,128)(2,1)S(1)}, bf16[384,384]{1,0:T(8,128)(2,1)}, u32[]{:S(2)}) %copy-start.5) | copy-done | bytes 294936
  25.9 0.0 copy-start.2
  25.9 4.8 %time_attention.1 = bf16[512,384]{1,0:T(8,128)(2,1)} custom-call(f32[12]{0:T(128)S(1)} %copy-done.8, bf16[16,104,128]{2,1,0:T(8,128)(2,1)S(1)} %all-to-all-done.block_ref, bf16[384,1152]{1,0:T(8,128)(2,1)S(1)} %copy-done.3, bf16[384,384]{1,0:T(8,128)(2,1)S(1)} %copy-done.5, bf16[512,384]{1,0:T(8,128)(2,1)S(1)} %get-tuple-element.23.earlier_ref.refs_4_), custom_call_target="tpu_custom_call" | custom-call | tf_op jit(solution)/shard_map/time_attention/pallas_call | solution.py:540
  30.7 3.6 %all-to-all-start.1 = ((bf16[32,16,384]{2,1,0:T(8,128)(2,1)}), bf16[32,16,384]{2,1,0:T(8,128)(2,1)S(1)}, u32[]{:S(2)}, u32[]{:S(2)}) async-start(bf16[32,16,384]{2,1,0:T(8,128)(2,1)} %bitcast.6), calls=%async_computation.1 | async-start | bytes 786432 | tf_op jit(solution)/shard_map/all_to_all | solution.py:568
  34.4 13.1 %all-to-all-done.1 = bf16[32,16,384]{2,1,0:T(8,128)(2,1)S(1)} async-done(((bf16[32,16,384]{2,1,0:T(8,128)(2,1)}), bf16[32,16,384]{2,1,0:T(8,128)(2,1)S(1)}, u32[]{:S(2)}, u32[]{:S(2)}) %all-to-all-start.1) | async-done | bytes 393248 | tf_op jit(solution)/shard_map/all_to_all | solution.py:568
  47.5 0.0 copy-done.2
  47.5 5.9 %column_attention.1 = (bf16[256,384]{1,0:T(8,128)(2,1)S(1)}, bf16[256,384]{1,0:T(8,128)(2,1)S(1)}, bf16[2,4,2,144,128]{4,3,2,1,0:T(8,128)(2,1)S(1)}, bf16[2,4,2,144,128]{4,3,2,1,0:T(8,128)(2,1)}) custom-call(s32[1]{0:T(128)} %bitcast.refs_0_.row_ref, s32[1]{0:T(128)} %bitcast.1.refs_1_, bf16[512,384]{1,0:T(8,128)(2,1)S(1)} %bitcast.17, ...), custom_call_target="tpu_custom_call" | custom-call | tf_op jit(solution)/shard_map/column_attention/pallas_call | solution.py:594
  53.4 0.0 collective-permute-start.2
  53.4 1.1 %collective-permute-start.1 = (bf16[256,384]{1,0:T(8,128)(2,1)S(1)}, bf16[256,384]{1,0:T(8,128)(2,1)S(1)}, u32[]{:S(2)}, u32[]{:S(2)}) collective-permute-start(bf16[256,384]{1,0:T(8,128)(2,1)S(1)} %get-tuple-element.26), channel_id=1, source_target_pairs={{0,1},{1,0},{2,3},{3,2},{4,5},{5,4},{6,7},{7,6},{8,9},{9,8},{10,11... | collective-permute-start | bytes 589832 | tf_op jit(solution)/shard_map/ppermute | solution.py:625
  54.5 1.1 %collective-permute-done.2.came_ref = bf16[2,4,2,144,128]{4,3,2,1,0:T(8,128)(2,1)S(1)} collective-permute-done((bf16[2,4,2,144,128]{4,3,2,1,0:T(8,128)(2,1)}, bf16[2,4,2,144,128]{4,3,2,1,0:T(8,128)(2,1)S(1)}, u32[]{:S(2)}, u32[]{:S(2)}) %collective-permute-start.2) | collective-permute-done | bytes 589856 | tf_op jit(solution)/shard_map/ppermute | solution.py:624
  55.6 0.1 halve_gradients.1
  55.8 1.6 %collective-permute-start.3 = (bf16[2,2,144,128]{3,2,1,0:T(8,128)(2,1)S(1)}, bf16[2,2,144,128]{3,2,1,0:T(8,128)(2,1)S(1)}, u32[]{:S(2)}, u32[]{:S(2)}) collective-permute-start(bf16[2,2,144,128]{3,2,1,0:T(8,128)(2,1)S(1)} %get-tuple-element.30), channel_id=1, source_target_pairs={{0,4},{4,0},{1,5},{5,1},{2,6},{6,2},{3,7},{7,3},{8,12},{12,8},{9,1... | collective-permute-start | bytes 442376 | tf_op jit(solution)/shard_map/ppermute | solution.py:640
  57.3 0.5 collective-permute-start.4
  57.9 3.9 %collective-permute-done.3.a_came = bf16[2,2,144,128]{3,2,1,0:T(8,128)(2,1)S(1)} collective-permute-done((bf16[2,2,144,128]{3,2,1,0:T(8,128)(2,1)S(1)}, bf16[2,2,144,128]{3,2,1,0:T(8,128)(2,1)S(1)}, u32[]{:S(2)}, u32[]{:S(2)}) %collective-permute-start.3) | collective-permute-done | bytes 147488 | tf_op jit(solution)/shard_map/ppermute | solution.py:640
  61.7 2.2 %collective-permute-done.4.b_came = bf16[2,2,144,128]{3,2,1,0:T(8,128)(2,1)S(1)} collective-permute-done((bf16[2,2,144,128]{3,2,1,0:T(8,128)(2,1)S(1)}, bf16[2,2,144,128]{3,2,1,0:T(8,128)(2,1)S(1)}, u32[]{:S(2)}, u32[]{:S(2)}) %collective-permute-start.4) | collective-permute-done | bytes 147488 | tf_op jit(solution)/shard_map/ppermute | solution.py:641
  63.9 0.1 halve_gradients_again.1
  64.0 1.1 %collective-permute-start.5 = (bf16[2,144,128]{2,1,0:T(8,128)(2,1)S(1)}, bf16[2,144,128]{2,1,0:T(8,128)(2,1)S(1)}, u32[]{:S(2)}, u32[]{:S(2)}) collective-permute-start(bf16[2,144,128]{2,1,0:T(8,128)(2,1)S(1)} %get-tuple-element.34), channel_id=1, source_target_pairs={{0,1},{1,0},{2,3},{3,2},{4,5},{5,4},{6,7},{7,6},{8,9},{9,8},{10,11... | collective-permute-start | bytes 221192 | tf_op jit(solution)/shard_map/ppermute | solution.py:649
  65.1 1.0 %collective-permute-start.6 = (bf16[2,144,128]{2,1,0:T(8,128)(2,1)S(1)}, bf16[2,144,128]{2,1,0:T(8,128)(2,1)S(1)}, u32[]{:S(2)}, u32[]{:S(2)}) collective-permute-start(bf16[2,144,128]{2,1,0:T(8,128)(2,1)S(1)} %get-tuple-element.36), channel_id=1, source_target_pairs={{0,4},{4,0},{1,5},{5,1},{2,6},{6,2},{3,7},{7,3},{8,12},{12,8},{9,1... | collective-permute-start | bytes 221192 | tf_op jit(solution)/shard_map/ppermute | solution.py:650
  66.0 0.0 collective-permute-done.1
  66.1 2.3 %collective-permute-done.5.a_came = bf16[2,144,128]{2,1,0:T(8,128)(2,1)S(1)} collective-permute-done((bf16[2,144,128]{2,1,0:T(8,128)(2,1)S(1)}, bf16[2,144,128]{2,1,0:T(8,128)(2,1)S(1)}, u32[]{:S(2)}, u32[]{:S(2)}) %collective-permute-start.5) | collective-permute-done | bytes 73760 | tf_op jit(solution)/shard_map/ppermute | solution.py:649
  68.4 1.0 %collective-permute-done.6.b_came = bf16[2,144,128]{2,1,0:T(8,128)(2,1)S(1)} collective-permute-done((bf16[2,144,128]{2,1,0:T(8,128)(2,1)S(1)}, bf16[2,144,128]{2,1,0:T(8,128)(2,1)S(1)}, u32[]{:S(2)}, u32[]{:S(2)}) %collective-permute-start.6) | collective-permute-done | bytes 73760 | tf_op jit(solution)/shard_map/ppermute | solution.py:650
  69.5 0.9 %collective-permute-start.7 = (bf16[144,128]{1,0:T(8,128)(2,1)S(1)}, bf16[144,128]{1,0:T(8,128)(2,1)S(1)}, u32[]{:S(2)}, u32[]{:S(2)}) collective-permute-start(bf16[144,128]{1,0:T(8,128)(2,1)S(1)} %get-tuple-element.38), channel_id=1, source_target_pairs={{0,8},{8,16},{16,24},{24,0},{1,9},{9,17},{17,25},{25,1},{2,10},{10... | collective-permute-start | bytes 110600 | tf_op jit(solution)/shard_map/ppermute | solution.py:662
  70.4 1.1 %collective-permute-start.8 = (bf16[144,128]{1,0:T(8,128)(2,1)S(1)}, bf16[144,128]{1,0:T(8,128)(2,1)S(1)}, u32[]{:S(2)}, u32[]{:S(2)}) collective-permute-start(bf16[144,128]{1,0:T(8,128)(2,1)S(1)} %get-tuple-element.39), channel_id=1, source_target_pairs={{0,16},{8,24},{16,0},{24,8},{1,17},{9,25},{17,1},{25,9},{2,18},{10... | collective-permute-start | bytes 110600 | tf_op jit(solution)/shard_map/ppermute | solution.py:662
  71.6 1.8 %collective-permute-start.9 = (bf16[144,128]{1,0:T(8,128)(2,1)S(1)}, bf16[144,128]{1,0:T(8,128)(2,1)S(1)}, u32[]{:S(2)}, u32[]{:S(2)}) collective-permute-start(bf16[144,128]{1,0:T(8,128)(2,1)S(1)} %get-tuple-element.40), channel_id=1, source_target_pairs={{0,24},{8,0},{16,8},{24,16},{1,25},{9,1},{17,9},{25,17},{2,26},{10... | collective-permute-start | bytes 110600 | tf_op jit(solution)/shard_map/ppermute | solution.py:662
  73.4 0.8 %copy_bitcast_fusion = bf16[2,16,16,384]{3,2,1,0:T(8,128)(2,1)} fusion(bf16[2,16,1,8,384]{4,3,1,0,2:T(8,128)(2,1)S(1)} %bitcast.22, bf16[2,16,1,8,384]{4,3,1,0,2:T(8,128)(2,1)S(1)} %bitcast.21), kind=kLoop, calls=%fused_computation.1 | loop fusion | flops 196608 | bytes 786432 | tf_op jit(solution)/shard_map/reshape | solution.py:696
  74.1 1.2 %collective-permute-done.7.refs_1_ = bf16[144,128]{1,0:T(8,128)(2,1)S(1)} collective-permute-done((bf16[144,128]{1,0:T(8,128)(2,1)S(1)}, bf16[144,128]{1,0:T(8,128)(2,1)S(1)}, u32[]{:S(2)}, u32[]{:S(2)}) %collective-permute-start.7) | collective-permute-done | bytes 36896 | tf_op jit(solution)/shard_map/ppermute | solution.py:662
  75.4 0.7 collective-permute-done.8.refs_2_
  76.1 0.0 collective-permute-done.9.refs_3_
  76.1 0.7 gradient_sum.1
  (3 shorter events, 0.1 us)
Async XLA Ops:
  0.6 1.0 %copy-start.4 = (bf16[2,16,16,384]{3,2,1,0:T(8,128)(2,1)S(1)}, bf16[2,16,16,384]{3,2,1,0:T(8,128)(2,1)}, u32[]{:S(2)}) copy-start(bf16[2,16,16,384]{3,2,1,0:T(8,128)(2,1)} %tokens_ref.1) | copy-start | bytes 1179652
  1.6 0.7 copy-start.6
  2.3 0.7 copy-start.7
  4.7 7.6 %copy-start.1 = (bf16[2,16,16,384]{3,2,1,0:T(8,128)(2,1)S(1)}, bf16[2,16,16,384]{3,2,1,0:T(8,128)(2,1)}, u32[]{:S(2)}) copy-start(bf16[2,16,16,384]{3,2,1,0:T(8,128)(2,1)} %param.17) | copy-start | bytes 1179652
  4.7 20.2 %all-to-all-start = ((bf16[16,104,128]{2,1,0:T(8,128)(2,1)}), bf16[16,104,128]{2,1,0:T(8,128)(2,1)S(1)}, u32[]{:S(2)}, u32[]{:S(2)}) async-start(bf16[16,104,128]{2,1,0:T(8,128)(2,1)} %pack_tokens.1), calls=%async_computation | async-start | bytes 851968 | tf_op jit(solution)/shard_map/all_to_all | solution.py:512
  12.3 7.4 %copy-start = (bf16[384,384]{1,0:T(8,128)(2,1)S(1)}, bf16[384,384]{1,0:T(8,128)(2,1)}, u32[]{:S(2)}) copy-start(bf16[384,384]{1,0:T(8,128)(2,1)} %refs_6_.1) | copy-start | bytes 884740
  12.3 12.7 %copy-start.3 = (bf16[384,1152]{1,0:T(8,128)(2,1)S(1)}, bf16[384,1152]{1,0:T(8,128)(2,1)}, u32[]{:S(2)}) copy-start(bf16[384,1152]{1,0:T(8,128)(2,1)} %project_ref.1) | copy-start | bytes 2654212
  12.3 7.3 %collective-permute-start = (bf16[2,16,8,384]{3,2,1,0:T(8,128)(2,1)S(1)}, bf16[2,16,8,384]{3,2,1,0:T(8,128)(2,1)S(1)}, u32[]{:S(2)}, u32[]{:S(2)}) collective-permute-start(bf16[2,16,8,384]{3,2,1,0:T(8,128)(2,1)S(1)} %dynamic-slice_bitcast_fusion), channel_id=1, source_target_pairs={{0,1},{1,0},{2,3},{3,2},{4,5},{5,4},{6,7},{7,6},{8,9},{9,8},{10,11... | collective-permute-start | bytes 589832 | tf_op jit(solution)/shard_map/ppermute | solution.py:497
  20.1 4.9 %copy-start.8 = (f32[12]{0:T(128)S(1)}, f32[12]{0:T(128)}, u32[]{:S(2)}) copy-start(f32[12]{0:T(128)} %slopes_ref.1) | copy-start | bytes 148
  25.0 1.0 %copy-start.5 = (bf16[384,384]{1,0:T(8,128)(2,1)S(1)}, bf16[384,384]{1,0:T(8,128)(2,1)}, u32[]{:S(2)}) copy-start(bf16[384,384]{1,0:T(8,128)(2,1)} %output_ref.1) | copy-start | bytes 884740
  25.9 21.5 %copy-start.2 = (bf16[384,1152]{1,0:T(8,128)(2,1)S(1)}, bf16[384,1152]{1,0:T(8,128)(2,1)}, u32[]{:S(2)}) copy-start(bf16[384,1152]{1,0:T(8,128)(2,1)} %refs_5_.1) | copy-start | bytes 2654212
  30.7 16.8 %all-to-all-start.1 = ((bf16[32,16,384]{2,1,0:T(8,128)(2,1)}), bf16[32,16,384]{2,1,0:T(8,128)(2,1)S(1)}, u32[]{:S(2)}, u32[]{:S(2)}) async-start(bf16[32,16,384]{2,1,0:T(8,128)(2,1)} %bitcast.6), calls=%async_computation.1 | async-start | bytes 786432 | tf_op jit(solution)/shard_map/all_to_all | solution.py:568
  53.4 2.2 %collective-permute-start.2 = (bf16[2,4,2,144,128]{4,3,2,1,0:T(8,128)(2,1)}, bf16[2,4,2,144,128]{4,3,2,1,0:T(8,128)(2,1)S(1)}, u32[]{:S(2)}, u32[]{:S(2)}) collective-permute-start(bf16[2,4,2,144,128]{4,3,2,1,0:T(8,128)(2,1)} %get-tuple-element.28), channel_id=1, source_target_pairs={{0,2},{2,0},{1,3},{3,1},{4,6},{6,4},{5,7},{7,5},{8,10},{10,8},{9,1... | collective-permute-start | bytes 1769480 | tf_op jit(solution)/shard_map/ppermute | solution.py:624
  53.4 12.6 %collective-permute-start.1 = (bf16[256,384]{1,0:T(8,128)(2,1)S(1)}, bf16[256,384]{1,0:T(8,128)(2,1)S(1)}, u32[]{:S(2)}, u32[]{:S(2)}) collective-permute-start(bf16[256,384]{1,0:T(8,128)(2,1)S(1)} %get-tuple-element.26), channel_id=1, source_target_pairs={{0,1},{1,0},{2,3},{3,2},{4,5},{5,4},{6,7},{7,6},{8,9},{9,8},{10,11... | collective-permute-start | bytes 589832 | tf_op jit(solution)/shard_map/ppermute | solution.py:625
  55.8 6.0 %collective-permute-start.3 = (bf16[2,2,144,128]{3,2,1,0:T(8,128)(2,1)S(1)}, bf16[2,2,144,128]{3,2,1,0:T(8,128)(2,1)S(1)}, u32[]{:S(2)}, u32[]{:S(2)}) collective-permute-start(bf16[2,2,144,128]{3,2,1,0:T(8,128)(2,1)S(1)} %get-tuple-element.30), channel_id=1, source_target_pairs={{0,4},{4,0},{1,5},{5,1},{2,6},{6,2},{3,7},{7,3},{8,12},{12,8},{9,1... | collective-permute-start | bytes 442376 | tf_op jit(solution)/shard_map/ppermute | solution.py:640
  57.3 6.6 %collective-permute-start.4 = (bf16[2,2,144,128]{3,2,1,0:T(8,128)(2,1)S(1)}, bf16[2,2,144,128]{3,2,1,0:T(8,128)(2,1)S(1)}, u32[]{:S(2)}, u32[]{:S(2)}) collective-permute-start(bf16[2,2,144,128]{3,2,1,0:T(8,128)(2,1)S(1)} %get-tuple-element.32), channel_id=1, source_target_pairs={{0,1},{1,0},{2,3},{3,2},{4,5},{5,4},{6,7},{7,6},{8,9},{9,8},{10,11... | collective-permute-start | bytes 442376 | tf_op jit(solution)/shard_map/ppermute | solution.py:641
  64.0 4.4 %collective-permute-start.5 = (bf16[2,144,128]{2,1,0:T(8,128)(2,1)S(1)}, bf16[2,144,128]{2,1,0:T(8,128)(2,1)S(1)}, u32[]{:S(2)}, u32[]{:S(2)}) collective-permute-start(bf16[2,144,128]{2,1,0:T(8,128)(2,1)S(1)} %get-tuple-element.34), channel_id=1, source_target_pairs={{0,1},{1,0},{2,3},{3,2},{4,5},{5,4},{6,7},{7,6},{8,9},{9,8},{10,11... | collective-permute-start | bytes 221192 | tf_op jit(solution)/shard_map/ppermute | solution.py:649
  65.1 4.4 %collective-permute-start.6 = (bf16[2,144,128]{2,1,0:T(8,128)(2,1)S(1)}, bf16[2,144,128]{2,1,0:T(8,128)(2,1)S(1)}, u32[]{:S(2)}, u32[]{:S(2)}) collective-permute-start(bf16[2,144,128]{2,1,0:T(8,128)(2,1)S(1)} %get-tuple-element.36), channel_id=1, source_target_pairs={{0,4},{4,0},{1,5},{5,1},{2,6},{6,2},{3,7},{7,3},{8,12},{12,8},{9,1... | collective-permute-start | bytes 221192 | tf_op jit(solution)/shard_map/ppermute | solution.py:650
  69.5 5.9 %collective-permute-start.7 = (bf16[144,128]{1,0:T(8,128)(2,1)S(1)}, bf16[144,128]{1,0:T(8,128)(2,1)S(1)}, u32[]{:S(2)}, u32[]{:S(2)}) collective-permute-start(bf16[144,128]{1,0:T(8,128)(2,1)S(1)} %get-tuple-element.38), channel_id=1, source_target_pairs={{0,8},{8,16},{16,24},{24,0},{1,9},{9,17},{17,25},{25,1},{2,10},{10... | collective-permute-start | bytes 110600 | tf_op jit(solution)/shard_map/ppermute | solution.py:662
  70.4 5.7 %collective-permute-start.8 = (bf16[144,128]{1,0:T(8,128)(2,1)S(1)}, bf16[144,128]{1,0:T(8,128)(2,1)S(1)}, u32[]{:S(2)}, u32[]{:S(2)}) collective-permute-start(bf16[144,128]{1,0:T(8,128)(2,1)S(1)} %get-tuple-element.39), channel_id=1, source_target_pairs={{0,16},{8,24},{16,0},{24,8},{1,17},{9,25},{17,1},{25,9},{2,18},{10... | collective-permute-start | bytes 110600 | tf_op jit(solution)/shard_map/ppermute | solution.py:662
  71.6 4.6 %collective-permute-start.9 = (bf16[144,128]{1,0:T(8,128)(2,1)S(1)}, bf16[144,128]{1,0:T(8,128)(2,1)S(1)}, u32[]{:S(2)}, u32[]{:S(2)}) collective-permute-start(bf16[144,128]{1,0:T(8,128)(2,1)S(1)} %get-tuple-element.40), channel_id=1, source_target_pairs={{0,24},{8,0},{16,8},{24,16},{1,25},{9,1},{17,9},{25,17},{2,26},{10... | collective-permute-start | bytes 110600 | tf_op jit(solution)/shard_map/ppermute | solution.py:662

commit v6 on v4

--- a/solution.py
+++ b/solution.py
@@ -10,9 +10,9 @@
 
 epsilon = 1e-06
 masked_score = -1e30
-units_each = 6
+units_each = 24
 dates = ("outer", "mid", "pair")
-vmem_limit = 48 * 1024 * 1024
+vmem_limit = 24 * 1024 * 1024
 low = jnp.bfloat16
 wide = jnp.float32
 
@@ -120,7 +120,6 @@
     block_ref,
     project_ref,
     output_ref,
-    earlier_ref,
     out_ref,
     seq_scr,
     token_scr,
@@ -204,7 +203,8 @@
 
 def cotangent_kernel(sizes, *refs):
     dates_each, row_parts, rows_each, columns_each, direct = sizes
-    output_ref, grad_low_ref, heads_grad_ref, grad_scr = refs[-4:]
+    output_ref, later_ref, grad_low_ref, heads_grad_ref, handed_ref, grad_scr = refs[-6:]
+    handed_ref[...] = later_ref[...]
     width = output_ref.shape[0]
     length = row_parts * rows_each
     groups = dates_each * columns_each
@@ -398,7 +398,8 @@
         b_send[outer] = added(b_kept[outer, 1 - mid], b_came[outer, 1 - mid])
 
 
-def spread_kernel(outer_ref, a_kept, a_came, b_kept, b_came, *refs):
+def spread_kernel(outer_ref, a_kept, a_came, b_kept, b_came, sent_ref, leave_ref, *refs):
+    leave_ref[...] = sent_ref[...]
     total = refs[-1]
     half = a_kept.shape[0]
     for outer in range(half):
@@ -468,6 +469,7 @@
     params = pltpu.CompilerParams(vmem_limit_bytes=vmem_limit)
     in_vmem = pl.BlockSpec(memory_space=pltpu.VMEM)
     in_smem = pl.BlockSpec(memory_space=pltpu.SMEM)
+    in_hbm = pl.BlockSpec(memory_space=pltpu.HBM)
     swap = [(0, 1), (1, 0)]
     column_tokens = date_local * row_count * columns_each
     half_tokens = column_tokens // row_size
@@ -475,14 +477,13 @@
         outgoing = pl.pallas_call(
             pack_kernel,
             out_shape=jax.ShapeDtypeStruct((date_size, tile_rows, 128), low),
-            in_specs=[pl.BlockSpec(memory_space=pl.ANY)] * 3,
+            in_specs=[in_hbm] * 3,
             scratch_shapes=[
                 pltpu.SMEM(date_numbers.shape, jnp.int32),
                 pltpu.VMEM(tokens.shape, low),
                 pltpu.VMEM(clear_flags.shape, jnp.int32),
                 pltpu.SemaphoreType.DMA((3,)),
             ],
-            compiler_params=params,
             name="pack_tokens",
         )(date_numbers, tokens, clear_flags)
         row_at = lax.axis_index("row")
@@ -511,24 +512,28 @@
             cotangent.reshape(local_patches * date_local, width),
             other_grad.reshape(half_tokens, width),
         )
-        in_specs = [in_smem] + [in_vmem] * 3
+        in_specs = [in_smem] + [in_vmem] * 4
     else:
         grads_in = (
             lax.all_to_all(cotangent, "row", split_axis=2, concat_axis=1, tiled=True).reshape(
                 column_tokens, width
             ),
         )
-        in_specs = [in_vmem] * 2
-    grad_low, heads_grad = pl.pallas_call(
+        in_specs = [in_vmem] * 3
+    grad_low, heads_grad, time_output = pl.pallas_call(
         functools.partial(
             cotangent_kernel, (date_local, row_size, row_local, columns_each, direct)
         ),
-        out_shape=(jax.ShapeDtypeStruct((column_tokens, width), low),) * 2,
+        out_shape=(
+            jax.ShapeDtypeStruct((column_tokens, width), low),
+            jax.ShapeDtypeStruct((column_tokens, width), low),
+            jax.ShapeDtypeStruct(time_output.shape, low),
+        ),
         in_specs=in_specs,
         scratch_shapes=[pltpu.VMEM((width // 128, column_tokens, 128), wide)],
         compiler_params=params,
         name="cotangent_heads",
-    )(*grads_in, column_output)
+    )(*grads_in, column_output, time_output)
 
     time_tokens = date_count * patches_each
     hidden = pl.pallas_call(
@@ -544,7 +549,7 @@
             ),
         ),
         out_shape=jax.ShapeDtypeStruct((time_tokens, width), low),
-        in_specs=[in_smem, in_vmem, in_vmem, in_vmem, pl.BlockSpec(memory_space=pl.ANY)],
+        in_specs=[in_smem, in_vmem, in_vmem, in_vmem],
         scratch_shapes=[
             pltpu.VMEM((width // 128, time_tokens, 128), wide),
             pltpu.VMEM((time_tokens, width), wide),
@@ -553,7 +558,7 @@
         ],
         compiler_params=params,
         name="time_attention",
-    )(decay_slopes, incoming, time_project, time_output, heads_grad)
+    )(decay_slopes, incoming, time_project, time_output)
 
     if direct:
         parts = hidden.reshape(row_size * date_size, date_local * columns_each, width)
@@ -614,7 +619,6 @@
     if direct:
         kept, sent, kept_grad, sent_grad = results
         arrived_grad = lax.ppermute(sent_grad, "pair", swap)
-        arrived = lax.ppermute(sent, "row", swap)
         mid_one, row_one = lax.axis_index("mid").reshape(1), row_at.reshape(1)
         outer_one = lax.axis_index("outer").reshape(1)
 
@@ -640,14 +644,15 @@
         )(mid_one, row_one, a_kept, a_came, b_kept, b_came)
         a_came = lax.ppermute(a_sent, "row", swap)
         b_came = lax.ppermute(b_sent, "mid", swap)
-        blocks = pl.pallas_call(
+        leaving, *blocks = pl.pallas_call(
             spread_kernel,
-            out_shape=(shaped(),) * outers,
-            in_specs=[in_smem] + [in_vmem] * 4,
+            out_shape=(half_shape, *(shaped(),) * outers),
+            in_specs=[in_smem] + [in_vmem] * 5,
             scratch_shapes=[pltpu.VMEM((outers, *block), low)],
             compiler_params=params,
             name="spread_gradients",
-        )(outer_one, a_kept, a_came, b_kept, b_came)
+        )(outer_one, a_kept, a_came, b_kept, b_came, sent)
+        arrived = lax.ppermute(leaving, "row", swap)
         terms = [blocks[0]]
         for step in range(1, outers):
             route = [(at, (at + step) % outers) for at in range(outers)]

time: 78.9 us -> 74.9 us (0.949)
  Pallas kernels: 15.5 us -> 13.4 us
  local copies, waits for them, and re-layouts: 3.38 us -> 1.73 us
    unnamed x18 -> x16, local copies, waits for them, and re-layouts: 3.35 us -> 1.7 us
    pallas_call x1, Pallas kernels: 5.48 us -> 4.1 us  [body(): pl.pallas_call(functools.partial(time_kernel, (date_size, date_local, pat...]
    ppermute x1, waiting for transfers between devices: 1.08 us -> 2.21 us  [body(): arrived_grad = lax.ppermute(sent_grad, 'pair', swap)]
    ppermute x1, waiting for transfers between devices: 2.17 us -> 1.2 us  [body(): b_came = lax.ppermute(b_sent, 'row', swap)]
    pallas_call x1, Pallas kernels: 6.83 us -> 5.95 us  [body(): pl.pallas_call(functools.partial(column_kernel, (date_local, row_size, ro...]
  transfers between devices with their start and end apart: 12 -> 12, of which waited for: 10 -> 10; matrix products, arithmetic and copies ran while one was open for 1% -> 0% of each run, Pallas kernels for 1% -> 2%
where the time goes in v6:
time: 74.9 us; the launch traced here: 74.6 us
  waiting for transfers between devices  36.1 us (48%)
  starting transfers between devices  21.8 us (29%)
  Pallas kernels  13.4 us (18%)
  local copies, waits for them, and re-layouts  1.73 us (2%)
  other arithmetic  0.83 us (1%)
  between operations  0.76 us (1%)
    all_to_all x1, waiting for transfers between devices, body(): lax.all_to_all(parts, ('row', *dates), split_axis=0, concat_axis=0, tiled...  13.1 us
    all_to_all x1, starting transfers between devices, body(): lax.all_to_all(outgoing, dates, split_axis=0, concat_axis=0, tiled=True)  7.5 us
    pallas_call x1, Pallas kernels, body(): pl.pallas_call(functools.partial(column_kernel, (date_local, row_size, ro...  5.95 us
    ppermute x1, waiting for transfers between devices, body(): other_grad = lax.ppermute(leaving, 'row', swap)  5.72 us
    all_to_all x1, waiting for transfers between devices, body(): lax.all_to_all(outgoing, dates, split_axis=0, concat_axis=0, tiled=True)  4.12 us
    pallas_call x1, Pallas kernels, body(): pl.pallas_call(functools.partial(time_kernel, (date_size, date_local, pat...  4.1 us
    ppermute x1, waiting for transfers between devices, body(): a_came = lax.ppermute(a_sent, 'mid', swap)  3.87 us
    ppermute x3, starting transfers between devices, body(): terms.append(lax.ppermute(blocks[step], 'outer', route))  3.83 us
  transfers between devices with their start and end apart: 12, of which 10 were waited for; matrix products, arithmetic and copies ran while one was open for 0% of the time, Pallas kernels for 2%

profile of v6, /device:TPU:0, one launch (start us, length us, event | category | flops | bytes accessed | tf_op | source)
XLA Modules:
  0.0 74.6 jit_solution(15936615788392609721)
XLA Ops:
  0.6 1.9 %pack_tokens.1 = bf16[16,104,128]{2,1,0:T(8,128)(2,1)} custom-call(s32[2]{0:T(128)} %numbers_ref.1, bf16[2,16,16,384]{3,2,1,0:T(8,128)(2,1)} %tokens_ref.1, s32[2,16,16]{2,1,0:T(8,128)} %flags_ref.1), custom_call_target="tpu_custom_call" | custom-call | tf_op jit(solution)/shard_map/pack_tokens/pallas_call | solution.py:477
  2.5 0.0 copy-start.2
  2.5 0.0 copy-start.4
  2.5 7.5 %all-to-all-start = ((bf16[16,104,128]{2,1,0:T(8,128)(2,1)}), bf16[16,104,128]{2,1,0:T(8,128)(2,1)S(1)}, u32[]{:S(2)}, u32[]{:S(2)}) async-start(bf16[16,104,128]{2,1,0:T(8,128)(2,1)} %pack_tokens.1), calls=%async_computation | async-start | bytes 851968 | tf_op jit(solution)/shard_map/all_to_all | solution.py:507
  10.0 0.0 copy-start
  10.0 0.0 copy-start.1
  10.1 0.0 copy-done.2
  10.1 1.6 %collective-permute-start = (bf16[2,16,8,384]{3,2,1,0:T(8,128)(2,1)S(1)}, bf16[2,16,8,384]{3,2,1,0:T(8,128)(2,1)S(1)}, u32[]{:S(2)}, u32[]{:S(2)}) collective-permute-start(bf16[2,16,8,384]{3,2,1,0:T(8,128)(2,1)S(1)} %dynamic-slice_bitcast_fusion), channel_id=1, source_target_pairs={{0,1},{1,0},{2,3},{3,2},{4,5},{5,4},{6,7},{7,6},{8,9},{9,8},{10,11... | collective-permute-start | bytes 589832 | tf_op jit(solution)/shard_map/ppermute | solution.py:492
  11.7 5.7 %collective-permute-done = bf16[2,16,8,384]{3,2,1,0:T(8,128)(2,1)S(1)} collective-permute-done((bf16[2,16,8,384]{3,2,1,0:T(8,128)(2,1)S(1)}, bf16[2,16,8,384]{3,2,1,0:T(8,128)(2,1)S(1)}, u32[]{:S(2)}, u32[]{:S(2)}) %collective-permute-start) | collective-permute-done | bytes 196640 | tf_op jit(solution)/shard_map/ppermute | solution.py:492
  17.4 0.0 copy-done.4
  17.4 0.0 copy-done
  17.4 0.5 cotangent_heads.1
  17.9 0.0 copy-start.5
  17.9 0.7 copy-done.5
  18.6 0.0 copy-start.7
  18.6 4.1 %all-to-all-done.block_ref = bf16[16,104,128]{2,1,0:T(8,128)(2,1)S(1)} async-done(((bf16[16,104,128]{2,1,0:T(8,128)(2,1)}), bf16[16,104,128]{2,1,0:T(8,128)(2,1)S(1)}, u32[]{:S(2)}, u32[]{:S(2)}) %all-to-all-start) | async-done | bytes 426016 | tf_op jit(solution)/shard_map/all_to_all | solution.py:507
  22.8 0.0 copy-done.1
  22.8 0.0 copy-done.7
  22.8 0.0 copy-start.6
  22.8 1.0 %copy-done.6 = bf16[384,384]{1,0:T(8,128)(2,1)S(1)} copy-done((bf16[384,384]{1,0:T(8,128)(2,1)S(1)}, bf16[384,384]{1,0:T(8,128)(2,1)}, u32[]{:S(2)}) %copy-start.6) | copy-done | bytes 294936
  23.7 0.0 copy-start.3
  23.7 4.1 %time_attention.1 = bf16[512,384]{1,0:T(8,128)(2,1)} custom-call(f32[12]{0:T(128)S(1)} %copy-done.7, bf16[16,104,128]{2,1,0:T(8,128)(2,1)S(1)} %all-to-all-done.block_ref, bf16[384,1152]{1,0:T(8,128)(2,1)S(1)} %copy-done.1, bf16[384,384]{1,0:T(8,128)(2,1)S(1)} %copy-done.6), custom_call_target="tpu_custom_call" | custom-call | tf_op jit(solution)/shard_map/time_attention/pallas_call | solution.py:539
  27.8 3.6 %all-to-all-start.1 = ((bf16[32,16,384]{2,1,0:T(8,128)(2,1)}), bf16[32,16,384]{2,1,0:T(8,128)(2,1)S(1)}, u32[]{:S(2)}, u32[]{:S(2)}) async-start(bf16[32,16,384]{2,1,0:T(8,128)(2,1)} %bitcast.6), calls=%async_computation.1 | async-start | bytes 786432 | tf_op jit(solution)/shard_map/all_to_all | solution.py:565
  31.5 13.1 %all-to-all-done.1 = bf16[32,16,384]{2,1,0:T(8,128)(2,1)S(1)} async-done(((bf16[32,16,384]{2,1,0:T(8,128)(2,1)}), bf16[32,16,384]{2,1,0:T(8,128)(2,1)S(1)}, u32[]{:S(2)}, u32[]{:S(2)}) %all-to-all-start.1) | async-done | bytes 393248 | tf_op jit(solution)/shard_map/all_to_all | solution.py:565
  44.6 0.0 copy-done.3
  44.6 5.9 %column_attention.1 = (bf16[256,384]{1,0:T(8,128)(2,1)S(1)}, bf16[256,384]{1,0:T(8,128)(2,1)S(1)}, bf16[2,4,2,144,128]{4,3,2,1,0:T(8,128)(2,1)S(1)}, bf16[2,4,2,144,128]{4,3,2,1,0:T(8,128)(2,1)}) custom-call(s32[1]{0:T(128)} %bitcast.refs_0_.row_ref, s32[1]{0:T(128)} %bitcast.1.refs_1_, bf16[512,384]{1,0:T(8,128)(2,1)S(1)} %bitcast.17, ...), custom_call_target="tpu_custom_call" | custom-call | tf_op jit(solution)/shard_map/column_attention/pallas_call | solution.py:591
  50.5 0.0 collective-permute-start.1
  50.5 2.2 %collective-permute-done.1.came_ref = bf16[2,4,2,144,128]{4,3,2,1,0:T(8,128)(2,1)S(1)} collective-permute-done((bf16[2,4,2,144,128]{4,3,2,1,0:T(8,128)(2,1)}, bf16[2,4,2,144,128]{4,3,2,1,0:T(8,128)(2,1)S(1)}, u32[]{:S(2)}, u32[]{:S(2)}) %collective-permute-start.1) | collective-permute-done | bytes 589856 | tf_op jit(solution)/shard_map/ppermute | solution.py:621
  52.7 0.1 halve_gradients.1
  52.9 1.5 %collective-permute-start.2 = (bf16[2,2,144,128]{3,2,1,0:T(8,128)(2,1)S(1)}, bf16[2,2,144,128]{3,2,1,0:T(8,128)(2,1)S(1)}, u32[]{:S(2)}, u32[]{:S(2)}) collective-permute-start(bf16[2,2,144,128]{3,2,1,0:T(8,128)(2,1)S(1)} %get-tuple-element.32), channel_id=1, source_target_pairs={{0,4},{4,0},{1,5},{5,1},{2,6},{6,2},{3,7},{7,3},{8,12},{12,8},{9,1... | collective-permute-start | bytes 442376 | tf_op jit(solution)/shard_map/ppermute | solution.py:636
  54.4 0.5 collective-permute-start.3
  55.0 3.9 %collective-permute-done.2.a_came = bf16[2,2,144,128]{3,2,1,0:T(8,128)(2,1)S(1)} collective-permute-done((bf16[2,2,144,128]{3,2,1,0:T(8,128)(2,1)S(1)}, bf16[2,2,144,128]{3,2,1,0:T(8,128)(2,1)S(1)}, u32[]{:S(2)}, u32[]{:S(2)}) %collective-permute-start.2) | collective-permute-done | bytes 147488 | tf_op jit(solution)/shard_map/ppermute | solution.py:636
  58.8 1.2 %collective-permute-done.3.b_came = bf16[2,2,144,128]{3,2,1,0:T(8,128)(2,1)S(1)} collective-permute-done((bf16[2,2,144,128]{3,2,1,0:T(8,128)(2,1)S(1)}, bf16[2,2,144,128]{3,2,1,0:T(8,128)(2,1)S(1)}, u32[]{:S(2)}, u32[]{:S(2)}) %collective-permute-start.3) | collective-permute-done | bytes 147488 | tf_op jit(solution)/shard_map/ppermute | solution.py:637
  60.0 0.1 halve_gradients_again.1
  60.1 0.6 collective-permute-start.4
  60.7 1.0 %collective-permute-start.5 = (bf16[2,144,128]{2,1,0:T(8,128)(2,1)S(1)}, bf16[2,144,128]{2,1,0:T(8,128)(2,1)S(1)}, u32[]{:S(2)}, u32[]{:S(2)}) collective-permute-start(bf16[2,144,128]{2,1,0:T(8,128)(2,1)S(1)} %get-tuple-element.38), channel_id=1, source_target_pairs={{0,4},{4,0},{1,5},{5,1},{2,6},{6,2},{3,7},{7,3},{8,12},{12,8},{9,1... | collective-permute-start | bytes 221192 | tf_op jit(solution)/shard_map/ppermute | solution.py:646
  61.7 2.8 %collective-permute-done.4.a_came = bf16[2,144,128]{2,1,0:T(8,128)(2,1)S(1)} collective-permute-done((bf16[2,144,128]{2,1,0:T(8,128)(2,1)S(1)}, bf16[2,144,128]{2,1,0:T(8,128)(2,1)S(1)}, u32[]{:S(2)}, u32[]{:S(2)}) %collective-permute-start.4) | collective-permute-done | bytes 73760 | tf_op jit(solution)/shard_map/ppermute | solution.py:645
  64.5 0.5 collective-permute-done.5.b_came
  65.1 0.1 spread_gradients.1
  65.1 1.6 %collective-permute-start.6 = (bf16[256,384]{1,0:T(8,128)(2,1)S(1)}, bf16[256,384]{1,0:T(8,128)(2,1)S(1)}, u32[]{:S(2)}, u32[]{:S(2)}) collective-permute-start(bf16[256,384]{1,0:T(8,128)(2,1)S(1)} %get-tuple-element.40), channel_id=1, source_target_pairs={{0,1},{1,0},{2,3},{3,2},{4,5},{5,4},{6,7},{7,6},{8,9},{9,8},{10,11... | collective-permute-start | bytes 589832 | tf_op jit(solution)/shard_map/ppermute | solution.py:655
  66.7 0.0 collective-permute-start.7
  66.7 1.6 %collective-permute-start.8 = (bf16[144,128]{1,0:T(8,128)(2,1)S(1)}, bf16[144,128]{1,0:T(8,128)(2,1)S(1)}, u32[]{:S(2)}, u32[]{:S(2)}) collective-permute-start(bf16[144,128]{1,0:T(8,128)(2,1)S(1)} %get-tuple-element.43), channel_id=1, source_target_pairs={{0,16},{8,24},{16,0},{24,8},{1,17},{9,25},{17,1},{25,9},{2,18},{10... | collective-permute-start | bytes 110600 | tf_op jit(solution)/shard_map/ppermute | solution.py:659
  68.3 2.2 %collective-permute-start.9 = (bf16[144,128]{1,0:T(8,128)(2,1)S(1)}, bf16[144,128]{1,0:T(8,128)(2,1)S(1)}, u32[]{:S(2)}, u32[]{:S(2)}) collective-permute-start(bf16[144,128]{1,0:T(8,128)(2,1)S(1)} %get-tuple-element.44), channel_id=1, source_target_pairs={{0,24},{8,0},{16,8},{24,16},{1,25},{9,1},{17,9},{25,17},{2,26},{10... | collective-permute-start | bytes 110600 | tf_op jit(solution)/shard_map/ppermute | solution.py:659
  70.5 1.9 %collective-permute-done.7.refs_1_ = bf16[144,128]{1,0:T(8,128)(2,1)S(1)} collective-permute-done((bf16[144,128]{1,0:T(8,128)(2,1)S(1)}, bf16[144,128]{1,0:T(8,128)(2,1)S(1)}, u32[]{:S(2)}, u32[]{:S(2)}) %collective-permute-start.7) | collective-permute-done | bytes 36896 | tf_op jit(solution)/shard_map/ppermute | solution.py:659
  72.4 0.0 collective-permute-done.8.refs_2_
  72.4 0.6 collective-permute-done.9.refs_3_
  73.0 0.7 gradient_sum.1
  73.7 0.0 collective-permute-done.6
  73.8 0.8 %copy_bitcast_fusion = bf16[2,16,16,384]{3,2,1,0:T(8,128)(2,1)} fusion(bf16[2,16,1,8,384]{4,3,1,0,2:T(8,128)(2,1)S(1)} %bitcast.22, bf16[2,16,1,8,384]{4,3,1,0,2:T(8,128)(2,1)S(1)} %bitcast.21), kind=kLoop, calls=%fused_computation.1 | loop fusion | flops 196608 | bytes 786432 | tf_op jit(solution)/shard_map/reshape | solution.py:693
  (2 shorter events, 0.1 us)
Async XLA Ops:
  2.5 7.6 %copy-start.2 = (bf16[2,16,16,384]{3,2,1,0:T(8,128)(2,1)S(1)}, bf16[2,16,16,384]{3,2,1,0:T(8,128)(2,1)}, u32[]{:S(2)}) copy-start(bf16[2,16,16,384]{3,2,1,0:T(8,128)(2,1)} %param.17) | copy-start | bytes 1179652
  2.5 14.9 %copy-start.4 = (bf16[384,384]{1,0:T(8,128)(2,1)S(1)}, bf16[384,384]{1,0:T(8,128)(2,1)}, u32[]{:S(2)}) copy-start(bf16[384,384]{1,0:T(8,128)(2,1)} %refs_4_.1) | copy-start | bytes 884740
  2.5 20.2 %all-to-all-start = ((bf16[16,104,128]{2,1,0:T(8,128)(2,1)}), bf16[16,104,128]{2,1,0:T(8,128)(2,1)S(1)}, u32[]{:S(2)}, u32[]{:S(2)}) async-start(bf16[16,104,128]{2,1,0:T(8,128)(2,1)} %pack_tokens.1), calls=%async_computation | async-start | bytes 851968 | tf_op jit(solution)/shard_map/all_to_all | solution.py:507
  10.0 7.4 %copy-start = (bf16[384,384]{1,0:T(8,128)(2,1)S(1)}, bf16[384,384]{1,0:T(8,128)(2,1)}, u32[]{:S(2)}) copy-start(bf16[384,384]{1,0:T(8,128)(2,1)} %refs_6_.1) | copy-start | bytes 884740
  10.0 12.7 %copy-start.1 = (bf16[384,1152]{1,0:T(8,128)(2,1)S(1)}, bf16[384,1152]{1,0:T(8,128)(2,1)}, u32[]{:S(2)}) copy-start(bf16[384,1152]{1,0:T(8,128)(2,1)} %project_ref.1) | copy-start | bytes 2654212
  10.1 7.3 %collective-permute-start = (bf16[2,16,8,384]{3,2,1,0:T(8,128)(2,1)S(1)}, bf16[2,16,8,384]{3,2,1,0:T(8,128)(2,1)S(1)}, u32[]{:S(2)}, u32[]{:S(2)}) collective-permute-start(bf16[2,16,8,384]{3,2,1,0:T(8,128)(2,1)S(1)} %dynamic-slice_bitcast_fusion), channel_id=1, source_target_pairs={{0,1},{1,0},{2,3},{3,2},{4,5},{5,4},{6,7},{7,6},{8,9},{9,8},{10,11... | collective-permute-start | bytes 589832 | tf_op jit(solution)/shard_map/ppermute | solution.py:492
  17.9 0.7 copy-start.5
  18.6 4.1 %copy-start.7 = (f32[12]{0:T(128)S(1)}, f32[12]{0:T(128)}, u32[]{:S(2)}) copy-start(f32[12]{0:T(128)} %slopes_ref.1) | copy-start | bytes 148
  22.8 1.0 %copy-start.6 = (bf16[384,384]{1,0:T(8,128)(2,1)S(1)}, bf16[384,384]{1,0:T(8,128)(2,1)}, u32[]{:S(2)}) copy-start(bf16[384,384]{1,0:T(8,128)(2,1)} %copy-done.5) | copy-start | bytes 884740
  23.7 20.8 %copy-start.3 = (bf16[384,1152]{1,0:T(8,128)(2,1)S(1)}, bf16[384,1152]{1,0:T(8,128)(2,1)}, u32[]{:S(2)}) copy-start(bf16[384,1152]{1,0:T(8,128)(2,1)} %refs_5_.1) | copy-start | bytes 2654212
  27.8 16.7 %all-to-all-start.1 = ((bf16[32,16,384]{2,1,0:T(8,128)(2,1)}), bf16[32,16,384]{2,1,0:T(8,128)(2,1)S(1)}, u32[]{:S(2)}, u32[]{:S(2)}) async-start(bf16[32,16,384]{2,1,0:T(8,128)(2,1)} %bitcast.6), calls=%async_computation.1 | async-start | bytes 786432 | tf_op jit(solution)/shard_map/all_to_all | solution.py:565
  50.5 2.2 %collective-permute-start.1 = (bf16[2,4,2,144,128]{4,3,2,1,0:T(8,128)(2,1)}, bf16[2,4,2,144,128]{4,3,2,1,0:T(8,128)(2,1)S(1)}, u32[]{:S(2)}, u32[]{:S(2)}) collective-permute-start(bf16[2,4,2,144,128]{4,3,2,1,0:T(8,128)(2,1)} %get-tuple-element.30), channel_id=1, source_target_pairs={{0,2},{2,0},{1,3},{3,1},{4,6},{6,4},{5,7},{7,5},{8,10},{10,8},{9,1... | collective-permute-start | bytes 1769480 | tf_op jit(solution)/shard_map/ppermute | solution.py:621
  52.9 6.0 %collective-permute-start.2 = (bf16[2,2,144,128]{3,2,1,0:T(8,128)(2,1)S(1)}, bf16[2,2,144,128]{3,2,1,0:T(8,128)(2,1)S(1)}, u32[]{:S(2)}, u32[]{:S(2)}) collective-permute-start(bf16[2,2,144,128]{3,2,1,0:T(8,128)(2,1)S(1)} %get-tuple-element.32), channel_id=1, source_target_pairs={{0,4},{4,0},{1,5},{5,1},{2,6},{6,2},{3,7},{7,3},{8,12},{12,8},{9,1... | collective-permute-start | bytes 442376 | tf_op jit(solution)/shard_map/ppermute | solution.py:636
  54.4 5.6 %collective-permute-start.3 = (bf16[2,2,144,128]{3,2,1,0:T(8,128)(2,1)S(1)}, bf16[2,2,144,128]{3,2,1,0:T(8,128)(2,1)S(1)}, u32[]{:S(2)}, u32[]{:S(2)}) collective-permute-start(bf16[2,2,144,128]{3,2,1,0:T(8,128)(2,1)S(1)} %get-tuple-element.34), channel_id=1, source_target_pairs={{0,1},{1,0},{2,3},{3,2},{4,5},{5,4},{6,7},{7,6},{8,9},{9,8},{10,11... | collective-permute-start | bytes 442376 | tf_op jit(solution)/shard_map/ppermute | solution.py:637
  60.1 4.4 %collective-permute-start.4 = (bf16[2,144,128]{2,1,0:T(8,128)(2,1)S(1)}, bf16[2,144,128]{2,1,0:T(8,128)(2,1)S(1)}, u32[]{:S(2)}, u32[]{:S(2)}) collective-permute-start(bf16[2,144,128]{2,1,0:T(8,128)(2,1)S(1)} %get-tuple-element.36), channel_id=1, source_target_pairs={{0,1},{1,0},{2,3},{3,2},{4,5},{5,4},{6,7},{7,6},{8,9},{9,8},{10,11... | collective-permute-start | bytes 221192 | tf_op jit(solution)/shard_map/ppermute | solution.py:645
  60.7 4.4 %collective-permute-start.5 = (bf16[2,144,128]{2,1,0:T(8,128)(2,1)S(1)}, bf16[2,144,128]{2,1,0:T(8,128)(2,1)S(1)}, u32[]{:S(2)}, u32[]{:S(2)}) collective-permute-start(bf16[2,144,128]{2,1,0:T(8,128)(2,1)S(1)} %get-tuple-element.38), channel_id=1, source_target_pairs={{0,4},{4,0},{1,5},{5,1},{2,6},{6,2},{3,7},{7,3},{8,12},{12,8},{9,1... | collective-permute-start | bytes 221192 | tf_op jit(solution)/shard_map/ppermute | solution.py:646
  65.1 8.6 %collective-permute-start.6 = (bf16[256,384]{1,0:T(8,128)(2,1)S(1)}, bf16[256,384]{1,0:T(8,128)(2,1)S(1)}, u32[]{:S(2)}, u32[]{:S(2)}) collective-permute-start(bf16[256,384]{1,0:T(8,128)(2,1)S(1)} %get-tuple-element.40), channel_id=1, source_target_pairs={{0,1},{1,0},{2,3},{3,2},{4,5},{5,4},{6,7},{7,6},{8,9},{9,8},{10,11... | collective-permute-start | bytes 589832 | tf_op jit(solution)/shard_map/ppermute | solution.py:655
  66.7 5.8 %collective-permute-start.7 = (bf16[144,128]{1,0:T(8,128)(2,1)S(1)}, bf16[144,128]{1,0:T(8,128)(2,1)S(1)}, u32[]{:S(2)}, u32[]{:S(2)}) collective-permute-start(bf16[144,128]{1,0:T(8,128)(2,1)S(1)} %get-tuple-element.42), channel_id=1, source_target_pairs={{0,8},{8,16},{16,24},{24,0},{1,9},{9,17},{17,25},{25,1},{2,10},{10... | collective-permute-start | bytes 110600 | tf_op jit(solution)/shard_map/ppermute | solution.py:659
  66.7 5.8 %collective-permute-start.8 = (bf16[144,128]{1,0:T(8,128)(2,1)S(1)}, bf16[144,128]{1,0:T(8,128)(2,1)S(1)}, u32[]{:S(2)}, u32[]{:S(2)}) collective-permute-start(bf16[144,128]{1,0:T(8,128)(2,1)S(1)} %get-tuple-element.43), channel_id=1, source_target_pairs={{0,16},{8,24},{16,0},{24,8},{1,17},{9,25},{17,1},{25,9},{2,18},{10... | collective-permute-start | bytes 110600 | tf_op jit(solution)/shard_map/ppermute | solution.py:659
  68.3 4.7 %collective-permute-start.9 = (bf16[144,128]{1,0:T(8,128)(2,1)S(1)}, bf16[144,128]{1,0:T(8,128)(2,1)S(1)}, u32[]{:S(2)}, u32[]{:S(2)}) collective-permute-start(bf16[144,128]{1,0:T(8,128)(2,1)S(1)} %get-tuple-element.44), channel_id=1, source_target_pairs={{0,24},{8,0},{16,8},{24,16},{1,25},{9,1},{17,9},{25,17},{2,26},{10... | collective-permute-start | bytes 110600 | tf_op jit(solution)/shard_map/ppermute | solution.py:659

commit v7 on v6

--- a/solution.py
+++ b/solution.py
@@ -203,8 +203,9 @@
 
 def cotangent_kernel(sizes, *refs):
     dates_each, row_parts, rows_each, columns_each, direct = sizes
-    output_ref, later_ref, grad_low_ref, heads_grad_ref, handed_ref, grad_scr = refs[-6:]
-    handed_ref[...] = later_ref[...]
+    output_ref, slopes_ref, grad_low_ref, heads_grad_ref, handed_ref, grad_scr = refs[-6:]
+    for head in range(slopes_ref.shape[0]):
+        handed_ref[head] = slopes_ref[head]
     width = output_ref.shape[0]
     length = row_parts * rows_each
     groups = dates_each * columns_each
@@ -235,22 +236,11 @@
     heads_grad_ref[...] = contract_last(grad_low_ref[...], output_ref[...]).astype(low)
 
 
-def column_kernel(sizes, *refs):
-    dates_each, row_parts, rows_each, columns_each, head_count, packed, date_size, direct = sizes
-    if direct:
-        row_ref, pair_ref, *refs = refs
-        kept_ref, sent_ref, first_grad_ref, second_grad_ref = refs[5:9]
-    else:
-        mixed_ref, first_grad_ref, second_grad_ref = refs[5:8]
-    hidden_ref, grad_low_scr, heads_grad_scr, project_ref, output_ref = refs[:5]
-    seq_scr, plane_scr, normed_scr, qkv_scr, heads_scr, qkv_grad_scr = refs[-6:]
-    width = hidden_ref.shape[1]
-    head_size = width // head_count
-    lanes = packed * head_size
+def load_planes(sizes, row_ref, hidden_ref, seq_scr, plane_scr):
+    dates_each, row_parts, rows_each, columns_each, direct = sizes
     length = row_parts * rows_each
     groups = dates_each * columns_each
     part_rows = rows_each * groups
-    inverse_root = 1.0 / math.sqrt(head_size)
     if direct:
         for part in range(row_parts):
             source = pl.multiple_of(((row_ref[0] + part) % row_parts) * part_rows, part_rows)
@@ -269,6 +259,58 @@
             first = (group // columns_each) * (length * columns_each) + group % columns_each
             at = pl.ds(first, length, stride=columns_each)
         plane_scr[rows, :] = get_tiles(seq_scr, at)
+
+
+def mixed_kernel(sizes, row_ref, hidden_ref, heads_ref, output_ref, *refs):
+    dates_each, row_parts, rows_each, columns_each, direct = sizes
+    *mixed_refs, seq_scr, plane_scr = refs
+    length = row_parts * rows_each
+    groups = dates_each * columns_each
+    part_rows = rows_each * groups
+    load_planes(sizes, row_ref, hidden_ref, seq_scr, plane_scr)
+    mixed = plane_scr[...] + matmul(heads_ref[...], output_ref[...])
+    for group in range(groups):
+        inner = (group // columns_each) * (rows_each * columns_each) + group % columns_each
+        for part in range(row_parts):
+            begin = group * length + part * rows_each
+            put_tiles(
+                seq_scr,
+                pl.ds(part * part_rows + inner, rows_each, stride=columns_each),
+                mixed[begin : begin + rows_each],
+            )
+    if direct:
+        kept_ref, sent_ref = mixed_refs
+        kept_ref[...] = get_tiles(seq_scr, slice(0, part_rows)).astype(low)
+        sent_ref[...] = get_tiles(seq_scr, slice(part_rows, 2 * part_rows)).astype(low)
+    else:
+        mixed_refs[0][...] = get_tiles(seq_scr, slice(None)).astype(low)
+
+
+def column_kernel(
+    sizes,
+    row_ref,
+    pair_ref,
+    hidden_ref,
+    grad_low_scr,
+    heads_grad_scr,
+    project_ref,
+    heads_scr,
+    first_grad_ref,
+    second_grad_ref,
+    seq_scr,
+    plane_scr,
+    normed_scr,
+    qkv_scr,
+    qkv_grad_scr,
+):
+    dates_each, row_parts, rows_each, columns_each, direct, head_count, packed, date_size = sizes
+    width = hidden_ref.shape[1]
+    head_size = width // head_count
+    lanes = packed * head_size
+    length = row_parts * rows_each
+    groups = dates_each * columns_each
+    inverse_root = 1.0 / math.sqrt(head_size)
+    load_planes(sizes[:5], row_ref, hidden_ref, seq_scr, plane_scr)
     normed_scr[...] = rms_norm(plane_scr[...])
     qkv_scr[...] = matmul(normed_scr[...], project_ref[...]).astype(low)
     mask = block_mask(length, packed, head_size)
@@ -319,21 +361,6 @@
             heads_scr[rows, at_query] = heads.astype(low)
             query_grad = own_blocks(query_full, length, packed, head_size) * inverse_root
             qkv_grad_scr[rows, at_query] = query_grad.astype(low)
-    mixed = plane_scr[...] + matmul(heads_scr[...], output_ref[...])
-    for group in range(groups):
-        inner = (group // columns_each) * (rows_each * columns_each) + group % columns_each
-        for part in range(row_parts):
-            begin = group * length + part * rows_each
-            put_tiles(
-                seq_scr,
-                pl.ds(part * part_rows + inner, rows_each, stride=columns_each),
-                mixed[begin : begin + rows_each],
-            )
-    if direct:
-        kept_ref[...] = get_tiles(seq_scr, slice(0, part_rows)).astype(low)
-        sent_ref[...] = get_tiles(seq_scr, slice(part_rows, 2 * part_rows)).astype(low)
-    else:
-        mixed_ref[...] = get_tiles(seq_scr, slice(None)).astype(low)
     project_grad = contract_rows(qkv_grad_scr[...], normed_scr[...])
     output_grad = contract_rows(grad_low_scr[...], heads_scr[...])
     if not direct:
@@ -365,55 +392,20 @@
             )
         for row_part in range(2):
             for first, one, two in zip((0, 2 * half), pair[0][row_part], pair[1][row_part]):
-                place = (row_part, outer // 2, outer % 2, slice(first, first + one.shape[0]))
+                place = (row_part, outer, slice(first, first + one.shape[0]))
                 keep_ref[place] = jnp.where(even, one, two).astype(low)
                 send_ref[place] = jnp.where(even, two, one).astype(low)
 
 
-def added(left, right):
-    return (left.astype(wide) + right.astype(wide)).astype(low)
-
-
-def halve_kernel(mid_ref, row_ref, kept_ref, came_ref, a_keep, a_send, b_keep, b_send):
-    rows, outers, mids = kept_ref.shape[:3]
-    mid, row = mid_ref[0], row_ref[0]
-    for outer in range(outers // 2):
-        for at in range(rows):
-            a_keep[at, outer] = added(kept_ref[at, outer, mid], came_ref[at, outer, mid])
-            a_send[at, outer] = added(kept_ref[at, outer, 1 - mid], came_ref[at, outer, 1 - mid])
-        later = outer + outers // 2
-        for at in range(mids):
-            b_keep[outer, at] = added(kept_ref[row, later, at], came_ref[row, later, at])
-            b_send[outer, at] = added(kept_ref[1 - row, later, at], came_ref[1 - row, later, at])
-
-
-def halve_again_kernel(
-    mid_ref, row_ref, a_kept, a_came, b_kept, b_came, a_keep, a_send, b_keep, b_send
-):
-    mid, row = mid_ref[0], row_ref[0]
-    for outer in range(a_kept.shape[1]):
-        a_keep[outer] = added(a_kept[row, outer], a_came[row, outer])
-        a_send[outer] = added(a_kept[1 - row, outer], a_came[1 - row, outer])
-        b_keep[outer] = added(b_kept[outer, mid], b_came[outer, mid])
-        b_send[outer] = added(b_kept[outer, 1 - mid], b_came[outer, 1 - mid])
-
-
-def spread_kernel(outer_ref, a_kept, a_came, b_kept, b_came, sent_ref, leave_ref, *refs):
-    leave_ref[...] = sent_ref[...]
-    total = refs[-1]
-    half = a_kept.shape[0]
-    for outer in range(half):
-        total[outer] = added(a_kept[outer], a_came[outer])
-        total[half + outer] = added(b_kept[outer], b_came[outer])
-    for step in range(2 * half):
-        refs[step][...] = total[(outer_ref[0] + step) % (2 * half)]
-
-
-def finish_kernel(project_each, row_ref, *refs):
-    *terms, project_ref, output_ref = refs
-    total = terms[0][...].astype(wide)
-    for term in terms[1:]:
-        total = total + term[...].astype(wide)
+def pair_kernel(row_ref, kept_ref, came_ref, sum_ref, handed_ref):
+    handed_ref[0] = row_ref[0]
+    sum_ref[...] = (kept_ref[...].astype(wide) + came_ref[...].astype(wide)).astype(low)
+
+
+def finish_kernel(project_each, row_ref, terms_ref, project_ref, output_ref):
+    total = terms_ref[0].astype(wide)
+    for source in range(1, terms_ref.shape[0]):
+        total = total + terms_ref[source].astype(wide)
     whole = 2 * total.shape[0] // 3
     main = total[:whole]
     tail = total[whole:]
@@ -469,7 +461,6 @@
     params = pltpu.CompilerParams(vmem_limit_bytes=vmem_limit)
     in_vmem = pl.BlockSpec(memory_space=pltpu.VMEM)
     in_smem = pl.BlockSpec(memory_space=pltpu.SMEM)
-    in_hbm = pl.BlockSpec(memory_space=pltpu.HBM)
     swap = [(0, 1), (1, 0)]
     column_tokens = date_local * row_count * columns_each
     half_tokens = column_tokens // row_size
@@ -477,7 +468,7 @@
         outgoing = pl.pallas_call(
             pack_kernel,
             out_shape=jax.ShapeDtypeStruct((date_size, tile_rows, 128), low),
-            in_specs=[in_hbm] * 3,
+            in_specs=[pl.BlockSpec(memory_space=pltpu.HBM)] * 3,
             scratch_shapes=[
                 pltpu.SMEM(date_numbers.shape, jnp.int32),
                 pltpu.VMEM(tokens.shape, low),
@@ -512,28 +503,28 @@
             cotangent.reshape(local_patches * date_local, width),
             other_grad.reshape(half_tokens, width),
         )
-        in_specs = [in_smem] + [in_vmem] * 4
+        in_specs = [in_smem] + [in_vmem] * 3 + [in_smem]
     else:
         grads_in = (
             lax.all_to_all(cotangent, "row", split_axis=2, concat_axis=1, tiled=True).reshape(
                 column_tokens, width
             ),
         )
-        in_specs = [in_vmem] * 3
-    grad_low, heads_grad, time_output = pl.pallas_call(
+        in_specs = [in_vmem] * 2 + [in_smem]
+    grad_low, heads_grad, slopes = pl.pallas_call(
         functools.partial(
             cotangent_kernel, (date_local, row_size, row_local, columns_each, direct)
         ),
         out_shape=(
             jax.ShapeDtypeStruct((column_tokens, width), low),
             jax.ShapeDtypeStruct((column_tokens, width), low),
-            jax.ShapeDtypeStruct(time_output.shape, low),
+            jax.ShapeDtypeStruct(decay_slopes.shape, wide),
         ),
         in_specs=in_specs,
+        out_specs=(in_vmem, in_vmem, in_smem),
         scratch_shapes=[pltpu.VMEM((width // 128, column_tokens, 128), wide)],
-        compiler_params=params,
         name="cotangent_heads",
-    )(*grads_in, column_output, time_output)
+    )(*grads_in, column_output, decay_slopes)
 
     time_tokens = date_count * patches_each
     hidden = pl.pallas_call(
@@ -558,7 +549,7 @@
         ],
         compiler_params=params,
         name="time_attention",
-    )(decay_slopes, incoming, time_project, time_output)
+    )(slopes, incoming, time_project, time_output)
 
     if direct:
         parts = hidden.reshape(row_size * date_size, date_local * columns_each, width)
@@ -573,111 +564,87 @@
     plane = plane.reshape(column_tokens, width)
     half_shape = jax.ShapeDtypeStruct((half_tokens, width), low)
     packed_rows = (project_each + output_each) * 3 // 2
-    block = (packed_rows, 128)
-    outers = date_size // 4
-    if direct:
-        half_grads = jax.ShapeDtypeStruct((row_size, outers, 2, *block), low)
-        places = (row_at.reshape(1), lax.axis_index("pair").reshape(1))
-        out_shape = (half_shape, half_shape, half_grads, half_grads)
-        in_specs = [in_smem] * 2 + [in_vmem] * 5
-    else:
-        places = ()
-        out_shape = (
-            jax.ShapeDtypeStruct((column_tokens, width), low),
+    row_one = lax.axis_index("row").reshape(1)
+    pair_one = lax.axis_index("pair").reshape(1)
+    sizes = (date_local, row_size, row_local, columns_each, direct)
+    if direct:
+        half_grads = jax.ShapeDtypeStruct((row_size, date_size // 2, packed_rows, 128), low)
+        grad_shapes = (half_grads, half_grads)
+        mixed_shapes = (half_shape, half_shape)
+    else:
+        grad_shapes = (
             jax.ShapeDtypeStruct((3 * width, width), wide),
             jax.ShapeDtypeStruct((width, width), wide),
         )
-        in_specs = [in_vmem] * 5
-    results = pl.pallas_call(
-        functools.partial(
-            column_kernel,
-            (
-                date_local,
-                row_size,
-                row_local,
-                columns_each,
-                head_count,
-                packed,
-                date_size,
-                direct,
-            ),
-        ),
-        out_shape=out_shape,
-        in_specs=in_specs,
+        mixed_shapes = (jax.ShapeDtypeStruct((column_tokens, width), low),)
+    column_heads, first_grad, second_grad = pl.pallas_call(
+        functools.partial(column_kernel, (*sizes, head_count, packed, date_size)),
+        out_shape=(jax.ShapeDtypeStruct((column_tokens, width), low), *grad_shapes),
+        in_specs=[in_smem] * 2 + [in_vmem] * 4,
         scratch_shapes=[
             pltpu.VMEM((width // 128, column_tokens, 128), wide),
             pltpu.VMEM((column_tokens, width), wide),
             pltpu.VMEM((column_tokens, width), low),
             pltpu.VMEM((column_tokens, 3 * width), low),
-            pltpu.VMEM((column_tokens, width), low),
             pltpu.VMEM((column_tokens, 3 * width), low),
         ],
         compiler_params=params,
         name="column_attention",
-    )(*places, plane, grad_low, heads_grad, column_project, column_output)
-
-    if direct:
-        kept, sent, kept_grad, sent_grad = results
-        arrived_grad = lax.ppermute(sent_grad, "pair", swap)
-        mid_one, row_one = lax.axis_index("mid").reshape(1), row_at.reshape(1)
-        outer_one = lax.axis_index("outer").reshape(1)
-
-        def shaped(*lead):
-            return jax.ShapeDtypeStruct((*lead, *block), low)
-
-        half = outers // 2
-        a_kept, a_sent, b_kept, b_sent = pl.pallas_call(
-            halve_kernel,
-            out_shape=(shaped(2, half), shaped(2, half), shaped(half, 2), shaped(half, 2)),
-            in_specs=[in_smem] * 2 + [in_vmem] * 2,
+    )(row_one, pair_one, plane, grad_low, heads_grad, column_project)
+    after_one = row_one
+    if direct:
+        came = lax.ppermute(second_grad, "pair", swap)
+        pair_sum, after_one = pl.pallas_call(
+            pair_kernel,
+            out_shape=(half_grads, jax.ShapeDtypeStruct((1,), jnp.int32)),
+            in_specs=[in_smem] + [in_vmem] * 2,
+            out_specs=(in_vmem, in_smem),
             compiler_params=params,
-            name="halve_gradients",
-        )(mid_one, row_one, kept_grad, arrived_grad)
-        a_came = lax.ppermute(a_sent, "mid", swap)
-        b_came = lax.ppermute(b_sent, "row", swap)
-        a_kept, a_sent, b_kept, b_sent = pl.pallas_call(
-            halve_again_kernel,
-            out_shape=(shaped(half),) * 4,
-            in_specs=[in_smem] * 2 + [in_vmem] * 4,
-            compiler_params=params,
-            name="halve_gradients_again",
-        )(mid_one, row_one, a_kept, a_came, b_kept, b_came)
-        a_came = lax.ppermute(a_sent, "row", swap)
-        b_came = lax.ppermute(b_sent, "mid", swap)
-        leaving, *blocks = pl.pallas_call(
-            spread_kernel,
-            out_shape=(half_shape, *(shaped(),) * outers),
-            in_specs=[in_smem] + [in_vmem] * 5,
-            scratch_shapes=[pltpu.VMEM((outers, *block), low)],
-            compiler_params=params,
-            name="spread_gradients",
-        )(outer_one, a_kept, a_came, b_kept, b_came, sent)
-        arrived = lax.ppermute(leaving, "row", swap)
-        terms = [blocks[0]]
-        for step in range(1, outers):
-            route = [(at, (at + step) % outers) for at in range(outers)]
-            terms.append(lax.ppermute(blocks[step], "outer", route))
+            name="pair_gradients",
+        )(row_one, first_grad, came)
+    mixed = pl.pallas_call(
+        functools.partial(mixed_kernel, sizes),
+        out_shape=mixed_shapes,
+        in_specs=[in_smem] + [in_vmem] * 3,
+        scratch_shapes=[
+            pltpu.VMEM((width // 128, column_tokens, 128), wide),
+            pltpu.VMEM((column_tokens, width), wide),
+        ],
+        compiler_params=params,
+        name="mixed_tokens",
+    )(after_one, plane, column_heads, column_output)
+
+    if direct:
+        terms = lax.all_to_all(
+            pair_sum.reshape(row_size * date_size // 2, packed_rows, 128),
+            ("row", "outer", "mid"),
+            split_axis=0,
+            concat_axis=0,
+            tiled=True,
+        )
         owned_project, owned_output = pl.pallas_call(
             functools.partial(finish_kernel, project_each),
             out_shape=(
                 jax.ShapeDtypeStruct((project_each, lane_each), wide),
                 jax.ShapeDtypeStruct((output_each, lane_each), wide),
             ),
-            in_specs=[in_smem] + [in_vmem] * outers,
+            in_specs=[in_smem, in_vmem],
             compiler_params=params,
             name="gradient_sum",
-        )(row_one, *terms)
+        )(row_one, terms)
+        kept, sent = mixed
+        arrived = lax.ppermute(sent, "row", swap)
         quarter = (date_local, row_local, 1, columns_each, width)
         kept, arrived = kept.reshape(quarter), arrived.reshape(quarter)
         mixed = jnp.concatenate(
             [jnp.where(row_at == 0, kept, arrived), jnp.where(row_at == 0, arrived, kept)], axis=2
         )
     else:
-        mixed, project_grad, output_grad = results
+        mixed = mixed[0]
         grads = jnp.concatenate(
             [
-                project_grad.reshape(date_size, project_each, row_size, lane_each),
-                output_grad.reshape(date_size, output_each, row_size, lane_each),
+                first_grad.reshape(date_size, project_each, row_size, lane_each),
+                second_grad.reshape(date_size, output_each, row_size, lane_each),
             ],
             axis=1,
         ).astype(low)

time: 74.9 us -> 73.7 us (0.984)
  starting transfers between devices: 21.8 us -> 18.9 us
  Pallas kernels: 13.4 us -> 16.3 us
  local copies, waits for them, and re-layouts: 1.73 us -> 0.74 us
    ppermute x9 -> x2, starting transfers between devices: 9.08 us -> 1.99 us  [the longest x1 1.92 us: body(): arrived = lax.ppermute(sent, 'row', swap)]
    all_to_all x0 -> x1, starting transfers between devices: none -> 3.73 us  [body(): lax.all_to_all(pair_sum.reshape(row_size * date_size // 2, packed_rows, 1...]
    all_to_all x0 -> x1, waiting for transfers between devices: none -> 3.53 us  [body(): lax.all_to_all(pair_sum.reshape(row_size * date_size // 2, packed_rows, 1...]
    pallas_call x1, Pallas kernels: 0.49 us -> 2.45 us  [body(): pl.pallas_call(functools.partial(cotangent_kernel, (date_local, row_size,...]
    ppermute x9 -> x2, waiting for transfers between devices: 13.1 us -> 11.2 us  [the longest x1 9.17 us: body(): arrived = lax.ppermute(sent, 'row', swap)]
    all_to_all x1, waiting for transfers between devices: 4.12 us -> 2.22 us  [body(): lax.all_to_all(outgoing, dates, split_axis=0, concat_axis=0, tiled=True)]
    unnamed x16 -> x18, local copies, waits for them, and re-layouts: 1.7 us -> 0.71 us
    pallas_call x4 -> x3, Pallas kernels: 6.22 us -> 7.13 us  [the longest x1 4.84 us: body(): pl.pallas_call(functools.partial(column_kernel, (*sizes, head_count, pack...]
  transfers between devices with their start and end apart: 12 -> 6, of which waited for: 10 -> 6; matrix products, arithmetic and copies ran while one was open for 0% -> 1% of each run, Pallas kernels for 2% -> 5%
where the time goes in v7:
time: 73.7 us; the launch traced here: 73.3 us
  waiting for transfers between devices  35.7 us (48%)
  starting transfers between devices  18.9 us (26%)
  Pallas kernels  16.3 us (22%)
  other arithmetic  0.83 us (1%)
  between operations  0.79 us (1%)
  local copies, waits for them, and re-layouts  0.74 us (1%)
    all_to_all x1, waiting for transfers between devices, body(): lax.all_to_all(parts, ('row', *dates), split_axis=0, concat_axis=0, tiled...  13.1 us
    ppermute x1, waiting for transfers between devices, body(): arrived = lax.ppermute(sent, 'row', swap)  9.17 us
    all_to_all x1, starting transfers between devices, body(): lax.all_to_all(outgoing, dates, split_axis=0, concat_axis=0, tiled=True)  7.5 us
    ppermute x1, waiting for transfers between devices, body(): other_grad = lax.ppermute(leaving, 'row', swap)  5.72 us
    pallas_call x1, Pallas kernels, body(): pl.pallas_call(functools.partial(column_kernel, (*sizes, head_count, pack...  4.84 us
    pallas_call x1, Pallas kernels, body(): pl.pallas_call(functools.partial(time_kernel, (date_size, date_local, pat...  4.1 us
    all_to_all x1, starting transfers between devices, body(): lax.all_to_all(parts, ('row', *dates), split_axis=0, concat_axis=0, tiled...  4.06 us
    all_to_all x1, starting transfers between devices, body(): lax.all_to_all(pair_sum.reshape(row_size * date_size // 2, packed_rows, 1...  3.73 us
  transfers between devices with their start and end apart: 6, of which 6 were waited for; matrix products, arithmetic and copies ran while one was open for 1% of the time, Pallas kernels for 5%

profile of v7, /device:TPU:0, one launch (start us, length us, event | category | flops | bytes accessed | tf_op | source)
XLA Modules:
  0.0 73.3 jit_solution(4772272327129863812)
XLA Ops:
  0.6 0.0 copy-start.7
  0.6 1.9 %pack_tokens.1 = bf16[16,104,128]{2,1,0:T(8,128)(2,1)} custom-call(s32[2]{0:T(128)} %numbers_ref.1, bf16[2,16,16,384]{3,2,1,0:T(8,128)(2,1)} %tokens_ref.1, s32[2,16,16]{2,1,0:T(8,128)} %flags_ref.1), custom_call_target="tpu_custom_call" | custom-call | tf_op jit(solution)/shard_map/pack_tokens/pallas_call | solution.py:468
  2.5 0.0 copy-start.2
  2.5 7.5 %all-to-all-start = ((bf16[16,104,128]{2,1,0:T(8,128)(2,1)}), bf16[16,104,128]{2,1,0:T(8,128)(2,1)S(1)}, u32[]{:S(2)}, u32[]{:S(2)}) async-start(bf16[16,104,128]{2,1,0:T(8,128)(2,1)} %pack_tokens.1), calls=%async_computation | async-start | bytes 851968 | tf_op jit(solution)/shard_map/all_to_all | solution.py:498
  10.1 0.0 copy-done.7
  10.1 1.6 %collective-permute-start = (bf16[2,16,8,384]{3,2,1,0:T(8,128)(2,1)S(1)}, bf16[2,16,8,384]{3,2,1,0:T(8,128)(2,1)S(1)}, u32[]{:S(2)}, u32[]{:S(2)}) collective-permute-start(bf16[2,16,8,384]{3,2,1,0:T(8,128)(2,1)S(1)} %dynamic-slice_bitcast_fusion), channel_id=1, source_target_pairs={{0,1},{1,0},{2,3},{3,2},{4,5},{5,4},{6,7},{7,6},{8,9},{9,8},{10,11... | collective-permute-start | bytes 589832 | tf_op jit(solution)/shard_map/ppermute | solution.py:483
  11.7 5.7 %collective-permute-done = bf16[2,16,8,384]{3,2,1,0:T(8,128)(2,1)S(1)} collective-permute-done((bf16[2,16,8,384]{3,2,1,0:T(8,128)(2,1)S(1)}, bf16[2,16,8,384]{3,2,1,0:T(8,128)(2,1)S(1)}, u32[]{:S(2)}, u32[]{:S(2)}) %collective-permute-start) | collective-permute-done | bytes 196640 | tf_op jit(solution)/shard_map/ppermute | solution.py:483
  17.4 0.0 copy-start.8
  17.4 0.7 copy-done.8
  18.1 0.0 copy-start.5
  18.1 2.5 %cotangent_heads.1 = (bf16[512,384]{1,0:T(8,128)(2,1)}, bf16[512,384]{1,0:T(8,128)(2,1)}, f32[12]{0:T(128)}) custom-call(s32[1]{0:T(128)} %bitcast.refs_0_.row_ref, bf16[512,384]{1,0:T(8,128)(2,1)} %bitcast.18, bf16[256,384]{1,0:T(8,128)(2,1)} %bitcast.22, bf16[384,384]{1,0:T(8,128)(2,1)} %output_ref.3, f32[12]{0:T(128)} %refs_4_.1), custom_call_target="tpu_custom_call" | custom-call | tf_op jit(solution)/shard_map/cotangent_heads/pallas_call | solution.py:514
  20.5 0.0 copy-start.6
  20.6 2.2 %all-to-all-done.block_ref = bf16[16,104,128]{2,1,0:T(8,128)(2,1)S(1)} async-done(((bf16[16,104,128]{2,1,0:T(8,128)(2,1)}), bf16[16,104,128]{2,1,0:T(8,128)(2,1)S(1)}, u32[]{:S(2)}, u32[]{:S(2)}) %all-to-all-start) | async-done | bytes 426016 | tf_op jit(solution)/shard_map/all_to_all | solution.py:498
  22.8 0.0 copy-done.2
  22.8 0.0 copy-done.5
  22.8 0.0 copy-done.6
  22.8 0.0 copy-start.1
  22.8 4.1 %time_attention.1 = bf16[512,384]{1,0:T(8,128)(2,1)} custom-call(f32[12]{0:T(128)S(1)} %copy-done.6, bf16[16,104,128]{2,1,0:T(8,128)(2,1)S(1)} %all-to-all-done.block_ref, bf16[384,1152]{1,0:T(8,128)(2,1)S(1)} %copy-done.2, bf16[384,384]{1,0:T(8,128)(2,1)S(1)} %copy-done.5), custom_call_target="tpu_custom_call" | custom-call | tf_op jit(solution)/shard_map/time_attention/pallas_call | solution.py:530
  26.9 0.0 copy-start.3
  26.9 0.0 copy-start.4
  26.9 4.1 %all-to-all-start.1 = ((bf16[32,16,384]{2,1,0:T(8,128)(2,1)}), bf16[32,16,384]{2,1,0:T(8,128)(2,1)S(1)}, u32[]{:S(2)}, u32[]{:S(2)}) async-start(bf16[32,16,384]{2,1,0:T(8,128)(2,1)} %bitcast.6), calls=%async_computation.1 | async-start | bytes 786432 | tf_op jit(solution)/shard_map/all_to_all | solution.py:556
  31.0 13.1 %all-to-all-done.1 = bf16[32,16,384]{2,1,0:T(8,128)(2,1)S(1)} async-done(((bf16[32,16,384]{2,1,0:T(8,128)(2,1)}), bf16[32,16,384]{2,1,0:T(8,128)(2,1)S(1)}, u32[]{:S(2)}, u32[]{:S(2)}) %all-to-all-start.1) | async-done | bytes 393248 | tf_op jit(solution)/shard_map/all_to_all | solution.py:556
  44.1 0.0 copy-done.1
  44.1 0.0 copy-done.3
  44.1 0.0 copy-done.4
  44.1 4.8 %column_attention.1 = (bf16[512,384]{1,0:T(8,128)(2,1)S(1)}, bf16[2,8,144,128]{3,2,1,0:T(8,128)(2,1)S(1)}, bf16[2,8,144,128]{3,2,1,0:T(8,128)(2,1)S(1)}) custom-call(s32[1]{0:T(128)} %bitcast.refs_0_.row_ref, s32[1]{0:T(128)} %bitcast.1.pair_ref, bf16[512,384]{1,0:T(8,128)(2,1)S(1)} %bitcast.16, bf16[512,384]{1,0:T(8,128)(2,1)S(1)} %copy-done.3, ...), custom_call_target="tpu_custom_call" | custom-call | tf_op jit(solution)/shard_map/column_attention/pallas_call | solution.py:580
  48.9 0.1 collective-permute-start.1
  49.0 2.0 %collective-permute-done.1.came_ref = bf16[2,8,144,128]{3,2,1,0:T(8,128)(2,1)S(1)} collective-permute-done((bf16[2,8,144,128]{3,2,1,0:T(8,128)(2,1)S(1)}, bf16[2,8,144,128]{3,2,1,0:T(8,128)(2,1)S(1)}, u32[]{:S(2)}, u32[]{:S(2)}) %collective-permute-start.1) | collective-permute-done | bytes 589856 | tf_op jit(solution)/shard_map/ppermute | solution.py:596
  51.0 1.0 %pair_gradients.1 = (bf16[2,8,144,128]{3,2,1,0:T(8,128)(2,1)}, s32[1]{0:T(128)}) custom-call(s32[1]{0:T(128)} %bitcast.refs_0_.row_ref, bf16[2,8,144,128]{3,2,1,0:T(8,128)(2,1)S(1)} %get-tuple-element.18.kept_ref, bf16[2,8,144,128]{3,2,1,0:T(8,128)(2,1)S(1)} %collective-permute-done.1.came_ref), custom_call_target="tpu_custom_call" | custom-call | tf_op jit(solution)/shard_map/pair_gradients/pallas_call | solution.py:597
  52.0 0.0 copy-start
  52.0 3.7 %all-to-all-start.2 = ((bf16[16,144,128]{2,1,0:T(8,128)(2,1)}), bf16[16,144,128]{2,1,0:T(8,128)(2,1)S(1)}, u32[]{:S(2)}, u32[]{:S(2)}) async-start(bf16[16,144,128]{2,1,0:T(8,128)(2,1)} %bitcast.11), calls=%async_computation.2 | async-start | bytes 1179648 | tf_op jit(solution)/shard_map/all_to_all | solution.py:618
  55.7 0.0 copy-done
  55.7 1.3 %mixed_tokens.1 = (bf16[256,384]{1,0:T(8,128)(2,1)S(1)}, bf16[256,384]{1,0:T(8,128)(2,1)S(1)}) custom-call(s32[1]{0:T(128)} %get-tuple-element.20.row_ref, bf16[512,384]{1,0:T(8,128)(2,1)S(1)} %bitcast.17, bf16[512,384]{1,0:T(8,128)(2,1)S(1)} %get-tuple-element.21.heads_ref, bf16[384,384]{1,0:T(8,128)(2,1)S(1)} %copy-done), custom_call_target="tpu_custom_call" | custom-call | tf_op jit(solution)/shard_map/mixed_tokens/pallas_call | solution.py:605
  57.1 1.9 %collective-permute-start.2 = (bf16[256,384]{1,0:T(8,128)(2,1)S(1)}, bf16[256,384]{1,0:T(8,128)(2,1)S(1)}, u32[]{:S(2)}, u32[]{:S(2)}) collective-permute-start(bf16[256,384]{1,0:T(8,128)(2,1)S(1)} %get-tuple-element.23), channel_id=1, source_target_pairs={{0,1},{1,0},{2,3},{3,2},{4,5},{5,4},{6,7},{7,6},{8,9},{9,8},{10,11... | collective-permute-start | bytes 589832 | tf_op jit(solution)/shard_map/ppermute | solution.py:636
  59.0 9.2 %collective-permute-done.2 = bf16[256,384]{1,0:T(8,128)(2,1)S(1)} collective-permute-done((bf16[256,384]{1,0:T(8,128)(2,1)S(1)}, bf16[256,384]{1,0:T(8,128)(2,1)S(1)}, u32[]{:S(2)}, u32[]{:S(2)}) %collective-permute-start.2) | collective-permute-done | bytes 196640 | tf_op jit(solution)/shard_map/ppermute | solution.py:636
  68.2 0.8 %copy_bitcast_fusion = bf16[2,16,16,384]{3,2,1,0:T(8,128)(2,1)} fusion(bf16[2,16,1,8,384]{4,3,1,0,2:T(8,128)(2,1)S(1)} %bitcast.21, bf16[2,16,1,8,384]{4,3,1,0,2:T(8,128)(2,1)S(1)} %bitcast.20), kind=kLoop, calls=%fused_computation.1 | loop fusion | flops 196608 | bytes 786432 | tf_op jit(solution)/shard_map/reshape | solution.py:660
  69.0 3.5 %all-to-all-done.2.terms_ref = bf16[16,144,128]{2,1,0:T(8,128)(2,1)S(1)} async-done(((bf16[16,144,128]{2,1,0:T(8,128)(2,1)}), bf16[16,144,128]{2,1,0:T(8,128)(2,1)S(1)}, u32[]{:S(2)}, u32[]{:S(2)}) %all-to-all-start.2) | async-done | bytes 589856 | tf_op jit(solution)/shard_map/all_to_all | solution.py:618
  72.5 0.8 %gradient_sum.1 = (f32[72,192]{1,0:T(8,128)}, f32[24,192]{1,0:T(8,128)}) custom-call(s32[1]{0:T(128)} %bitcast.refs_0_.row_ref, bf16[16,144,128]{2,1,0:T(8,128)(2,1)S(1)} %all-to-all-done.2.terms_ref), custom_call_target="tpu_custom_call" | custom-call | tf_op jit(solution)/shard_map/gradient_sum/pallas_call | solution.py:625
  (2 shorter events, 0.1 us)
Async XLA Ops:
  0.6 9.4 %copy-start.7 = (bf16[2,16,16,384]{3,2,1,0:T(8,128)(2,1)S(1)}, bf16[2,16,16,384]{3,2,1,0:T(8,128)(2,1)}, u32[]{:S(2)}) copy-start(bf16[2,16,16,384]{3,2,1,0:T(8,128)(2,1)} %param.17) | copy-start | bytes 1179652
  2.5 20.2 %copy-start.2 = (bf16[384,1152]{1,0:T(8,128)(2,1)S(1)}, bf16[384,1152]{1,0:T(8,128)(2,1)}, u32[]{:S(2)}) copy-start(bf16[384,1152]{1,0:T(8,128)(2,1)} %project_ref.2) | copy-start | bytes 2654212
  2.5 20.2 %all-to-all-start = ((bf16[16,104,128]{2,1,0:T(8,128)(2,1)}), bf16[16,104,128]{2,1,0:T(8,128)(2,1)S(1)}, u32[]{:S(2)}, u32[]{:S(2)}) async-start(bf16[16,104,128]{2,1,0:T(8,128)(2,1)} %pack_tokens.1), calls=%async_computation | async-start | bytes 851968 | tf_op jit(solution)/shard_map/all_to_all | solution.py:498
  10.1 7.3 %collective-permute-start = (bf16[2,16,8,384]{3,2,1,0:T(8,128)(2,1)S(1)}, bf16[2,16,8,384]{3,2,1,0:T(8,128)(2,1)S(1)}, u32[]{:S(2)}, u32[]{:S(2)}) collective-permute-start(bf16[2,16,8,384]{3,2,1,0:T(8,128)(2,1)S(1)} %dynamic-slice_bitcast_fusion), channel_id=1, source_target_pairs={{0,1},{1,0},{2,3},{3,2},{4,5},{5,4},{6,7},{7,6},{8,9},{9,8},{10,11... | collective-permute-start | bytes 589832 | tf_op jit(solution)/shard_map/ppermute | solution.py:483
  17.4 0.7 copy-start.8
  18.1 4.7 %copy-start.5 = (bf16[384,384]{1,0:T(8,128)(2,1)S(1)}, bf16[384,384]{1,0:T(8,128)(2,1)}, u32[]{:S(2)}) copy-start(bf16[384,384]{1,0:T(8,128)(2,1)} %output_ref.2) | copy-start | bytes 884740
  20.5 2.2 %copy-start.6 = (f32[12]{0:T(128)S(1)}, f32[12]{0:T(128)}, u32[]{:S(2)}) copy-start(f32[12]{0:T(128)} %get-tuple-element.15.slopes_ref) | copy-start | bytes 148
  22.8 21.3 %copy-start.1 = (bf16[384,1152]{1,0:T(8,128)(2,1)S(1)}, bf16[384,1152]{1,0:T(8,128)(2,1)}, u32[]{:S(2)}) copy-start(bf16[384,1152]{1,0:T(8,128)(2,1)} %project_ref.3) | copy-start | bytes 2654212
  26.9 17.2 %copy-start.3 = (bf16[512,384]{1,0:T(8,128)(2,1)S(1)}, bf16[512,384]{1,0:T(8,128)(2,1)}, u32[]{:S(2)}) copy-start(bf16[512,384]{1,0:T(8,128)(2,1)} %get-tuple-element.16.grad_low_scr) | copy-start | bytes 1179652
  26.9 17.2 %copy-start.4 = (bf16[512,384]{1,0:T(8,128)(2,1)S(1)}, bf16[512,384]{1,0:T(8,128)(2,1)}, u32[]{:S(2)}) copy-start(bf16[512,384]{1,0:T(8,128)(2,1)} %get-tuple-element.17.heads_grad_scr) | copy-start | bytes 1179652
  26.9 17.2 %all-to-all-start.1 = ((bf16[32,16,384]{2,1,0:T(8,128)(2,1)}), bf16[32,16,384]{2,1,0:T(8,128)(2,1)S(1)}, u32[]{:S(2)}, u32[]{:S(2)}) async-start(bf16[32,16,384]{2,1,0:T(8,128)(2,1)} %bitcast.6), calls=%async_computation.1 | async-start | bytes 786432 | tf_op jit(solution)/shard_map/all_to_all | solution.py:556
  48.9 2.1 %collective-permute-start.1 = (bf16[2,8,144,128]{3,2,1,0:T(8,128)(2,1)S(1)}, bf16[2,8,144,128]{3,2,1,0:T(8,128)(2,1)S(1)}, u32[]{:S(2)}, u32[]{:S(2)}) collective-permute-start(bf16[2,8,144,128]{3,2,1,0:T(8,128)(2,1)S(1)} %get-tuple-element.19), channel_id=1, source_target_pairs={{0,2},{2,0},{1,3},{3,1},{4,6},{6,4},{5,7},{7,5},{8,10},{10,8},{9,1... | collective-permute-start | bytes 1769480 | tf_op jit(solution)/shard_map/ppermute | solution.py:596
  52.0 3.7 %copy-start = (bf16[384,384]{1,0:T(8,128)(2,1)S(1)}, bf16[384,384]{1,0:T(8,128)(2,1)}, u32[]{:S(2)}) copy-start(bf16[384,384]{1,0:T(8,128)(2,1)} %output_ref.3) | copy-start | bytes 884740
  52.0 20.5 %all-to-all-start.2 = ((bf16[16,144,128]{2,1,0:T(8,128)(2,1)}), bf16[16,144,128]{2,1,0:T(8,128)(2,1)S(1)}, u32[]{:S(2)}, u32[]{:S(2)}) async-start(bf16[16,144,128]{2,1,0:T(8,128)(2,1)} %bitcast.11), calls=%async_computation.2 | async-start | bytes 1179648 | tf_op jit(solution)/shard_map/all_to_all | solution.py:618
  57.1 11.1 %collective-permute-start.2 = (bf16[256,384]{1,0:T(8,128)(2,1)S(1)}, bf16[256,384]{1,0:T(8,128)(2,1)S(1)}, u32[]{:S(2)}, u32[]{:S(2)}) collective-permute-start(bf16[256,384]{1,0:T(8,128)(2,1)S(1)} %get-tuple-element.23), channel_id=1, source_target_pairs={{0,1},{1,0},{2,3},{3,2},{4,5},{5,4},{6,7},{7,6},{8,9},{9,8},{10,11... | collective-permute-start | bytes 589832 | tf_op jit(solution)/shard_map/ppermute | solution.py:636

commit v8 on v7

--- a/solution.py
+++ b/solution.py
@@ -120,12 +120,15 @@
     block_ref,
     project_ref,
     output_ref,
+    earlier_ref,
     out_ref,
+    after_ref,
     seq_scr,
     token_scr,
     qkv_scr,
     heads_scr,
 ):
+    after_ref[0] = jnp.int32(0)
     sources, dates_each, groups, head_count, packed, columns_each = sizes
     width = project_ref.shape[0]
     tile_lanes = block_ref.shape[2]
@@ -203,9 +206,7 @@
 
 def cotangent_kernel(sizes, *refs):
     dates_each, row_parts, rows_each, columns_each, direct = sizes
-    output_ref, slopes_ref, grad_low_ref, heads_grad_ref, handed_ref, grad_scr = refs[-6:]
-    for head in range(slopes_ref.shape[0]):
-        handed_ref[head] = slopes_ref[head]
+    output_ref, _, grad_low_ref, heads_grad_ref, grad_scr = refs[-5:]
     width = output_ref.shape[0]
     length = row_parts * rows_each
     groups = dates_each * columns_each
@@ -397,15 +398,38 @@
                 send_ref[place] = jnp.where(even, two, one).astype(low)
 
 
-def pair_kernel(row_ref, kept_ref, came_ref, sum_ref, handed_ref):
+def pair_kernel(
+    row_ref, mid_ref, kept_ref, came_ref, own_ref, mid_out, row_out, both_out, handed_ref
+):
     handed_ref[0] = row_ref[0]
-    sum_ref[...] = (kept_ref[...].astype(wide) + came_ref[...].astype(wide)).astype(low)
-
-
-def finish_kernel(project_each, row_ref, terms_ref, project_ref, output_ref):
-    total = terms_ref[0].astype(wide)
-    for source in range(1, terms_ref.shape[0]):
-        total = total + terms_ref[source].astype(wide)
+    row, mid = row_ref[0], mid_ref[0]
+    for outer in range(own_ref.shape[0]):
+        for out_ref, row_at, mid_at in (
+            (mid_out, row, 1 - mid),
+            (row_out, 1 - row, mid),
+            (both_out, 1 - row, 1 - mid),
+            (own_ref, row, mid),
+        ):
+            place = (row_at, 2 * outer + mid_at)
+            out_ref[outer] = (kept_ref[place].astype(wide) + came_ref[place].astype(wide)).astype(
+                low
+            )
+
+
+def spread_kernel(outer_ref, own_ref, mid_ref, row_ref, both_ref, *refs):
+    count = own_ref.shape[0]
+    for step in range(count):
+        at = (outer_ref[0] + step) % count
+        total = own_ref[at].astype(wide) + mid_ref[at].astype(wide)
+        total = total + (row_ref[at].astype(wide) + both_ref[at].astype(wide))
+        refs[step][...] = total.astype(low)
+
+
+def finish_kernel(project_each, row_ref, *refs):
+    *terms, project_ref, output_ref = refs
+    total = terms[0][...].astype(wide)
+    for term in terms[1:]:
+        total = total + term[...].astype(wide)
     whole = 2 * total.shape[0] // 3
     main = total[:whole]
     tail = total[whole:]
@@ -511,23 +535,8 @@
             ),
         )
         in_specs = [in_vmem] * 2 + [in_smem]
-    grad_low, heads_grad, slopes = pl.pallas_call(
-        functools.partial(
-            cotangent_kernel, (date_local, row_size, row_local, columns_each, direct)
-        ),
-        out_shape=(
-            jax.ShapeDtypeStruct((column_tokens, width), low),
-            jax.ShapeDtypeStruct((column_tokens, width), low),
-            jax.ShapeDtypeStruct(decay_slopes.shape, wide),
-        ),
-        in_specs=in_specs,
-        out_specs=(in_vmem, in_vmem, in_smem),
-        scratch_shapes=[pltpu.VMEM((width // 128, column_tokens, 128), wide)],
-        name="cotangent_heads",
-    )(*grads_in, column_output, decay_slopes)
-
     time_tokens = date_count * patches_each
-    hidden = pl.pallas_call(
+    hidden, after_time = pl.pallas_call(
         functools.partial(
             time_kernel,
             (
@@ -539,8 +548,12 @@
                 columns_each if direct else patches_each,
             ),
         ),
-        out_shape=jax.ShapeDtypeStruct((time_tokens, width), low),
-        in_specs=[in_smem, in_vmem, in_vmem, in_vmem],
+        out_shape=(
+            jax.ShapeDtypeStruct((time_tokens, width), low),
+            jax.ShapeDtypeStruct((1,), jnp.int32),
+        ),
+        in_specs=[in_smem, in_vmem, in_vmem, in_vmem, pl.BlockSpec(memory_space=pl.ANY)],
+        out_specs=(in_vmem, in_smem),
         scratch_shapes=[
             pltpu.VMEM((width // 128, time_tokens, 128), wide),
             pltpu.VMEM((time_tokens, width), wide),
@@ -549,7 +562,20 @@
         ],
         compiler_params=params,
         name="time_attention",
-    )(slopes, incoming, time_project, time_output)
+    )(decay_slopes, incoming, time_project, time_output, grads_in[-1])
+
+    grad_low, heads_grad = pl.pallas_call(
+        functools.partial(
+            cotangent_kernel, (date_local, row_size, row_local, columns_each, direct)
+        ),
+        out_shape=(
+            jax.ShapeDtypeStruct((column_tokens, width), low),
+            jax.ShapeDtypeStruct((column_tokens, width), low),
+        ),
+        in_specs=in_specs,
+        scratch_shapes=[pltpu.VMEM((width // 128, column_tokens, 128), wide)],
+        name="cotangent_heads",
+    )(*grads_in, column_output, after_time)
 
     if direct:
         parts = hidden.reshape(row_size * date_size, date_local * columns_each, width)
@@ -594,14 +620,20 @@
     after_one = row_one
     if direct:
         came = lax.ppermute(second_grad, "pair", swap)
-        pair_sum, after_one = pl.pallas_call(
+        outers = date_size // 4
+        block = jax.ShapeDtypeStruct((packed_rows, 128), low)
+        blocks = jax.ShapeDtypeStruct((outers, packed_rows, 128), low)
+        own_grad, mid_grad, row_grad, both_grad, after_one = pl.pallas_call(
             pair_kernel,
-            out_shape=(half_grads, jax.ShapeDtypeStruct((1,), jnp.int32)),
-            in_specs=[in_smem] + [in_vmem] * 2,
-            out_specs=(in_vmem, in_smem),
+            out_shape=(blocks,) * 4 + (jax.ShapeDtypeStruct((1,), jnp.int32),),
+            in_specs=[in_smem] * 2 + [in_vmem] * 2,
+            out_specs=(in_vmem,) * 4 + (in_smem,),
             compiler_params=params,
             name="pair_gradients",
-        )(row_one, first_grad, came)
+        )(row_one, lax.axis_index("mid").reshape(1), first_grad, came)
+        both_grad = lax.ppermute(both_grad, ("mid", "row"), [(0, 3), (3, 0), (1, 2), (2, 1)])
+        mid_grad = lax.ppermute(mid_grad, "mid", swap)
+        row_grad = lax.ppermute(row_grad, "row", swap)
     mixed = pl.pallas_call(
         functools.partial(mixed_kernel, sizes),
         out_shape=mixed_shapes,
@@ -615,23 +647,27 @@
     )(after_one, plane, column_heads, column_output)
 
     if direct:
-        terms = lax.all_to_all(
-            pair_sum.reshape(row_size * date_size // 2, packed_rows, 128),
-            ("row", "outer", "mid"),
-            split_axis=0,
-            concat_axis=0,
-            tiled=True,
-        )
+        steps = pl.pallas_call(
+            spread_kernel,
+            out_shape=(block,) * outers,
+            in_specs=[in_smem] + [in_vmem] * 4,
+            compiler_params=params,
+            name="spread_gradients",
+        )(lax.axis_index("outer").reshape(1), own_grad, mid_grad, row_grad, both_grad)
+        terms = [steps[0]]
+        for step in range(1, outers):
+            route = [(at, (at + step) % outers) for at in range(outers)]
+            terms.append(lax.ppermute(steps[step], "outer", route))
         owned_project, owned_output = pl.pallas_call(
             functools.partial(finish_kernel, project_each),
             out_shape=(
                 jax.ShapeDtypeStruct((project_each, lane_each), wide),
                 jax.ShapeDtypeStruct((output_each, lane_each), wide),
             ),
-            in_specs=[in_smem, in_vmem],
+            in_specs=[in_smem] + [in_vmem] * outers,
             compiler_params=params,
             name="gradient_sum",
-        )(row_one, terms)
+        )(row_one, *terms)
         kept, sent = mixed
         arrived = lax.ppermute(sent, "row", swap)
         quarter = (date_local, row_local, 1, columns_each, width)

time: 73.7 us -> 77.2 us (1.047)
  starting transfers between devices: 18.9 us -> 21.2 us
  local copies, waits for them, and re-layouts: 0.74 us -> 2.44 us
  waiting for transfers between devices: 35.7 us -> 34.8 us
    ppermute x0 -> x6, waiting for transfers between devices: none -> 11.7 us  [the longest x1 5.51 us: body(): row_grad = lax.ppermute(row_grad, 'row', swap)]
    ppermute x1, waiting for transfers between devices: 9.17 us -> 0.01 us  [body(): arrived = lax.ppermute(sent, 'row', swap)]
    ppermute x0 -> x6, starting transfers between devices: none -> 7.37 us  [the longest x3 3.88 us: body(): terms.append(lax.ppermute(steps[step], 'outer', route))]
    all_to_all x1 -> x0, starting transfers between devices: 3.73 us -> none  [body(): lax.all_to_all(pair_sum.reshape(row_size * date_size // 2, packed_rows, 1...]
    all_to_all x1 -> x0, waiting for transfers between devices: 3.53 us -> none  [body(): lax.all_to_all(pair_sum.reshape(row_size * date_size // 2, packed_rows, 1...]
    all_to_all x1, waiting for transfers between devices: 2.22 us -> 5.34 us  [body(): lax.all_to_all(outgoing, dates, split_axis=0, concat_axis=0, tiled=True)]
    all_to_all x1, waiting for transfers between devices: 13.1 us -> 10 us  [body(): lax.all_to_all(parts, ('row', *dates), split_axis=0, concat_axis=0, tiled...]
    unnamed x18, local copies, waits for them, and re-layouts: 0.71 us -> 2.41 us
  transfers between devices with their start and end apart: 6 -> 11, of which waited for: 6 -> 8; matrix products, arithmetic and copies ran while one was open for 1% -> 0% of each run, Pallas kernels for 5% -> 5%
where the time goes in v8:
time: 77.2 us; the launch traced here: 76.7 us
  waiting for transfers between devices  34.8 us (45%)
  starting transfers between devices  21.2 us (27%)
  Pallas kernels  16.6 us (22%)
  local copies, waits for them, and re-layouts  2.44 us (3%)
  other arithmetic  0.83 us (1%)
  between operations  0.79 us (1%)
    all_to_all x1, waiting for transfers between devices, body(): lax.all_to_all(parts, ('row', *dates), split_axis=0, concat_axis=0, tiled...  10 us
    all_to_all x1, starting transfers between devices, body(): lax.all_to_all(outgoing, dates, split_axis=0, concat_axis=0, tiled=True)  7.5 us
    ppermute x1, waiting for transfers between devices, body(): other_grad = lax.ppermute(leaving, 'row', swap)  5.72 us
    ppermute x1, waiting for transfers between devices, body(): row_grad = lax.ppermute(row_grad, 'row', swap)  5.51 us
    all_to_all x1, waiting for transfers between devices, body(): lax.all_to_all(outgoing, dates, split_axis=0, concat_axis=0, tiled=True)  5.34 us
    pallas_call x1, Pallas kernels, body(): pl.pallas_call(functools.partial(column_kernel, (*sizes, head_count, pack...  4.82 us
    pallas_call x1, Pallas kernels, body(): pl.pallas_call(functools.partial(time_kernel, (date_size, date_local, pat...  4.1 us
    ppermute x3, starting transfers between devices, body(): terms.append(lax.ppermute(steps[step], 'outer', route))  3.88 us
  transfers between devices with their start and end apart: 11, of which 8 were waited for; matrix products, arithmetic and copies ran while one was open for 0% of the time, Pallas kernels for 5%

profile of v8, /device:TPU:0, one launch (start us, length us, event | category | flops | bytes accessed | tf_op | source)
XLA Modules:
  0.0 76.7 jit_solution(17240872668338653259)
XLA Ops:
  0.6 0.0 copy-start.2
  0.6 1.9 %pack_tokens.1 = bf16[16,104,128]{2,1,0:T(8,128)(2,1)} custom-call(s32[2]{0:T(128)} %numbers_ref.1, bf16[2,16,16,384]{3,2,1,0:T(8,128)(2,1)} %tokens_ref.1, s32[2,16,16]{2,1,0:T(8,128)} %flags_ref.1), custom_call_target="tpu_custom_call" | custom-call | tf_op jit(solution)/shard_map/pack_tokens/pallas_call | solution.py:492
  2.6 0.0 copy-start.8
  2.6 7.5 %all-to-all-start = ((bf16[16,104,128]{2,1,0:T(8,128)(2,1)}), bf16[16,104,128]{2,1,0:T(8,128)(2,1)S(1)}, u32[]{:S(2)}, u32[]{:S(2)}) async-start(bf16[16,104,128]{2,1,0:T(8,128)(2,1)} %pack_tokens.1), calls=%async_computation | async-start | bytes 851968 | tf_op jit(solution)/shard_map/all_to_all | solution.py:522
  10.1 0.0 copy-start.6
  10.1 0.0 copy-done.8
  10.2 0.0 copy-start.7
  10.2 1.6 %collective-permute-start = (bf16[2,16,8,384]{3,2,1,0:T(8,128)(2,1)S(1)}, bf16[2,16,8,384]{3,2,1,0:T(8,128)(2,1)S(1)}, u32[]{:S(2)}, u32[]{:S(2)}) collective-permute-start(bf16[2,16,8,384]{3,2,1,0:T(8,128)(2,1)S(1)} %dynamic-slice_bitcast_fusion), channel_id=1, source_target_pairs={{0,1},{1,0},{2,3},{3,2},{4,5},{5,4},{6,7},{7,6},{8,9},{9,8},{10,11... | collective-permute-start | bytes 589832 | tf_op jit(solution)/shard_map/ppermute | solution.py:507
  11.8 5.7 %collective-permute-done = bf16[2,16,8,384]{3,2,1,0:T(8,128)(2,1)S(1)} collective-permute-done((bf16[2,16,8,384]{3,2,1,0:T(8,128)(2,1)S(1)}, bf16[2,16,8,384]{3,2,1,0:T(8,128)(2,1)S(1)}, u32[]{:S(2)}, u32[]{:S(2)}) %collective-permute-start) | collective-permute-done | bytes 196640 | tf_op jit(solution)/shard_map/ppermute | solution.py:507
  17.5 0.0 copy-start.3
  17.5 5.3 %all-to-all-done.block_ref = bf16[16,104,128]{2,1,0:T(8,128)(2,1)S(1)} async-done(((bf16[16,104,128]{2,1,0:T(8,128)(2,1)}), bf16[16,104,128]{2,1,0:T(8,128)(2,1)S(1)}, u32[]{:S(2)}, u32[]{:S(2)}) %all-to-all-start) | async-done | bytes 426016 | tf_op jit(solution)/shard_map/all_to_all | solution.py:522
  22.8 0.0 copy-done.2
  22.8 0.0 copy-done.6
  22.8 0.0 copy-done.7
  22.8 4.1 %time_attention.1 = (bf16[512,384]{1,0:T(8,128)(2,1)}, s32[1]{0:T(128)}) custom-call(f32[12]{0:T(128)S(1)} %copy-done.7, bf16[16,104,128]{2,1,0:T(8,128)(2,1)S(1)} %all-to-all-done.block_ref, bf16[384,1152]{1,0:T(8,128)(2,1)S(1)} %copy-done.2, bf16[384,384]{1,0:T(8,128)(2,1)S(1)} %copy-done.6, bf16[256,384]{1,0:T(8,128)(2,1)S(1)} %bitcast.19), custom_call_target="tpu_custom_call" | custom-call | tf_op jit(solution)/shard_map/time_attention/pallas_call | solution.py:539
  26.9 0.0 copy-done.3
  27.0 0.0 copy-start.1
  27.0 3.6 %all-to-all-start.1 = ((bf16[32,16,384]{2,1,0:T(8,128)(2,1)}), bf16[32,16,384]{2,1,0:T(8,128)(2,1)S(1)}, u32[]{:S(2)}, u32[]{:S(2)}) async-start(bf16[32,16,384]{2,1,0:T(8,128)(2,1)} %bitcast.6), calls=%async_computation.1 | async-start | bytes 786432 | tf_op jit(solution)/shard_map/all_to_all | solution.py:582
  30.6 3.1 %cotangent_heads.1 = (bf16[512,384]{1,0:T(8,128)(2,1)}, bf16[512,384]{1,0:T(8,128)(2,1)}) custom-call(s32[1]{0:T(128)} %bitcast.refs_0_.row_ref, bf16[512,384]{1,0:T(8,128)(2,1)} %bitcast.21, bf16[256,384]{1,0:T(8,128)(2,1)} %bitcast.20, bf16[384,384]{1,0:T(8,128)(2,1)} %output_ref.3, s32[1]{0:T(128)} %get-tuple-element.24.refs_4_), custom_call_target="tpu_custom_call" | custom-call | tf_op jit(solution)/shard_map/cotangent_heads/pallas_call | solution.py:567
  33.7 10.0 %all-to-all-done.1 = bf16[32,16,384]{2,1,0:T(8,128)(2,1)S(1)} async-done(((bf16[32,16,384]{2,1,0:T(8,128)(2,1)}), bf16[32,16,384]{2,1,0:T(8,128)(2,1)S(1)}, u32[]{:S(2)}, u32[]{:S(2)}) %all-to-all-start.1) | async-done | bytes 393248 | tf_op jit(solution)/shard_map/all_to_all | solution.py:582
  43.7 0.0 copy-done.1
  43.7 0.0 copy-start.4
  43.7 1.0 %copy-done.4 = bf16[512,384]{1,0:T(8,128)(2,1)S(1)} copy-done((bf16[512,384]{1,0:T(8,128)(2,1)S(1)}, bf16[512,384]{1,0:T(8,128)(2,1)}, u32[]{:S(2)}) %copy-start.4) | copy-done | bytes 393240
  44.7 0.0 copy-start.5
  44.7 1.0 %copy-done.5 = bf16[512,384]{1,0:T(8,128)(2,1)S(1)} copy-done((bf16[512,384]{1,0:T(8,128)(2,1)S(1)}, bf16[512,384]{1,0:T(8,128)(2,1)}, u32[]{:S(2)}) %copy-start.5) | copy-done | bytes 393240
  45.7 4.8 %column_attention.1 = (bf16[512,384]{1,0:T(8,128)(2,1)S(1)}, bf16[2,8,144,128]{3,2,1,0:T(8,128)(2,1)S(1)}, bf16[2,8,144,128]{3,2,1,0:T(8,128)(2,1)S(1)}) custom-call(s32[1]{0:T(128)} %bitcast.refs_0_.row_ref, s32[1]{0:T(128)} %bitcast.2.pair_ref, bf16[512,384]{1,0:T(8,128)(2,1)S(1)} %bitcast.17, bf16[512,384]{1,0:T(8,128)(2,1)S(1)} %copy-done.4, ...), custom_call_target="tpu_custom_call" | custom-call | tf_op jit(solution)/shard_map/column_attention/pallas_call | solution.py:606
  50.5 0.1 collective-permute-start.1
  50.6 2.0 %collective-permute-done.1.came_ref = bf16[2,8,144,128]{3,2,1,0:T(8,128)(2,1)S(1)} collective-permute-done((bf16[2,8,144,128]{3,2,1,0:T(8,128)(2,1)S(1)}, bf16[2,8,144,128]{3,2,1,0:T(8,128)(2,1)S(1)}, u32[]{:S(2)}, u32[]{:S(2)}) %collective-permute-start.1) | collective-permute-done | bytes 589856 | tf_op jit(solution)/shard_map/ppermute | solution.py:622
  52.6 0.0 copy-start
  52.6 0.6 pair_gradients.1
  53.2 0.4 copy-done
  53.6 1.3 %mixed_tokens.1 = (bf16[256,384]{1,0:T(8,128)(2,1)S(1)}, bf16[256,384]{1,0:T(8,128)(2,1)S(1)}) custom-call(s32[1]{0:T(128)} %get-tuple-element.29.row_ref, bf16[512,384]{1,0:T(8,128)(2,1)S(1)} %bitcast.18, bf16[512,384]{1,0:T(8,128)(2,1)S(1)} %get-tuple-element.30.heads_ref, bf16[384,384]{1,0:T(8,128)(2,1)S(1)} %copy-done), custom_call_target="tpu_custom_call" | custom-call | tf_op jit(solution)/shard_map/mixed_tokens/pallas_call | solution.py:637
  54.9 1.1 %collective-permute-start.2 = (bf16[256,384]{1,0:T(8,128)(2,1)S(1)}, bf16[256,384]{1,0:T(8,128)(2,1)S(1)}, u32[]{:S(2)}, u32[]{:S(2)}) collective-permute-start(bf16[256,384]{1,0:T(8,128)(2,1)S(1)} %get-tuple-element.32), channel_id=1, source_target_pairs={{0,1},{1,0},{2,3},{3,2},{4,5},{5,4},{6,7},{7,6},{8,9},{9,8},{10,11... | collective-permute-start | bytes 589832 | tf_op jit(solution)/shard_map/ppermute | solution.py:672
  56.0 1.0 %collective-permute-start.3 = (bf16[4,144,128]{2,1,0:T(8,128)(2,1)S(1)}, bf16[4,144,128]{2,1,0:T(8,128)(2,1)S(1)}, u32[]{:S(2)}, u32[]{:S(2)}) collective-permute-start(bf16[4,144,128]{2,1,0:T(8,128)(2,1)S(1)} %get-tuple-element.34), channel_id=1, source_target_pairs={{0,4},{4,0},{1,5},{5,1},{2,6},{6,2},{3,7},{7,3},{8,12},{12,8},{9,1... | collective-permute-start | bytes 442376 | tf_op jit(solution)/shard_map/ppermute | solution.py:635
  57.0 1.5 %collective-permute-start.4 = (bf16[4,144,128]{2,1,0:T(8,128)(2,1)S(1)}, bf16[4,144,128]{2,1,0:T(8,128)(2,1)S(1)}, u32[]{:S(2)}, u32[]{:S(2)}) collective-permute-start(bf16[4,144,128]{2,1,0:T(8,128)(2,1)S(1)} %get-tuple-element.35), channel_id=1, source_target_pairs={{0,1},{1,0},{2,3},{3,2},{4,5},{5,4},{6,7},{7,6},{8,9},{9,8},{10,11... | collective-permute-start | bytes 442376 | tf_op jit(solution)/shard_map/ppermute | solution.py:636
  58.5 1.0 %collective-permute-start.5 = (bf16[4,144,128]{2,1,0:T(8,128)(2,1)S(1)}, bf16[4,144,128]{2,1,0:T(8,128)(2,1)S(1)}, u32[]{:S(2)}, u32[]{:S(2)}) collective-permute-start(bf16[4,144,128]{2,1,0:T(8,128)(2,1)S(1)} %get-tuple-element.36), channel_id=1, source_target_pairs={{0,5},{5,0},{1,4},{4,1},{2,7},{7,2},{3,6},{6,3},{8,13},{13,8},{9,1... | collective-permute-start | bytes 442376 | tf_op jit(solution)/shard_map/ppermute | solution.py:634
  59.5 3.2 %collective-permute-done.3.mid_ref = bf16[4,144,128]{2,1,0:T(8,128)(2,1)S(1)} collective-permute-done((bf16[4,144,128]{2,1,0:T(8,128)(2,1)S(1)}, bf16[4,144,128]{2,1,0:T(8,128)(2,1)S(1)}, u32[]{:S(2)}, u32[]{:S(2)}) %collective-permute-start.3) | collective-permute-done | bytes 147488 | tf_op jit(solution)/shard_map/ppermute | solution.py:635
  62.7 5.5 %collective-permute-done.4.row_ref = bf16[4,144,128]{2,1,0:T(8,128)(2,1)S(1)} collective-permute-done((bf16[4,144,128]{2,1,0:T(8,128)(2,1)S(1)}, bf16[4,144,128]{2,1,0:T(8,128)(2,1)S(1)}, u32[]{:S(2)}, u32[]{:S(2)}) %collective-permute-start.4) | collective-permute-done | bytes 147488 | tf_op jit(solution)/shard_map/ppermute | solution.py:636
  68.2 0.0 collective-permute-done.5.both_ref
  68.2 0.1 spread_gradients.1
  68.3 1.0 %collective-permute-start.6 = (bf16[144,128]{1,0:T(8,128)(2,1)S(1)}, bf16[144,128]{1,0:T(8,128)(2,1)S(1)}, u32[]{:S(2)}, u32[]{:S(2)}) collective-permute-start(bf16[144,128]{1,0:T(8,128)(2,1)S(1)} %get-tuple-element.38), channel_id=1, source_target_pairs={{0,8},{8,16},{16,24},{24,0},{1,9},{9,17},{17,25},{25,1},{2,10},{10... | collective-permute-start | bytes 110600 | tf_op jit(solution)/shard_map/ppermute | solution.py:660
  69.3 1.6 %collective-permute-start.7 = (bf16[144,128]{1,0:T(8,128)(2,1)S(1)}, bf16[144,128]{1,0:T(8,128)(2,1)S(1)}, u32[]{:S(2)}, u32[]{:S(2)}) collective-permute-start(bf16[144,128]{1,0:T(8,128)(2,1)S(1)} %get-tuple-element.39), channel_id=1, source_target_pairs={{0,16},{8,24},{16,0},{24,8},{1,17},{9,25},{17,1},{25,9},{2,18},{10... | collective-permute-start | bytes 110600 | tf_op jit(solution)/shard_map/ppermute | solution.py:660
  70.9 1.3 %collective-permute-start.8 = (bf16[144,128]{1,0:T(8,128)(2,1)S(1)}, bf16[144,128]{1,0:T(8,128)(2,1)S(1)}, u32[]{:S(2)}, u32[]{:S(2)}) collective-permute-start(bf16[144,128]{1,0:T(8,128)(2,1)S(1)} %get-tuple-element.40), channel_id=1, source_target_pairs={{0,24},{8,0},{16,8},{24,16},{1,25},{9,1},{17,9},{25,17},{2,26},{10... | collective-permute-start | bytes 110600 | tf_op jit(solution)/shard_map/ppermute | solution.py:660
  72.2 2.0 %collective-permute-done.6.refs_1_ = bf16[144,128]{1,0:T(8,128)(2,1)S(1)} collective-permute-done((bf16[144,128]{1,0:T(8,128)(2,1)S(1)}, bf16[144,128]{1,0:T(8,128)(2,1)S(1)}, u32[]{:S(2)}, u32[]{:S(2)}) %collective-permute-start.6) | collective-permute-done | bytes 36896 | tf_op jit(solution)/shard_map/ppermute | solution.py:660
  74.2 0.9 %collective-permute-done.7.refs_2_ = bf16[144,128]{1,0:T(8,128)(2,1)S(1)} collective-permute-done((bf16[144,128]{1,0:T(8,128)(2,1)S(1)}, bf16[144,128]{1,0:T(8,128)(2,1)S(1)}, u32[]{:S(2)}, u32[]{:S(2)}) %collective-permute-start.7) | collective-permute-done | bytes 36896 | tf_op jit(solution)/shard_map/ppermute | solution.py:660
  75.2 0.0 collective-permute-done.8.refs_3_
  75.2 0.7 gradient_sum.1
  75.9 0.0 collective-permute-done.2
  76.0 0.8 %copy_bitcast_fusion = bf16[2,16,16,384]{3,2,1,0:T(8,128)(2,1)} fusion(bf16[2,16,1,8,384]{4,3,1,0,2:T(8,128)(2,1)S(1)} %bitcast.24, bf16[2,16,1,8,384]{4,3,1,0,2:T(8,128)(2,1)S(1)} %bitcast.23), kind=kLoop, calls=%fused_computation.1 | loop fusion | flops 196608 | bytes 786432 | tf_op jit(solution)/shard_map/reshape | solution.py:696
  (2 shorter events, 0.1 us)
Async XLA Ops:
  0.6 22.2 %copy-start.2 = (bf16[384,1152]{1,0:T(8,128)(2,1)S(1)}, bf16[384,1152]{1,0:T(8,128)(2,1)}, u32[]{:S(2)}) copy-start(bf16[384,1152]{1,0:T(8,128)(2,1)} %project_ref.2) | copy-start | bytes 2654212
  2.6 7.5 %copy-start.8 = (bf16[2,16,16,384]{3,2,1,0:T(8,128)(2,1)S(1)}, bf16[2,16,16,384]{3,2,1,0:T(8,128)(2,1)}, u32[]{:S(2)}) copy-start(bf16[2,16,16,384]{3,2,1,0:T(8,128)(2,1)} %param.17) | copy-start | bytes 1179652
  2.6 20.2 %all-to-all-start = ((bf16[16,104,128]{2,1,0:T(8,128)(2,1)}), bf16[16,104,128]{2,1,0:T(8,128)(2,1)S(1)}, u32[]{:S(2)}, u32[]{:S(2)}) async-start(bf16[16,104,128]{2,1,0:T(8,128)(2,1)} %pack_tokens.1), calls=%async_computation | async-start | bytes 851968 | tf_op jit(solution)/shard_map/all_to_all | solution.py:522
  10.1 12.7 %copy-start.6 = (bf16[384,384]{1,0:T(8,128)(2,1)S(1)}, bf16[384,384]{1,0:T(8,128)(2,1)}, u32[]{:S(2)}) copy-start(bf16[384,384]{1,0:T(8,128)(2,1)} %output_ref.2) | copy-start | bytes 884740
  10.2 12.7 %copy-start.7 = (f32[12]{0:T(128)S(1)}, f32[12]{0:T(128)}, u32[]{:S(2)}) copy-start(f32[12]{0:T(128)} %slopes_ref.1) | copy-start | bytes 148
  10.2 7.3 %collective-permute-start = (bf16[2,16,8,384]{3,2,1,0:T(8,128)(2,1)S(1)}, bf16[2,16,8,384]{3,2,1,0:T(8,128)(2,1)S(1)}, u32[]{:S(2)}, u32[]{:S(2)}) collective-permute-start(bf16[2,16,8,384]{3,2,1,0:T(8,128)(2,1)S(1)} %dynamic-slice_bitcast_fusion), channel_id=1, source_target_pairs={{0,1},{1,0},{2,3},{3,2},{4,5},{5,4},{6,7},{7,6},{8,9},{9,8},{10,11... | collective-permute-start | bytes 589832 | tf_op jit(solution)/shard_map/ppermute | solution.py:507
  17.5 9.5 %copy-start.3 = (bf16[2,16,8,384]{3,2,1,0:T(8,128)(2,1)}, bf16[2,16,8,384]{3,2,1,0:T(8,128)(2,1)S(1)}, u32[]{:S(2)}) copy-start(bf16[2,16,8,384]{3,2,1,0:T(8,128)(2,1)S(1)} %collective-permute-done) | copy-start | bytes 589828
  27.0 16.8 %copy-start.1 = (bf16[384,1152]{1,0:T(8,128)(2,1)S(1)}, bf16[384,1152]{1,0:T(8,128)(2,1)}, u32[]{:S(2)}) copy-start(bf16[384,1152]{1,0:T(8,128)(2,1)} %project_ref.3) | copy-start | bytes 2654212
  27.0 16.8 %all-to-all-start.1 = ((bf16[32,16,384]{2,1,0:T(8,128)(2,1)}), bf16[32,16,384]{2,1,0:T(8,128)(2,1)S(1)}, u32[]{:S(2)}, u32[]{:S(2)}) async-start(bf16[32,16,384]{2,1,0:T(8,128)(2,1)} %bitcast.6), calls=%async_computation.1 | async-start | bytes 786432 | tf_op jit(solution)/shard_map/all_to_all | solution.py:582
  43.7 1.0 %copy-start.4 = (bf16[512,384]{1,0:T(8,128)(2,1)S(1)}, bf16[512,384]{1,0:T(8,128)(2,1)}, u32[]{:S(2)}) copy-start(bf16[512,384]{1,0:T(8,128)(2,1)} %get-tuple-element.25.grad_low_scr) | copy-start | bytes 1179652
  44.7 1.0 %copy-start.5 = (bf16[512,384]{1,0:T(8,128)(2,1)S(1)}, bf16[512,384]{1,0:T(8,128)(2,1)}, u32[]{:S(2)}) copy-start(bf16[512,384]{1,0:T(8,128)(2,1)} %get-tuple-element.26.heads_grad_scr) | copy-start | bytes 1179652
  50.5 2.1 %collective-permute-start.1 = (bf16[2,8,144,128]{3,2,1,0:T(8,128)(2,1)S(1)}, bf16[2,8,144,128]{3,2,1,0:T(8,128)(2,1)S(1)}, u32[]{:S(2)}, u32[]{:S(2)}) collective-permute-start(bf16[2,8,144,128]{3,2,1,0:T(8,128)(2,1)S(1)} %get-tuple-element.28), channel_id=1, source_target_pairs={{0,2},{2,0},{1,3},{3,1},{4,6},{6,4},{5,7},{7,5},{8,10},{10,8},{9,1... | collective-permute-start | bytes 1769480 | tf_op jit(solution)/shard_map/ppermute | solution.py:622
  52.6 1.0 %copy-start = (bf16[384,384]{1,0:T(8,128)(2,1)S(1)}, bf16[384,384]{1,0:T(8,128)(2,1)}, u32[]{:S(2)}) copy-start(bf16[384,384]{1,0:T(8,128)(2,1)} %output_ref.3) | copy-start | bytes 884740
  54.9 21.0 %collective-permute-start.2 = (bf16[256,384]{1,0:T(8,128)(2,1)S(1)}, bf16[256,384]{1,0:T(8,128)(2,1)S(1)}, u32[]{:S(2)}, u32[]{:S(2)}) collective-permute-start(bf16[256,384]{1,0:T(8,128)(2,1)S(1)} %get-tuple-element.32), channel_id=1, source_target_pairs={{0,1},{1,0},{2,3},{3,2},{4,5},{5,4},{6,7},{7,6},{8,9},{9,8},{10,11... | collective-permute-start | bytes 589832 | tf_op jit(solution)/shard_map/ppermute | solution.py:672
  56.0 6.7 %collective-permute-start.3 = (bf16[4,144,128]{2,1,0:T(8,128)(2,1)S(1)}, bf16[4,144,128]{2,1,0:T(8,128)(2,1)S(1)}, u32[]{:S(2)}, u32[]{:S(2)}) collective-permute-start(bf16[4,144,128]{2,1,0:T(8,128)(2,1)S(1)} %get-tuple-element.34), channel_id=1, source_target_pairs={{0,4},{4,0},{1,5},{5,1},{2,6},{6,2},{3,7},{7,3},{8,12},{12,8},{9,1... | collective-permute-start | bytes 442376 | tf_op jit(solution)/shard_map/ppermute | solution.py:635
  57.0 11.2 %collective-permute-start.4 = (bf16[4,144,128]{2,1,0:T(8,128)(2,1)S(1)}, bf16[4,144,128]{2,1,0:T(8,128)(2,1)S(1)}, u32[]{:S(2)}, u32[]{:S(2)}) collective-permute-start(bf16[4,144,128]{2,1,0:T(8,128)(2,1)S(1)} %get-tuple-element.35), channel_id=1, source_target_pairs={{0,1},{1,0},{2,3},{3,2},{4,5},{5,4},{6,7},{7,6},{8,9},{9,8},{10,11... | collective-permute-start | bytes 442376 | tf_op jit(solution)/shard_map/ppermute | solution.py:636
  58.5 9.8 %collective-permute-start.5 = (bf16[4,144,128]{2,1,0:T(8,128)(2,1)S(1)}, bf16[4,144,128]{2,1,0:T(8,128)(2,1)S(1)}, u32[]{:S(2)}, u32[]{:S(2)}) collective-permute-start(bf16[4,144,128]{2,1,0:T(8,128)(2,1)S(1)} %get-tuple-element.36), channel_id=1, source_target_pairs={{0,5},{5,0},{1,4},{4,1},{2,7},{7,2},{3,6},{6,3},{8,13},{13,8},{9,1... | collective-permute-start | bytes 442376 | tf_op jit(solution)/shard_map/ppermute | solution.py:634
  68.3 5.9 %collective-permute-start.6 = (bf16[144,128]{1,0:T(8,128)(2,1)S(1)}, bf16[144,128]{1,0:T(8,128)(2,1)S(1)}, u32[]{:S(2)}, u32[]{:S(2)}) collective-permute-start(bf16[144,128]{1,0:T(8,128)(2,1)S(1)} %get-tuple-element.38), channel_id=1, source_target_pairs={{0,8},{8,16},{16,24},{24,0},{1,9},{9,17},{17,25},{25,1},{2,10},{10... | collective-permute-start | bytes 110600 | tf_op jit(solution)/shard_map/ppermute | solution.py:660
  69.3 5.9 %collective-permute-start.7 = (bf16[144,128]{1,0:T(8,128)(2,1)S(1)}, bf16[144,128]{1,0:T(8,128)(2,1)S(1)}, u32[]{:S(2)}, u32[]{:S(2)}) collective-permute-start(bf16[144,128]{1,0:T(8,128)(2,1)S(1)} %get-tuple-element.39), channel_id=1, source_target_pairs={{0,16},{8,24},{16,0},{24,8},{1,17},{9,25},{17,1},{25,9},{2,18},{10... | collective-permute-start | bytes 110600 | tf_op jit(solution)/shard_map/ppermute | solution.py:660
  70.9 4.3 %collective-permute-start.8 = (bf16[144,128]{1,0:T(8,128)(2,1)S(1)}, bf16[144,128]{1,0:T(8,128)(2,1)S(1)}, u32[]{:S(2)}, u32[]{:S(2)}) collective-permute-start(bf16[144,128]{1,0:T(8,128)(2,1)S(1)} %get-tuple-element.40), channel_id=1, source_target_pairs={{0,24},{8,0},{16,8},{24,16},{1,25},{9,1},{17,9},{25,17},{2,26},{10... | collective-permute-start | bytes 110600 | tf_op jit(solution)/shard_map/ppermute | solution.py:660

commit v9 on v8

--- a/solution.py
+++ b/solution.py
@@ -416,7 +416,8 @@
             )
 
 
-def spread_kernel(outer_ref, own_ref, mid_ref, row_ref, both_ref, *refs):
+def spread_kernel(outer_ref, own_ref, mid_ref, row_ref, both_ref, sent_ref, leave_ref, *refs):
+    leave_ref[...] = sent_ref[...]
     count = own_ref.shape[0]
     for step in range(count):
         at = (outer_ref[0] + step) % count
@@ -574,6 +575,7 @@
         ),
         in_specs=in_specs,
         scratch_shapes=[pltpu.VMEM((width // 128, column_tokens, 128), wide)],
+        compiler_params=params,
         name="cotangent_heads",
     )(*grads_in, column_output, after_time)
 
@@ -647,13 +649,14 @@
     )(after_one, plane, column_heads, column_output)
 
     if direct:
-        steps = pl.pallas_call(
+        kept, sent = mixed
+        leaving, *steps = pl.pallas_call(
             spread_kernel,
-            out_shape=(block,) * outers,
-            in_specs=[in_smem] + [in_vmem] * 4,
+            out_shape=(half_shape,) + (block,) * outers,
+            in_specs=[in_smem] + [in_vmem] * 5,
             compiler_params=params,
             name="spread_gradients",
-        )(lax.axis_index("outer").reshape(1), own_grad, mid_grad, row_grad, both_grad)
+        )(lax.axis_index("outer").reshape(1), own_grad, mid_grad, row_grad, both_grad, sent)
         terms = [steps[0]]
         for step in range(1, outers):
             route = [(at, (at + step) % outers) for at in range(outers)]
@@ -668,8 +671,7 @@
             compiler_params=params,
             name="gradient_sum",
         )(row_one, *terms)
-        kept, sent = mixed
-        arrived = lax.ppermute(sent, "row", swap)
+        arrived = lax.ppermute(leaving, "row", swap)
         quarter = (date_local, row_local, 1, columns_each, width)
         kept, arrived = kept.reshape(quarter), arrived.reshape(quarter)
         mixed = jnp.concatenate(

time: 77.2 us -> 71.5 us (0.926)
  local copies, waits for them, and re-layouts: 2.44 us -> 0.06 us
  waiting for transfers between devices: 34.8 us -> 33.3 us
  Pallas kernels: 16.6 us -> 15.5 us
    unnamed x18 -> x12, local copies, waits for them, and re-layouts: 2.41 us -> 0.04 us
    pallas_call x1, Pallas kernels: 3.06 us -> 1.11 us  [body(): pl.pallas_call(functools.partial(cotangent_kernel, (date_local, row_size,...]
    all_to_all x1, waiting for transfers between devices: 10 us -> 12 us  [body(): lax.all_to_all(parts, ('row', *dates), split_axis=0, concat_axis=0, tiled...]
    ppermute x1, waiting for transfers between devices: 5.51 us -> 3.65 us  [body(): row_grad = lax.ppermute(row_grad, 'row', swap)]
    ppermute x1, waiting for transfers between devices: 3.25 us -> 1.79 us  [body(): mid_grad = lax.ppermute(mid_grad, 'mid', swap)]
    ppermute x1, starting transfers between devices: 1.49 us -> 0.53 us  [body(): row_grad = lax.ppermute(row_grad, 'row', swap)]
    pallas_call x1, Pallas kernels: 4.82 us -> 5.67 us  [body(): pl.pallas_call(functools.partial(column_kernel, (*sizes, head_count, pack...]
  transfers between devices with their start and end apart: 11 -> 11, of which waited for: 8 -> 8; matrix products, arithmetic and copies ran while one was open for 0% -> 0% of each run, Pallas kernels for 5% -> 4%
where the time goes in v9:
time: 71.5 us; the launch traced here: 71.2 us
  waiting for transfers between devices  33.3 us (47%)
  starting transfers between devices  20.7 us (29%)
  Pallas kernels  15.5 us (22%)
  other arithmetic  0.83 us (1%)
  between operations  0.79 us (1%)
    all_to_all x1, waiting for transfers between devices, body(): lax.all_to_all(parts, ('row', *dates), split_axis=0, concat_axis=0, tiled...  12 us
    all_to_all x1, starting transfers between devices, body(): lax.all_to_all(outgoing, dates, split_axis=0, concat_axis=0, tiled=True)  7.5 us
    ppermute x1, waiting for transfers between devices, body(): other_grad = lax.ppermute(leaving, 'row', swap)  5.72 us
    pallas_call x1, Pallas kernels, body(): pl.pallas_call(functools.partial(column_kernel, (*sizes, head_count, pack...  5.67 us
    all_to_all x1, waiting for transfers between devices, body(): lax.all_to_all(outgoing, dates, split_axis=0, concat_axis=0, tiled=True)  5.35 us
    pallas_call x1, Pallas kernels, body(): pl.pallas_call(functools.partial(time_kernel, (date_size, date_local, pat...  4.1 us
    ppermute x3, starting transfers between devices, body(): terms.append(lax.ppermute(steps[step], 'outer', route))  3.83 us
    ppermute x1, waiting for transfers between devices, body(): row_grad = lax.ppermute(row_grad, 'row', swap)  3.65 us
  transfers between devices with their start and end apart: 11, of which 8 were waited for; matrix products, arithmetic and copies ran while one was open for 0% of the time, Pallas kernels for 4%

profile of v9, /device:TPU:0, one launch (start us, length us, event | category | flops | bytes accessed | tf_op | source)
XLA Modules:
  0.0 71.2 jit_solution(10391863200991260383)
XLA Ops:
  0.6 0.0 copy-start.3
  0.6 1.9 %pack_tokens.1 = bf16[16,104,128]{2,1,0:T(8,128)(2,1)} custom-call(s32[2]{0:T(128)} %numbers_ref.1, bf16[2,16,16,384]{3,2,1,0:T(8,128)(2,1)} %tokens_ref.1, s32[2,16,16]{2,1,0:T(8,128)} %flags_ref.1), custom_call_target="tpu_custom_call" | custom-call | tf_op jit(solution)/shard_map/pack_tokens/pallas_call | solution.py:493
  2.6 0.0 copy-start.2
  2.6 7.5 %all-to-all-start = ((bf16[16,104,128]{2,1,0:T(8,128)(2,1)}), bf16[16,104,128]{2,1,0:T(8,128)(2,1)S(1)}, u32[]{:S(2)}, u32[]{:S(2)}) async-start(bf16[16,104,128]{2,1,0:T(8,128)(2,1)} %pack_tokens.1), calls=%async_computation | async-start | bytes 851968 | tf_op jit(solution)/shard_map/all_to_all | solution.py:523
  10.1 0.0 copy-start.4
  10.1 0.0 copy-done.2
  10.2 0.0 copy-start.5
  10.2 1.6 %collective-permute-start = (bf16[2,16,8,384]{3,2,1,0:T(8,128)(2,1)S(1)}, bf16[2,16,8,384]{3,2,1,0:T(8,128)(2,1)S(1)}, u32[]{:S(2)}, u32[]{:S(2)}) collective-permute-start(bf16[2,16,8,384]{3,2,1,0:T(8,128)(2,1)S(1)} %dynamic-slice_bitcast_fusion), channel_id=1, source_target_pairs={{0,1},{1,0},{2,3},{3,2},{4,5},{5,4},{6,7},{7,6},{8,9},{9,8},{10,11... | collective-permute-start | bytes 589832 | tf_op jit(solution)/shard_map/ppermute | solution.py:508
  11.8 5.7 %collective-permute-done = bf16[2,16,8,384]{3,2,1,0:T(8,128)(2,1)S(1)} collective-permute-done((bf16[2,16,8,384]{3,2,1,0:T(8,128)(2,1)S(1)}, bf16[2,16,8,384]{3,2,1,0:T(8,128)(2,1)S(1)}, u32[]{:S(2)}, u32[]{:S(2)}) %collective-permute-start) | collective-permute-done | bytes 196640 | tf_op jit(solution)/shard_map/ppermute | solution.py:508
  17.5 5.3 %all-to-all-done.block_ref = bf16[16,104,128]{2,1,0:T(8,128)(2,1)S(1)} async-done(((bf16[16,104,128]{2,1,0:T(8,128)(2,1)}), bf16[16,104,128]{2,1,0:T(8,128)(2,1)S(1)}, u32[]{:S(2)}, u32[]{:S(2)}) %all-to-all-start) | async-done | bytes 426016 | tf_op jit(solution)/shard_map/all_to_all | solution.py:523
  22.8 0.0 copy-done.3
  22.8 0.0 copy-done.4
  22.8 0.0 copy-done.5
  22.8 0.0 copy-start.1
  22.8 4.1 %time_attention.1 = (bf16[512,384]{1,0:T(8,128)(2,1)}, s32[1]{0:T(128)}) custom-call(f32[12]{0:T(128)S(1)} %copy-done.5, bf16[16,104,128]{2,1,0:T(8,128)(2,1)S(1)} %all-to-all-done.block_ref, bf16[384,1152]{1,0:T(8,128)(2,1)S(1)} %copy-done.3, bf16[384,384]{1,0:T(8,128)(2,1)S(1)} %copy-done.4, bf16[256,384]{1,0:T(8,128)(2,1)S(1)} %bitcast.21), custom_call_target="tpu_custom_call" | custom-call | tf_op jit(solution)/shard_map/time_attention/pallas_call | solution.py:540
  27.0 0.0 copy-start
  27.0 3.6 %all-to-all-start.1 = ((bf16[32,16,384]{2,1,0:T(8,128)(2,1)}), bf16[32,16,384]{2,1,0:T(8,128)(2,1)S(1)}, u32[]{:S(2)}, u32[]{:S(2)}) async-start(bf16[32,16,384]{2,1,0:T(8,128)(2,1)} %bitcast.6), calls=%async_computation.1 | async-start | bytes 786432 | tf_op jit(solution)/shard_map/all_to_all | solution.py:584
  30.6 0.0 copy-done
  30.6 1.1 %cotangent_heads.1 = (bf16[512,384]{1,0:T(8,128)(2,1)S(1)}, bf16[512,384]{1,0:T(8,128)(2,1)S(1)}) custom-call(s32[1]{0:T(128)} %bitcast.refs_0_.row_ref, bf16[512,384]{1,0:T(8,128)(2,1)S(1)} %bitcast.20, bf16[256,384]{1,0:T(8,128)(2,1)S(1)} %bitcast.22, bf16[384,384]{1,0:T(8,128)(2,1)S(1)} %copy-done, s32[1]{0:T(128)} %get-tuple-element.25.refs_4_), custom_call_target="tpu_custom_call" | custom-call | tf_op jit(solution)/shard_map/cotangent_heads/pallas_call | solution.py:568
  31.7 12.0 %all-to-all-done.1 = bf16[32,16,384]{2,1,0:T(8,128)(2,1)S(1)} async-done(((bf16[32,16,384]{2,1,0:T(8,128)(2,1)}), bf16[32,16,384]{2,1,0:T(8,128)(2,1)S(1)}, u32[]{:S(2)}, u32[]{:S(2)}) %all-to-all-start.1) | async-done | bytes 393248 | tf_op jit(solution)/shard_map/all_to_all | solution.py:584
  43.7 0.0 copy-done.1
  43.7 5.7 %column_attention.1 = (bf16[512,384]{1,0:T(8,128)(2,1)S(1)}, bf16[2,8,144,128]{3,2,1,0:T(8,128)(2,1)S(1)}, bf16[2,8,144,128]{3,2,1,0:T(8,128)(2,1)}) custom-call(s32[1]{0:T(128)} %bitcast.refs_0_.row_ref, s32[1]{0:T(128)} %bitcast.2.pair_ref, bf16[512,384]{1,0:T(8,128)(2,1)S(1)} %bitcast.17, bf16[512,384]{1,0:T(8,128)(2,1)S(1)} %get-tuple-element.26.grad_low_scr, ...), custom_call_target="tpu_custom_call" | custom-call | tf_op jit(solution)/shard_map/column_attention/pallas_call | solution.py:608
  49.4 0.0 collective-permute-start.1
  49.4 2.2 %collective-permute-done.1.came_ref = bf16[2,8,144,128]{3,2,1,0:T(8,128)(2,1)S(1)} collective-permute-done((bf16[2,8,144,128]{3,2,1,0:T(8,128)(2,1)}, bf16[2,8,144,128]{3,2,1,0:T(8,128)(2,1)S(1)}, u32[]{:S(2)}, u32[]{:S(2)}) %collective-permute-start.1) | collective-permute-done | bytes 589856 | tf_op jit(solution)/shard_map/ppermute | solution.py:624
  51.6 0.6 pair_gradients.1
  52.2 1.5 %collective-permute-start.2 = (bf16[4,144,128]{2,1,0:T(8,128)(2,1)S(1)}, bf16[4,144,128]{2,1,0:T(8,128)(2,1)S(1)}, u32[]{:S(2)}, u32[]{:S(2)}) collective-permute-start(bf16[4,144,128]{2,1,0:T(8,128)(2,1)S(1)} %get-tuple-element.34), channel_id=1, source_target_pairs={{0,4},{4,0},{1,5},{5,1},{2,6},{6,2},{3,7},{7,3},{8,12},{12,8},{9,1... | collective-permute-start | bytes 442376 | tf_op jit(solution)/shard_map/ppermute | solution.py:637
  53.7 0.5 collective-permute-start.3
  54.3 1.5 %collective-permute-start.4 = (bf16[4,144,128]{2,1,0:T(8,128)(2,1)S(1)}, bf16[4,144,128]{2,1,0:T(8,128)(2,1)S(1)}, u32[]{:S(2)}, u32[]{:S(2)}) collective-permute-start(bf16[4,144,128]{2,1,0:T(8,128)(2,1)S(1)} %get-tuple-element.36), channel_id=1, source_target_pairs={{0,5},{5,0},{1,4},{4,1},{2,7},{7,2},{3,6},{6,3},{8,13},{13,8},{9,1... | collective-permute-start | bytes 442376 | tf_op jit(solution)/shard_map/ppermute | solution.py:636
  55.7 1.3 %mixed_tokens.1 = (bf16[256,384]{1,0:T(8,128)(2,1)S(1)}, bf16[256,384]{1,0:T(8,128)(2,1)S(1)}) custom-call(s32[1]{0:T(128)} %get-tuple-element.30.row_ref, bf16[512,384]{1,0:T(8,128)(2,1)S(1)} %bitcast.18, bf16[512,384]{1,0:T(8,128)(2,1)S(1)} %get-tuple-element.31.heads_ref, bf16[384,384]{1,0:T(8,128)(2,1)S(1)} %copy-done), custom_call_target="tpu_custom_call" | custom-call | tf_op jit(solution)/shard_map/mixed_tokens/pallas_call | solution.py:639
  57.1 1.8 %collective-permute-done.2.mid_ref = bf16[4,144,128]{2,1,0:T(8,128)(2,1)S(1)} collective-permute-done((bf16[4,144,128]{2,1,0:T(8,128)(2,1)S(1)}, bf16[4,144,128]{2,1,0:T(8,128)(2,1)S(1)}, u32[]{:S(2)}, u32[]{:S(2)}) %collective-permute-start.2) | collective-permute-done | bytes 147488 | tf_op jit(solution)/shard_map/ppermute | solution.py:637
  58.8 3.7 %collective-permute-done.3.row_ref = bf16[4,144,128]{2,1,0:T(8,128)(2,1)S(1)} collective-permute-done((bf16[4,144,128]{2,1,0:T(8,128)(2,1)S(1)}, bf16[4,144,128]{2,1,0:T(8,128)(2,1)S(1)}, u32[]{:S(2)}, u32[]{:S(2)}) %collective-permute-start.3) | collective-permute-done | bytes 147488 | tf_op jit(solution)/shard_map/ppermute | solution.py:638
  62.5 0.0 collective-permute-done.4.both_ref
  62.5 0.1 spread_gradients.1
  62.6 0.6 collective-permute-start.5
  63.2 0.6 collective-permute-start.6
  63.8 1.6 %collective-permute-start.7 = (bf16[144,128]{1,0:T(8,128)(2,1)S(1)}, bf16[144,128]{1,0:T(8,128)(2,1)S(1)}, u32[]{:S(2)}, u32[]{:S(2)}) collective-permute-start(bf16[144,128]{1,0:T(8,128)(2,1)S(1)} %get-tuple-element.41), channel_id=1, source_target_pairs={{0,16},{8,24},{16,0},{24,8},{1,17},{9,25},{17,1},{25,9},{2,18},{10... | collective-permute-start | bytes 110600 | tf_op jit(solution)/shard_map/ppermute | solution.py:663
  65.4 1.6 %collective-permute-start.8 = (bf16[144,128]{1,0:T(8,128)(2,1)S(1)}, bf16[144,128]{1,0:T(8,128)(2,1)S(1)}, u32[]{:S(2)}, u32[]{:S(2)}) collective-permute-start(bf16[144,128]{1,0:T(8,128)(2,1)S(1)} %get-tuple-element.42), channel_id=1, source_target_pairs={{0,24},{8,0},{16,8},{24,16},{1,25},{9,1},{17,9},{25,17},{2,26},{10... | collective-permute-start | bytes 110600 | tf_op jit(solution)/shard_map/ppermute | solution.py:663
  67.0 2.0 %collective-permute-done.6.refs_1_ = bf16[144,128]{1,0:T(8,128)(2,1)S(1)} collective-permute-done((bf16[144,128]{1,0:T(8,128)(2,1)S(1)}, bf16[144,128]{1,0:T(8,128)(2,1)S(1)}, u32[]{:S(2)}, u32[]{:S(2)}) %collective-permute-start.6) | collective-permute-done | bytes 36896 | tf_op jit(solution)/shard_map/ppermute | solution.py:663
  69.1 0.5 collective-permute-done.7.refs_2_
  69.6 0.0 collective-permute-done.8.refs_3_
  69.6 0.7 %gradient_sum.1 = (f32[72,192]{1,0:T(8,128)}, f32[24,192]{1,0:T(8,128)}) custom-call(s32[1]{0:T(128)} %bitcast.refs_0_.row_ref, bf16[144,128]{1,0:T(8,128)(2,1)S(1)} %get-tuple-element.39.refs_0_, bf16[144,128]{1,0:T(8,128)(2,1)S(1)} %collective-permute-done.6.refs_1_, bf16[144,128]{1,0:T(8,128)(2,1)S(1)} %collective-permute-done.7.refs_2_, ...), custom_call_target="tpu_custom_call" | custom-call | tf_op jit(solution)/shard_map/gradient_sum/pallas_call | solution.py:664
  70.3 0.0 collective-permute-done.5
  70.4 0.8 %copy_bitcast_fusion = bf16[2,16,16,384]{3,2,1,0:T(8,128)(2,1)} fusion(bf16[2,16,1,8,384]{4,3,1,0,2:T(8,128)(2,1)S(1)} %bitcast.24, bf16[2,16,1,8,384]{4,3,1,0,2:T(8,128)(2,1)S(1)} %bitcast.23), kind=kLoop, calls=%fused_computation.1 | loop fusion | flops 196608 | bytes 786432 | tf_op jit(solution)/shard_map/reshape | solution.py:698
  (2 shorter events, 0.1 us)
Async XLA Ops:
  0.6 22.2 %copy-start.3 = (bf16[384,1152]{1,0:T(8,128)(2,1)S(1)}, bf16[384,1152]{1,0:T(8,128)(2,1)}, u32[]{:S(2)}) copy-start(bf16[384,1152]{1,0:T(8,128)(2,1)} %project_ref.2) | copy-start | bytes 2654212
  2.6 7.5 %copy-start.2 = (bf16[2,16,16,384]{3,2,1,0:T(8,128)(2,1)S(1)}, bf16[2,16,16,384]{3,2,1,0:T(8,128)(2,1)}, u32[]{:S(2)}) copy-start(bf16[2,16,16,384]{3,2,1,0:T(8,128)(2,1)} %param.17) | copy-start | bytes 1179652
  2.6 20.2 %all-to-all-start = ((bf16[16,104,128]{2,1,0:T(8,128)(2,1)}), bf16[16,104,128]{2,1,0:T(8,128)(2,1)S(1)}, u32[]{:S(2)}, u32[]{:S(2)}) async-start(bf16[16,104,128]{2,1,0:T(8,128)(2,1)} %pack_tokens.1), calls=%async_computation | async-start | bytes 851968 | tf_op jit(solution)/shard_map/all_to_all | solution.py:523
  10.1 12.7 %copy-start.4 = (bf16[384,384]{1,0:T(8,128)(2,1)S(1)}, bf16[384,384]{1,0:T(8,128)(2,1)}, u32[]{:S(2)}) copy-start(bf16[384,384]{1,0:T(8,128)(2,1)} %output_ref.2) | copy-start | bytes 884740
  10.2 12.7 %copy-start.5 = (f32[12]{0:T(128)S(1)}, f32[12]{0:T(128)}, u32[]{:S(2)}) copy-start(f32[12]{0:T(128)} %slopes_ref.1) | copy-start | bytes 148
  10.2 7.3 %collective-permute-start = (bf16[2,16,8,384]{3,2,1,0:T(8,128)(2,1)S(1)}, bf16[2,16,8,384]{3,2,1,0:T(8,128)(2,1)S(1)}, u32[]{:S(2)}, u32[]{:S(2)}) collective-permute-start(bf16[2,16,8,384]{3,2,1,0:T(8,128)(2,1)S(1)} %dynamic-slice_bitcast_fusion), channel_id=1, source_target_pairs={{0,1},{1,0},{2,3},{3,2},{4,5},{5,4},{6,7},{7,6},{8,9},{9,8},{10,11... | collective-permute-start | bytes 589832 | tf_op jit(solution)/shard_map/ppermute | solution.py:508
  22.8 20.9 %copy-start.1 = (bf16[384,1152]{1,0:T(8,128)(2,1)S(1)}, bf16[384,1152]{1,0:T(8,128)(2,1)}, u32[]{:S(2)}) copy-start(bf16[384,1152]{1,0:T(8,128)(2,1)} %project_ref.3) | copy-start | bytes 2654212
  27.0 3.7 %copy-start = (bf16[384,384]{1,0:T(8,128)(2,1)S(1)}, bf16[384,384]{1,0:T(8,128)(2,1)}, u32[]{:S(2)}) copy-start(bf16[384,384]{1,0:T(8,128)(2,1)} %output_ref.3) | copy-start | bytes 884740
  27.0 16.8 %all-to-all-start.1 = ((bf16[32,16,384]{2,1,0:T(8,128)(2,1)}), bf16[32,16,384]{2,1,0:T(8,128)(2,1)S(1)}, u32[]{:S(2)}, u32[]{:S(2)}) async-start(bf16[32,16,384]{2,1,0:T(8,128)(2,1)} %bitcast.6), calls=%async_computation.1 | async-start | bytes 786432 | tf_op jit(solution)/shard_map/all_to_all | solution.py:584
  49.4 2.2 %collective-permute-start.1 = (bf16[2,8,144,128]{3,2,1,0:T(8,128)(2,1)}, bf16[2,8,144,128]{3,2,1,0:T(8,128)(2,1)S(1)}, u32[]{:S(2)}, u32[]{:S(2)}) collective-permute-start(bf16[2,8,144,128]{3,2,1,0:T(8,128)(2,1)} %get-tuple-element.29), channel_id=1, source_target_pairs={{0,2},{2,0},{1,3},{3,1},{4,6},{6,4},{5,7},{7,5},{8,10},{10,8},{9,1... | collective-permute-start | bytes 1769480 | tf_op jit(solution)/shard_map/ppermute | solution.py:624
  52.2 6.7 %collective-permute-start.2 = (bf16[4,144,128]{2,1,0:T(8,128)(2,1)S(1)}, bf16[4,144,128]{2,1,0:T(8,128)(2,1)S(1)}, u32[]{:S(2)}, u32[]{:S(2)}) collective-permute-start(bf16[4,144,128]{2,1,0:T(8,128)(2,1)S(1)} %get-tuple-element.34), channel_id=1, source_target_pairs={{0,4},{4,0},{1,5},{5,1},{2,6},{6,2},{3,7},{7,3},{8,12},{12,8},{9,1... | collective-permute-start | bytes 442376 | tf_op jit(solution)/shard_map/ppermute | solution.py:637
  53.7 8.8 %collective-permute-start.3 = (bf16[4,144,128]{2,1,0:T(8,128)(2,1)S(1)}, bf16[4,144,128]{2,1,0:T(8,128)(2,1)S(1)}, u32[]{:S(2)}, u32[]{:S(2)}) collective-permute-start(bf16[4,144,128]{2,1,0:T(8,128)(2,1)S(1)} %get-tuple-element.35), channel_id=1, source_target_pairs={{0,1},{1,0},{2,3},{3,2},{4,5},{5,4},{6,7},{7,6},{8,9},{9,8},{10,11... | collective-permute-start | bytes 442376 | tf_op jit(solution)/shard_map/ppermute | solution.py:638
  54.3 8.2 %collective-permute-start.4 = (bf16[4,144,128]{2,1,0:T(8,128)(2,1)S(1)}, bf16[4,144,128]{2,1,0:T(8,128)(2,1)S(1)}, u32[]{:S(2)}, u32[]{:S(2)}) collective-permute-start(bf16[4,144,128]{2,1,0:T(8,128)(2,1)S(1)} %get-tuple-element.36), channel_id=1, source_target_pairs={{0,5},{5,0},{1,4},{4,1},{2,7},{7,2},{3,6},{6,3},{8,13},{13,8},{9,1... | collective-permute-start | bytes 442376 | tf_op jit(solution)/shard_map/ppermute | solution.py:636
  62.6 7.7 %collective-permute-start.5 = (bf16[256,384]{1,0:T(8,128)(2,1)S(1)}, bf16[256,384]{1,0:T(8,128)(2,1)S(1)}, u32[]{:S(2)}, u32[]{:S(2)}) collective-permute-start(bf16[256,384]{1,0:T(8,128)(2,1)S(1)} %get-tuple-element.38), channel_id=1, source_target_pairs={{0,1},{1,0},{2,3},{3,2},{4,5},{5,4},{6,7},{7,6},{8,9},{9,8},{10,11... | collective-permute-start | bytes 589832 | tf_op jit(solution)/shard_map/ppermute | solution.py:674
  63.2 5.9 %collective-permute-start.6 = (bf16[144,128]{1,0:T(8,128)(2,1)S(1)}, bf16[144,128]{1,0:T(8,128)(2,1)S(1)}, u32[]{:S(2)}, u32[]{:S(2)}) collective-permute-start(bf16[144,128]{1,0:T(8,128)(2,1)S(1)} %get-tuple-element.40), channel_id=1, source_target_pairs={{0,8},{8,16},{16,24},{24,0},{1,9},{9,17},{17,25},{25,1},{2,10},{10... | collective-permute-start | bytes 110600 | tf_op jit(solution)/shard_map/ppermute | solution.py:663
  63.8 5.8 %collective-permute-start.7 = (bf16[144,128]{1,0:T(8,128)(2,1)S(1)}, bf16[144,128]{1,0:T(8,128)(2,1)S(1)}, u32[]{:S(2)}, u32[]{:S(2)}) collective-permute-start(bf16[144,128]{1,0:T(8,128)(2,1)S(1)} %get-tuple-element.41), channel_id=1, source_target_pairs={{0,16},{8,24},{16,0},{24,8},{1,17},{9,25},{17,1},{25,9},{2,18},{10... | collective-permute-start | bytes 110600 | tf_op jit(solution)/shard_map/ppermute | solution.py:663
  65.4 4.2 %collective-permute-start.8 = (bf16[144,128]{1,0:T(8,128)(2,1)S(1)}, bf16[144,128]{1,0:T(8,128)(2,1)S(1)}, u32[]{:S(2)}, u32[]{:S(2)}) collective-permute-start(bf16[144,128]{1,0:T(8,128)(2,1)S(1)} %get-tuple-element.42), channel_id=1, source_target_pairs={{0,24},{8,0},{16,8},{24,16},{1,25},{9,1},{17,9},{25,17},{2,26},{10... | collective-permute-start | bytes 110600 | tf_op jit(solution)/shard_map/ppermute | solution.py:663

commit v10 on v9

--- a/solution.py
+++ b/solution.py
@@ -10,9 +10,10 @@
 
 epsilon = 1e-06
 masked_score = -1e30
-units_each = 24
+time_units = 48
+column_units = 24
 dates = ("outer", "mid", "pair")
-vmem_limit = 24 * 1024 * 1024
+vmem_limit = 12 * 1024 * 1024
 low = jnp.bfloat16
 wide = jnp.float32
 
@@ -74,16 +75,34 @@
 
 
 def pack_kernel(
-    numbers_ref, tokens_ref, flags_ref, out_ref, numbers_scr, tokens_scr, flags_scr, copied
+    numbers_ref,
+    tokens_ref,
+    flags_ref,
+    out_ref,
+    numbers_scr,
+    tokens_scr,
+    flags_scr,
+    out_scr,
+    small_copied,
+    came,
+    left,
 ):
-    copies = [
-        pltpu.make_async_copy(tokens_ref, tokens_scr, copied.at[0]),
-        pltpu.make_async_copy(flags_ref, flags_scr, copied.at[1]),
-        pltpu.make_async_copy(numbers_ref, numbers_scr, copied.at[2]),
+    dates_each, parts, patches, width = tokens_ref.shape
+    chunks = came.shape[0]
+    each = parts // chunks
+    small = [
+        pltpu.make_async_copy(flags_ref, flags_scr, small_copied.at[0]),
+        pltpu.make_async_copy(numbers_ref, numbers_scr, small_copied.at[1]),
     ]
-    for copy in copies:
+    arrivals, departures = [], []
+    for chunk in range(chunks):
+        at = pl.ds(chunk * each, each)
+        arrivals.append(
+            pltpu.make_async_copy(tokens_ref.at[:, at], tokens_scr.at[:, at], came.at[chunk])
+        )
+        departures.append(pltpu.make_async_copy(out_scr.at[at], out_ref.at[at], left.at[chunk]))
+    for copy in small + arrivals:
         copy.start()
-    dates_each, parts, patches, width = tokens_ref.shape
     lanes = out_ref.shape[2]
     tiles = width // lanes
     spare = out_ref.shape[1] - tiles * dates_each * patches
@@ -92,8 +111,8 @@
     place = jnp.where(place == lane, 1.0, 0.0).astype(low)
     lane = lax.broadcasted_iota(jnp.int32, (parts, lanes), 1)
     row = lax.broadcasted_iota(jnp.int32, (spare, lanes), 0)
-    copies[1].wait()
-    copies[2].wait()
+    for copy in small:
+        copy.wait()
     infos = []
     for date in range(dates_each):
         number = numbers_scr[date]
@@ -102,16 +121,20 @@
         info = matmul(flags_scr[date].astype(wide).astype(low), place)
         info = jnp.where(lane == patches, upper, info)
         infos.append(jnp.where(lane == patches + 1, under, info))
-    copies[0].wait()
-    for part in range(parts):
-        tokens = jnp.concatenate(
-            [tokens_scr[date, part].astype(wide) for date in range(dates_each)], axis=0
-        )
-        extra = jnp.zeros((spare, lanes), wide)
-        for date in range(dates_each):
-            extra = jnp.where(row == date, infos[date][part : part + 1], extra)
-        pieces = [tokens[:, tile * lanes : (tile + 1) * lanes] for tile in range(tiles)]
-        out_ref[part] = jnp.concatenate(pieces + [extra], axis=0).astype(low)
+    for chunk in range(chunks):
+        arrivals[chunk].wait()
+        for part in range(chunk * each, (chunk + 1) * each):
+            tokens = jnp.concatenate(
+                [tokens_scr[date, part].astype(wide) for date in range(dates_each)], axis=0
+            )
+            extra = jnp.zeros((spare, lanes), wide)
+            for date in range(dates_each):
+                extra = jnp.where(row == date, infos[date][part : part + 1], extra)
+            pieces = [tokens[:, tile * lanes : (tile + 1) * lanes] for tile in range(tiles)]
+            out_scr[part] = jnp.concatenate(pieces + [extra], axis=0).astype(low)
+        departures[chunk].start()
+    for copy in departures:
+        copy.wait()
 
 
 def time_kernel(
@@ -170,7 +193,7 @@
         for head in range(1, packed):
             slope = jnp.where(head_at == head, slopes_ref[first + head], slope)
         biases.append(-slope * gap_days)
-    for units in batches(groups, head_count // packed, units_each):
+    for units in batches(groups, head_count // packed, time_units):
         all_scores = []
         for group, part in units:
             rows = slice(group * length, (group + 1) * length)
@@ -315,7 +338,7 @@
     normed_scr[...] = rms_norm(plane_scr[...])
     qkv_scr[...] = matmul(normed_scr[...], project_ref[...]).astype(low)
     mask = block_mask(length, packed, head_size)
-    for units in batches(groups, head_count // packed, units_each):
+    for units in batches(groups, head_count // packed, column_units):
         places = []
         for group, part in units:
             start = part * lanes
@@ -427,7 +450,7 @@
 
 
 def finish_kernel(project_each, row_ref, *refs):
-    *terms, project_ref, output_ref = refs
+    *terms, _, project_ref, output_ref = refs
     total = terms[0][...].astype(wide)
     for term in terms[1:]:
         total = total + term[...].astype(wide)
@@ -494,11 +517,15 @@
             pack_kernel,
             out_shape=jax.ShapeDtypeStruct((date_size, tile_rows, 128), low),
             in_specs=[pl.BlockSpec(memory_space=pltpu.HBM)] * 3,
+            out_specs=pl.BlockSpec(memory_space=pltpu.HBM),
             scratch_shapes=[
                 pltpu.SMEM(date_numbers.shape, jnp.int32),
                 pltpu.VMEM(tokens.shape, low),
                 pltpu.VMEM(clear_flags.shape, jnp.int32),
-                pltpu.SemaphoreType.DMA((3,)),
+                pltpu.VMEM((date_size, tile_rows, 128), low),
+                pltpu.SemaphoreType.DMA((2,)),
+                pltpu.SemaphoreType.DMA((4,)),
+                pltpu.SemaphoreType.DMA((4,)),
             ],
             name="pack_tokens",
         )(date_numbers, tokens, clear_flags)
@@ -661,22 +688,22 @@
         for step in range(1, outers):
             route = [(at, (at + step) % outers) for at in range(outers)]
             terms.append(lax.ppermute(steps[step], "outer", route))
+        arrived = lax.ppermute(leaving, "row", swap)
+        quarter = (date_local, row_local, 1, columns_each, width)
+        kept, arrived = kept.reshape(quarter), arrived.reshape(quarter)
+        mixed = jnp.concatenate(
+            [jnp.where(row_at == 0, kept, arrived), jnp.where(row_at == 0, arrived, kept)], axis=2
+        )
         owned_project, owned_output = pl.pallas_call(
             functools.partial(finish_kernel, project_each),
             out_shape=(
                 jax.ShapeDtypeStruct((project_each, lane_each), wide),
                 jax.ShapeDtypeStruct((output_each, lane_each), wide),
             ),
-            in_specs=[in_smem] + [in_vmem] * outers,
+            in_specs=[in_smem] + [in_vmem] * outers + [pl.BlockSpec(memory_space=pl.ANY)],
             compiler_params=params,
             name="gradient_sum",
-        )(row_one, *terms)
-        arrived = lax.ppermute(leaving, "row", swap)
-        quarter = (date_local, row_local, 1, columns_each, width)
-        kept, arrived = kept.reshape(quarter), arrived.reshape(quarter)
-        mixed = jnp.concatenate(
-            [jnp.where(row_at == 0, kept, arrived), jnp.where(row_at == 0, arrived, kept)], axis=2
-        )
+        )(row_one, *terms, mixed)
     else:
         mixed = mixed[0]
         grads = jnp.concatenate(

time: 71.5 us -> 70.6 us (0.987)
  waiting for transfers between devices: 33.3 us -> 32.4 us
    ppermute x3, waiting for transfers between devices: 2.57 us -> 0.4 us  [body(): terms.append(lax.ppermute(steps[step], 'outer', route))]
    ppermute x1, waiting for transfers between devices: 0.01 us -> 1.31 us  [body(): arrived = lax.ppermute(leaving, 'row', swap)]
    concatenate x0 -> x1, other arithmetic: none -> 0.82 us  [body(): jnp.concatenate([jnp.where(row_at == 0, kept, arrived), jnp.where(row_at...]
    reshape x1 -> x0, other arithmetic: 0.79 us -> none  [body(): mixed = mixed.reshape(date_local, row_local, column_count, width)]
  transfers between devices with their start and end apart: 11 -> 11, of which waited for: 8 -> 8; matrix products, arithmetic and copies ran while one was open for 0% -> 1% of each run, Pallas kernels for 4% -> 3%
where the time goes in v10:
time: 70.6 us; the launch traced here: 70.2 us
  waiting for transfers between devices  32.4 us (46%)
  starting transfers between devices  20.7 us (29%)
  Pallas kernels  15.4 us (22%)
  other arithmetic  0.86 us (1%)
  between operations  0.79 us (1%)
    all_to_all x1, waiting for transfers between devices, body(): lax.all_to_all(parts, ('row', *dates), split_axis=0, concat_axis=0, tiled...  12 us
    all_to_all x1, starting transfers between devices, body(): lax.all_to_all(outgoing, dates, split_axis=0, concat_axis=0, tiled=True)  7.5 us
    ppermute x1, waiting for transfers between devices, body(): other_grad = lax.ppermute(leaving, 'row', swap)  5.72 us
    pallas_call x1, Pallas kernels, body(): pl.pallas_call(functools.partial(column_kernel, (*sizes, head_count, pack...  5.67 us
    all_to_all x1, waiting for transfers between devices, body(): lax.all_to_all(outgoing, dates, split_axis=0, concat_axis=0, tiled=True)  5.35 us
    pallas_call x1, Pallas kernels, body(): pl.pallas_call(functools.partial(time_kernel, (date_size, date_local, pat...  4.06 us
    ppermute x3, starting transfers between devices, body(): terms.append(lax.ppermute(steps[step], 'outer', route))  3.83 us
    ppermute x1, waiting for transfers between devices, body(): row_grad = lax.ppermute(row_grad, 'row', swap)  3.65 us
  transfers between devices with their start and end apart: 11, of which 8 were waited for; matrix products, arithmetic and copies ran while one was open for 1% of the time, Pallas kernels for 3%

profile of v10, /device:TPU:0, one launch (start us, length us, event | category | flops | bytes accessed | tf_op | source)
XLA Modules:
  0.0 70.2 jit_solution(18295698119970994725)
XLA Ops:
  0.6 0.0 copy-start.3
  0.6 1.9 %pack_tokens.1 = bf16[16,104,128]{2,1,0:T(8,128)(2,1)} custom-call(s32[2]{0:T(128)} %numbers_ref.1, bf16[2,16,16,384]{3,2,1,0:T(8,128)(2,1)} %tokens_ref.1, s32[2,16,16]{2,1,0:T(8,128)} %flags_ref.1), custom_call_target="tpu_custom_call" | custom-call | tf_op jit(solution)/shard_map/pack_tokens/pallas_call | solution.py:516
  2.5 0.0 copy-start.2
  2.5 7.5 %all-to-all-start = ((bf16[16,104,128]{2,1,0:T(8,128)(2,1)}), bf16[16,104,128]{2,1,0:T(8,128)(2,1)S(1)}, u32[]{:S(2)}, u32[]{:S(2)}) async-start(bf16[16,104,128]{2,1,0:T(8,128)(2,1)} %pack_tokens.1), calls=%async_computation | async-start | bytes 851968 | tf_op jit(solution)/shard_map/all_to_all | solution.py:550
  10.1 0.0 copy-start.4
  10.1 0.0 copy-done.2
  10.1 0.0 copy-start.5
  10.1 1.6 %collective-permute-start = (bf16[2,16,8,384]{3,2,1,0:T(8,128)(2,1)S(1)}, bf16[2,16,8,384]{3,2,1,0:T(8,128)(2,1)S(1)}, u32[]{:S(2)}, u32[]{:S(2)}) collective-permute-start(bf16[2,16,8,384]{3,2,1,0:T(8,128)(2,1)S(1)} %dynamic-slice_bitcast_fusion), channel_id=1, source_target_pairs={{0,1},{1,0},{2,3},{3,2},{4,5},{5,4},{6,7},{7,6},{8,9},{9,8},{10,11... | collective-permute-start | bytes 589832 | tf_op jit(solution)/shard_map/ppermute | solution.py:535
  11.7 5.7 %collective-permute-done = bf16[2,16,8,384]{3,2,1,0:T(8,128)(2,1)S(1)} collective-permute-done((bf16[2,16,8,384]{3,2,1,0:T(8,128)(2,1)S(1)}, bf16[2,16,8,384]{3,2,1,0:T(8,128)(2,1)S(1)}, u32[]{:S(2)}, u32[]{:S(2)}) %collective-permute-start) | collective-permute-done | bytes 196640 | tf_op jit(solution)/shard_map/ppermute | solution.py:535
  17.4 5.3 %all-to-all-done.block_ref = bf16[16,104,128]{2,1,0:T(8,128)(2,1)S(1)} async-done(((bf16[16,104,128]{2,1,0:T(8,128)(2,1)}), bf16[16,104,128]{2,1,0:T(8,128)(2,1)S(1)}, u32[]{:S(2)}, u32[]{:S(2)}) %all-to-all-start) | async-done | bytes 426016 | tf_op jit(solution)/shard_map/all_to_all | solution.py:550
  22.8 0.0 copy-done.3
  22.8 0.0 copy-done.4
  22.8 0.0 copy-done.5
  22.8 0.0 copy-start.1
  22.8 4.1 %time_attention.1 = (bf16[512,384]{1,0:T(8,128)(2,1)}, s32[1]{0:T(128)}) custom-call(f32[12]{0:T(128)S(1)} %copy-done.5, bf16[16,104,128]{2,1,0:T(8,128)(2,1)S(1)} %all-to-all-done.block_ref, bf16[384,1152]{1,0:T(8,128)(2,1)S(1)} %copy-done.3, bf16[384,384]{1,0:T(8,128)(2,1)S(1)} %copy-done.4, bf16[256,384]{1,0:T(8,128)(2,1)S(1)} %bitcast.21), custom_call_target="tpu_custom_call" | custom-call | tf_op jit(solution)/shard_map/time_attention/pallas_call | solution.py:567
  26.9 0.0 copy-start
  26.9 3.6 %all-to-all-start.1 = ((bf16[32,16,384]{2,1,0:T(8,128)(2,1)}), bf16[32,16,384]{2,1,0:T(8,128)(2,1)S(1)}, u32[]{:S(2)}, u32[]{:S(2)}) async-start(bf16[32,16,384]{2,1,0:T(8,128)(2,1)} %bitcast.6), calls=%async_computation.1 | async-start | bytes 786432 | tf_op jit(solution)/shard_map/all_to_all | solution.py:611
  30.5 0.0 copy-done
  30.5 1.1 %cotangent_heads.1 = (bf16[512,384]{1,0:T(8,128)(2,1)S(1)}, bf16[512,384]{1,0:T(8,128)(2,1)S(1)}) custom-call(s32[1]{0:T(128)} %bitcast.refs_0_.row_ref, bf16[512,384]{1,0:T(8,128)(2,1)S(1)} %bitcast.20, bf16[256,384]{1,0:T(8,128)(2,1)S(1)} %bitcast.22, bf16[384,384]{1,0:T(8,128)(2,1)S(1)} %copy-done, s32[1]{0:T(128)} %get-tuple-element.25.refs_4_), custom_call_target="tpu_custom_call" | custom-call | tf_op jit(solution)/shard_map/cotangent_heads/pallas_call | solution.py:595
  31.7 12.0 %all-to-all-done.1 = bf16[32,16,384]{2,1,0:T(8,128)(2,1)S(1)} async-done(((bf16[32,16,384]{2,1,0:T(8,128)(2,1)}), bf16[32,16,384]{2,1,0:T(8,128)(2,1)S(1)}, u32[]{:S(2)}, u32[]{:S(2)}) %all-to-all-start.1) | async-done | bytes 393248 | tf_op jit(solution)/shard_map/all_to_all | solution.py:611
  43.6 0.0 copy-done.1
  43.6 5.7 %column_attention.1 = (bf16[512,384]{1,0:T(8,128)(2,1)S(1)}, bf16[2,8,144,128]{3,2,1,0:T(8,128)(2,1)S(1)}, bf16[2,8,144,128]{3,2,1,0:T(8,128)(2,1)}) custom-call(s32[1]{0:T(128)} %bitcast.refs_0_.row_ref, s32[1]{0:T(128)} %bitcast.2.pair_ref, bf16[512,384]{1,0:T(8,128)(2,1)S(1)} %bitcast.17, bf16[512,384]{1,0:T(8,128)(2,1)S(1)} %get-tuple-element.26.grad_low_scr, ...), custom_call_target="tpu_custom_call" | custom-call | tf_op jit(solution)/shard_map/column_attention/pallas_call | solution.py:635
  49.3 0.0 collective-permute-start.1
  49.3 2.2 %collective-permute-done.1.came_ref = bf16[2,8,144,128]{3,2,1,0:T(8,128)(2,1)S(1)} collective-permute-done((bf16[2,8,144,128]{3,2,1,0:T(8,128)(2,1)}, bf16[2,8,144,128]{3,2,1,0:T(8,128)(2,1)S(1)}, u32[]{:S(2)}, u32[]{:S(2)}) %collective-permute-start.1) | collective-permute-done | bytes 589856 | tf_op jit(solution)/shard_map/ppermute | solution.py:651
  51.5 0.6 pair_gradients.1
  52.1 1.5 %collective-permute-start.2 = (bf16[4,144,128]{2,1,0:T(8,128)(2,1)S(1)}, bf16[4,144,128]{2,1,0:T(8,128)(2,1)S(1)}, u32[]{:S(2)}, u32[]{:S(2)}) collective-permute-start(bf16[4,144,128]{2,1,0:T(8,128)(2,1)S(1)} %get-tuple-element.34), channel_id=1, source_target_pairs={{0,4},{4,0},{1,5},{5,1},{2,6},{6,2},{3,7},{7,3},{8,12},{12,8},{9,1... | collective-permute-start | bytes 442376 | tf_op jit(solution)/shard_map/ppermute | solution.py:664
  53.6 0.5 collective-permute-start.3
  54.2 1.5 %collective-permute-start.4 = (bf16[4,144,128]{2,1,0:T(8,128)(2,1)S(1)}, bf16[4,144,128]{2,1,0:T(8,128)(2,1)S(1)}, u32[]{:S(2)}, u32[]{:S(2)}) collective-permute-start(bf16[4,144,128]{2,1,0:T(8,128)(2,1)S(1)} %get-tuple-element.36), channel_id=1, source_target_pairs={{0,5},{5,0},{1,4},{4,1},{2,7},{7,2},{3,6},{6,3},{8,13},{13,8},{9,1... | collective-permute-start | bytes 442376 | tf_op jit(solution)/shard_map/ppermute | solution.py:663
  55.7 1.3 %mixed_tokens.1 = (bf16[256,384]{1,0:T(8,128)(2,1)S(1)}, bf16[256,384]{1,0:T(8,128)(2,1)S(1)}) custom-call(s32[1]{0:T(128)} %get-tuple-element.30.row_ref, bf16[512,384]{1,0:T(8,128)(2,1)S(1)} %bitcast.18, bf16[512,384]{1,0:T(8,128)(2,1)S(1)} %get-tuple-element.31.heads_ref, bf16[384,384]{1,0:T(8,128)(2,1)S(1)} %copy-done), custom_call_target="tpu_custom_call" | custom-call | tf_op jit(solution)/shard_map/mixed_tokens/pallas_call | solution.py:666
  57.0 1.8 %collective-permute-done.2.mid_ref = bf16[4,144,128]{2,1,0:T(8,128)(2,1)S(1)} collective-permute-done((bf16[4,144,128]{2,1,0:T(8,128)(2,1)S(1)}, bf16[4,144,128]{2,1,0:T(8,128)(2,1)S(1)}, u32[]{:S(2)}, u32[]{:S(2)}) %collective-permute-start.2) | collective-permute-done | bytes 147488 | tf_op jit(solution)/shard_map/ppermute | solution.py:664
  58.8 3.7 %collective-permute-done.3.row_ref = bf16[4,144,128]{2,1,0:T(8,128)(2,1)S(1)} collective-permute-done((bf16[4,144,128]{2,1,0:T(8,128)(2,1)S(1)}, bf16[4,144,128]{2,1,0:T(8,128)(2,1)S(1)}, u32[]{:S(2)}, u32[]{:S(2)}) %collective-permute-start.3) | collective-permute-done | bytes 147488 | tf_op jit(solution)/shard_map/ppermute | solution.py:665
  62.4 0.0 collective-permute-done.4.both_ref
  62.4 0.1 spread_gradients.1
  62.5 0.6 collective-permute-start.5
  63.1 0.6 collective-permute-start.6
  63.7 1.6 %collective-permute-start.7 = (bf16[144,128]{1,0:T(8,128)(2,1)S(1)}, bf16[144,128]{1,0:T(8,128)(2,1)S(1)}, u32[]{:S(2)}, u32[]{:S(2)}) collective-permute-start(bf16[144,128]{1,0:T(8,128)(2,1)S(1)} %get-tuple-element.41), channel_id=1, source_target_pairs={{0,16},{8,24},{16,0},{24,8},{1,17},{9,25},{17,1},{25,9},{2,18},{10... | collective-permute-start | bytes 110600 | tf_op jit(solution)/shard_map/ppermute | solution.py:690
  65.3 1.6 %collective-permute-start.8 = (bf16[144,128]{1,0:T(8,128)(2,1)S(1)}, bf16[144,128]{1,0:T(8,128)(2,1)S(1)}, u32[]{:S(2)}, u32[]{:S(2)}) collective-permute-start(bf16[144,128]{1,0:T(8,128)(2,1)S(1)} %get-tuple-element.42), channel_id=1, source_target_pairs={{0,24},{8,0},{16,8},{24,16},{1,25},{9,1},{17,9},{25,17},{2,26},{10... | collective-permute-start | bytes 110600 | tf_op jit(solution)/shard_map/ppermute | solution.py:690
  66.9 1.3 %collective-permute-done.5 = bf16[256,384]{1,0:T(8,128)(2,1)S(1)} collective-permute-done((bf16[256,384]{1,0:T(8,128)(2,1)S(1)}, bf16[256,384]{1,0:T(8,128)(2,1)S(1)}, u32[]{:S(2)}, u32[]{:S(2)}) %collective-permute-start.5) | collective-permute-done | bytes 196640 | tf_op jit(solution)/shard_map/ppermute | solution.py:691
  68.3 0.8 %pad_maximum_fusion = (bf16[2,16,2,8,384]{4,3,2,1,0:T(8,128)(2,1)S(1)}, bf16[2,16,16,384]{3,2,1,0:T(8,128)(2,1)}) fusion(bf16[2,16,1,8,384]{4,3,2,1,0:T(8,128)(2,1)S(1)} %bitcast.24, bf16[2,16,1,8,384]{4,3,2,1,0:T(8,128)(2,1)S(1)} %bitcast.23), kind=kLoop, calls=%fused_computation | loop fusion | flops 196608 | bytes 1179648 | tf_op jit(solution)/shard_map/concatenate | solution.py:694
  69.1 0.0 collective-permute-done.6.refs_1_
  69.1 0.4 collective-permute-done.7.refs_2_
  69.5 0.0 collective-permute-done.8.refs_3_
  69.5 0.7 %gradient_sum.1 = (f32[72,192]{1,0:T(8,128)}, f32[24,192]{1,0:T(8,128)}) custom-call(s32[1]{0:T(128)} %bitcast.refs_0_.row_ref, bf16[144,128]{1,0:T(8,128)(2,1)S(1)} %get-tuple-element.39.refs_0_, bf16[144,128]{1,0:T(8,128)(2,1)S(1)} %collective-permute-done.6.refs_1_, bf16[144,128]{1,0:T(8,128)(2,1)S(1)} %collective-permute-done.7.refs_2_, ...), custom_call_target="tpu_custom_call" | custom-call | tf_op jit(solution)/shard_map/gradient_sum/pallas_call | solution.py:697
  (2 shorter events, 0.1 us)
Async XLA Ops:
  0.6 22.2 %copy-start.3 = (bf16[384,1152]{1,0:T(8,128)(2,1)S(1)}, bf16[384,1152]{1,0:T(8,128)(2,1)}, u32[]{:S(2)}) copy-start(bf16[384,1152]{1,0:T(8,128)(2,1)} %project_ref.2) | copy-start | bytes 2654212
  2.5 7.5 %copy-start.2 = (bf16[2,16,16,384]{3,2,1,0:T(8,128)(2,1)S(1)}, bf16[2,16,16,384]{3,2,1,0:T(8,128)(2,1)}, u32[]{:S(2)}) copy-start(bf16[2,16,16,384]{3,2,1,0:T(8,128)(2,1)} %param.17) | copy-start | bytes 1179652
  2.5 20.2 %all-to-all-start = ((bf16[16,104,128]{2,1,0:T(8,128)(2,1)}), bf16[16,104,128]{2,1,0:T(8,128)(2,1)S(1)}, u32[]{:S(2)}, u32[]{:S(2)}) async-start(bf16[16,104,128]{2,1,0:T(8,128)(2,1)} %pack_tokens.1), calls=%async_computation | async-start | bytes 851968 | tf_op jit(solution)/shard_map/all_to_all | solution.py:550
  10.1 12.7 %copy-start.4 = (bf16[384,384]{1,0:T(8,128)(2,1)S(1)}, bf16[384,384]{1,0:T(8,128)(2,1)}, u32[]{:S(2)}) copy-start(bf16[384,384]{1,0:T(8,128)(2,1)} %output_ref.2) | copy-start | bytes 884740
  10.1 12.7 %copy-start.5 = (f32[12]{0:T(128)S(1)}, f32[12]{0:T(128)}, u32[]{:S(2)}) copy-start(f32[12]{0:T(128)} %slopes_ref.1) | copy-start | bytes 148
  10.1 7.3 %collective-permute-start = (bf16[2,16,8,384]{3,2,1,0:T(8,128)(2,1)S(1)}, bf16[2,16,8,384]{3,2,1,0:T(8,128)(2,1)S(1)}, u32[]{:S(2)}, u32[]{:S(2)}) collective-permute-start(bf16[2,16,8,384]{3,2,1,0:T(8,128)(2,1)S(1)} %dynamic-slice_bitcast_fusion), channel_id=1, source_target_pairs={{0,1},{1,0},{2,3},{3,2},{4,5},{5,4},{6,7},{7,6},{8,9},{9,8},{10,11... | collective-permute-start | bytes 589832 | tf_op jit(solution)/shard_map/ppermute | solution.py:535
  22.8 20.8 %copy-start.1 = (bf16[384,1152]{1,0:T(8,128)(2,1)S(1)}, bf16[384,1152]{1,0:T(8,128)(2,1)}, u32[]{:S(2)}) copy-start(bf16[384,1152]{1,0:T(8,128)(2,1)} %project_ref.3) | copy-start | bytes 2654212
  26.9 3.7 %copy-start = (bf16[384,384]{1,0:T(8,128)(2,1)S(1)}, bf16[384,384]{1,0:T(8,128)(2,1)}, u32[]{:S(2)}) copy-start(bf16[384,384]{1,0:T(8,128)(2,1)} %output_ref.3) | copy-start | bytes 884740
  26.9 16.8 %all-to-all-start.1 = ((bf16[32,16,384]{2,1,0:T(8,128)(2,1)}), bf16[32,16,384]{2,1,0:T(8,128)(2,1)S(1)}, u32[]{:S(2)}, u32[]{:S(2)}) async-start(bf16[32,16,384]{2,1,0:T(8,128)(2,1)} %bitcast.6), calls=%async_computation.1 | async-start | bytes 786432 | tf_op jit(solution)/shard_map/all_to_all | solution.py:611
  49.3 2.2 %collective-permute-start.1 = (bf16[2,8,144,128]{3,2,1,0:T(8,128)(2,1)}, bf16[2,8,144,128]{3,2,1,0:T(8,128)(2,1)S(1)}, u32[]{:S(2)}, u32[]{:S(2)}) collective-permute-start(bf16[2,8,144,128]{3,2,1,0:T(8,128)(2,1)} %get-tuple-element.29), channel_id=1, source_target_pairs={{0,2},{2,0},{1,3},{3,1},{4,6},{6,4},{5,7},{7,5},{8,10},{10,8},{9,1... | collective-permute-start | bytes 1769480 | tf_op jit(solution)/shard_map/ppermute | solution.py:651
  52.1 6.7 %collective-permute-start.2 = (bf16[4,144,128]{2,1,0:T(8,128)(2,1)S(1)}, bf16[4,144,128]{2,1,0:T(8,128)(2,1)S(1)}, u32[]{:S(2)}, u32[]{:S(2)}) collective-permute-start(bf16[4,144,128]{2,1,0:T(8,128)(2,1)S(1)} %get-tuple-element.34), channel_id=1, source_target_pairs={{0,4},{4,0},{1,5},{5,1},{2,6},{6,2},{3,7},{7,3},{8,12},{12,8},{9,1... | collective-permute-start | bytes 442376 | tf_op jit(solution)/shard_map/ppermute | solution.py:664
  53.6 8.8 %collective-permute-start.3 = (bf16[4,144,128]{2,1,0:T(8,128)(2,1)S(1)}, bf16[4,144,128]{2,1,0:T(8,128)(2,1)S(1)}, u32[]{:S(2)}, u32[]{:S(2)}) collective-permute-start(bf16[4,144,128]{2,1,0:T(8,128)(2,1)S(1)} %get-tuple-element.35), channel_id=1, source_target_pairs={{0,1},{1,0},{2,3},{3,2},{4,5},{5,4},{6,7},{7,6},{8,9},{9,8},{10,11... | collective-permute-start | bytes 442376 | tf_op jit(solution)/shard_map/ppermute | solution.py:665
  54.2 8.2 %collective-permute-start.4 = (bf16[4,144,128]{2,1,0:T(8,128)(2,1)S(1)}, bf16[4,144,128]{2,1,0:T(8,128)(2,1)S(1)}, u32[]{:S(2)}, u32[]{:S(2)}) collective-permute-start(bf16[4,144,128]{2,1,0:T(8,128)(2,1)S(1)} %get-tuple-element.36), channel_id=1, source_target_pairs={{0,5},{5,0},{1,4},{4,1},{2,7},{7,2},{3,6},{6,3},{8,13},{13,8},{9,1... | collective-permute-start | bytes 442376 | tf_op jit(solution)/shard_map/ppermute | solution.py:663
  62.5 5.7 %collective-permute-start.5 = (bf16[256,384]{1,0:T(8,128)(2,1)S(1)}, bf16[256,384]{1,0:T(8,128)(2,1)S(1)}, u32[]{:S(2)}, u32[]{:S(2)}) collective-permute-start(bf16[256,384]{1,0:T(8,128)(2,1)S(1)} %get-tuple-element.38), channel_id=1, source_target_pairs={{0,1},{1,0},{2,3},{3,2},{4,5},{5,4},{6,7},{7,6},{8,9},{9,8},{10,11... | collective-permute-start | bytes 589832 | tf_op jit(solution)/shard_map/ppermute | solution.py:691
  63.1 6.0 %collective-permute-start.6 = (bf16[144,128]{1,0:T(8,128)(2,1)S(1)}, bf16[144,128]{1,0:T(8,128)(2,1)S(1)}, u32[]{:S(2)}, u32[]{:S(2)}) collective-permute-start(bf16[144,128]{1,0:T(8,128)(2,1)S(1)} %get-tuple-element.40), channel_id=1, source_target_pairs={{0,8},{8,16},{16,24},{24,0},{1,9},{9,17},{17,25},{25,1},{2,10},{10... | collective-permute-start | bytes 110600 | tf_op jit(solution)/shard_map/ppermute | solution.py:690
  63.7 5.8 %collective-permute-start.7 = (bf16[144,128]{1,0:T(8,128)(2,1)S(1)}, bf16[144,128]{1,0:T(8,128)(2,1)S(1)}, u32[]{:S(2)}, u32[]{:S(2)}) collective-permute-start(bf16[144,128]{1,0:T(8,128)(2,1)S(1)} %get-tuple-element.41), channel_id=1, source_target_pairs={{0,16},{8,24},{16,0},{24,8},{1,17},{9,25},{17,1},{25,9},{2,18},{10... | collective-permute-start | bytes 110600 | tf_op jit(solution)/shard_map/ppermute | solution.py:690
  65.3 4.2 %collective-permute-start.8 = (bf16[144,128]{1,0:T(8,128)(2,1)S(1)}, bf16[144,128]{1,0:T(8,128)(2,1)S(1)}, u32[]{:S(2)}, u32[]{:S(2)}) collective-permute-start(bf16[144,128]{1,0:T(8,128)(2,1)S(1)} %get-tuple-element.42), channel_id=1, source_target_pairs={{0,24},{8,0},{16,8},{24,16},{1,25},{9,1},{17,9},{25,17},{2,26},{10... | collective-permute-start | bytes 110600 | tf_op jit(solution)/shard_map/ppermute | solution.py:690

commit v11 on v10

--- a/solution.py
+++ b/solution.py
@@ -145,13 +145,11 @@
     output_ref,
     earlier_ref,
     out_ref,
-    after_ref,
     seq_scr,
     token_scr,
     qkv_scr,
     heads_scr,
 ):
-    after_ref[0] = jnp.int32(0)
     sources, dates_each, groups, head_count, packed, columns_each = sizes
     width = project_ref.shape[0]
     tile_lanes = block_ref.shape[2]
@@ -285,7 +283,7 @@
         plane_scr[rows, :] = get_tiles(seq_scr, at)
 
 
-def mixed_kernel(sizes, row_ref, hidden_ref, heads_ref, output_ref, *refs):
+def mixed_kernel(sizes, row_ref, hidden_ref, heads_ref, output_ref, _, *refs):
     dates_each, row_parts, rows_each, columns_each, direct = sizes
     *mixed_refs, seq_scr, plane_scr = refs
     length = row_parts * rows_each
@@ -421,10 +419,7 @@
                 send_ref[place] = jnp.where(even, two, one).astype(low)
 
 
-def pair_kernel(
-    row_ref, mid_ref, kept_ref, came_ref, own_ref, mid_out, row_out, both_out, handed_ref
-):
-    handed_ref[0] = row_ref[0]
+def pair_kernel(row_ref, mid_ref, kept_ref, came_ref, own_ref, mid_out, row_out, both_out):
     row, mid = row_ref[0], mid_ref[0]
     for outer in range(own_ref.shape[0]):
         for out_ref, row_at, mid_at in (
@@ -509,6 +504,7 @@
     params = pltpu.CompilerParams(vmem_limit_bytes=vmem_limit)
     in_vmem = pl.BlockSpec(memory_space=pltpu.VMEM)
     in_smem = pl.BlockSpec(memory_space=pltpu.SMEM)
+    in_any = pl.BlockSpec(memory_space=pl.ANY)
     swap = [(0, 1), (1, 0)]
     column_tokens = date_local * row_count * columns_each
     half_tokens = column_tokens // row_size
@@ -555,16 +551,16 @@
             cotangent.reshape(local_patches * date_local, width),
             other_grad.reshape(half_tokens, width),
         )
-        in_specs = [in_smem] + [in_vmem] * 3 + [in_smem]
+        in_specs = [in_smem] + [in_vmem] * 3 + [in_any]
     else:
         grads_in = (
             lax.all_to_all(cotangent, "row", split_axis=2, concat_axis=1, tiled=True).reshape(
                 column_tokens, width
             ),
         )
-        in_specs = [in_vmem] * 2 + [in_smem]
+        in_specs = [in_vmem] * 2 + [in_any]
     time_tokens = date_count * patches_each
-    hidden, after_time = pl.pallas_call(
+    hidden = pl.pallas_call(
         functools.partial(
             time_kernel,
             (
@@ -576,12 +572,8 @@
                 columns_each if direct else patches_each,
             ),
         ),
-        out_shape=(
-            jax.ShapeDtypeStruct((time_tokens, width), low),
-            jax.ShapeDtypeStruct((1,), jnp.int32),
-        ),
-        in_specs=[in_smem, in_vmem, in_vmem, in_vmem, pl.BlockSpec(memory_space=pl.ANY)],
-        out_specs=(in_vmem, in_smem),
+        out_shape=jax.ShapeDtypeStruct((time_tokens, width), low),
+        in_specs=[in_smem, in_vmem, in_vmem, in_vmem, in_any],
         scratch_shapes=[
             pltpu.VMEM((width // 128, time_tokens, 128), wide),
             pltpu.VMEM((time_tokens, width), wide),
@@ -604,7 +596,7 @@
         scratch_shapes=[pltpu.VMEM((width // 128, column_tokens, 128), wide)],
         compiler_params=params,
         name="cotangent_heads",
-    )(*grads_in, column_output, after_time)
+    )(*grads_in, column_output, hidden)
 
     if direct:
         parts = hidden.reshape(row_size * date_size, date_local * columns_each, width)
@@ -636,6 +628,7 @@
         functools.partial(column_kernel, (*sizes, head_count, packed, date_size)),
         out_shape=(jax.ShapeDtypeStruct((column_tokens, width), low), *grad_shapes),
         in_specs=[in_smem] * 2 + [in_vmem] * 4,
+        input_output_aliases={4: 0},
         scratch_shapes=[
             pltpu.VMEM((width // 128, column_tokens, 128), wide),
             pltpu.VMEM((column_tokens, width), wide),
@@ -646,17 +639,17 @@
         compiler_params=params,
         name="column_attention",
     )(row_one, pair_one, plane, grad_low, heads_grad, column_project)
-    after_one = row_one
+    own_grad = first_grad
     if direct:
         came = lax.ppermute(second_grad, "pair", swap)
         outers = date_size // 4
         block = jax.ShapeDtypeStruct((packed_rows, 128), low)
         blocks = jax.ShapeDtypeStruct((outers, packed_rows, 128), low)
-        own_grad, mid_grad, row_grad, both_grad, after_one = pl.pallas_call(
+        own_grad, mid_grad, row_grad, both_grad = pl.pallas_call(
             pair_kernel,
-            out_shape=(blocks,) * 4 + (jax.ShapeDtypeStruct((1,), jnp.int32),),
+            out_shape=(blocks,) * 4,
             in_specs=[in_smem] * 2 + [in_vmem] * 2,
-            out_specs=(in_vmem,) * 4 + (in_smem,),
+            out_specs=(in_vmem,) * 4,
             compiler_params=params,
             name="pair_gradients",
         )(row_one, lax.axis_index("mid").reshape(1), first_grad, came)
@@ -666,14 +659,14 @@
     mixed = pl.pallas_call(
         functools.partial(mixed_kernel, sizes),
         out_shape=mixed_shapes,
-        in_specs=[in_smem] + [in_vmem] * 3,
+        in_specs=[in_smem] + [in_vmem] * 3 + [in_any],
         scratch_shapes=[
             pltpu.VMEM((width // 128, column_tokens, 128), wide),
             pltpu.VMEM((column_tokens, width), wide),
         ],
         compiler_params=params,
         name="mixed_tokens",
-    )(after_one, plane, column_heads, column_output)
+    )(row_one, plane, column_heads, column_output, own_grad)
 
     if direct:
         kept, sent = mixed
@@ -700,7 +693,7 @@
                 jax.ShapeDtypeStruct((project_each, lane_each), wide),
                 jax.ShapeDtypeStruct((output_each, lane_each), wide),
             ),
-            in_specs=[in_smem] + [in_vmem] * outers + [pl.BlockSpec(memory_space=pl.ANY)],
+            in_specs=[in_smem] + [in_vmem] * outers + [in_any],
             compiler_params=params,
             name="gradient_sum",
         )(row_one, *terms, mixed)

time: 70.6 us -> 69.1 us (0.979)
  Pallas kernels: 15.4 us -> 12.8 us
  waiting for transfers between devices: 32.4 us -> 33.5 us
    pallas_call x1, Pallas kernels: 5.67 us -> 4.82 us  [body(): pl.pallas_call(functools.partial(column_kernel, (*sizes, head_count, pack...]
  transfers between devices with their start and end apart: 11 -> 11, of which waited for: 8 -> 8; matrix products, arithmetic and copies ran while one was open for 1% -> 1% of each run, Pallas kernels for 3% -> 2%
where the time goes in v11:
time: 69.1 us; the launch traced here: 68.8 us
  waiting for transfers between devices  33.5 us (48%)
  starting transfers between devices  20.8 us (30%)
  Pallas kernels  12.8 us (19%)
  other arithmetic  0.86 us (1%)
  between operations  0.78 us (1%)
    all_to_all x1, waiting for transfers between devices, body(): lax.all_to_all(parts, ('row', *dates), split_axis=0, concat_axis=0, tiled...  12.6 us
    all_to_all x1, starting transfers between devices, body(): lax.all_to_all(outgoing, dates, split_axis=0, concat_axis=0, tiled=True)  7.5 us
    ppermute x1, waiting for transfers between devices, body(): other_grad = lax.ppermute(leaving, 'row', swap)  5.72 us
    all_to_all x1, waiting for transfers between devices, body(): lax.all_to_all(outgoing, dates, split_axis=0, concat_axis=0, tiled=True)  5.35 us
    pallas_call x1, Pallas kernels, body(): pl.pallas_call(functools.partial(column_kernel, (*sizes, head_count, pack...  4.82 us
    pallas_call x1, Pallas kernels, body(): pl.pallas_call(functools.partial(time_kernel, (date_size, date_local, pat...  4.05 us
    ppermute x3, starting transfers between devices, body(): terms.append(lax.ppermute(steps[step], 'outer', route))  3.83 us
    ppermute x1, waiting for transfers between devices, body(): row_grad = lax.ppermute(row_grad, 'row', swap)  3.65 us
  transfers between devices with their start and end apart: 11, of which 8 were waited for; matrix products, arithmetic and copies ran while one was open for 1% of the time, Pallas kernels for 2%

profile of v11, /device:TPU:0, one launch (start us, length us, event | category | flops | bytes accessed | tf_op | source)
XLA Modules:
  0.0 68.8 jit_solution(17549721657146324999)
XLA Ops:
  0.6 0.0 copy-start.2
  0.6 1.9 %pack_tokens.1 = bf16[16,104,128]{2,1,0:T(8,128)(2,1)} custom-call(s32[2]{0:T(128)} %numbers_ref.1, bf16[2,16,16,384]{3,2,1,0:T(8,128)(2,1)} %tokens_ref.1, s32[2,16,16]{2,1,0:T(8,128)} %flags_ref.1), custom_call_target="tpu_custom_call" | custom-call | tf_op jit(solution)/shard_map/pack_tokens/pallas_call | solution.py:512
  2.5 0.0 copy-start.3
  2.5 7.5 %all-to-all-start = ((bf16[16,104,128]{2,1,0:T(8,128)(2,1)}), bf16[16,104,128]{2,1,0:T(8,128)(2,1)S(1)}, u32[]{:S(2)}, u32[]{:S(2)}) async-start(bf16[16,104,128]{2,1,0:T(8,128)(2,1)} %pack_tokens.1), calls=%async_computation | async-start | bytes 851968 | tf_op jit(solution)/shard_map/all_to_all | solution.py:546
  10.1 0.0 copy-start.4
  10.1 0.0 copy-done.3
  10.1 0.0 copy-start.5
  10.1 1.6 %collective-permute-start = (bf16[2,16,8,384]{3,2,1,0:T(8,128)(2,1)S(1)}, bf16[2,16,8,384]{3,2,1,0:T(8,128)(2,1)S(1)}, u32[]{:S(2)}, u32[]{:S(2)}) collective-permute-start(bf16[2,16,8,384]{3,2,1,0:T(8,128)(2,1)S(1)} %dynamic-slice_bitcast_fusion), channel_id=1, source_target_pairs={{0,1},{1,0},{2,3},{3,2},{4,5},{5,4},{6,7},{7,6},{8,9},{9,8},{10,11... | collective-permute-start | bytes 589832 | tf_op jit(solution)/shard_map/ppermute | solution.py:531
  11.7 5.7 %collective-permute-done = bf16[2,16,8,384]{3,2,1,0:T(8,128)(2,1)S(1)} collective-permute-done((bf16[2,16,8,384]{3,2,1,0:T(8,128)(2,1)S(1)}, bf16[2,16,8,384]{3,2,1,0:T(8,128)(2,1)S(1)}, u32[]{:S(2)}, u32[]{:S(2)}) %collective-permute-start) | collective-permute-done | bytes 196640 | tf_op jit(solution)/shard_map/ppermute | solution.py:531
  17.4 5.3 %all-to-all-done.block_ref = bf16[16,104,128]{2,1,0:T(8,128)(2,1)S(1)} async-done(((bf16[16,104,128]{2,1,0:T(8,128)(2,1)}), bf16[16,104,128]{2,1,0:T(8,128)(2,1)S(1)}, u32[]{:S(2)}, u32[]{:S(2)}) %all-to-all-start) | async-done | bytes 426016 | tf_op jit(solution)/shard_map/all_to_all | solution.py:546
  22.8 0.0 copy-done.2
  22.8 0.0 copy-done.4
  22.8 0.0 copy-done.5
  22.8 4.0 %time_attention.1.refs_4_ = bf16[512,384]{1,0:T(8,128)(2,1)} custom-call(f32[12]{0:T(128)S(1)} %copy-done.5, bf16[16,104,128]{2,1,0:T(8,128)(2,1)S(1)} %all-to-all-done.block_ref, bf16[384,1152]{1,0:T(8,128)(2,1)S(1)} %copy-done.2, bf16[384,384]{1,0:T(8,128)(2,1)S(1)} %copy-done.4, bf16[256,384]{1,0:T(8,128)(2,1)S(1)} %bitcast.21), custom_call_target="tpu_custom_call" | custom-call | tf_op jit(solution)/shard_map/time_attention/pallas_call | solution.py:563
  26.8 0.0 copy-start
  26.8 0.0 copy-start.1
  26.8 3.6 %all-to-all-start.1 = ((bf16[32,16,384]{2,1,0:T(8,128)(2,1)}), bf16[32,16,384]{2,1,0:T(8,128)(2,1)S(1)}, u32[]{:S(2)}, u32[]{:S(2)}) async-start(bf16[32,16,384]{2,1,0:T(8,128)(2,1)} %bitcast.4), calls=%async_computation.1 | async-start | bytes 786432 | tf_op jit(solution)/shard_map/all_to_all | solution.py:603
  30.5 0.0 copy-done
  30.5 0.5 cotangent_heads.1
  31.0 12.6 %all-to-all-done.1 = bf16[32,16,384]{2,1,0:T(8,128)(2,1)S(1)} async-done(((bf16[32,16,384]{2,1,0:T(8,128)(2,1)}), bf16[32,16,384]{2,1,0:T(8,128)(2,1)S(1)}, u32[]{:S(2)}, u32[]{:S(2)}) %all-to-all-start.1) | async-done | bytes 393248 | tf_op jit(solution)/shard_map/all_to_all | solution.py:603
  43.6 0.0 copy-done.1
  43.6 4.8 %column_attention.1 = (bf16[512,384]{1,0:T(8,128)(2,1)S(1)}, bf16[2,8,144,128]{3,2,1,0:T(8,128)(2,1)S(1)}, bf16[2,8,144,128]{3,2,1,0:T(8,128)(2,1)S(1)}) custom-call(s32[1]{0:T(128)} %bitcast.refs_0_.row_ref, s32[1]{0:T(128)} %bitcast.6.pair_ref, bf16[512,384]{1,0:T(8,128)(2,1)S(1)} %bitcast.17, ...), custom_call_target="tpu_custom_call", output_to_operand_aliasing={{0}: (4, {})} | custom-call | tf_op jit(solution)/shard_map/column_attention/pallas_call | solution.py:627
  48.4 0.1 collective-permute-start.1
  48.5 2.0 %collective-permute-done.1.came_ref = bf16[2,8,144,128]{3,2,1,0:T(8,128)(2,1)S(1)} collective-permute-done((bf16[2,8,144,128]{3,2,1,0:T(8,128)(2,1)S(1)}, bf16[2,8,144,128]{3,2,1,0:T(8,128)(2,1)S(1)}, u32[]{:S(2)}, u32[]{:S(2)}) %collective-permute-start.1) | collective-permute-done | bytes 589856 | tf_op jit(solution)/shard_map/ppermute | solution.py:644
  50.5 0.1 pair_gradients.1
  50.6 1.5 %collective-permute-start.2 = (bf16[4,144,128]{2,1,0:T(8,128)(2,1)S(1)}, bf16[4,144,128]{2,1,0:T(8,128)(2,1)S(1)}, u32[]{:S(2)}, u32[]{:S(2)}) collective-permute-start(bf16[4,144,128]{2,1,0:T(8,128)(2,1)S(1)} %get-tuple-element.28), channel_id=1, source_target_pairs={{0,4},{4,0},{1,5},{5,1},{2,6},{6,2},{3,7},{7,3},{8,12},{12,8},{9,1... | collective-permute-start | bytes 442376 | tf_op jit(solution)/shard_map/ppermute | solution.py:657
  52.2 0.5 collective-permute-start.3
  52.7 1.5 %collective-permute-start.4 = (bf16[4,144,128]{2,1,0:T(8,128)(2,1)S(1)}, bf16[4,144,128]{2,1,0:T(8,128)(2,1)S(1)}, u32[]{:S(2)}, u32[]{:S(2)}) collective-permute-start(bf16[4,144,128]{2,1,0:T(8,128)(2,1)S(1)} %get-tuple-element.30), channel_id=1, source_target_pairs={{0,5},{5,0},{1,4},{4,1},{2,7},{7,2},{3,6},{6,3},{8,13},{13,8},{9,1... | collective-permute-start | bytes 442376 | tf_op jit(solution)/shard_map/ppermute | solution.py:656
  54.2 0.7 mixed_tokens.1
  54.9 2.4 %collective-permute-done.2.mid_ref = bf16[4,144,128]{2,1,0:T(8,128)(2,1)S(1)} collective-permute-done((bf16[4,144,128]{2,1,0:T(8,128)(2,1)S(1)}, bf16[4,144,128]{2,1,0:T(8,128)(2,1)S(1)}, u32[]{:S(2)}, u32[]{:S(2)}) %collective-permute-start.2) | collective-permute-done | bytes 147488 | tf_op jit(solution)/shard_map/ppermute | solution.py:657
  57.3 3.7 %collective-permute-done.3.row_ref = bf16[4,144,128]{2,1,0:T(8,128)(2,1)S(1)} collective-permute-done((bf16[4,144,128]{2,1,0:T(8,128)(2,1)S(1)}, bf16[4,144,128]{2,1,0:T(8,128)(2,1)S(1)}, u32[]{:S(2)}, u32[]{:S(2)}) %collective-permute-start.3) | collective-permute-done | bytes 147488 | tf_op jit(solution)/shard_map/ppermute | solution.py:658
  60.9 0.0 collective-permute-done.4.both_ref
  60.9 0.1 spread_gradients.1
  61.0 0.6 collective-permute-start.5
  61.6 0.6 collective-permute-start.6
  62.3 1.6 %collective-permute-start.7 = (bf16[144,128]{1,0:T(8,128)(2,1)S(1)}, bf16[144,128]{1,0:T(8,128)(2,1)S(1)}, u32[]{:S(2)}, u32[]{:S(2)}) collective-permute-start(bf16[144,128]{1,0:T(8,128)(2,1)S(1)} %get-tuple-element.35), channel_id=1, source_target_pairs={{0,16},{8,24},{16,0},{24,8},{1,17},{9,25},{17,1},{25,9},{2,18},{10... | collective-permute-start | bytes 110600 | tf_op jit(solution)/shard_map/ppermute | solution.py:683
  63.9 1.6 %collective-permute-start.8 = (bf16[144,128]{1,0:T(8,128)(2,1)S(1)}, bf16[144,128]{1,0:T(8,128)(2,1)S(1)}, u32[]{:S(2)}, u32[]{:S(2)}) collective-permute-start(bf16[144,128]{1,0:T(8,128)(2,1)S(1)} %get-tuple-element.36), channel_id=1, source_target_pairs={{0,24},{8,0},{16,8},{24,16},{1,25},{9,1},{17,9},{25,17},{2,26},{10... | collective-permute-start | bytes 110600 | tf_op jit(solution)/shard_map/ppermute | solution.py:683
  65.5 1.3 %collective-permute-done.5 = bf16[256,384]{1,0:T(8,128)(2,1)S(1)} collective-permute-done((bf16[256,384]{1,0:T(8,128)(2,1)S(1)}, bf16[256,384]{1,0:T(8,128)(2,1)S(1)}, u32[]{:S(2)}, u32[]{:S(2)}) %collective-permute-start.5) | collective-permute-done | bytes 196640 | tf_op jit(solution)/shard_map/ppermute | solution.py:684
  66.8 0.8 %pad_maximum_fusion = (bf16[2,16,2,8,384]{4,3,2,1,0:T(8,128)(2,1)S(1)}, bf16[2,16,16,384]{3,2,1,0:T(8,128)(2,1)}) fusion(bf16[2,16,1,8,384]{4,3,2,1,0:T(8,128)(2,1)S(1)} %bitcast.24, bf16[2,16,1,8,384]{4,3,2,1,0:T(8,128)(2,1)S(1)} %bitcast.23), kind=kLoop, calls=%fused_computation | loop fusion | flops 196608 | bytes 1179648 | tf_op jit(solution)/shard_map/concatenate | solution.py:687
  67.6 0.0 collective-permute-done.6.refs_1_
  67.6 0.4 collective-permute-done.7.refs_2_
  68.0 0.0 collective-permute-done.8.refs_3_
  68.0 0.7 %gradient_sum.1 = (f32[72,192]{1,0:T(8,128)}, f32[24,192]{1,0:T(8,128)}) custom-call(s32[1]{0:T(128)} %bitcast.refs_0_.row_ref, bf16[144,128]{1,0:T(8,128)(2,1)S(1)} %get-tuple-element.33.refs_0_, bf16[144,128]{1,0:T(8,128)(2,1)S(1)} %collective-permute-done.6.refs_1_, bf16[144,128]{1,0:T(8,128)(2,1)S(1)} %collective-permute-done.7.refs_2_, ...), custom_call_target="tpu_custom_call" | custom-call | tf_op jit(solution)/shard_map/gradient_sum/pallas_call | solution.py:690
  (2 shorter events, 0.1 us)
Async XLA Ops:
  0.6 22.1 %copy-start.2 = (bf16[384,1152]{1,0:T(8,128)(2,1)S(1)}, bf16[384,1152]{1,0:T(8,128)(2,1)}, u32[]{:S(2)}) copy-start(bf16[384,1152]{1,0:T(8,128)(2,1)} %project_ref.2) | copy-start | bytes 2654212
  2.5 7.5 %copy-start.3 = (bf16[2,16,16,384]{3,2,1,0:T(8,128)(2,1)S(1)}, bf16[2,16,16,384]{3,2,1,0:T(8,128)(2,1)}, u32[]{:S(2)}) copy-start(bf16[2,16,16,384]{3,2,1,0:T(8,128)(2,1)} %param.17) | copy-start | bytes 1179652
  2.5 20.2 %all-to-all-start = ((bf16[16,104,128]{2,1,0:T(8,128)(2,1)}), bf16[16,104,128]{2,1,0:T(8,128)(2,1)S(1)}, u32[]{:S(2)}, u32[]{:S(2)}) async-start(bf16[16,104,128]{2,1,0:T(8,128)(2,1)} %pack_tokens.1), calls=%async_computation | async-start | bytes 851968 | tf_op jit(solution)/shard_map/all_to_all | solution.py:546
  10.1 12.7 %copy-start.4 = (bf16[384,384]{1,0:T(8,128)(2,1)S(1)}, bf16[384,384]{1,0:T(8,128)(2,1)}, u32[]{:S(2)}) copy-start(bf16[384,384]{1,0:T(8,128)(2,1)} %output_ref.2) | copy-start | bytes 884740
  10.1 12.7 %copy-start.5 = (f32[12]{0:T(128)S(1)}, f32[12]{0:T(128)}, u32[]{:S(2)}) copy-start(f32[12]{0:T(128)} %slopes_ref.1) | copy-start | bytes 148
  10.1 7.3 %collective-permute-start = (bf16[2,16,8,384]{3,2,1,0:T(8,128)(2,1)S(1)}, bf16[2,16,8,384]{3,2,1,0:T(8,128)(2,1)S(1)}, u32[]{:S(2)}, u32[]{:S(2)}) collective-permute-start(bf16[2,16,8,384]{3,2,1,0:T(8,128)(2,1)S(1)} %dynamic-slice_bitcast_fusion), channel_id=1, source_target_pairs={{0,1},{1,0},{2,3},{3,2},{4,5},{5,4},{6,7},{7,6},{8,9},{9,8},{10,11... | collective-permute-start | bytes 589832 | tf_op jit(solution)/shard_map/ppermute | solution.py:531
  26.8 3.7 %copy-start = (bf16[384,384]{1,0:T(8,128)(2,1)S(1)}, bf16[384,384]{1,0:T(8,128)(2,1)}, u32[]{:S(2)}) copy-start(bf16[384,384]{1,0:T(8,128)(2,1)} %output_ref.3) | copy-start | bytes 884740
  26.8 16.8 %copy-start.1 = (bf16[384,1152]{1,0:T(8,128)(2,1)S(1)}, bf16[384,1152]{1,0:T(8,128)(2,1)}, u32[]{:S(2)}) copy-start(bf16[384,1152]{1,0:T(8,128)(2,1)} %project_ref.3) | copy-start | bytes 2654212
  26.8 16.7 %all-to-all-start.1 = ((bf16[32,16,384]{2,1,0:T(8,128)(2,1)}), bf16[32,16,384]{2,1,0:T(8,128)(2,1)S(1)}, u32[]{:S(2)}, u32[]{:S(2)}) async-start(bf16[32,16,384]{2,1,0:T(8,128)(2,1)} %bitcast.4), calls=%async_computation.1 | async-start | bytes 786432 | tf_op jit(solution)/shard_map/all_to_all | solution.py:603
  48.4 2.1 %collective-permute-start.1 = (bf16[2,8,144,128]{3,2,1,0:T(8,128)(2,1)S(1)}, bf16[2,8,144,128]{3,2,1,0:T(8,128)(2,1)S(1)}, u32[]{:S(2)}, u32[]{:S(2)}) collective-permute-start(bf16[2,8,144,128]{3,2,1,0:T(8,128)(2,1)S(1)} %get-tuple-element.25), channel_id=1, source_target_pairs={{0,2},{2,0},{1,3},{3,1},{4,6},{6,4},{5,7},{7,5},{8,10},{10,8},{9,1... | collective-permute-start | bytes 1769480 | tf_op jit(solution)/shard_map/ppermute | solution.py:644
  50.6 6.7 %collective-permute-start.2 = (bf16[4,144,128]{2,1,0:T(8,128)(2,1)S(1)}, bf16[4,144,128]{2,1,0:T(8,128)(2,1)S(1)}, u32[]{:S(2)}, u32[]{:S(2)}) collective-permute-start(bf16[4,144,128]{2,1,0:T(8,128)(2,1)S(1)} %get-tuple-element.28), channel_id=1, source_target_pairs={{0,4},{4,0},{1,5},{5,1},{2,6},{6,2},{3,7},{7,3},{8,12},{12,8},{9,1... | collective-permute-start | bytes 442376 | tf_op jit(solution)/shard_map/ppermute | solution.py:657
  52.2 8.8 %collective-permute-start.3 = (bf16[4,144,128]{2,1,0:T(8,128)(2,1)S(1)}, bf16[4,144,128]{2,1,0:T(8,128)(2,1)S(1)}, u32[]{:S(2)}, u32[]{:S(2)}) collective-permute-start(bf16[4,144,128]{2,1,0:T(8,128)(2,1)S(1)} %get-tuple-element.29), channel_id=1, source_target_pairs={{0,1},{1,0},{2,3},{3,2},{4,5},{5,4},{6,7},{7,6},{8,9},{9,8},{10,11... | collective-permute-start | bytes 442376 | tf_op jit(solution)/shard_map/ppermute | solution.py:658
  52.7 8.2 %collective-permute-start.4 = (bf16[4,144,128]{2,1,0:T(8,128)(2,1)S(1)}, bf16[4,144,128]{2,1,0:T(8,128)(2,1)S(1)}, u32[]{:S(2)}, u32[]{:S(2)}) collective-permute-start(bf16[4,144,128]{2,1,0:T(8,128)(2,1)S(1)} %get-tuple-element.30), channel_id=1, source_target_pairs={{0,5},{5,0},{1,4},{4,1},{2,7},{7,2},{3,6},{6,3},{8,13},{13,8},{9,1... | collective-permute-start | bytes 442376 | tf_op jit(solution)/shard_map/ppermute | solution.py:656
  61.0 5.7 %collective-permute-start.5 = (bf16[256,384]{1,0:T(8,128)(2,1)S(1)}, bf16[256,384]{1,0:T(8,128)(2,1)S(1)}, u32[]{:S(2)}, u32[]{:S(2)}) collective-permute-start(bf16[256,384]{1,0:T(8,128)(2,1)S(1)} %get-tuple-element.32), channel_id=1, source_target_pairs={{0,1},{1,0},{2,3},{3,2},{4,5},{5,4},{6,7},{7,6},{8,9},{9,8},{10,11... | collective-permute-start | bytes 589832 | tf_op jit(solution)/shard_map/ppermute | solution.py:684
  61.6 6.0 %collective-permute-start.6 = (bf16[144,128]{1,0:T(8,128)(2,1)S(1)}, bf16[144,128]{1,0:T(8,128)(2,1)S(1)}, u32[]{:S(2)}, u32[]{:S(2)}) collective-permute-start(bf16[144,128]{1,0:T(8,128)(2,1)S(1)} %get-tuple-element.34), channel_id=1, source_target_pairs={{0,8},{8,16},{16,24},{24,0},{1,9},{9,17},{17,25},{25,1},{2,10},{10... | collective-permute-start | bytes 110600 | tf_op jit(solution)/shard_map/ppermute | solution.py:683
  62.3 5.8 %collective-permute-start.7 = (bf16[144,128]{1,0:T(8,128)(2,1)S(1)}, bf16[144,128]{1,0:T(8,128)(2,1)S(1)}, u32[]{:S(2)}, u32[]{:S(2)}) collective-permute-start(bf16[144,128]{1,0:T(8,128)(2,1)S(1)} %get-tuple-element.35), channel_id=1, source_target_pairs={{0,16},{8,24},{16,0},{24,8},{1,17},{9,25},{17,1},{25,9},{2,18},{10... | collective-permute-start | bytes 110600 | tf_op jit(solution)/shard_map/ppermute | solution.py:683
  63.9 4.2 %collective-permute-start.8 = (bf16[144,128]{1,0:T(8,128)(2,1)S(1)}, bf16[144,128]{1,0:T(8,128)(2,1)S(1)}, u32[]{:S(2)}, u32[]{:S(2)}) collective-permute-start(bf16[144,128]{1,0:T(8,128)(2,1)S(1)} %get-tuple-element.36), channel_id=1, source_target_pairs={{0,24},{8,0},{16,8},{24,16},{1,25},{9,1},{17,9},{25,17},{2,26},{10... | collective-permute-start | bytes 110600 | tf_op jit(solution)/shard_map/ppermute | solution.py:683

commit v12 on v11

--- a/solution.py
+++ b/solution.py
@@ -149,6 +149,8 @@
     token_scr,
     qkv_scr,
     heads_scr,
+    out_scr,
+    left,
 ):
     sources, dates_each, groups, head_count, packed, columns_each = sizes
     width = project_ref.shape[0]
@@ -214,15 +216,23 @@
             heads_scr[rows, part * lanes : (part + 1) * lanes] = own_blocks(
                 full, length, packed, head_size
             ).astype(low)
-    hidden = token_scr[...] + matmul(heads_scr[...], output_ref[...])
-    for group in range(groups):
-        first = (group // columns_each) * (length * columns_each) + group % columns_each
-        put_tiles(
-            seq_scr,
-            pl.ds(first, length, stride=columns_each),
-            hidden[group * length : (group + 1) * length],
-        )
-    out_ref[...] = get_tiles(seq_scr, slice(None)).astype(low)
+    copies = []
+    chunk_rows = columns_each * length
+    for chunk in range(groups // columns_each):
+        rows = slice(chunk * chunk_rows, (chunk + 1) * chunk_rows)
+        hidden = token_scr[rows, :] + matmul(heads_scr[rows, :], output_ref[...])
+        for column in range(columns_each):
+            put_tiles(
+                seq_scr,
+                pl.ds(chunk * chunk_rows + column, length, stride=columns_each),
+                hidden[column * length : (column + 1) * length],
+            )
+        out_scr[rows, :] = get_tiles(seq_scr, rows).astype(low)
+        at = pl.ds(chunk * chunk_rows, chunk_rows)
+        copies.append(pltpu.make_async_copy(out_scr.at[at], out_ref.at[at], left.at[chunk]))
+        copies[-1].start()
+    for copy in copies:
+        copy.wait()
 
 
 def cotangent_kernel(sizes, *refs):
@@ -438,7 +448,7 @@
     leave_ref[...] = sent_ref[...]
     count = own_ref.shape[0]
     for step in range(count):
-        at = (outer_ref[0] + step) % count
+        at = outer_ref[0] ^ step
         total = own_ref[at].astype(wide) + mid_ref[at].astype(wide)
         total = total + (row_ref[at].astype(wide) + both_ref[at].astype(wide))
         refs[step][...] = total.astype(low)
@@ -492,6 +502,7 @@
         patches_each == column_count
         and column_count % 16 == 0
         and date_size % 8 == 0
+        and date_size & (date_size - 1) == 0
         and row_size == 2
         and lane_each == 192
         and project_each % 8 == 0
@@ -574,11 +585,14 @@
         ),
         out_shape=jax.ShapeDtypeStruct((time_tokens, width), low),
         in_specs=[in_smem, in_vmem, in_vmem, in_vmem, in_any],
+        out_specs=pl.BlockSpec(memory_space=pltpu.HBM),
         scratch_shapes=[
             pltpu.VMEM((width // 128, time_tokens, 128), wide),
             pltpu.VMEM((time_tokens, width), wide),
             pltpu.VMEM((time_tokens, 3 * width), low),
             pltpu.VMEM((time_tokens, width), low),
+            pltpu.VMEM((time_tokens, width), low),
+            pltpu.SemaphoreType.DMA((patches_each // (columns_each if direct else patches_each),)),
         ],
         compiler_params=params,
         name="time_attention",
@@ -679,7 +693,7 @@
         )(lax.axis_index("outer").reshape(1), own_grad, mid_grad, row_grad, both_grad, sent)
         terms = [steps[0]]
         for step in range(1, outers):
-            route = [(at, (at + step) % outers) for at in range(outers)]
+            route = [(at, at ^ step) for at in range(outers)]
             terms.append(lax.ppermute(steps[step], "outer", route))
         arrived = lax.ppermute(leaving, "row", swap)
         quarter = (date_local, row_local, 1, columns_each, width)

time: 69.1 us -> 70.6 us (1.022)
  waiting for transfers between devices: 33.5 us -> 34.5 us
    ppermute x3, waiting for transfers between devices: 0.4 us -> 1.97 us  [body(): terms.append(lax.ppermute(steps[step], 'outer', route))]
where the time goes in v12:
time: 70.6 us; the launch traced here: 70.3 us
  waiting for transfers between devices  34.5 us (49%)
  starting transfers between devices  21.3 us (30%)
  Pallas kernels  12.8 us (18%)
  other arithmetic  0.86 us (1%)
  between operations  0.8 us (1%)
    all_to_all x1, waiting for transfers between devices, body(): lax.all_to_all(parts, ('row', *dates), split_axis=0, concat_axis=0, tiled...  12.6 us
    all_to_all x1, starting transfers between devices, body(): lax.all_to_all(outgoing, dates, split_axis=0, concat_axis=0, tiled=True)  7.5 us
    ppermute x1, waiting for transfers between devices, body(): other_grad = lax.ppermute(leaving, 'row', swap)  5.72 us
    all_to_all x1, waiting for transfers between devices, body(): lax.all_to_all(outgoing, dates, split_axis=0, concat_axis=0, tiled=True)  5.35 us
    pallas_call x1, Pallas kernels, body(): pl.pallas_call(functools.partial(column_kernel, (*sizes, head_count, pack...  4.82 us
    ppermute x3, starting transfers between devices, body(): terms.append(lax.ppermute(steps[step], 'outer', route))  4.39 us
    pallas_call x1, Pallas kernels, body(): pl.pallas_call(functools.partial(time_kernel, (date_size, date_local, pat...  4 us
    ppermute x1, waiting for transfers between devices, body(): row_grad = lax.ppermute(row_grad, 'row', swap)  3.65 us
  transfers between devices with their start and end apart: 11, of which 8 were waited for; matrix products, arithmetic and copies ran while one was open for 1% of the time, Pallas kernels for 2%

profile of v12, /device:TPU:0, one launch (start us, length us, event | category | flops | bytes accessed | tf_op | source)
XLA Modules:
  0.0 70.3 jit_solution(1564283555544645705)
XLA Ops:
  0.6 0.0 copy-start.2
  0.6 1.9 %pack_tokens.1 = bf16[16,104,128]{2,1,0:T(8,128)(2,1)} custom-call(s32[2]{0:T(128)} %numbers_ref.1, bf16[2,16,16,384]{3,2,1,0:T(8,128)(2,1)} %tokens_ref.1, s32[2,16,16]{2,1,0:T(8,128)} %flags_ref.1), custom_call_target="tpu_custom_call" | custom-call | tf_op jit(solution)/shard_map/pack_tokens/pallas_call | solution.py:523
  2.5 0.0 copy-start.3
  2.5 7.5 %all-to-all-start = ((bf16[16,104,128]{2,1,0:T(8,128)(2,1)}), bf16[16,104,128]{2,1,0:T(8,128)(2,1)S(1)}, u32[]{:S(2)}, u32[]{:S(2)}) async-start(bf16[16,104,128]{2,1,0:T(8,128)(2,1)} %pack_tokens.1), calls=%async_computation | async-start | bytes 851968 | tf_op jit(solution)/shard_map/all_to_all | solution.py:557
  10.1 0.0 copy-start.4
  10.1 0.0 copy-done.3
  10.1 0.0 copy-start.5
  10.1 1.6 %collective-permute-start = (bf16[2,16,8,384]{3,2,1,0:T(8,128)(2,1)S(1)}, bf16[2,16,8,384]{3,2,1,0:T(8,128)(2,1)S(1)}, u32[]{:S(2)}, u32[]{:S(2)}) collective-permute-start(bf16[2,16,8,384]{3,2,1,0:T(8,128)(2,1)S(1)} %dynamic-slice_bitcast_fusion), channel_id=1, source_target_pairs={{0,1},{1,0},{2,3},{3,2},{4,5},{5,4},{6,7},{7,6},{8,9},{9,8},{10,11... | collective-permute-start | bytes 589832 | tf_op jit(solution)/shard_map/ppermute | solution.py:542
  11.7 5.7 %collective-permute-done = bf16[2,16,8,384]{3,2,1,0:T(8,128)(2,1)S(1)} collective-permute-done((bf16[2,16,8,384]{3,2,1,0:T(8,128)(2,1)S(1)}, bf16[2,16,8,384]{3,2,1,0:T(8,128)(2,1)S(1)}, u32[]{:S(2)}, u32[]{:S(2)}) %collective-permute-start) | collective-permute-done | bytes 196640 | tf_op jit(solution)/shard_map/ppermute | solution.py:542
  17.4 5.3 %all-to-all-done.block_ref = bf16[16,104,128]{2,1,0:T(8,128)(2,1)S(1)} async-done(((bf16[16,104,128]{2,1,0:T(8,128)(2,1)}), bf16[16,104,128]{2,1,0:T(8,128)(2,1)S(1)}, u32[]{:S(2)}, u32[]{:S(2)}) %all-to-all-start) | async-done | bytes 426016 | tf_op jit(solution)/shard_map/all_to_all | solution.py:557
  22.8 0.0 copy-done.2
  22.8 0.0 copy-done.4
  22.8 0.0 copy-done.5
  22.8 4.0 %time_attention.1.refs_4_ = bf16[512,384]{1,0:T(8,128)(2,1)} custom-call(f32[12]{0:T(128)S(1)} %copy-done.5, bf16[16,104,128]{2,1,0:T(8,128)(2,1)S(1)} %all-to-all-done.block_ref, bf16[384,1152]{1,0:T(8,128)(2,1)S(1)} %copy-done.2, bf16[384,384]{1,0:T(8,128)(2,1)S(1)} %copy-done.4, bf16[256,384]{1,0:T(8,128)(2,1)S(1)} %bitcast.21), custom_call_target="tpu_custom_call" | custom-call | tf_op jit(solution)/shard_map/time_attention/pallas_call | solution.py:574
  26.8 0.0 copy-start
  26.8 0.0 copy-start.1
  26.8 3.6 %all-to-all-start.1 = ((bf16[32,16,384]{2,1,0:T(8,128)(2,1)}), bf16[32,16,384]{2,1,0:T(8,128)(2,1)S(1)}, u32[]{:S(2)}, u32[]{:S(2)}) async-start(bf16[32,16,384]{2,1,0:T(8,128)(2,1)} %bitcast.4), calls=%async_computation.1 | async-start | bytes 786432 | tf_op jit(solution)/shard_map/all_to_all | solution.py:617
  30.5 0.0 copy-done
  30.5 0.5 cotangent_heads.1
  31.0 12.6 %all-to-all-done.1 = bf16[32,16,384]{2,1,0:T(8,128)(2,1)S(1)} async-done(((bf16[32,16,384]{2,1,0:T(8,128)(2,1)}), bf16[32,16,384]{2,1,0:T(8,128)(2,1)S(1)}, u32[]{:S(2)}, u32[]{:S(2)}) %all-to-all-start.1) | async-done | bytes 393248 | tf_op jit(solution)/shard_map/all_to_all | solution.py:617
  43.6 0.0 copy-done.1
  43.6 4.8 %column_attention.1 = (bf16[512,384]{1,0:T(8,128)(2,1)S(1)}, bf16[2,8,144,128]{3,2,1,0:T(8,128)(2,1)S(1)}, bf16[2,8,144,128]{3,2,1,0:T(8,128)(2,1)S(1)}) custom-call(s32[1]{0:T(128)} %bitcast.refs_0_.row_ref, s32[1]{0:T(128)} %bitcast.6.pair_ref, bf16[512,384]{1,0:T(8,128)(2,1)S(1)} %bitcast.17, ...), custom_call_target="tpu_custom_call", output_to_operand_aliasing={{0}: (4, {})} | custom-call | tf_op jit(solution)/shard_map/column_attention/pallas_call | solution.py:641
  48.4 0.1 collective-permute-start.1
  48.5 2.0 %collective-permute-done.1.came_ref = bf16[2,8,144,128]{3,2,1,0:T(8,128)(2,1)S(1)} collective-permute-done((bf16[2,8,144,128]{3,2,1,0:T(8,128)(2,1)S(1)}, bf16[2,8,144,128]{3,2,1,0:T(8,128)(2,1)S(1)}, u32[]{:S(2)}, u32[]{:S(2)}) %collective-permute-start.1) | collective-permute-done | bytes 589856 | tf_op jit(solution)/shard_map/ppermute | solution.py:658
  50.5 0.1 pair_gradients.1
  50.6 1.5 %collective-permute-start.2 = (bf16[4,144,128]{2,1,0:T(8,128)(2,1)S(1)}, bf16[4,144,128]{2,1,0:T(8,128)(2,1)S(1)}, u32[]{:S(2)}, u32[]{:S(2)}) collective-permute-start(bf16[4,144,128]{2,1,0:T(8,128)(2,1)S(1)} %get-tuple-element.28), channel_id=1, source_target_pairs={{0,4},{4,0},{1,5},{5,1},{2,6},{6,2},{3,7},{7,3},{8,12},{12,8},{9,1... | collective-permute-start | bytes 442376 | tf_op jit(solution)/shard_map/ppermute | solution.py:671
  52.2 0.5 collective-permute-start.3
  52.7 1.5 %collective-permute-start.4 = (bf16[4,144,128]{2,1,0:T(8,128)(2,1)S(1)}, bf16[4,144,128]{2,1,0:T(8,128)(2,1)S(1)}, u32[]{:S(2)}, u32[]{:S(2)}) collective-permute-start(bf16[4,144,128]{2,1,0:T(8,128)(2,1)S(1)} %get-tuple-element.30), channel_id=1, source_target_pairs={{0,5},{5,0},{1,4},{4,1},{2,7},{7,2},{3,6},{6,3},{8,13},{13,8},{9,1... | collective-permute-start | bytes 442376 | tf_op jit(solution)/shard_map/ppermute | solution.py:670
  54.2 0.7 mixed_tokens.1
  54.8 2.4 %collective-permute-done.2.mid_ref = bf16[4,144,128]{2,1,0:T(8,128)(2,1)S(1)} collective-permute-done((bf16[4,144,128]{2,1,0:T(8,128)(2,1)S(1)}, bf16[4,144,128]{2,1,0:T(8,128)(2,1)S(1)}, u32[]{:S(2)}, u32[]{:S(2)}) %collective-permute-start.2) | collective-permute-done | bytes 147488 | tf_op jit(solution)/shard_map/ppermute | solution.py:671
  57.3 3.7 %collective-permute-done.3.row_ref = bf16[4,144,128]{2,1,0:T(8,128)(2,1)S(1)} collective-permute-done((bf16[4,144,128]{2,1,0:T(8,128)(2,1)S(1)}, bf16[4,144,128]{2,1,0:T(8,128)(2,1)S(1)}, u32[]{:S(2)}, u32[]{:S(2)}) %collective-permute-start.3) | collective-permute-done | bytes 147488 | tf_op jit(solution)/shard_map/ppermute | solution.py:672
  60.9 0.0 collective-permute-done.4.both_ref
  60.9 0.1 spread_gradients.1
  61.0 0.6 collective-permute-start.5
  61.6 0.6 collective-permute-start.6
  62.3 1.6 %collective-permute-start.7 = (bf16[144,128]{1,0:T(8,128)(2,1)S(1)}, bf16[144,128]{1,0:T(8,128)(2,1)S(1)}, u32[]{:S(2)}, u32[]{:S(2)}) collective-permute-start(bf16[144,128]{1,0:T(8,128)(2,1)S(1)} %get-tuple-element.35), channel_id=1, source_target_pairs={{0,16},{8,24},{16,0},{24,8},{1,17},{9,25},{17,1},{25,9},{2,18},{10... | collective-permute-start | bytes 110600 | tf_op jit(solution)/shard_map/ppermute | solution.py:697
  63.8 2.2 %collective-permute-start.8 = (bf16[144,128]{1,0:T(8,128)(2,1)S(1)}, bf16[144,128]{1,0:T(8,128)(2,1)S(1)}, u32[]{:S(2)}, u32[]{:S(2)}) collective-permute-start(bf16[144,128]{1,0:T(8,128)(2,1)S(1)} %get-tuple-element.36), channel_id=1, source_target_pairs={{0,24},{8,16},{16,8},{24,0},{1,25},{9,17},{17,9},{25,1},{2,26},{10... | collective-permute-start | bytes 110600 | tf_op jit(solution)/shard_map/ppermute | solution.py:697
  66.0 0.7 %collective-permute-done.5 = bf16[256,384]{1,0:T(8,128)(2,1)S(1)} collective-permute-done((bf16[256,384]{1,0:T(8,128)(2,1)S(1)}, bf16[256,384]{1,0:T(8,128)(2,1)S(1)}, u32[]{:S(2)}, u32[]{:S(2)}) %collective-permute-start.5) | collective-permute-done | bytes 196640 | tf_op jit(solution)/shard_map/ppermute | solution.py:698
  66.8 0.8 %pad_maximum_fusion = (bf16[2,16,2,8,384]{4,3,2,1,0:T(8,128)(2,1)S(1)}, bf16[2,16,16,384]{3,2,1,0:T(8,128)(2,1)}) fusion(bf16[2,16,1,8,384]{4,3,2,1,0:T(8,128)(2,1)S(1)} %bitcast.24, bf16[2,16,1,8,384]{4,3,2,1,0:T(8,128)(2,1)S(1)} %bitcast.23), kind=kLoop, calls=%fused_computation | loop fusion | flops 196608 | bytes 1179648 | tf_op jit(solution)/shard_map/concatenate | solution.py:701
  67.6 0.0 collective-permute-done.6.refs_1_
  67.6 0.0 collective-permute-done.7.refs_2_
  67.6 2.0 %collective-permute-done.8.refs_3_ = bf16[144,128]{1,0:T(8,128)(2,1)S(1)} collective-permute-done((bf16[144,128]{1,0:T(8,128)(2,1)S(1)}, bf16[144,128]{1,0:T(8,128)(2,1)S(1)}, u32[]{:S(2)}, u32[]{:S(2)}) %collective-permute-start.8) | collective-permute-done | bytes 36896 | tf_op jit(solution)/shard_map/ppermute | solution.py:697
  69.6 0.7 %gradient_sum.1 = (f32[72,192]{1,0:T(8,128)}, f32[24,192]{1,0:T(8,128)}) custom-call(s32[1]{0:T(128)} %bitcast.refs_0_.row_ref, bf16[144,128]{1,0:T(8,128)(2,1)S(1)} %get-tuple-element.33.refs_0_, bf16[144,128]{1,0:T(8,128)(2,1)S(1)} %collective-permute-done.6.refs_1_, bf16[144,128]{1,0:T(8,128)(2,1)S(1)} %collective-permute-done.7.refs_2_, ...), custom_call_target="tpu_custom_call" | custom-call | tf_op jit(solution)/shard_map/gradient_sum/pallas_call | solution.py:704
  (2 shorter events, 0.1 us)
Async XLA Ops:
  0.6 22.1 %copy-start.2 = (bf16[384,1152]{1,0:T(8,128)(2,1)S(1)}, bf16[384,1152]{1,0:T(8,128)(2,1)}, u32[]{:S(2)}) copy-start(bf16[384,1152]{1,0:T(8,128)(2,1)} %project_ref.2) | copy-start | bytes 2654212
  2.5 7.5 %copy-start.3 = (bf16[2,16,16,384]{3,2,1,0:T(8,128)(2,1)S(1)}, bf16[2,16,16,384]{3,2,1,0:T(8,128)(2,1)}, u32[]{:S(2)}) copy-start(bf16[2,16,16,384]{3,2,1,0:T(8,128)(2,1)} %param.17) | copy-start | bytes 1179652
  2.5 20.2 %all-to-all-start = ((bf16[16,104,128]{2,1,0:T(8,128)(2,1)}), bf16[16,104,128]{2,1,0:T(8,128)(2,1)S(1)}, u32[]{:S(2)}, u32[]{:S(2)}) async-start(bf16[16,104,128]{2,1,0:T(8,128)(2,1)} %pack_tokens.1), calls=%async_computation | async-start | bytes 851968 | tf_op jit(solution)/shard_map/all_to_all | solution.py:557
  10.1 12.7 %copy-start.4 = (bf16[384,384]{1,0:T(8,128)(2,1)S(1)}, bf16[384,384]{1,0:T(8,128)(2,1)}, u32[]{:S(2)}) copy-start(bf16[384,384]{1,0:T(8,128)(2,1)} %output_ref.2) | copy-start | bytes 884740
  10.1 12.7 %copy-start.5 = (f32[12]{0:T(128)S(1)}, f32[12]{0:T(128)}, u32[]{:S(2)}) copy-start(f32[12]{0:T(128)} %slopes_ref.1) | copy-start | bytes 148
  10.1 7.3 %collective-permute-start = (bf16[2,16,8,384]{3,2,1,0:T(8,128)(2,1)S(1)}, bf16[2,16,8,384]{3,2,1,0:T(8,128)(2,1)S(1)}, u32[]{:S(2)}, u32[]{:S(2)}) collective-permute-start(bf16[2,16,8,384]{3,2,1,0:T(8,128)(2,1)S(1)} %dynamic-slice_bitcast_fusion), channel_id=1, source_target_pairs={{0,1},{1,0},{2,3},{3,2},{4,5},{5,4},{6,7},{7,6},{8,9},{9,8},{10,11... | collective-permute-start | bytes 589832 | tf_op jit(solution)/shard_map/ppermute | solution.py:542
  26.8 3.7 %copy-start = (bf16[384,384]{1,0:T(8,128)(2,1)S(1)}, bf16[384,384]{1,0:T(8,128)(2,1)}, u32[]{:S(2)}) copy-start(bf16[384,384]{1,0:T(8,128)(2,1)} %output_ref.3) | copy-start | bytes 884740
  26.8 16.8 %copy-start.1 = (bf16[384,1152]{1,0:T(8,128)(2,1)S(1)}, bf16[384,1152]{1,0:T(8,128)(2,1)}, u32[]{:S(2)}) copy-start(bf16[384,1152]{1,0:T(8,128)(2,1)} %project_ref.3) | copy-start | bytes 2654212
  26.8 16.8 %all-to-all-start.1 = ((bf16[32,16,384]{2,1,0:T(8,128)(2,1)}), bf16[32,16,384]{2,1,0:T(8,128)(2,1)S(1)}, u32[]{:S(2)}, u32[]{:S(2)}) async-start(bf16[32,16,384]{2,1,0:T(8,128)(2,1)} %bitcast.4), calls=%async_computation.1 | async-start | bytes 786432 | tf_op jit(solution)/shard_map/all_to_all | solution.py:617
  48.4 2.1 %collective-permute-start.1 = (bf16[2,8,144,128]{3,2,1,0:T(8,128)(2,1)S(1)}, bf16[2,8,144,128]{3,2,1,0:T(8,128)(2,1)S(1)}, u32[]{:S(2)}, u32[]{:S(2)}) collective-permute-start(bf16[2,8,144,128]{3,2,1,0:T(8,128)(2,1)S(1)} %get-tuple-element.25), channel_id=1, source_target_pairs={{0,2},{2,0},{1,3},{3,1},{4,6},{6,4},{5,7},{7,5},{8,10},{10,8},{9,1... | collective-permute-start | bytes 1769480 | tf_op jit(solution)/shard_map/ppermute | solution.py:658
  50.6 6.7 %collective-permute-start.2 = (bf16[4,144,128]{2,1,0:T(8,128)(2,1)S(1)}, bf16[4,144,128]{2,1,0:T(8,128)(2,1)S(1)}, u32[]{:S(2)}, u32[]{:S(2)}) collective-permute-start(bf16[4,144,128]{2,1,0:T(8,128)(2,1)S(1)} %get-tuple-element.28), channel_id=1, source_target_pairs={{0,4},{4,0},{1,5},{5,1},{2,6},{6,2},{3,7},{7,3},{8,12},{12,8},{9,1... | collective-permute-start | bytes 442376 | tf_op jit(solution)/shard_map/ppermute | solution.py:671
  52.2 8.8 %collective-permute-start.3 = (bf16[4,144,128]{2,1,0:T(8,128)(2,1)S(1)}, bf16[4,144,128]{2,1,0:T(8,128)(2,1)S(1)}, u32[]{:S(2)}, u32[]{:S(2)}) collective-permute-start(bf16[4,144,128]{2,1,0:T(8,128)(2,1)S(1)} %get-tuple-element.29), channel_id=1, source_target_pairs={{0,1},{1,0},{2,3},{3,2},{4,5},{5,4},{6,7},{7,6},{8,9},{9,8},{10,11... | collective-permute-start | bytes 442376 | tf_op jit(solution)/shard_map/ppermute | solution.py:672
  52.7 8.2 %collective-permute-start.4 = (bf16[4,144,128]{2,1,0:T(8,128)(2,1)S(1)}, bf16[4,144,128]{2,1,0:T(8,128)(2,1)S(1)}, u32[]{:S(2)}, u32[]{:S(2)}) collective-permute-start(bf16[4,144,128]{2,1,0:T(8,128)(2,1)S(1)} %get-tuple-element.30), channel_id=1, source_target_pairs={{0,5},{5,0},{1,4},{4,1},{2,7},{7,2},{3,6},{6,3},{8,13},{13,8},{9,1... | collective-permute-start | bytes 442376 | tf_op jit(solution)/shard_map/ppermute | solution.py:670
  61.0 5.7 %collective-permute-start.5 = (bf16[256,384]{1,0:T(8,128)(2,1)S(1)}, bf16[256,384]{1,0:T(8,128)(2,1)S(1)}, u32[]{:S(2)}, u32[]{:S(2)}) collective-permute-start(bf16[256,384]{1,0:T(8,128)(2,1)S(1)} %get-tuple-element.32), channel_id=1, source_target_pairs={{0,1},{1,0},{2,3},{3,2},{4,5},{5,4},{6,7},{7,6},{8,9},{9,8},{10,11... | collective-permute-start | bytes 589832 | tf_op jit(solution)/shard_map/ppermute | solution.py:698
  61.6 6.0 %collective-permute-start.6 = (bf16[144,128]{1,0:T(8,128)(2,1)S(1)}, bf16[144,128]{1,0:T(8,128)(2,1)S(1)}, u32[]{:S(2)}, u32[]{:S(2)}) collective-permute-start(bf16[144,128]{1,0:T(8,128)(2,1)S(1)} %get-tuple-element.34), channel_id=1, source_target_pairs={{0,8},{8,0},{16,24},{24,16},{1,9},{9,1},{17,25},{25,17},{2,10},{10... | collective-permute-start | bytes 110600 | tf_op jit(solution)/shard_map/ppermute | solution.py:697
  62.3 5.4 %collective-permute-start.7 = (bf16[144,128]{1,0:T(8,128)(2,1)S(1)}, bf16[144,128]{1,0:T(8,128)(2,1)S(1)}, u32[]{:S(2)}, u32[]{:S(2)}) collective-permute-start(bf16[144,128]{1,0:T(8,128)(2,1)S(1)} %get-tuple-element.35), channel_id=1, source_target_pairs={{0,16},{8,24},{16,0},{24,8},{1,17},{9,25},{17,1},{25,9},{2,18},{10... | collective-permute-start | bytes 110600 | tf_op jit(solution)/shard_map/ppermute | solution.py:697
  63.8 5.8 %collective-permute-start.8 = (bf16[144,128]{1,0:T(8,128)(2,1)S(1)}, bf16[144,128]{1,0:T(8,128)(2,1)S(1)}, u32[]{:S(2)}, u32[]{:S(2)}) collective-permute-start(bf16[144,128]{1,0:T(8,128)(2,1)S(1)} %get-tuple-element.36), channel_id=1, source_target_pairs={{0,24},{8,16},{16,8},{24,0},{1,25},{9,17},{17,9},{25,1},{2,26},{10... | collective-permute-start | bytes 110600 | tf_op jit(solution)/shard_map/ppermute | solution.py:697

commit v13 on v11

--- a/solution.py
+++ b/solution.py
@@ -434,11 +434,11 @@
             )
 
 
-def spread_kernel(outer_ref, own_ref, mid_ref, row_ref, both_ref, sent_ref, leave_ref, *refs):
+def spread_kernel(outer_ref, own_ref, row_ref, both_ref, mid_ref, sent_ref, leave_ref, *refs):
     leave_ref[...] = sent_ref[...]
     count = own_ref.shape[0]
     for step in range(count):
-        at = (outer_ref[0] + step) % count
+        at = outer_ref[0] ^ step
         total = own_ref[at].astype(wide) + mid_ref[at].astype(wide)
         total = total + (row_ref[at].astype(wide) + both_ref[at].astype(wide))
         refs[step][...] = total.astype(low)
@@ -492,6 +492,7 @@
         patches_each == column_count
         and column_count % 16 == 0
         and date_size % 8 == 0
+        and date_size & (date_size - 1) == 0
         and row_size == 2
         and lane_each == 192
         and project_each % 8 == 0
@@ -653,9 +654,9 @@
             compiler_params=params,
             name="pair_gradients",
         )(row_one, lax.axis_index("mid").reshape(1), first_grad, came)
+        row_grad = lax.ppermute(row_grad, "row", swap)
         both_grad = lax.ppermute(both_grad, ("mid", "row"), [(0, 3), (3, 0), (1, 2), (2, 1)])
         mid_grad = lax.ppermute(mid_grad, "mid", swap)
-        row_grad = lax.ppermute(row_grad, "row", swap)
     mixed = pl.pallas_call(
         functools.partial(mixed_kernel, sizes),
         out_shape=mixed_shapes,
@@ -676,10 +677,10 @@
             in_specs=[in_smem] + [in_vmem] * 5,
             compiler_params=params,
             name="spread_gradients",
-        )(lax.axis_index("outer").reshape(1), own_grad, mid_grad, row_grad, both_grad, sent)
+        )(lax.axis_index("outer").reshape(1), own_grad, row_grad, both_grad, mid_grad, sent)
         terms = [steps[0]]
-        for step in range(1, outers):
-            route = [(at, (at + step) % outers) for at in range(outers)]
+        for step in range(outers - 1, 0, -1):
+            route = [(at, at ^ step) for at in range(outers)]
             terms.append(lax.ppermute(steps[step], "outer", route))
         arrived = lax.ppermute(leaving, "row", swap)
         quarter = (date_local, row_local, 1, columns_each, width)

time: 69.1 us -> 69.9 us (1.012)
  starting transfers between devices: 20.8 us -> 21.8 us
    ppermute x1, waiting for transfers between devices: 3.65 us -> 4.88 us  [body(): row_grad = lax.ppermute(row_grad, 'row', swap)]
    ppermute x1, waiting for transfers between devices: 2.43 us -> 1.23 us  [body(): mid_grad = lax.ppermute(mid_grad, 'mid', swap)]
    ppermute x1, starting transfers between devices: 1.54 us -> 0.55 us  [body(): mid_grad = lax.ppermute(mid_grad, 'mid', swap)]
    ppermute x1, waiting for transfers between devices: 1.31 us -> 0.45 us  [body(): arrived = lax.ppermute(leaving, 'row', swap)]
  transfers between devices with their start and end apart: 11 -> 11, of which waited for: 8 -> 10; matrix products, arithmetic and copies ran while one was open for 1% -> 1% of each run, Pallas kernels for 2% -> 2%
where the time goes in v13:
time: 69.9 us; the launch traced here: 69.6 us
  waiting for transfers between devices  33.2 us (47%)
  starting transfers between devices  21.8 us (31%)
  Pallas kernels  12.8 us (18%)
  other arithmetic  0.86 us (1%)
  between operations  0.78 us (1%)
    all_to_all x1, waiting for transfers between devices, body(): lax.all_to_all(parts, ('row', *dates), split_axis=0, concat_axis=0, tiled...  12.6 us
    all_to_all x1, starting transfers between devices, body(): lax.all_to_all(outgoing, dates, split_axis=0, concat_axis=0, tiled=True)  7.5 us
    ppermute x1, waiting for transfers between devices, body(): other_grad = lax.ppermute(leaving, 'row', swap)  5.72 us
    all_to_all x1, waiting for transfers between devices, body(): lax.all_to_all(outgoing, dates, split_axis=0, concat_axis=0, tiled=True)  5.35 us
    ppermute x1, waiting for transfers between devices, body(): row_grad = lax.ppermute(row_grad, 'row', swap)  4.88 us
    pallas_call x1, Pallas kernels, body(): pl.pallas_call(functools.partial(column_kernel, (*sizes, head_count, pack...  4.82 us
    ppermute x3, starting transfers between devices, body(): terms.append(lax.ppermute(steps[step], 'outer', route))  4.39 us
    pallas_call x1, Pallas kernels, body(): pl.pallas_call(functools.partial(time_kernel, (date_size, date_local, pat...  4.05 us
  transfers between devices with their start and end apart: 11, of which 10 were waited for; matrix products, arithmetic and copies ran while one was open for 1% of the time, Pallas kernels for 2%

profile of v13, /device:TPU:0, one launch (start us, length us, event | category | flops | bytes accessed | tf_op | source)
XLA Modules:
  0.0 69.6 jit_solution(4787241810928796955)
XLA Ops:
  0.6 0.0 copy-start.2
  0.6 1.9 %pack_tokens.1 = bf16[16,104,128]{2,1,0:T(8,128)(2,1)} custom-call(s32[2]{0:T(128)} %numbers_ref.1, bf16[2,16,16,384]{3,2,1,0:T(8,128)(2,1)} %tokens_ref.1, s32[2,16,16]{2,1,0:T(8,128)} %flags_ref.1), custom_call_target="tpu_custom_call" | custom-call | tf_op jit(solution)/shard_map/pack_tokens/pallas_call | solution.py:513
  2.5 0.0 copy-start.3
  2.5 7.5 %all-to-all-start = ((bf16[16,104,128]{2,1,0:T(8,128)(2,1)}), bf16[16,104,128]{2,1,0:T(8,128)(2,1)S(1)}, u32[]{:S(2)}, u32[]{:S(2)}) async-start(bf16[16,104,128]{2,1,0:T(8,128)(2,1)} %pack_tokens.1), calls=%async_computation | async-start | bytes 851968 | tf_op jit(solution)/shard_map/all_to_all | solution.py:547
  10.1 0.0 copy-start.4
  10.1 0.0 copy-done.3
  10.1 0.0 copy-start.5
  10.1 1.6 %collective-permute-start = (bf16[2,16,8,384]{3,2,1,0:T(8,128)(2,1)S(1)}, bf16[2,16,8,384]{3,2,1,0:T(8,128)(2,1)S(1)}, u32[]{:S(2)}, u32[]{:S(2)}) collective-permute-start(bf16[2,16,8,384]{3,2,1,0:T(8,128)(2,1)S(1)} %dynamic-slice_bitcast_fusion), channel_id=1, source_target_pairs={{0,1},{1,0},{2,3},{3,2},{4,5},{5,4},{6,7},{7,6},{8,9},{9,8},{10,11... | collective-permute-start | bytes 589832 | tf_op jit(solution)/shard_map/ppermute | solution.py:532
  11.7 5.7 %collective-permute-done = bf16[2,16,8,384]{3,2,1,0:T(8,128)(2,1)S(1)} collective-permute-done((bf16[2,16,8,384]{3,2,1,0:T(8,128)(2,1)S(1)}, bf16[2,16,8,384]{3,2,1,0:T(8,128)(2,1)S(1)}, u32[]{:S(2)}, u32[]{:S(2)}) %collective-permute-start) | collective-permute-done | bytes 196640 | tf_op jit(solution)/shard_map/ppermute | solution.py:532
  17.4 5.3 %all-to-all-done.block_ref = bf16[16,104,128]{2,1,0:T(8,128)(2,1)S(1)} async-done(((bf16[16,104,128]{2,1,0:T(8,128)(2,1)}), bf16[16,104,128]{2,1,0:T(8,128)(2,1)S(1)}, u32[]{:S(2)}, u32[]{:S(2)}) %all-to-all-start) | async-done | bytes 426016 | tf_op jit(solution)/shard_map/all_to_all | solution.py:547
  22.8 0.0 copy-done.2
  22.8 0.0 copy-done.4
  22.8 0.0 copy-done.5
  22.8 4.0 %time_attention.1.refs_4_ = bf16[512,384]{1,0:T(8,128)(2,1)} custom-call(f32[12]{0:T(128)S(1)} %copy-done.5, bf16[16,104,128]{2,1,0:T(8,128)(2,1)S(1)} %all-to-all-done.block_ref, bf16[384,1152]{1,0:T(8,128)(2,1)S(1)} %copy-done.2, bf16[384,384]{1,0:T(8,128)(2,1)S(1)} %copy-done.4, bf16[256,384]{1,0:T(8,128)(2,1)S(1)} %bitcast.21), custom_call_target="tpu_custom_call" | custom-call | tf_op jit(solution)/shard_map/time_attention/pallas_call | solution.py:564
  26.8 0.0 copy-start
  26.8 0.0 copy-start.1
  26.8 3.6 %all-to-all-start.1 = ((bf16[32,16,384]{2,1,0:T(8,128)(2,1)}), bf16[32,16,384]{2,1,0:T(8,128)(2,1)S(1)}, u32[]{:S(2)}, u32[]{:S(2)}) async-start(bf16[32,16,384]{2,1,0:T(8,128)(2,1)} %bitcast.4), calls=%async_computation.1 | async-start | bytes 786432 | tf_op jit(solution)/shard_map/all_to_all | solution.py:604
  30.5 0.0 copy-done
  30.5 0.5 cotangent_heads.1
  31.0 12.6 %all-to-all-done.1 = bf16[32,16,384]{2,1,0:T(8,128)(2,1)S(1)} async-done(((bf16[32,16,384]{2,1,0:T(8,128)(2,1)}), bf16[32,16,384]{2,1,0:T(8,128)(2,1)S(1)}, u32[]{:S(2)}, u32[]{:S(2)}) %all-to-all-start.1) | async-done | bytes 393248 | tf_op jit(solution)/shard_map/all_to_all | solution.py:604
  43.6 0.0 copy-done.1
  43.6 4.8 %column_attention.1 = (bf16[512,384]{1,0:T(8,128)(2,1)S(1)}, bf16[2,8,144,128]{3,2,1,0:T(8,128)(2,1)S(1)}, bf16[2,8,144,128]{3,2,1,0:T(8,128)(2,1)S(1)}) custom-call(s32[1]{0:T(128)} %bitcast.refs_0_.row_ref, s32[1]{0:T(128)} %bitcast.6.pair_ref, bf16[512,384]{1,0:T(8,128)(2,1)S(1)} %bitcast.17, ...), custom_call_target="tpu_custom_call", output_to_operand_aliasing={{0}: (4, {})} | custom-call | tf_op jit(solution)/shard_map/column_attention/pallas_call | solution.py:628
  48.4 0.1 collective-permute-start.1
  48.5 2.0 %collective-permute-done.1.came_ref = bf16[2,8,144,128]{3,2,1,0:T(8,128)(2,1)S(1)} collective-permute-done((bf16[2,8,144,128]{3,2,1,0:T(8,128)(2,1)S(1)}, bf16[2,8,144,128]{3,2,1,0:T(8,128)(2,1)S(1)}, u32[]{:S(2)}, u32[]{:S(2)}) %collective-permute-start.1) | collective-permute-done | bytes 589856 | tf_op jit(solution)/shard_map/ppermute | solution.py:645
  50.5 0.1 pair_gradients.1
  50.6 1.1 %collective-permute-start.2 = (bf16[4,144,128]{2,1,0:T(8,128)(2,1)S(1)}, bf16[4,144,128]{2,1,0:T(8,128)(2,1)S(1)}, u32[]{:S(2)}, u32[]{:S(2)}) collective-permute-start(bf16[4,144,128]{2,1,0:T(8,128)(2,1)S(1)} %get-tuple-element.28), channel_id=1, source_target_pairs={{0,1},{1,0},{2,3},{3,2},{4,5},{5,4},{6,7},{7,6},{8,9},{9,8},{10,11... | collective-permute-start | bytes 442376 | tf_op jit(solution)/shard_map/ppermute | solution.py:657
  51.7 1.9 %collective-permute-start.3 = (bf16[4,144,128]{2,1,0:T(8,128)(2,1)S(1)}, bf16[4,144,128]{2,1,0:T(8,128)(2,1)S(1)}, u32[]{:S(2)}, u32[]{:S(2)}) collective-permute-start(bf16[4,144,128]{2,1,0:T(8,128)(2,1)S(1)} %get-tuple-element.29), channel_id=1, source_target_pairs={{0,5},{5,0},{1,4},{4,1},{2,7},{7,2},{3,6},{6,3},{8,13},{13,8},{9,1... | collective-permute-start | bytes 442376 | tf_op jit(solution)/shard_map/ppermute | solution.py:658
  53.6 0.5 collective-permute-start.4
  54.2 0.7 mixed_tokens.1
  54.9 4.9 %collective-permute-done.2.row_ref = bf16[4,144,128]{2,1,0:T(8,128)(2,1)S(1)} collective-permute-done((bf16[4,144,128]{2,1,0:T(8,128)(2,1)S(1)}, bf16[4,144,128]{2,1,0:T(8,128)(2,1)S(1)}, u32[]{:S(2)}, u32[]{:S(2)}) %collective-permute-start.2) | collective-permute-done | bytes 147488 | tf_op jit(solution)/shard_map/ppermute | solution.py:657
  59.7 0.0 collective-permute-done.3.both_ref
  59.7 1.2 %collective-permute-done.4.mid_ref = bf16[4,144,128]{2,1,0:T(8,128)(2,1)S(1)} collective-permute-done((bf16[4,144,128]{2,1,0:T(8,128)(2,1)S(1)}, bf16[4,144,128]{2,1,0:T(8,128)(2,1)S(1)}, u32[]{:S(2)}, u32[]{:S(2)}) %collective-permute-start.4) | collective-permute-done | bytes 147488 | tf_op jit(solution)/shard_map/ppermute | solution.py:659
  61.0 0.1 spread_gradients.1
  61.1 1.1 %collective-permute-start.5 = (bf16[256,384]{1,0:T(8,128)(2,1)S(1)}, bf16[256,384]{1,0:T(8,128)(2,1)S(1)}, u32[]{:S(2)}, u32[]{:S(2)}) collective-permute-start(bf16[256,384]{1,0:T(8,128)(2,1)S(1)} %get-tuple-element.32), channel_id=1, source_target_pairs={{0,1},{1,0},{2,3},{3,2},{4,5},{5,4},{6,7},{7,6},{8,9},{9,8},{10,11... | collective-permute-start | bytes 589832 | tf_op jit(solution)/shard_map/ppermute | solution.py:685
  62.1 1.5 %collective-permute-start.6 = (bf16[144,128]{1,0:T(8,128)(2,1)S(1)}, bf16[144,128]{1,0:T(8,128)(2,1)S(1)}, u32[]{:S(2)}, u32[]{:S(2)}) collective-permute-start(bf16[144,128]{1,0:T(8,128)(2,1)S(1)} %get-tuple-element.34), channel_id=1, source_target_pairs={{0,24},{8,16},{16,8},{24,0},{1,25},{9,17},{17,9},{25,1},{2,26},{10... | collective-permute-start | bytes 110600 | tf_op jit(solution)/shard_map/ppermute | solution.py:684
  63.6 0.9 %collective-permute-start.7 = (bf16[144,128]{1,0:T(8,128)(2,1)S(1)}, bf16[144,128]{1,0:T(8,128)(2,1)S(1)}, u32[]{:S(2)}, u32[]{:S(2)}) collective-permute-start(bf16[144,128]{1,0:T(8,128)(2,1)S(1)} %get-tuple-element.35), channel_id=1, source_target_pairs={{0,16},{8,24},{16,0},{24,8},{1,17},{9,25},{17,1},{25,9},{2,18},{10... | collective-permute-start | bytes 110600 | tf_op jit(solution)/shard_map/ppermute | solution.py:684
  64.5 2.0 %collective-permute-start.8 = (bf16[144,128]{1,0:T(8,128)(2,1)S(1)}, bf16[144,128]{1,0:T(8,128)(2,1)S(1)}, u32[]{:S(2)}, u32[]{:S(2)}) collective-permute-start(bf16[144,128]{1,0:T(8,128)(2,1)S(1)} %get-tuple-element.36), channel_id=1, source_target_pairs={{0,8},{8,0},{16,24},{24,16},{1,9},{9,1},{17,25},{25,17},{2,10},{10... | collective-permute-start | bytes 110600 | tf_op jit(solution)/shard_map/ppermute | solution.py:684
  66.5 0.4 collective-permute-done.5
  67.0 0.8 %pad_maximum_fusion = (bf16[2,16,2,8,384]{4,3,2,1,0:T(8,128)(2,1)S(1)}, bf16[2,16,16,384]{3,2,1,0:T(8,128)(2,1)}) fusion(bf16[2,16,1,8,384]{4,3,2,1,0:T(8,128)(2,1)S(1)} %bitcast.24, bf16[2,16,1,8,384]{4,3,2,1,0:T(8,128)(2,1)S(1)} %bitcast.23), kind=kLoop, calls=%fused_computation | loop fusion | flops 196608 | bytes 1179648 | tf_op jit(solution)/shard_map/concatenate | solution.py:688
  67.8 0.1 collective-permute-done.6.refs_1_
  67.9 0.9 %collective-permute-done.7.refs_2_ = bf16[144,128]{1,0:T(8,128)(2,1)S(1)} collective-permute-done((bf16[144,128]{1,0:T(8,128)(2,1)S(1)}, bf16[144,128]{1,0:T(8,128)(2,1)S(1)}, u32[]{:S(2)}, u32[]{:S(2)}) %collective-permute-start.7) | collective-permute-done | bytes 36896 | tf_op jit(solution)/shard_map/ppermute | solution.py:684
  68.8 0.1 collective-permute-done.8.refs_3_
  68.9 0.7 %gradient_sum.1 = (f32[72,192]{1,0:T(8,128)}, f32[24,192]{1,0:T(8,128)}) custom-call(s32[1]{0:T(128)} %bitcast.refs_0_.row_ref, bf16[144,128]{1,0:T(8,128)(2,1)S(1)} %get-tuple-element.33.refs_0_, bf16[144,128]{1,0:T(8,128)(2,1)S(1)} %collective-permute-done.6.refs_1_, bf16[144,128]{1,0:T(8,128)(2,1)S(1)} %collective-permute-done.7.refs_2_, ...), custom_call_target="tpu_custom_call" | custom-call | tf_op jit(solution)/shard_map/gradient_sum/pallas_call | solution.py:691
  (2 shorter events, 0.1 us)
Async XLA Ops:
  0.6 22.1 %copy-start.2 = (bf16[384,1152]{1,0:T(8,128)(2,1)S(1)}, bf16[384,1152]{1,0:T(8,128)(2,1)}, u32[]{:S(2)}) copy-start(bf16[384,1152]{1,0:T(8,128)(2,1)} %project_ref.2) | copy-start | bytes 2654212
  2.5 7.5 %copy-start.3 = (bf16[2,16,16,384]{3,2,1,0:T(8,128)(2,1)S(1)}, bf16[2,16,16,384]{3,2,1,0:T(8,128)(2,1)}, u32[]{:S(2)}) copy-start(bf16[2,16,16,384]{3,2,1,0:T(8,128)(2,1)} %param.17) | copy-start | bytes 1179652
  2.5 20.2 %all-to-all-start = ((bf16[16,104,128]{2,1,0:T(8,128)(2,1)}), bf16[16,104,128]{2,1,0:T(8,128)(2,1)S(1)}, u32[]{:S(2)}, u32[]{:S(2)}) async-start(bf16[16,104,128]{2,1,0:T(8,128)(2,1)} %pack_tokens.1), calls=%async_computation | async-start | bytes 851968 | tf_op jit(solution)/shard_map/all_to_all | solution.py:547
  10.1 12.7 %copy-start.4 = (bf16[384,384]{1,0:T(8,128)(2,1)S(1)}, bf16[384,384]{1,0:T(8,128)(2,1)}, u32[]{:S(2)}) copy-start(bf16[384,384]{1,0:T(8,128)(2,1)} %output_ref.2) | copy-start | bytes 884740
  10.1 12.7 %copy-start.5 = (f32[12]{0:T(128)S(1)}, f32[12]{0:T(128)}, u32[]{:S(2)}) copy-start(f32[12]{0:T(128)} %slopes_ref.1) | copy-start | bytes 148
  10.1 7.3 %collective-permute-start = (bf16[2,16,8,384]{3,2,1,0:T(8,128)(2,1)S(1)}, bf16[2,16,8,384]{3,2,1,0:T(8,128)(2,1)S(1)}, u32[]{:S(2)}, u32[]{:S(2)}) collective-permute-start(bf16[2,16,8,384]{3,2,1,0:T(8,128)(2,1)S(1)} %dynamic-slice_bitcast_fusion), channel_id=1, source_target_pairs={{0,1},{1,0},{2,3},{3,2},{4,5},{5,4},{6,7},{7,6},{8,9},{9,8},{10,11... | collective-permute-start | bytes 589832 | tf_op jit(solution)/shard_map/ppermute | solution.py:532
  26.8 3.7 %copy-start = (bf16[384,384]{1,0:T(8,128)(2,1)S(1)}, bf16[384,384]{1,0:T(8,128)(2,1)}, u32[]{:S(2)}) copy-start(bf16[384,384]{1,0:T(8,128)(2,1)} %output_ref.3) | copy-start | bytes 884740
  26.8 16.8 %copy-start.1 = (bf16[384,1152]{1,0:T(8,128)(2,1)S(1)}, bf16[384,1152]{1,0:T(8,128)(2,1)}, u32[]{:S(2)}) copy-start(bf16[384,1152]{1,0:T(8,128)(2,1)} %project_ref.3) | copy-start | bytes 2654212
  26.8 16.7 %all-to-all-start.1 = ((bf16[32,16,384]{2,1,0:T(8,128)(2,1)}), bf16[32,16,384]{2,1,0:T(8,128)(2,1)S(1)}, u32[]{:S(2)}, u32[]{:S(2)}) async-start(bf16[32,16,384]{2,1,0:T(8,128)(2,1)} %bitcast.4), calls=%async_computation.1 | async-start | bytes 786432 | tf_op jit(solution)/shard_map/all_to_all | solution.py:604
  48.4 2.1 %collective-permute-start.1 = (bf16[2,8,144,128]{3,2,1,0:T(8,128)(2,1)S(1)}, bf16[2,8,144,128]{3,2,1,0:T(8,128)(2,1)S(1)}, u32[]{:S(2)}, u32[]{:S(2)}) collective-permute-start(bf16[2,8,144,128]{3,2,1,0:T(8,128)(2,1)S(1)} %get-tuple-element.25), channel_id=1, source_target_pairs={{0,2},{2,0},{1,3},{3,1},{4,6},{6,4},{5,7},{7,5},{8,10},{10,8},{9,1... | collective-permute-start | bytes 1769480 | tf_op jit(solution)/shard_map/ppermute | solution.py:645
  50.6 9.1 %collective-permute-start.2 = (bf16[4,144,128]{2,1,0:T(8,128)(2,1)S(1)}, bf16[4,144,128]{2,1,0:T(8,128)(2,1)S(1)}, u32[]{:S(2)}, u32[]{:S(2)}) collective-permute-start(bf16[4,144,128]{2,1,0:T(8,128)(2,1)S(1)} %get-tuple-element.28), channel_id=1, source_target_pairs={{0,1},{1,0},{2,3},{3,2},{4,5},{5,4},{6,7},{7,6},{8,9},{9,8},{10,11... | collective-permute-start | bytes 442376 | tf_op jit(solution)/shard_map/ppermute | solution.py:657
  51.7 8.0 %collective-permute-start.3 = (bf16[4,144,128]{2,1,0:T(8,128)(2,1)S(1)}, bf16[4,144,128]{2,1,0:T(8,128)(2,1)S(1)}, u32[]{:S(2)}, u32[]{:S(2)}) collective-permute-start(bf16[4,144,128]{2,1,0:T(8,128)(2,1)S(1)} %get-tuple-element.29), channel_id=1, source_target_pairs={{0,5},{5,0},{1,4},{4,1},{2,7},{7,2},{3,6},{6,3},{8,13},{13,8},{9,1... | collective-permute-start | bytes 442376 | tf_op jit(solution)/shard_map/ppermute | solution.py:658
  53.6 7.3 %collective-permute-start.4 = (bf16[4,144,128]{2,1,0:T(8,128)(2,1)S(1)}, bf16[4,144,128]{2,1,0:T(8,128)(2,1)S(1)}, u32[]{:S(2)}, u32[]{:S(2)}) collective-permute-start(bf16[4,144,128]{2,1,0:T(8,128)(2,1)S(1)} %get-tuple-element.30), channel_id=1, source_target_pairs={{0,4},{4,0},{1,5},{5,1},{2,6},{6,2},{3,7},{7,3},{8,12},{12,8},{9,1... | collective-permute-start | bytes 442376 | tf_op jit(solution)/shard_map/ppermute | solution.py:659
  61.1 5.9 %collective-permute-start.5 = (bf16[256,384]{1,0:T(8,128)(2,1)S(1)}, bf16[256,384]{1,0:T(8,128)(2,1)S(1)}, u32[]{:S(2)}, u32[]{:S(2)}) collective-permute-start(bf16[256,384]{1,0:T(8,128)(2,1)S(1)} %get-tuple-element.32), channel_id=1, source_target_pairs={{0,1},{1,0},{2,3},{3,2},{4,5},{5,4},{6,7},{7,6},{8,9},{9,8},{10,11... | collective-permute-start | bytes 589832 | tf_op jit(solution)/shard_map/ppermute | solution.py:685
  62.1 5.8 %collective-permute-start.6 = (bf16[144,128]{1,0:T(8,128)(2,1)S(1)}, bf16[144,128]{1,0:T(8,128)(2,1)S(1)}, u32[]{:S(2)}, u32[]{:S(2)}) collective-permute-start(bf16[144,128]{1,0:T(8,128)(2,1)S(1)} %get-tuple-element.34), channel_id=1, source_target_pairs={{0,24},{8,16},{16,8},{24,0},{1,25},{9,17},{17,9},{25,1},{2,26},{10... | collective-permute-start | bytes 110600 | tf_op jit(solution)/shard_map/ppermute | solution.py:684
  63.6 5.2 %collective-permute-start.7 = (bf16[144,128]{1,0:T(8,128)(2,1)S(1)}, bf16[144,128]{1,0:T(8,128)(2,1)S(1)}, u32[]{:S(2)}, u32[]{:S(2)}) collective-permute-start(bf16[144,128]{1,0:T(8,128)(2,1)S(1)} %get-tuple-element.35), channel_id=1, source_target_pairs={{0,16},{8,24},{16,0},{24,8},{1,17},{9,25},{17,1},{25,9},{2,18},{10... | collective-permute-start | bytes 110600 | tf_op jit(solution)/shard_map/ppermute | solution.py:684
  64.5 4.4 %collective-permute-start.8 = (bf16[144,128]{1,0:T(8,128)(2,1)S(1)}, bf16[144,128]{1,0:T(8,128)(2,1)S(1)}, u32[]{:S(2)}, u32[]{:S(2)}) collective-permute-start(bf16[144,128]{1,0:T(8,128)(2,1)S(1)} %get-tuple-element.36), channel_id=1, source_target_pairs={{0,8},{8,0},{16,24},{24,16},{1,9},{9,1},{17,25},{25,17},{2,10},{10... | collective-permute-start | bytes 110600 | tf_op jit(solution)/shard_map/ppermute | solution.py:684

commit v14 on v11

--- a/solution.py
+++ b/solution.py
@@ -11,7 +11,7 @@
 epsilon = 1e-06
 masked_score = -1e30
 time_units = 48
-column_units = 24
+column_units = 48
 dates = ("outer", "mid", "pair")
 vmem_limit = 12 * 1024 * 1024
 low = jnp.bfloat16

time: 69.1 us -> 69 us (level)
  no operation moved by 1% of the time
where the time goes in v14:
time: 69 us; the launch traced here: 68.7 us
  waiting for transfers between devices  33.5 us (49%)
  starting transfers between devices  20.8 us (30%)
  Pallas kernels  12.8 us (19%)
  other arithmetic  0.86 us (1%)
  between operations  0.78 us (1%)
    all_to_all x1, waiting for transfers between devices, body(): lax.all_to_all(parts, ('row', *dates), split_axis=0, concat_axis=0, tiled...  12.6 us
    all_to_all x1, starting transfers between devices, body(): lax.all_to_all(outgoing, dates, split_axis=0, concat_axis=0, tiled=True)  7.5 us
    ppermute x1, waiting for transfers between devices, body(): other_grad = lax.ppermute(leaving, 'row', swap)  5.72 us
    all_to_all x1, waiting for transfers between devices, body(): lax.all_to_all(outgoing, dates, split_axis=0, concat_axis=0, tiled=True)  5.35 us
    pallas_call x1, Pallas kernels, body(): pl.pallas_call(functools.partial(column_kernel, (*sizes, head_count, pack...  4.78 us
    pallas_call x1, Pallas kernels, body(): pl.pallas_call(functools.partial(time_kernel, (date_size, date_local, pat...  4.05 us
    ppermute x3, starting transfers between devices, body(): terms.append(lax.ppermute(steps[step], 'outer', route))  3.83 us
    ppermute x1, waiting for transfers between devices, body(): row_grad = lax.ppermute(row_grad, 'row', swap)  3.65 us
  transfers between devices with their start and end apart: 11, of which 8 were waited for; matrix products, arithmetic and copies ran while one was open for 1% of the time, Pallas kernels for 2%

profile of v14, /device:TPU:0, one launch (start us, length us, event | category | flops | bytes accessed | tf_op | source)
XLA Modules:
  0.0 68.7 jit_solution(9422442459433803029)
XLA Ops:
  0.6 0.0 copy-start.2
  0.6 1.9 %pack_tokens.1 = bf16[16,104,128]{2,1,0:T(8,128)(2,1)} custom-call(s32[2]{0:T(128)} %numbers_ref.1, bf16[2,16,16,384]{3,2,1,0:T(8,128)(2,1)} %tokens_ref.1, s32[2,16,16]{2,1,0:T(8,128)} %flags_ref.1), custom_call_target="tpu_custom_call" | custom-call | tf_op jit(solution)/shard_map/pack_tokens/pallas_call | solution.py:512
  2.5 0.0 copy-start.3
  2.5 7.5 %all-to-all-start = ((bf16[16,104,128]{2,1,0:T(8,128)(2,1)}), bf16[16,104,128]{2,1,0:T(8,128)(2,1)S(1)}, u32[]{:S(2)}, u32[]{:S(2)}) async-start(bf16[16,104,128]{2,1,0:T(8,128)(2,1)} %pack_tokens.1), calls=%async_computation | async-start | bytes 851968 | tf_op jit(solution)/shard_map/all_to_all | solution.py:546
  10.1 0.0 copy-start.4
  10.1 0.0 copy-done.3
  10.1 0.0 copy-start.5
  10.1 1.6 %collective-permute-start = (bf16[2,16,8,384]{3,2,1,0:T(8,128)(2,1)S(1)}, bf16[2,16,8,384]{3,2,1,0:T(8,128)(2,1)S(1)}, u32[]{:S(2)}, u32[]{:S(2)}) collective-permute-start(bf16[2,16,8,384]{3,2,1,0:T(8,128)(2,1)S(1)} %dynamic-slice_bitcast_fusion), channel_id=1, source_target_pairs={{0,1},{1,0},{2,3},{3,2},{4,5},{5,4},{6,7},{7,6},{8,9},{9,8},{10,11... | collective-permute-start | bytes 589832 | tf_op jit(solution)/shard_map/ppermute | solution.py:531
  11.7 5.7 %collective-permute-done = bf16[2,16,8,384]{3,2,1,0:T(8,128)(2,1)S(1)} collective-permute-done((bf16[2,16,8,384]{3,2,1,0:T(8,128)(2,1)S(1)}, bf16[2,16,8,384]{3,2,1,0:T(8,128)(2,1)S(1)}, u32[]{:S(2)}, u32[]{:S(2)}) %collective-permute-start) | collective-permute-done | bytes 196640 | tf_op jit(solution)/shard_map/ppermute | solution.py:531
  17.4 5.3 %all-to-all-done.block_ref = bf16[16,104,128]{2,1,0:T(8,128)(2,1)S(1)} async-done(((bf16[16,104,128]{2,1,0:T(8,128)(2,1)}), bf16[16,104,128]{2,1,0:T(8,128)(2,1)S(1)}, u32[]{:S(2)}, u32[]{:S(2)}) %all-to-all-start) | async-done | bytes 426016 | tf_op jit(solution)/shard_map/all_to_all | solution.py:546
  22.8 0.0 copy-done.2
  22.8 0.0 copy-done.4
  22.8 0.0 copy-done.5
  22.8 4.0 %time_attention.1.refs_4_ = bf16[512,384]{1,0:T(8,128)(2,1)} custom-call(f32[12]{0:T(128)S(1)} %copy-done.5, bf16[16,104,128]{2,1,0:T(8,128)(2,1)S(1)} %all-to-all-done.block_ref, bf16[384,1152]{1,0:T(8,128)(2,1)S(1)} %copy-done.2, bf16[384,384]{1,0:T(8,128)(2,1)S(1)} %copy-done.4, bf16[256,384]{1,0:T(8,128)(2,1)S(1)} %bitcast.21), custom_call_target="tpu_custom_call" | custom-call | tf_op jit(solution)/shard_map/time_attention/pallas_call | solution.py:563
  26.8 0.0 copy-start
  26.8 0.0 copy-start.1
  26.8 3.6 %all-to-all-start.1 = ((bf16[32,16,384]{2,1,0:T(8,128)(2,1)}), bf16[32,16,384]{2,1,0:T(8,128)(2,1)S(1)}, u32[]{:S(2)}, u32[]{:S(2)}) async-start(bf16[32,16,384]{2,1,0:T(8,128)(2,1)} %bitcast.4), calls=%async_computation.1 | async-start | bytes 786432 | tf_op jit(solution)/shard_map/all_to_all | solution.py:603
  30.5 0.0 copy-done
  30.5 0.5 cotangent_heads.1
  31.0 12.6 %all-to-all-done.1 = bf16[32,16,384]{2,1,0:T(8,128)(2,1)S(1)} async-done(((bf16[32,16,384]{2,1,0:T(8,128)(2,1)}), bf16[32,16,384]{2,1,0:T(8,128)(2,1)S(1)}, u32[]{:S(2)}, u32[]{:S(2)}) %all-to-all-start.1) | async-done | bytes 393248 | tf_op jit(solution)/shard_map/all_to_all | solution.py:603
  43.6 0.0 copy-done.1
  43.6 4.8 %column_attention.1 = (bf16[512,384]{1,0:T(8,128)(2,1)S(1)}, bf16[2,8,144,128]{3,2,1,0:T(8,128)(2,1)S(1)}, bf16[2,8,144,128]{3,2,1,0:T(8,128)(2,1)S(1)}) custom-call(s32[1]{0:T(128)} %bitcast.refs_0_.row_ref, s32[1]{0:T(128)} %bitcast.6.pair_ref, bf16[512,384]{1,0:T(8,128)(2,1)S(1)} %bitcast.17, ...), custom_call_target="tpu_custom_call", output_to_operand_aliasing={{0}: (4, {})} | custom-call | tf_op jit(solution)/shard_map/column_attention/pallas_call | solution.py:627
  48.4 0.1 collective-permute-start.1
  48.5 2.0 %collective-permute-done.1.came_ref = bf16[2,8,144,128]{3,2,1,0:T(8,128)(2,1)S(1)} collective-permute-done((bf16[2,8,144,128]{3,2,1,0:T(8,128)(2,1)S(1)}, bf16[2,8,144,128]{3,2,1,0:T(8,128)(2,1)S(1)}, u32[]{:S(2)}, u32[]{:S(2)}) %collective-permute-start.1) | collective-permute-done | bytes 589856 | tf_op jit(solution)/shard_map/ppermute | solution.py:644
  50.4 0.1 pair_gradients.1
  50.6 1.5 %collective-permute-start.2 = (bf16[4,144,128]{2,1,0:T(8,128)(2,1)S(1)}, bf16[4,144,128]{2,1,0:T(8,128)(2,1)S(1)}, u32[]{:S(2)}, u32[]{:S(2)}) collective-permute-start(bf16[4,144,128]{2,1,0:T(8,128)(2,1)S(1)} %get-tuple-element.28), channel_id=1, source_target_pairs={{0,4},{4,0},{1,5},{5,1},{2,6},{6,2},{3,7},{7,3},{8,12},{12,8},{9,1... | collective-permute-start | bytes 442376 | tf_op jit(solution)/shard_map/ppermute | solution.py:657
  52.1 0.5 collective-permute-start.3
  52.7 1.5 %collective-permute-start.4 = (bf16[4,144,128]{2,1,0:T(8,128)(2,1)S(1)}, bf16[4,144,128]{2,1,0:T(8,128)(2,1)S(1)}, u32[]{:S(2)}, u32[]{:S(2)}) collective-permute-start(bf16[4,144,128]{2,1,0:T(8,128)(2,1)S(1)} %get-tuple-element.30), channel_id=1, source_target_pairs={{0,5},{5,0},{1,4},{4,1},{2,7},{7,2},{3,6},{6,3},{8,13},{13,8},{9,1... | collective-permute-start | bytes 442376 | tf_op jit(solution)/shard_map/ppermute | solution.py:656
  54.1 0.7 mixed_tokens.1
  54.8 2.4 %collective-permute-done.2.mid_ref = bf16[4,144,128]{2,1,0:T(8,128)(2,1)S(1)} collective-permute-done((bf16[4,144,128]{2,1,0:T(8,128)(2,1)S(1)}, bf16[4,144,128]{2,1,0:T(8,128)(2,1)S(1)}, u32[]{:S(2)}, u32[]{:S(2)}) %collective-permute-start.2) | collective-permute-done | bytes 147488 | tf_op jit(solution)/shard_map/ppermute | solution.py:657
  57.2 3.7 %collective-permute-done.3.row_ref = bf16[4,144,128]{2,1,0:T(8,128)(2,1)S(1)} collective-permute-done((bf16[4,144,128]{2,1,0:T(8,128)(2,1)S(1)}, bf16[4,144,128]{2,1,0:T(8,128)(2,1)S(1)}, u32[]{:S(2)}, u32[]{:S(2)}) %collective-permute-start.3) | collective-permute-done | bytes 147488 | tf_op jit(solution)/shard_map/ppermute | solution.py:658
  60.9 0.0 collective-permute-done.4.both_ref
  60.9 0.1 spread_gradients.1
  61.0 0.6 collective-permute-start.5
  61.6 0.6 collective-permute-start.6
  62.2 1.6 %collective-permute-start.7 = (bf16[144,128]{1,0:T(8,128)(2,1)S(1)}, bf16[144,128]{1,0:T(8,128)(2,1)S(1)}, u32[]{:S(2)}, u32[]{:S(2)}) collective-permute-start(bf16[144,128]{1,0:T(8,128)(2,1)S(1)} %get-tuple-element.35), channel_id=1, source_target_pairs={{0,16},{8,24},{16,0},{24,8},{1,17},{9,25},{17,1},{25,9},{2,18},{10... | collective-permute-start | bytes 110600 | tf_op jit(solution)/shard_map/ppermute | solution.py:683
  63.8 1.6 %collective-permute-start.8 = (bf16[144,128]{1,0:T(8,128)(2,1)S(1)}, bf16[144,128]{1,0:T(8,128)(2,1)S(1)}, u32[]{:S(2)}, u32[]{:S(2)}) collective-permute-start(bf16[144,128]{1,0:T(8,128)(2,1)S(1)} %get-tuple-element.36), channel_id=1, source_target_pairs={{0,24},{8,0},{16,8},{24,16},{1,25},{9,1},{17,9},{25,17},{2,26},{10... | collective-permute-start | bytes 110600 | tf_op jit(solution)/shard_map/ppermute | solution.py:683
  65.4 1.3 %collective-permute-done.5 = bf16[256,384]{1,0:T(8,128)(2,1)S(1)} collective-permute-done((bf16[256,384]{1,0:T(8,128)(2,1)S(1)}, bf16[256,384]{1,0:T(8,128)(2,1)S(1)}, u32[]{:S(2)}, u32[]{:S(2)}) %collective-permute-start.5) | collective-permute-done | bytes 196640 | tf_op jit(solution)/shard_map/ppermute | solution.py:684
  66.8 0.8 %pad_maximum_fusion = (bf16[2,16,2,8,384]{4,3,2,1,0:T(8,128)(2,1)S(1)}, bf16[2,16,16,384]{3,2,1,0:T(8,128)(2,1)}) fusion(bf16[2,16,1,8,384]{4,3,2,1,0:T(8,128)(2,1)S(1)} %bitcast.24, bf16[2,16,1,8,384]{4,3,2,1,0:T(8,128)(2,1)S(1)} %bitcast.23), kind=kLoop, calls=%fused_computation | loop fusion | flops 196608 | bytes 1179648 | tf_op jit(solution)/shard_map/concatenate | solution.py:687
  67.6 0.0 collective-permute-done.6.refs_1_
  67.6 0.4 collective-permute-done.7.refs_2_
  68.0 0.0 collective-permute-done.8.refs_3_
  68.0 0.7 %gradient_sum.1 = (f32[72,192]{1,0:T(8,128)}, f32[24,192]{1,0:T(8,128)}) custom-call(s32[1]{0:T(128)} %bitcast.refs_0_.row_ref, bf16[144,128]{1,0:T(8,128)(2,1)S(1)} %get-tuple-element.33.refs_0_, bf16[144,128]{1,0:T(8,128)(2,1)S(1)} %collective-permute-done.6.refs_1_, bf16[144,128]{1,0:T(8,128)(2,1)S(1)} %collective-permute-done.7.refs_2_, ...), custom_call_target="tpu_custom_call" | custom-call | tf_op jit(solution)/shard_map/gradient_sum/pallas_call | solution.py:690
  (2 shorter events, 0.1 us)
Async XLA Ops:
  0.6 22.1 %copy-start.2 = (bf16[384,1152]{1,0:T(8,128)(2,1)S(1)}, bf16[384,1152]{1,0:T(8,128)(2,1)}, u32[]{:S(2)}) copy-start(bf16[384,1152]{1,0:T(8,128)(2,1)} %project_ref.2) | copy-start | bytes 2654212
  2.5 7.5 %copy-start.3 = (bf16[2,16,16,384]{3,2,1,0:T(8,128)(2,1)S(1)}, bf16[2,16,16,384]{3,2,1,0:T(8,128)(2,1)}, u32[]{:S(2)}) copy-start(bf16[2,16,16,384]{3,2,1,0:T(8,128)(2,1)} %param.17) | copy-start | bytes 1179652
  2.5 20.2 %all-to-all-start = ((bf16[16,104,128]{2,1,0:T(8,128)(2,1)}), bf16[16,104,128]{2,1,0:T(8,128)(2,1)S(1)}, u32[]{:S(2)}, u32[]{:S(2)}) async-start(bf16[16,104,128]{2,1,0:T(8,128)(2,1)} %pack_tokens.1), calls=%async_computation | async-start | bytes 851968 | tf_op jit(solution)/shard_map/all_to_all | solution.py:546
  10.1 12.7 %copy-start.4 = (bf16[384,384]{1,0:T(8,128)(2,1)S(1)}, bf16[384,384]{1,0:T(8,128)(2,1)}, u32[]{:S(2)}) copy-start(bf16[384,384]{1,0:T(8,128)(2,1)} %output_ref.2) | copy-start | bytes 884740
  10.1 12.7 %copy-start.5 = (f32[12]{0:T(128)S(1)}, f32[12]{0:T(128)}, u32[]{:S(2)}) copy-start(f32[12]{0:T(128)} %slopes_ref.1) | copy-start | bytes 148
  10.1 7.3 %collective-permute-start = (bf16[2,16,8,384]{3,2,1,0:T(8,128)(2,1)S(1)}, bf16[2,16,8,384]{3,2,1,0:T(8,128)(2,1)S(1)}, u32[]{:S(2)}, u32[]{:S(2)}) collective-permute-start(bf16[2,16,8,384]{3,2,1,0:T(8,128)(2,1)S(1)} %dynamic-slice_bitcast_fusion), channel_id=1, source_target_pairs={{0,1},{1,0},{2,3},{3,2},{4,5},{5,4},{6,7},{7,6},{8,9},{9,8},{10,11... | collective-permute-start | bytes 589832 | tf_op jit(solution)/shard_map/ppermute | solution.py:531
  26.8 3.7 %copy-start = (bf16[384,384]{1,0:T(8,128)(2,1)S(1)}, bf16[384,384]{1,0:T(8,128)(2,1)}, u32[]{:S(2)}) copy-start(bf16[384,384]{1,0:T(8,128)(2,1)} %output_ref.3) | copy-start | bytes 884740
  26.8 16.8 %copy-start.1 = (bf16[384,1152]{1,0:T(8,128)(2,1)S(1)}, bf16[384,1152]{1,0:T(8,128)(2,1)}, u32[]{:S(2)}) copy-start(bf16[384,1152]{1,0:T(8,128)(2,1)} %project_ref.3) | copy-start | bytes 2654212
  26.8 16.7 %all-to-all-start.1 = ((bf16[32,16,384]{2,1,0:T(8,128)(2,1)}), bf16[32,16,384]{2,1,0:T(8,128)(2,1)S(1)}, u32[]{:S(2)}, u32[]{:S(2)}) async-start(bf16[32,16,384]{2,1,0:T(8,128)(2,1)} %bitcast.4), calls=%async_computation.1 | async-start | bytes 786432 | tf_op jit(solution)/shard_map/all_to_all | solution.py:603
  48.4 2.1 %collective-permute-start.1 = (bf16[2,8,144,128]{3,2,1,0:T(8,128)(2,1)S(1)}, bf16[2,8,144,128]{3,2,1,0:T(8,128)(2,1)S(1)}, u32[]{:S(2)}, u32[]{:S(2)}) collective-permute-start(bf16[2,8,144,128]{3,2,1,0:T(8,128)(2,1)S(1)} %get-tuple-element.25), channel_id=1, source_target_pairs={{0,2},{2,0},{1,3},{3,1},{4,6},{6,4},{5,7},{7,5},{8,10},{10,8},{9,1... | collective-permute-start | bytes 1769480 | tf_op jit(solution)/shard_map/ppermute | solution.py:644
  50.6 6.7 %collective-permute-start.2 = (bf16[4,144,128]{2,1,0:T(8,128)(2,1)S(1)}, bf16[4,144,128]{2,1,0:T(8,128)(2,1)S(1)}, u32[]{:S(2)}, u32[]{:S(2)}) collective-permute-start(bf16[4,144,128]{2,1,0:T(8,128)(2,1)S(1)} %get-tuple-element.28), channel_id=1, source_target_pairs={{0,4},{4,0},{1,5},{5,1},{2,6},{6,2},{3,7},{7,3},{8,12},{12,8},{9,1... | collective-permute-start | bytes 442376 | tf_op jit(solution)/shard_map/ppermute | solution.py:657
  52.1 8.8 %collective-permute-start.3 = (bf16[4,144,128]{2,1,0:T(8,128)(2,1)S(1)}, bf16[4,144,128]{2,1,0:T(8,128)(2,1)S(1)}, u32[]{:S(2)}, u32[]{:S(2)}) collective-permute-start(bf16[4,144,128]{2,1,0:T(8,128)(2,1)S(1)} %get-tuple-element.29), channel_id=1, source_target_pairs={{0,1},{1,0},{2,3},{3,2},{4,5},{5,4},{6,7},{7,6},{8,9},{9,8},{10,11... | collective-permute-start | bytes 442376 | tf_op jit(solution)/shard_map/ppermute | solution.py:658
  52.7 8.2 %collective-permute-start.4 = (bf16[4,144,128]{2,1,0:T(8,128)(2,1)S(1)}, bf16[4,144,128]{2,1,0:T(8,128)(2,1)S(1)}, u32[]{:S(2)}, u32[]{:S(2)}) collective-permute-start(bf16[4,144,128]{2,1,0:T(8,128)(2,1)S(1)} %get-tuple-element.30), channel_id=1, source_target_pairs={{0,5},{5,0},{1,4},{4,1},{2,7},{7,2},{3,6},{6,3},{8,13},{13,8},{9,1... | collective-permute-start | bytes 442376 | tf_op jit(solution)/shard_map/ppermute | solution.py:656
  61.0 5.7 %collective-permute-start.5 = (bf16[256,384]{1,0:T(8,128)(2,1)S(1)}, bf16[256,384]{1,0:T(8,128)(2,1)S(1)}, u32[]{:S(2)}, u32[]{:S(2)}) collective-permute-start(bf16[256,384]{1,0:T(8,128)(2,1)S(1)} %get-tuple-element.32), channel_id=1, source_target_pairs={{0,1},{1,0},{2,3},{3,2},{4,5},{5,4},{6,7},{7,6},{8,9},{9,8},{10,11... | collective-permute-start | bytes 589832 | tf_op jit(solution)/shard_map/ppermute | solution.py:684
  61.6 6.0 %collective-permute-start.6 = (bf16[144,128]{1,0:T(8,128)(2,1)S(1)}, bf16[144,128]{1,0:T(8,128)(2,1)S(1)}, u32[]{:S(2)}, u32[]{:S(2)}) collective-permute-start(bf16[144,128]{1,0:T(8,128)(2,1)S(1)} %get-tuple-element.34), channel_id=1, source_target_pairs={{0,8},{8,16},{16,24},{24,0},{1,9},{9,17},{17,25},{25,1},{2,10},{10... | collective-permute-start | bytes 110600 | tf_op jit(solution)/shard_map/ppermute | solution.py:683
  62.2 5.8 %collective-permute-start.7 = (bf16[144,128]{1,0:T(8,128)(2,1)S(1)}, bf16[144,128]{1,0:T(8,128)(2,1)S(1)}, u32[]{:S(2)}, u32[]{:S(2)}) collective-permute-start(bf16[144,128]{1,0:T(8,128)(2,1)S(1)} %get-tuple-element.35), channel_id=1, source_target_pairs={{0,16},{8,24},{16,0},{24,8},{1,17},{9,25},{17,1},{25,9},{2,18},{10... | collective-permute-start | bytes 110600 | tf_op jit(solution)/shard_map/ppermute | solution.py:683
  63.8 4.2 %collective-permute-start.8 = (bf16[144,128]{1,0:T(8,128)(2,1)S(1)}, bf16[144,128]{1,0:T(8,128)(2,1)S(1)}, u32[]{:S(2)}, u32[]{:S(2)}) collective-permute-start(bf16[144,128]{1,0:T(8,128)(2,1)S(1)} %get-tuple-element.36), channel_id=1, source_target_pairs={{0,24},{8,0},{16,8},{24,16},{1,25},{9,1},{17,9},{25,17},{2,26},{10... | collective-permute-start | bytes 110600 | tf_op jit(solution)/shard_map/ppermute | solution.py:683

commit v15 on v11

--- a/solution.py
+++ b/solution.py
@@ -678,7 +678,7 @@
             name="spread_gradients",
         )(lax.axis_index("outer").reshape(1), own_grad, mid_grad, row_grad, both_grad, sent)
         terms = [steps[0]]
-        for step in range(1, outers):
+        for step in sorted(range(1, outers), key=lambda step: abs(step - outers // 2)):
             route = [(at, (at + step) % outers) for at in range(outers)]
             terms.append(lax.ppermute(steps[step], "outer", route))
         arrived = lax.ppermute(leaving, "row", swap)

time: 69.1 us -> 69.2 us (level)
  transfers between devices with their start and end apart: 11 -> 11, of which waited for: 8 -> 9; matrix products, arithmetic and copies ran while one was open for 1% -> 1% of each run, Pallas kernels for 2% -> 2%
where the time goes in v15:
time: 69.2 us; the launch traced here: 68.9 us
  waiting for transfers between devices  33.1 us (48%)
  starting transfers between devices  21.3 us (31%)
  Pallas kernels  12.8 us (18%)
  other arithmetic  0.86 us (1%)
  between operations  0.78 us (1%)
    all_to_all x1, waiting for transfers between devices, body(): lax.all_to_all(parts, ('row', *dates), split_axis=0, concat_axis=0, tiled...  12.6 us
    all_to_all x1, starting transfers between devices, body(): lax.all_to_all(outgoing, dates, split_axis=0, concat_axis=0, tiled=True)  7.5 us
    ppermute x1, waiting for transfers between devices, body(): other_grad = lax.ppermute(leaving, 'row', swap)  5.72 us
    all_to_all x1, waiting for transfers between devices, body(): lax.all_to_all(outgoing, dates, split_axis=0, concat_axis=0, tiled=True)  5.35 us
    pallas_call x1, Pallas kernels, body(): pl.pallas_call(functools.partial(column_kernel, (*sizes, head_count, pack...  4.82 us
    ppermute x3, starting transfers between devices, body(): terms.append(lax.ppermute(steps[step], 'outer', route))  4.34 us
    pallas_call x1, Pallas kernels, body(): pl.pallas_call(functools.partial(time_kernel, (date_size, date_local, pat...  4.05 us
    ppermute x1, waiting for transfers between devices, body(): row_grad = lax.ppermute(row_grad, 'row', swap)  3.65 us
  transfers between devices with their start and end apart: 11, of which 9 were waited for; matrix products, arithmetic and copies ran while one was open for 1% of the time, Pallas kernels for 2%

profile of v15, /device:TPU:0, one launch (start us, length us, event | category | flops | bytes accessed | tf_op | source)
XLA Modules:
  0.0 68.9 jit_solution(14577951695329548410)
XLA Ops:
  0.6 0.0 copy-start.2
  0.6 1.9 %pack_tokens.1 = bf16[16,104,128]{2,1,0:T(8,128)(2,1)} custom-call(s32[2]{0:T(128)} %numbers_ref.1, bf16[2,16,16,384]{3,2,1,0:T(8,128)(2,1)} %tokens_ref.1, s32[2,16,16]{2,1,0:T(8,128)} %flags_ref.1), custom_call_target="tpu_custom_call" | custom-call | tf_op jit(solution)/shard_map/pack_tokens/pallas_call | solution.py:512
  2.5 0.0 copy-start.3
  2.5 7.5 %all-to-all-start = ((bf16[16,104,128]{2,1,0:T(8,128)(2,1)}), bf16[16,104,128]{2,1,0:T(8,128)(2,1)S(1)}, u32[]{:S(2)}, u32[]{:S(2)}) async-start(bf16[16,104,128]{2,1,0:T(8,128)(2,1)} %pack_tokens.1), calls=%async_computation | async-start | bytes 851968 | tf_op jit(solution)/shard_map/all_to_all | solution.py:546
  10.1 0.0 copy-start.4
  10.1 0.0 copy-done.3
  10.1 0.0 copy-start.5
  10.1 1.6 %collective-permute-start = (bf16[2,16,8,384]{3,2,1,0:T(8,128)(2,1)S(1)}, bf16[2,16,8,384]{3,2,1,0:T(8,128)(2,1)S(1)}, u32[]{:S(2)}, u32[]{:S(2)}) collective-permute-start(bf16[2,16,8,384]{3,2,1,0:T(8,128)(2,1)S(1)} %dynamic-slice_bitcast_fusion), channel_id=1, source_target_pairs={{0,1},{1,0},{2,3},{3,2},{4,5},{5,4},{6,7},{7,6},{8,9},{9,8},{10,11... | collective-permute-start | bytes 589832 | tf_op jit(solution)/shard_map/ppermute | solution.py:531
  11.7 5.7 %collective-permute-done = bf16[2,16,8,384]{3,2,1,0:T(8,128)(2,1)S(1)} collective-permute-done((bf16[2,16,8,384]{3,2,1,0:T(8,128)(2,1)S(1)}, bf16[2,16,8,384]{3,2,1,0:T(8,128)(2,1)S(1)}, u32[]{:S(2)}, u32[]{:S(2)}) %collective-permute-start) | collective-permute-done | bytes 196640 | tf_op jit(solution)/shard_map/ppermute | solution.py:531
  17.4 5.3 %all-to-all-done.block_ref = bf16[16,104,128]{2,1,0:T(8,128)(2,1)S(1)} async-done(((bf16[16,104,128]{2,1,0:T(8,128)(2,1)}), bf16[16,104,128]{2,1,0:T(8,128)(2,1)S(1)}, u32[]{:S(2)}, u32[]{:S(2)}) %all-to-all-start) | async-done | bytes 426016 | tf_op jit(solution)/shard_map/all_to_all | solution.py:546
  22.8 0.0 copy-done.2
  22.8 0.0 copy-done.4
  22.8 0.0 copy-done.5
  22.8 4.0 %time_attention.1.refs_4_ = bf16[512,384]{1,0:T(8,128)(2,1)} custom-call(f32[12]{0:T(128)S(1)} %copy-done.5, bf16[16,104,128]{2,1,0:T(8,128)(2,1)S(1)} %all-to-all-done.block_ref, bf16[384,1152]{1,0:T(8,128)(2,1)S(1)} %copy-done.2, bf16[384,384]{1,0:T(8,128)(2,1)S(1)} %copy-done.4, bf16[256,384]{1,0:T(8,128)(2,1)S(1)} %bitcast.21), custom_call_target="tpu_custom_call" | custom-call | tf_op jit(solution)/shard_map/time_attention/pallas_call | solution.py:563
  26.8 0.0 copy-start
  26.8 0.0 copy-start.1
  26.8 3.6 %all-to-all-start.1 = ((bf16[32,16,384]{2,1,0:T(8,128)(2,1)}), bf16[32,16,384]{2,1,0:T(8,128)(2,1)S(1)}, u32[]{:S(2)}, u32[]{:S(2)}) async-start(bf16[32,16,384]{2,1,0:T(8,128)(2,1)} %bitcast.4), calls=%async_computation.1 | async-start | bytes 786432 | tf_op jit(solution)/shard_map/all_to_all | solution.py:603
  30.5 0.0 copy-done
  30.5 0.5 cotangent_heads.1
  31.0 12.6 %all-to-all-done.1 = bf16[32,16,384]{2,1,0:T(8,128)(2,1)S(1)} async-done(((bf16[32,16,384]{2,1,0:T(8,128)(2,1)}), bf16[32,16,384]{2,1,0:T(8,128)(2,1)S(1)}, u32[]{:S(2)}, u32[]{:S(2)}) %all-to-all-start.1) | async-done | bytes 393248 | tf_op jit(solution)/shard_map/all_to_all | solution.py:603
  43.6 0.0 copy-done.1
  43.6 4.8 %column_attention.1 = (bf16[512,384]{1,0:T(8,128)(2,1)S(1)}, bf16[2,8,144,128]{3,2,1,0:T(8,128)(2,1)S(1)}, bf16[2,8,144,128]{3,2,1,0:T(8,128)(2,1)S(1)}) custom-call(s32[1]{0:T(128)} %bitcast.refs_0_.row_ref, s32[1]{0:T(128)} %bitcast.6.pair_ref, bf16[512,384]{1,0:T(8,128)(2,1)S(1)} %bitcast.17, ...), custom_call_target="tpu_custom_call", output_to_operand_aliasing={{0}: (4, {})} | custom-call | tf_op jit(solution)/shard_map/column_attention/pallas_call | solution.py:627
  48.4 0.1 collective-permute-start.1
  48.5 2.0 %collective-permute-done.1.came_ref = bf16[2,8,144,128]{3,2,1,0:T(8,128)(2,1)S(1)} collective-permute-done((bf16[2,8,144,128]{3,2,1,0:T(8,128)(2,1)S(1)}, bf16[2,8,144,128]{3,2,1,0:T(8,128)(2,1)S(1)}, u32[]{:S(2)}, u32[]{:S(2)}) %collective-permute-start.1) | collective-permute-done | bytes 589856 | tf_op jit(solution)/shard_map/ppermute | solution.py:644
  50.5 0.1 pair_gradients.1
  50.6 1.5 %collective-permute-start.2 = (bf16[4,144,128]{2,1,0:T(8,128)(2,1)S(1)}, bf16[4,144,128]{2,1,0:T(8,128)(2,1)S(1)}, u32[]{:S(2)}, u32[]{:S(2)}) collective-permute-start(bf16[4,144,128]{2,1,0:T(8,128)(2,1)S(1)} %get-tuple-element.28), channel_id=1, source_target_pairs={{0,4},{4,0},{1,5},{5,1},{2,6},{6,2},{3,7},{7,3},{8,12},{12,8},{9,1... | collective-permute-start | bytes 442376 | tf_op jit(solution)/shard_map/ppermute | solution.py:657
  52.2 0.5 collective-permute-start.3
  52.7 1.5 %collective-permute-start.4 = (bf16[4,144,128]{2,1,0:T(8,128)(2,1)S(1)}, bf16[4,144,128]{2,1,0:T(8,128)(2,1)S(1)}, u32[]{:S(2)}, u32[]{:S(2)}) collective-permute-start(bf16[4,144,128]{2,1,0:T(8,128)(2,1)S(1)} %get-tuple-element.30), channel_id=1, source_target_pairs={{0,5},{5,0},{1,4},{4,1},{2,7},{7,2},{3,6},{6,3},{8,13},{13,8},{9,1... | collective-permute-start | bytes 442376 | tf_op jit(solution)/shard_map/ppermute | solution.py:656
  54.2 0.7 mixed_tokens.1
  54.9 2.4 %collective-permute-done.2.mid_ref = bf16[4,144,128]{2,1,0:T(8,128)(2,1)S(1)} collective-permute-done((bf16[4,144,128]{2,1,0:T(8,128)(2,1)S(1)}, bf16[4,144,128]{2,1,0:T(8,128)(2,1)S(1)}, u32[]{:S(2)}, u32[]{:S(2)}) %collective-permute-start.2) | collective-permute-done | bytes 147488 | tf_op jit(solution)/shard_map/ppermute | solution.py:657
  57.3 3.7 %collective-permute-done.3.row_ref = bf16[4,144,128]{2,1,0:T(8,128)(2,1)S(1)} collective-permute-done((bf16[4,144,128]{2,1,0:T(8,128)(2,1)S(1)}, bf16[4,144,128]{2,1,0:T(8,128)(2,1)S(1)}, u32[]{:S(2)}, u32[]{:S(2)}) %collective-permute-start.3) | collective-permute-done | bytes 147488 | tf_op jit(solution)/shard_map/ppermute | solution.py:658
  60.9 0.0 collective-permute-done.4.both_ref
  60.9 0.1 spread_gradients.1
  61.0 0.6 collective-permute-start.5
  61.6 0.5 collective-permute-start.6
  62.2 1.7 %collective-permute-start.7 = (bf16[144,128]{1,0:T(8,128)(2,1)S(1)}, bf16[144,128]{1,0:T(8,128)(2,1)S(1)}, u32[]{:S(2)}, u32[]{:S(2)}) collective-permute-start(bf16[144,128]{1,0:T(8,128)(2,1)S(1)} %get-tuple-element.35), channel_id=1, source_target_pairs={{0,8},{8,16},{16,24},{24,0},{1,9},{9,17},{17,25},{25,1},{2,10},{10... | collective-permute-start | bytes 110600 | tf_op jit(solution)/shard_map/ppermute | solution.py:683
  63.9 2.1 %collective-permute-start.8 = (bf16[144,128]{1,0:T(8,128)(2,1)S(1)}, bf16[144,128]{1,0:T(8,128)(2,1)S(1)}, u32[]{:S(2)}, u32[]{:S(2)}) collective-permute-start(bf16[144,128]{1,0:T(8,128)(2,1)S(1)} %get-tuple-element.36), channel_id=1, source_target_pairs={{0,24},{8,0},{16,8},{24,16},{1,25},{9,1},{17,9},{25,17},{2,26},{10... | collective-permute-start | bytes 110600 | tf_op jit(solution)/shard_map/ppermute | solution.py:683
  66.0 0.8 %collective-permute-done.5 = bf16[256,384]{1,0:T(8,128)(2,1)S(1)} collective-permute-done((bf16[256,384]{1,0:T(8,128)(2,1)S(1)}, bf16[256,384]{1,0:T(8,128)(2,1)S(1)}, u32[]{:S(2)}, u32[]{:S(2)}) %collective-permute-start.5) | collective-permute-done | bytes 196640 | tf_op jit(solution)/shard_map/ppermute | solution.py:684
  66.8 0.8 %pad_maximum_fusion = (bf16[2,16,2,8,384]{4,3,2,1,0:T(8,128)(2,1)S(1)}, bf16[2,16,16,384]{3,2,1,0:T(8,128)(2,1)}) fusion(bf16[2,16,1,8,384]{4,3,2,1,0:T(8,128)(2,1)S(1)} %bitcast.24, bf16[2,16,1,8,384]{4,3,2,1,0:T(8,128)(2,1)S(1)} %bitcast.23), kind=kLoop, calls=%fused_computation | loop fusion | flops 196608 | bytes 1179648 | tf_op jit(solution)/shard_map/concatenate | solution.py:687
  67.6 0.0 collective-permute-done.6.refs_1_
  67.6 0.4 collective-permute-done.7.refs_2_
  68.0 0.2 collective-permute-done.8.refs_3_
  68.2 0.7 %gradient_sum.1 = (f32[72,192]{1,0:T(8,128)}, f32[24,192]{1,0:T(8,128)}) custom-call(s32[1]{0:T(128)} %bitcast.refs_0_.row_ref, bf16[144,128]{1,0:T(8,128)(2,1)S(1)} %get-tuple-element.33.refs_0_, bf16[144,128]{1,0:T(8,128)(2,1)S(1)} %collective-permute-done.6.refs_1_, bf16[144,128]{1,0:T(8,128)(2,1)S(1)} %collective-permute-done.7.refs_2_, ...), custom_call_target="tpu_custom_call" | custom-call | tf_op jit(solution)/shard_map/gradient_sum/pallas_call | solution.py:690
  (2 shorter events, 0.1 us)
Async XLA Ops:
  0.6 22.1 %copy-start.2 = (bf16[384,1152]{1,0:T(8,128)(2,1)S(1)}, bf16[384,1152]{1,0:T(8,128)(2,1)}, u32[]{:S(2)}) copy-start(bf16[384,1152]{1,0:T(8,128)(2,1)} %project_ref.2) | copy-start | bytes 2654212
  2.5 7.5 %copy-start.3 = (bf16[2,16,16,384]{3,2,1,0:T(8,128)(2,1)S(1)}, bf16[2,16,16,384]{3,2,1,0:T(8,128)(2,1)}, u32[]{:S(2)}) copy-start(bf16[2,16,16,384]{3,2,1,0:T(8,128)(2,1)} %param.17) | copy-start | bytes 1179652
  2.5 20.2 %all-to-all-start = ((bf16[16,104,128]{2,1,0:T(8,128)(2,1)}), bf16[16,104,128]{2,1,0:T(8,128)(2,1)S(1)}, u32[]{:S(2)}, u32[]{:S(2)}) async-start(bf16[16,104,128]{2,1,0:T(8,128)(2,1)} %pack_tokens.1), calls=%async_computation | async-start | bytes 851968 | tf_op jit(solution)/shard_map/all_to_all | solution.py:546
  10.1 12.7 %copy-start.4 = (bf16[384,384]{1,0:T(8,128)(2,1)S(1)}, bf16[384,384]{1,0:T(8,128)(2,1)}, u32[]{:S(2)}) copy-start(bf16[384,384]{1,0:T(8,128)(2,1)} %output_ref.2) | copy-start | bytes 884740
  10.1 12.7 %copy-start.5 = (f32[12]{0:T(128)S(1)}, f32[12]{0:T(128)}, u32[]{:S(2)}) copy-start(f32[12]{0:T(128)} %slopes_ref.1) | copy-start | bytes 148
  10.1 7.3 %collective-permute-start = (bf16[2,16,8,384]{3,2,1,0:T(8,128)(2,1)S(1)}, bf16[2,16,8,384]{3,2,1,0:T(8,128)(2,1)S(1)}, u32[]{:S(2)}, u32[]{:S(2)}) collective-permute-start(bf16[2,16,8,384]{3,2,1,0:T(8,128)(2,1)S(1)} %dynamic-slice_bitcast_fusion), channel_id=1, source_target_pairs={{0,1},{1,0},{2,3},{3,2},{4,5},{5,4},{6,7},{7,6},{8,9},{9,8},{10,11... | collective-permute-start | bytes 589832 | tf_op jit(solution)/shard_map/ppermute | solution.py:531
  26.8 3.7 %copy-start = (bf16[384,384]{1,0:T(8,128)(2,1)S(1)}, bf16[384,384]{1,0:T(8,128)(2,1)}, u32[]{:S(2)}) copy-start(bf16[384,384]{1,0:T(8,128)(2,1)} %output_ref.3) | copy-start | bytes 884740
  26.8 16.8 %copy-start.1 = (bf16[384,1152]{1,0:T(8,128)(2,1)S(1)}, bf16[384,1152]{1,0:T(8,128)(2,1)}, u32[]{:S(2)}) copy-start(bf16[384,1152]{1,0:T(8,128)(2,1)} %project_ref.3) | copy-start | bytes 2654212
  26.8 16.7 %all-to-all-start.1 = ((bf16[32,16,384]{2,1,0:T(8,128)(2,1)}), bf16[32,16,384]{2,1,0:T(8,128)(2,1)S(1)}, u32[]{:S(2)}, u32[]{:S(2)}) async-start(bf16[32,16,384]{2,1,0:T(8,128)(2,1)} %bitcast.4), calls=%async_computation.1 | async-start | bytes 786432 | tf_op jit(solution)/shard_map/all_to_all | solution.py:603
  48.4 2.1 %collective-permute-start.1 = (bf16[2,8,144,128]{3,2,1,0:T(8,128)(2,1)S(1)}, bf16[2,8,144,128]{3,2,1,0:T(8,128)(2,1)S(1)}, u32[]{:S(2)}, u32[]{:S(2)}) collective-permute-start(bf16[2,8,144,128]{3,2,1,0:T(8,128)(2,1)S(1)} %get-tuple-element.25), channel_id=1, source_target_pairs={{0,2},{2,0},{1,3},{3,1},{4,6},{6,4},{5,7},{7,5},{8,10},{10,8},{9,1... | collective-permute-start | bytes 1769480 | tf_op jit(solution)/shard_map/ppermute | solution.py:644
  50.6 6.7 %collective-permute-start.2 = (bf16[4,144,128]{2,1,0:T(8,128)(2,1)S(1)}, bf16[4,144,128]{2,1,0:T(8,128)(2,1)S(1)}, u32[]{:S(2)}, u32[]{:S(2)}) collective-permute-start(bf16[4,144,128]{2,1,0:T(8,128)(2,1)S(1)} %get-tuple-element.28), channel_id=1, source_target_pairs={{0,4},{4,0},{1,5},{5,1},{2,6},{6,2},{3,7},{7,3},{8,12},{12,8},{9,1... | collective-permute-start | bytes 442376 | tf_op jit(solution)/shard_map/ppermute | solution.py:657
  52.2 8.8 %collective-permute-start.3 = (bf16[4,144,128]{2,1,0:T(8,128)(2,1)S(1)}, bf16[4,144,128]{2,1,0:T(8,128)(2,1)S(1)}, u32[]{:S(2)}, u32[]{:S(2)}) collective-permute-start(bf16[4,144,128]{2,1,0:T(8,128)(2,1)S(1)} %get-tuple-element.29), channel_id=1, source_target_pairs={{0,1},{1,0},{2,3},{3,2},{4,5},{5,4},{6,7},{7,6},{8,9},{9,8},{10,11... | collective-permute-start | bytes 442376 | tf_op jit(solution)/shard_map/ppermute | solution.py:658
  52.7 8.2 %collective-permute-start.4 = (bf16[4,144,128]{2,1,0:T(8,128)(2,1)S(1)}, bf16[4,144,128]{2,1,0:T(8,128)(2,1)S(1)}, u32[]{:S(2)}, u32[]{:S(2)}) collective-permute-start(bf16[4,144,128]{2,1,0:T(8,128)(2,1)S(1)} %get-tuple-element.30), channel_id=1, source_target_pairs={{0,5},{5,0},{1,4},{4,1},{2,7},{7,2},{3,6},{6,3},{8,13},{13,8},{9,1... | collective-permute-start | bytes 442376 | tf_op jit(solution)/shard_map/ppermute | solution.py:656
  61.0 5.7 %collective-permute-start.5 = (bf16[256,384]{1,0:T(8,128)(2,1)S(1)}, bf16[256,384]{1,0:T(8,128)(2,1)S(1)}, u32[]{:S(2)}, u32[]{:S(2)}) collective-permute-start(bf16[256,384]{1,0:T(8,128)(2,1)S(1)} %get-tuple-element.32), channel_id=1, source_target_pairs={{0,1},{1,0},{2,3},{3,2},{4,5},{5,4},{6,7},{7,6},{8,9},{9,8},{10,11... | collective-permute-start | bytes 589832 | tf_op jit(solution)/shard_map/ppermute | solution.py:684
  61.6 6.0 %collective-permute-start.6 = (bf16[144,128]{1,0:T(8,128)(2,1)S(1)}, bf16[144,128]{1,0:T(8,128)(2,1)S(1)}, u32[]{:S(2)}, u32[]{:S(2)}) collective-permute-start(bf16[144,128]{1,0:T(8,128)(2,1)S(1)} %get-tuple-element.34), channel_id=1, source_target_pairs={{0,16},{8,24},{16,0},{24,8},{1,17},{9,25},{17,1},{25,9},{2,18},{10... | collective-permute-start | bytes 110600 | tf_op jit(solution)/shard_map/ppermute | solution.py:683
  62.2 5.9 %collective-permute-start.7 = (bf16[144,128]{1,0:T(8,128)(2,1)S(1)}, bf16[144,128]{1,0:T(8,128)(2,1)S(1)}, u32[]{:S(2)}, u32[]{:S(2)}) collective-permute-start(bf16[144,128]{1,0:T(8,128)(2,1)S(1)} %get-tuple-element.35), channel_id=1, source_target_pairs={{0,8},{8,16},{16,24},{24,0},{1,9},{9,17},{17,25},{25,1},{2,10},{10... | collective-permute-start | bytes 110600 | tf_op jit(solution)/shard_map/ppermute | solution.py:683
  63.9 4.4 %collective-permute-start.8 = (bf16[144,128]{1,0:T(8,128)(2,1)S(1)}, bf16[144,128]{1,0:T(8,128)(2,1)S(1)}, u32[]{:S(2)}, u32[]{:S(2)}) collective-permute-start(bf16[144,128]{1,0:T(8,128)(2,1)S(1)} %get-tuple-element.36), channel_id=1, source_target_pairs={{0,24},{8,0},{16,8},{24,16},{1,25},{9,1},{17,9},{25,17},{2,26},{10... | collective-permute-start | bytes 110600 | tf_op jit(solution)/shard_map/ppermute | solution.py:683
